TPU v7x, 32 devices: a whole 2x2x4 slice. The times are simulated.
32 devices in a mesh: shard: 8 (over z, x), tensor: 4 (over y, core).
Axes of the slice: x: 2, y: 2, z: 4, core: 2. Of those that a mesh axis runs over, the one named last changes fastest.
Arguments:
- gradient: bfloat16 [768, 3072], P('shard', 'tensor'), may hold values from -12 to 12
- moment_one: float32 [768, 3072], P('shard', 'tensor'), may hold values from -6 to 6
- moment_two: float32 [768, 3072], P('shard', 'tensor'), may hold values from 0.5 to 8
- stat_left: float32 [768, 768], P('shard'), may hold values from -1 to 3, as said below
- stat_right: float32 [3072, 3072], P('shard', 'tensor'), may hold values from -1 to 3, as said below
- basis_left: float32 [768, 768], P('shard'), may hold values from -3 to 25, as said below
- basis_right: float32 [3072, 3072], P('shard', 'tensor'), may hold values from -3 to 47, as said below
Outputs:
- update: bfloat16 [768, 3072], P('shard', 'tensor')
- new_moment_one: float32 [768, 3072], P('shard', 'tensor')
- new_moment_two: float32 [768, 3072], P('shard', 'tensor')
- new_stat_left: float32 [768, 768], P('shard')
- new_stat_right: float32 [3072, 3072], P('shard', 'tensor')
- new_basis_left: float32 [768, 768], P('shard')
- new_basis_right: float32 [3072, 3072], P('shard', 'tensor')
Inputs may be any that keep to these rules, and one draw needn't show every extreme that they name: `stat_left`: symmetric and positive definite. `stat_right`: symmetric and positive definite. `basis_left`: full rank. `basis_right`: full rank.
All inputs are finite; a program needn't handle non-finite values.
Results may differ from a plain program's by a relative error of at most 0.011.
Values may be sent and summed in bfloat16 or wider, within the bound.
No kernel may reach another device: no remote copies, remote signals or barrier semaphores. Data moves between devices by JAX's collectives and lax.ppermute only.
A program may use at most 64 MiB of HBM per device.

v0:
```python
import math

import jax
import jax.numpy as jnp
from jax import lax
from jax.sharding import PartitionSpec as P

D = 768
FF = 3072
NS_STEPS = 2


beta_one = 0.95
beta_two = 0.95
beta_stat = 0.95
correction = 1.0 - 0.95**10
adam_eps = 1e-08
highest = lax.Precision.HIGHEST


def blend_stat(previous, product, divisor):
    return beta_stat * previous + (1.0 - beta_stat) * (product / divisor)


def adam_moments(rotated, moment_one, moment_two):
    first_moment = beta_one * moment_one + (1.0 - beta_one) * rotated
    second_moment = beta_two * moment_two + (1.0 - beta_two) * (rotated * rotated)
    direction = (
        first_moment / correction / (jnp.sqrt(second_moment / correction) + adam_eps)
    ).astype(jnp.bfloat16)
    return (first_moment, second_moment, direction)


def local(gradient, moment_one, moment_two, stat_left, stat_right, basis_left, basis_right):
    rows_left = gradient.shape[0]
    rows_right = stat_right.shape[0]
    cols_right = stat_right.shape[1]
    shard_pos = lax.axis_index("shard")
    tensor_pos = lax.axis_index("tensor")
    row_start = shard_pos * rows_left
    grad_cols = lax.all_gather(gradient, "shard", axis=0, tiled=True)
    left_terms = jnp.dot(gradient, grad_cols.T, preferred_element_type=jnp.float32)
    gram_rows = lax.psum(left_terms.astype(jnp.bfloat16), "tensor").astype(jnp.float32)
    new_stat_left = blend_stat(stat_left, gram_rows, FF)
    grad_whole = lax.all_gather(grad_cols, "tensor", axis=1, tiled=True)
    picked = lax.dynamic_slice_in_dim(grad_whole, shard_pos * rows_right, rows_right, 1)
    gram_block = jnp.dot(picked.T, grad_cols, preferred_element_type=jnp.float32)
    new_stat_right = blend_stat(stat_right, gram_block, D)
    basis_all = lax.all_gather(basis_left, "shard", axis=0, tiled=True)
    left_q_all = basis_all / math.sqrt(D)
    left_qb_all = left_q_all.astype(jnp.bfloat16)
    left_qb_own = lax.dynamic_slice_in_dim(left_qb_all, row_start, rows_left, 0)
    left_cols_own = lax.dynamic_slice_in_dim(left_qb_all, row_start, rows_left, 1)
    half_rotated = jnp.dot(left_cols_own.T, grad_cols, preferred_element_type=jnp.float32).astype(
        jnp.bfloat16
    )
    right_q = basis_right / math.sqrt(FF)
    right_qb = right_q.astype(jnp.bfloat16)
    right_cols_b = lax.all_gather(right_qb, "shard", axis=0, tiled=True)
    half_full = lax.all_gather(half_rotated, "tensor", axis=1, tiled=True)
    rotated = jnp.dot(half_full, right_cols_b, preferred_element_type=jnp.float32)
    new_moment_one, new_moment_two, direction = adam_moments(rotated, moment_one, moment_two)
    back_half = jnp.dot(
        left_qb_own,
        lax.all_gather(direction, "shard", axis=0, tiled=True),
        preferred_element_type=jnp.float32,
    ).astype(jnp.bfloat16)
    back_terms = jnp.dot(back_half, right_cols_b.T, preferred_element_type=jnp.float32)
    update = lax.psum_scatter(back_terms, "tensor", scatter_dimension=1, tiled=True).astype(
        jnp.bfloat16
    )
    stat_rows = lax.all_gather(new_stat_right, "tensor", axis=1, tiled=True)
    power_right = jnp.dot(
        stat_rows,
        lax.all_gather(right_q, "shard", axis=0, tiled=True),
        precision=highest,
        preferred_element_type=jnp.float32,
    )
    power_left = jnp.dot(
        new_stat_left, left_q_all, precision=highest, preferred_element_type=jnp.float32
    )
    local_left = jnp.sum(power_left * power_left)
    local_right = jnp.sum(power_right * power_right)
    total_left = lax.psum(local_left, "shard")
    total_right = lax.psum(local_right, ("shard", "tensor"))
    iterate_left = power_left * (math.sqrt(D) / (4.0 * jnp.sqrt(total_left)))
    for iteration in range(NS_STEPS):
        partial_gram = jnp.dot(
            iterate_left.T, iterate_left, precision=highest, preferred_element_type=jnp.float32
        )
        gram_left = lax.psum(partial_gram.astype(jnp.bfloat16), "shard").astype(jnp.float32)
        iterate_left = 1.5 * iterate_left - 0.5 * jnp.dot(
            iterate_left, gram_left, precision=highest, preferred_element_type=jnp.float32
        )
    iterate_right = power_right * (math.sqrt(FF) / (4.0 * jnp.sqrt(total_right)))
    row_ids = shard_pos * rows_right + lax.broadcasted_iota(jnp.int32, (rows_right, cols_right), 0)
    col_ids = tensor_pos * cols_right + lax.broadcasted_iota(jnp.int32, (rows_right, cols_right), 1)
    identity_tile = (row_ids == col_ids).astype(jnp.float32)
    for iteration in range(NS_STEPS):
        rounded_iterate = iterate_right.astype(jnp.bfloat16)
        iterate_rows = lax.all_gather(rounded_iterate, "tensor", axis=1, tiled=True)
        gram_right = lax.psum_scatter(
            jnp.dot(iterate_rows.T, rounded_iterate, preferred_element_type=jnp.float32).astype(
                jnp.bfloat16
            ),
            "shard",
            scatter_dimension=0,
            tiled=True,
        ).astype(jnp.float32)
        mixing = (1.5 * identity_tile - 0.5 * gram_right).astype(jnp.bfloat16)
        iterate_right = jnp.dot(
            iterate_rows,
            lax.all_gather(mixing, "shard", axis=0, tiled=True),
            preferred_element_type=jnp.float32,
        )
    return (
        update,
        new_moment_one,
        new_moment_two,
        new_stat_left,
        new_stat_right,
        iterate_left * math.sqrt(D),
        iterate_right * math.sqrt(FF),
    )


def solution(mesh):
    placed = (
        P("shard", "tensor"),
        P("shard", "tensor"),
        P("shard", "tensor"),
        P("shard", None),
        P("shard", "tensor"),
        P("shard", None),
        P("shard", "tensor"),
    )
    return jax.shard_map(
        local,
        mesh=mesh,
        in_specs=placed,
        out_specs=(
            P("shard", "tensor"),
            P("shard", "tensor"),
            P("shard", "tensor"),
            P("shard", None),
            P("shard", "tensor"),
            P("shard", None),
            P("shard", "tensor"),
        ),
        check_vma=False,
    )
```

profile of v0, /device:TPU:9, one launch (start us, length us, event | category | flops | bytes accessed | tf_op | source)
XLA Modules:
  0.0 1156.9 jit_solution(11626227218246106481)
XLA Ops:
  7.9 43.1 %all-gather.14.cloned.1.call-done = bf16[768,768]{1,0:T(8,128)(2,1)} async-done(((bf16[96,768]{1,0:T(8,128)(2,1)}), bf16[768,768]{1,0:T(8,128)(2,1)}) %all-gather.14.cloned.1.call-update) | async-done | bytes 1179664 | tf_op jit(solution)/shard_map/all_gather | solution.py:41
  51.1 39.6 %all-gather.20.cloned.1.call-done = bf16[768,3072]{1,0:T(8,128)(2,1)} async-done(((bf16[768,768]{1,0:T(8,128)(2,1)}), bf16[768,3072]{1,0:T(8,128)(2,1)}) %all-gather.20.cloned.1.call-update) | async-done | bytes 4718608 | tf_op jit(solution)/shard_map/all_gather | solution.py:45
  96.5 35.0 %all-gather.22.cloned.1.call-done = f32[384,3072]{1,0:T(8,128)} async-done(((f32[384,768]{1,0:T(8,128)}), f32[384,3072]{1,0:T(8,128)}) %all-gather.22.cloned.1.call-update) | async-done | bytes 4718608 | tf_op jit(solution)/shard_map/all_gather | solution.py:72
  131.5 138.0 %all-gather.24.cloned.1.call-done = f32[3072,768]{1,0:T(8,128)} async-done(((f32[384,768]{1,0:T(8,128)}), f32[3072,768]{1,0:T(8,128)}) %all-gather.24.cloned.1.call-update) | async-done | bytes 9437200 | tf_op jit(solution)/shard_map/all_gather | solution.py:75
  269.5 15.4 %multiply_reduce_fusion = (f32[]{:T(128)}, f32[384,768]{1,0:T(8,128)S(1)}) fusion(f32[384,3072]{1,0:T(8,128)} %all-gather.22.cloned.1.call-done, f32[3072,768]{1,0:T(8,128)} %all-gather.24.cloned.1.call-done), kind=kOutput, calls=%fused_computation.16 | convolution fusion | flops 10872225792 | bytes 15335428 | tf_op jit(solution)/shard_map/dot_general | solution.py:73
  284.9 40.1 %psum.39 = f32[]{:T(128)} all-reduce(f32[]{:T(128)} %get-tuple-element.14), channel_id=1, replica_groups=mesh['shard'=8,'tensor'=4] {'shard','tensor'}, use_global_device_ids=true, to_apply=%region_7.0 | all-reduce | flops 1 | bytes 8 | tf_op jit(solution)/shard_map/psum | solution.py:85
  326.6 26.3 %all-gather.26.cloned.1.call-done = bf16[384,3072]{1,0:T(8,128)(2,1)} async-done(((bf16[384,768]{1,0:T(8,128)(2,1)}), bf16[384,3072]{1,0:T(8,128)(2,1)}) %all-gather.26.cloned.1.call-update) | async-done | bytes 2359312 | tf_op jit(solution)/shard_map/all_gather | solution.py:101
  352.9 6.6 convolution_convert_fusion.1
  359.6 95.0 %reduce-scatter.6.cloned.1.call-done = bf16[384,768]{1,0:T(8,128)(2,1)} async-done(((bf16[3072,768]{1,0:T(8,128)(2,1)}), bf16[384,768]{1,0:T(8,128)(2,1)}) %reduce-scatter.6.cloned.1.call-update) | async-done | bytes 589840 | tf_op jit(solution)/shard_map/reduce_scatter | solution.py:102
  459.4 75.7 %all-gather.28.cloned.1.call-done = bf16[3072,768]{1,0:T(8,128)(2,1)} async-done(((bf16[384,768]{1,0:T(8,128)(2,1)}), bf16[3072,768]{1,0:T(8,128)(2,1)}) %all-gather.28.cloned.1.call-update) | async-done | bytes 4718608 | tf_op jit(solution)/shard_map/all_gather | solution.py:113
  535.1 5.9 convolution_convert_fusion.4
  541.3 27.4 %all-reduce.4.cloned.1.call-done = bf16[96,768]{1,0:T(8,128)(2,1)} async-done(((bf16[96,768]{1,0:T(8,128)(2,1)}), bf16[96,768]{1,0:T(8,128)(2,1)}) %all-reduce.4.cloned.1.call-update) | async-done | bytes 147472 | tf_op jit(solution)/shard_map/psum | solution.py:43
  569.7 53.5 %all-gather.12.cloned.1.call-done = f32[768,768]{1,0:T(8,128)} async-done(((f32[96,768]{1,0:T(8,128)}), f32[768,768]{1,0:T(8,128)}) %all-gather.12.cloned.1.call-update) | async-done | bytes 2359312 | tf_op jit(solution)/shard_map/all_gather | solution.py:49
  627.7 15.0 %psum.36 = f32[]{:T(128)} all-reduce(f32[]{:T(128)} %get-tuple-element.12), channel_id=1, replica_groups=mesh['shard'=8,'tensor'=4] {'shard'}, use_global_device_ids=true, to_apply=%region_3.0 | all-reduce | flops 1 | bytes 8 | tf_op jit(solution)/shard_map/psum | solution.py:84
  649.1 11.2 all_gather.38
  660.3 42.9 %all-gather.16.cloned.1.call-done = bf16[3072,768]{1,0:T(8,128)(2,1)} async-done(((bf16[384,768]{1,0:T(8,128)(2,1)}), bf16[3072,768]{1,0:T(8,128)(2,1)}) %all-gather.16.cloned.1.call-update) | async-done | bytes 4718608 | tf_op jit(solution)/shard_map/all_gather | solution.py:59
  707.5 22.0 %all-gather.30.cloned.1.call-done = bf16[384,3072]{1,0:T(8,128)(2,1)} async-done(((bf16[384,768]{1,0:T(8,128)(2,1)}), bf16[384,3072]{1,0:T(8,128)(2,1)}) %all-gather.30.cloned.1.call-update) | async-done | bytes 2359312 | tf_op jit(solution)/shard_map/all_gather | solution.py:101
  729.5 6.5 convolution_convert_fusion
  736.0 75.8 %all-reduce.6.cloned.1.call-done = bf16[768,768]{1,0:T(8,128)(2,1)} async-done(((bf16[768,768]{1,0:T(8,128)(2,1)}), bf16[768,768]{1,0:T(8,128)(2,1)}) %all-reduce.6.cloned.1.call-update) | async-done | bytes 1179664 | tf_op jit(solution)/shard_map/psum | solution.py:91
  817.0 37.7 %all-gather.18.cloned.1.call-done = bf16[768,768]{1,0:T(8,128)(2,1)} async-done(((bf16[96,768]{1,0:T(8,128)(2,1)}), bf16[768,768]{1,0:T(8,128)(2,1)}) %all-gather.18.cloned.1.call-update) | async-done | bytes 1179664 | tf_op jit(solution)/shard_map/all_gather | solution.py:65
  860.3 93.3 %reduce-scatter.8.cloned.1.call-done = bf16[384,768]{1,0:T(8,128)(2,1)} async-done(((bf16[3072,768]{1,0:T(8,128)(2,1)}), bf16[384,768]{1,0:T(8,128)(2,1)}) %reduce-scatter.8.cloned.1.call-update) | async-done | bytes 589840 | tf_op jit(solution)/shard_map/reduce_scatter | solution.py:102
  955.8 80.0 %all-reduce.8.cloned.1.call-done = bf16[768,768]{1,0:T(8,128)(2,1)} async-done(((bf16[768,768]{1,0:T(8,128)(2,1)}), bf16[768,768]{1,0:T(8,128)(2,1)}) %all-reduce.8.cloned.1.call-update) | async-done | bytes 1179664 | tf_op jit(solution)/shard_map/psum | solution.py:91
  1038.4 26.1 %reduce-scatter.4.cloned.1.call-done = f32[96,768]{1,0:T(8,128)} async-done(((f32[96,3072]{1,0:T(8,128)}), f32[96,768]{1,0:T(8,128)}) %reduce-scatter.4.cloned.1.call-update) | async-done | bytes 294928 | tf_op jit(solution)/shard_map/reduce_scatter | solution.py:69
  1066.1 78.9 %all-gather.32.cloned.1.call-done = bf16[3072,768]{1,0:T(8,128)(2,1)} async-done(((bf16[384,768]{1,0:T(8,128)(2,1)}), bf16[3072,768]{1,0:T(8,128)(2,1)}) %all-gather.32.cloned.1.call-update) | async-done | bytes 4718608 | tf_op jit(solution)/shard_map/all_gather | solution.py:113
  (78 shorter events, 50.5 us)
Async XLA Ops:
  7.2 43.8 %all-gather.14.cloned.1.call-start = ((), (), s32[]{:S(2)}) async-start(), calls=%async_computation.4 | async-start | bytes 1327104 | tf_op jit(solution)/shard_map/all_gather | solution.py:41
  7.9 82.8 %all-gather.20.cloned.1.call-start = ((), (), s32[]{:S(2)}) async-start(), calls=%async_computation.9 | async-start | bytes 5898240 | tf_op jit(solution)/shard_map/all_gather | solution.py:45
  51.0 80.4 %all-gather.22.cloned.1.call-start = ((), (), s32[]{:S(2)}) async-start(), calls=%async_computation.12 | async-start | bytes 5898240 | tf_op jit(solution)/shard_map/all_gather | solution.py:72
  93.9 175.7 %all-gather.24.cloned.1.call-start = ((), (), s32[]{:S(2)}) async-start(), calls=%async_computation.13 | async-start | bytes 10616832 | tf_op jit(solution)/shard_map/all_gather | solution.py:75
  96.5 256.5 %all-gather.26.cloned.1.call-start = ((), (), s32[]{:S(2)}) async-start(), calls=%async_computation.14 | async-start | bytes 2949120 | tf_op jit(solution)/shard_map/all_gather | solution.py:101
  326.6 128.0 %reduce-scatter.6.cloned.1.call-start = ((), (), s32[]{:S(2)}) async-start(), calls=%async_computation.15 | async-start | bytes 5308416 | tf_op jit(solution)/shard_map/reduce_scatter | solution.py:102
  359.5 97.3 %copy-start.6 = (bf16[96,768]{1,0:T(8,128)(2,1)S(1)}, bf16[96,768]{1,0:T(8,128)(2,1)}, u32[]{:S(2)}) copy-start(bf16[96,768]{1,0:T(8,128)(2,1)} %param.7) | copy-start | bytes 442372
  359.5 175.6 %all-gather.28.cloned.1.call-start = ((), (), s32[]{:S(2)}) async-start(), calls=%async_computation.16 | async-start | bytes 5308416 | tf_op jit(solution)/shard_map/all_gather | solution.py:113
  456.8 112.0 %all-reduce.4.cloned.1.call-start = ((), (), s32[]{:S(2)}) async-start(), calls=%async_computation.8 | async-start | bytes 294912 | tf_op jit(solution)/shard_map/psum | solution.py:43
  458.0 165.1 %all-gather.12.cloned.1.call-start = ((), (), s32[]{:S(2)}) async-start(), calls=%async_computation.3 | async-start | bytes 2654208 | tf_op jit(solution)/shard_map/all_gather | solution.py:49
  458.8 244.4 %all-gather.16.cloned.1.call-start = ((), (), s32[]{:S(2)}) async-start(), calls=%async_computation.5 | async-start | bytes 5308416 | tf_op jit(solution)/shard_map/all_gather | solution.py:59
  459.3 109.4 %copy-start.10 = (f32[96,768]{1,0:T(8,128)S(1)}, f32[96,768]{1,0:T(8,128)}, u32[]{:S(2)}) copy-start(f32[96,768]{1,0:T(8,128)} %param.10) | copy-start | bytes 884740
  459.4 270.1 %all-gather.30.cloned.1.call-start = ((), (), s32[]{:S(2)}) async-start(), calls=%async_computation.17 | async-start | bytes 2949120 | tf_op jit(solution)/shard_map/all_gather | solution.py:101
  541.1 270.8 %all-reduce.6.cloned.1.call-start = ((), (), s32[]{:S(2)}) async-start(), calls=%async_computation.10 | async-start | bytes 2359296 | tf_op jit(solution)/shard_map/psum | solution.py:91
  569.7 58.0 %copy-start.4 = (f32[96,768]{1,0:T(8,128)}, f32[96,768]{1,0:T(8,128)S(1)}, u32[]{:S(2)}) copy-start(f32[96,768]{1,0:T(8,128)S(1)} %multiply_add_fusion) | copy-start | bytes 884740
  647.8 206.9 %all-gather.18.cloned.1.call-start = ((), (), s32[]{:S(2)}) async-start(), calls=%async_computation.6 | async-start | bytes 1327104 | tf_op jit(solution)/shard_map/all_gather | solution.py:65
  648.1 55.1 %copy-start.8 = (f32[96,768]{1,0:T(8,128)S(1)}, f32[96,768]{1,0:T(8,128)}, u32[]{:S(2)}) copy-start(f32[96,768]{1,0:T(8,128)} %param.8) | copy-start | bytes 884740
  660.3 69.2 %copy-start.7 = (bf16[384,768]{1,0:T(8,128)(2,1)S(1)}, bf16[384,768]{1,0:T(8,128)(2,1)}, u32[]{:S(2)}) copy-start(bf16[384,768]{1,0:T(8,128)(2,1)} %convolution_convert_fusion.4) | copy-start | bytes 1769476
  707.4 246.2 %reduce-scatter.8.cloned.1.call-start = ((), (), s32[]{:S(2)}) async-start(), calls=%async_computation.18 | async-start | bytes 5308416 | tf_op jit(solution)/shard_map/reduce_scatter | solution.py:102
  735.9 75.9 %copy-start.2 = (f32[96,768]{1,0:T(8,128)S(1)}, f32[96,768]{1,0:T(8,128)}, u32[]{:S(2)}) copy-start(f32[96,768]{1,0:T(8,128)} %get-tuple-element.13) | copy-start | bytes 884740
  736.0 299.8 %all-reduce.8.cloned.1.call-start = ((), (), s32[]{:S(2)}) async-start(), calls=%async_computation.11 | async-start | bytes 2359296 | tf_op jit(solution)/shard_map/psum | solution.py:91
  816.9 247.6 %reduce-scatter.4.cloned.1.call-start = ((), (), s32[]{:S(2)}) async-start(), calls=%async_computation.7 | async-start | bytes 1474560 | tf_op jit(solution)/shard_map/reduce_scatter | solution.py:69
  860.0 285.0 %all-gather.32.cloned.1.call-start = ((), (), s32[]{:S(2)}) async-start(), calls=%async_computation.19 | async-start | bytes 5308416 | tf_op jit(solution)/shard_map/all_gather | solution.py:113
  955.7 189.3 %copy-start.11 = (bf16[384,3072]{1,0:T(8,128)(2,1)S(1)}, bf16[384,3072]{1,0:T(8,128)(2,1)}, u32[]{:S(2)}) copy-start(bf16[384,3072]{1,0:T(8,128)(2,1)} %all-gather.30.cloned.1.call-done) | copy-start | bytes 7077892
  (5 other events, 101.4 us)
Sparse Core Ops, SparseCore 0:
  10.2 40.7 all-gather.13
  52.6 38.0 all-gather.19
  94.0 37.4 all-gather.21
  134.1 135.3 all-gather.23
  326.7 26.1 all-gather.25
  359.6 94.9 reduce-scatter.5
  457.4 77.6 all-gather.27
  538.0 30.6 all-reduce.3
  571.1 51.9 all-gather.11
  625.4 77.7 all-gather.15
  704.8 24.5 all-gather.29
  733.2 78.5 all-reduce.5
  814.6 40.0 all-gather.17
  858.1 95.4 reduce-scatter.7
  957.0 78.7 all-reduce.7
  1038.3 26.1 reduce-scatter.3
  1067.1 77.8 all-gather.31
where the time goes:
time: 1160 us
  waiting for transfers between devices  992 us (86%)
  matrix products  70.6 us (6%)
  blocking collectives  66.3 us (6%)
  between operations  15.6 us (1%)
    reduce_scatter x2, waiting for transfers between devices, local(): lax.psum_scatter(jnp.dot(iterate_rows.T, rounded_iterate, preferred_eleme...  188 us
    psum x2, waiting for transfers between devices, local(): lax.psum(partial_gram.astype(jnp.bfloat16), 'shard').astype(jnp.float32)  156 us
    all_gather x2, waiting for transfers between devices, local(): lax.all_gather(mixing, 'shard', axis=0, tiled=True)  155 us
    all_gather x1, waiting for transfers between devices, local(): lax.all_gather(right_q, 'shard', axis=0, tiled=True)  138 us
    all_gather x1, waiting for transfers between devices, local(): basis_all = lax.all_gather(basis_left, 'shard', axis=0, tiled=True)  53.5 us
    all_gather x2, waiting for transfers between devices, local(): iterate_rows = lax.all_gather(rounded_iterate, 'tensor', axis=1, tiled=True)  48.3 us
    all_gather x1, waiting for transfers between devices, local(): grad_cols = lax.all_gather(gradient, 'shard', axis=0, tiled=True)  43.1 us
    all_gather x1, waiting for transfers between devices, local(): right_cols_b = lax.all_gather(right_qb, 'shard', axis=0, tiled=True)  42.9 us
  transfers between devices with their start and end apart: 17, of which 17 were waited for; matrix products, arithmetic and copies ran while one was open for 4% of the time, Pallas kernels for 0%

commit v1 on v0

--- a/solution.py
+++ b/solution.py
@@ -3,6 +3,8 @@
 import jax
 import jax.numpy as jnp
 from jax import lax
+from jax.experimental import pallas as pl
+from jax.experimental.pallas import tpu as pltpu
 from jax.sharding import PartitionSpec as P
 
 D = 768
@@ -31,7 +33,7 @@
     return (first_moment, second_moment, direction)
 
 
-def local(gradient, moment_one, moment_two, stat_left, stat_right, basis_left, basis_right):
+def local_general(gradient, moment_one, moment_two, stat_left, stat_right, basis_left, basis_right):
     rows_left = gradient.shape[0]
     rows_right = stat_right.shape[0]
     cols_right = stat_right.shape[1]
@@ -124,7 +126,300 @@
     )
 
 
+BF = jnp.bfloat16
+F32 = jnp.float32
+AXES = ("shard", "tensor")
+PATTERN = (4, 2, 2, 2)
+
+
+def dot_nn(a, b):
+    return jnp.dot(a, b, preferred_element_type=F32)
+
+
+def dot_nt(a, b):
+    return lax.dot_general(a, b, (((1,), (1,)), ((), ())), preferred_element_type=F32)
+
+
+def dot_tn(a, b):
+    return lax.dot_general(a, b, (((0,), (0,)), ((), ())), preferred_element_type=F32)
+
+
+def pairs(move):
+    nz, nx, ny, nc = PATTERN
+    out = []
+    for z in range(nz):
+        for x in range(nx):
+            for y in range(ny):
+                for c in range(nc):
+                    to = move(z, x, y, c)
+                    if 0 <= to[0] < nz:
+                        source = ((z * nx + x) * ny + y) * nc + c
+                        target = ((to[0] * nx + to[1]) * ny + to[2]) * nc + to[3]
+                        out.append((source, target))
+    return out
+
+
+def swap_x(a):
+    return lax.ppermute(a, AXES, pairs(lambda z, x, y, c: (z, 1 - x, y, c)))
+
+
+def swap_y(a):
+    return lax.ppermute(a, AXES, pairs(lambda z, x, y, c: (z, x, 1 - y, c)))
+
+
+def swap_core(a):
+    return lax.ppermute(a, AXES, pairs(lambda z, x, y, c: (z, x, y, 1 - c)))
+
+
+def step_z(a, by, first, last):
+    full = pairs(lambda z, x, y, c: (z + by if first <= z <= last else -1, x, y, c))
+    return lax.ppermute(a, AXES, full)
+
+
+def gather_z(a, z):
+    up1 = step_z(a, 1, 0, 2)
+    down1 = step_z(a, -1, 1, 3)
+    up2 = step_z(up1, 1, 1, 2)
+    down2 = step_z(down1, -1, 1, 2)
+    up3 = step_z(up2, 1, 2, 2)
+    down3 = step_z(down2, -1, 1, 1)
+    near = jnp.where(z % 2 == 0, down1, up1)
+    mid = jnp.where(z == 0, down2, jnp.where(z == 1, down1, jnp.where(z == 2, up1, up2)))
+    far = jnp.where(z == 0, down3, jnp.where(z == 1, down2, jnp.where(z == 2, up2, up3)))
+    return [a, near, mid, far]
+
+
+def places_z(z):
+    near = z + 1 - 2 * (z % 2)
+    mid = jnp.where(z == 0, 2, jnp.where(z == 1, 2, 1))
+    far = jnp.where(z < 2, 3, 0)
+    return [z, near, mid, far]
+
+
+def put(whole, part, row, col):
+    return lax.dynamic_update_slice(whole, part, (row, col))
+
+
+def gather_rows_zx(a, z, x):
+    rows = a.shape[0]
+    whole = jnp.zeros((8 * rows, a.shape[1]), a.dtype)
+    for block, place in zip(gather_z(a, z), places_z(z)):
+        whole = put(whole, block, (2 * place + x) * rows, 0)
+        whole = put(whole, swap_x(block), (2 * place + 1 - x) * rows, 0)
+    return whole
+
+
+def gather_rows_xz(a, z, x):
+    rows = a.shape[0]
+    other = swap_x(a)
+    pair = jnp.where(x == 0, jnp.concatenate([a, other]), jnp.concatenate([other, a]))
+    whole = jnp.zeros((8 * rows, a.shape[1]), a.dtype)
+    for block, place in zip(gather_z(pair, z), places_z(z)):
+        whole = put(whole, block, 2 * place * rows, 0)
+    return whole
+
+
+def gather_cols(a, y, core):
+    cols = a.shape[1]
+    far = swap_y(a)
+    whole = jnp.zeros((a.shape[0], 4 * cols), a.dtype)
+    whole = put(whole, a, 0, (2 * y + core) * cols)
+    whole = put(whole, swap_core(a), 0, (2 * y + 1 - core) * cols)
+    whole = put(whole, far, 0, (2 - 2 * y + core) * cols)
+    whole = put(whole, swap_core(far), 0, (3 - 2 * y - core) * cols)
+    return whole
+
+
+def gather_slabs(a, z):
+    half = a.shape[0] // 2
+    slabs = []
+    for block in gather_z(a, z):
+        over_x = swap_x(block)
+        over_y = swap_y(block)
+        diagonal = jnp.concatenate([swap_y(over_x[:half]), swap_x(over_y[half:])])
+        slab = jnp.concatenate(
+            [
+                jnp.concatenate([block, over_y], axis=1),
+                jnp.concatenate([over_x, diagonal], axis=1),
+            ]
+        )
+        slabs.append((slab, swap_core(slab)))
+    return slabs
+
+
+def refresh_kernel(scale_ref, *refs):
+    slabs = refs[:8]
+    rows_ref, out_ref, whole, inner, held, total, first, sems = refs[8:]
+    size = whole.shape[0]
+    tall = size // 4
+    wide = size // 2
+    square = scale_ref[0]
+
+    def copy(k):
+        return pltpu.make_async_copy(
+            slabs[k],
+            whole.at[pl.ds((k // 2) * tall, tall), pl.ds((k % 2) * wide, wide)],
+            sems.at[k],
+        )
+
+    for k in range(8):
+        copy(k).start()
+    held[...] = rows_ref[...]
+    total[...] = rows_ref[...].astype(F32)
+
+    def one_pass(i, carry):
+        def towards(j, carry):
+            @pl.when(i == 0)
+            def _():
+                for k in range(4):
+
+                    @pl.when(j == k)
+                    def _():
+                        copy(2 * k).wait()
+                        copy(2 * k + 1).wait()
+
+            span = pl.ds(pl.multiple_of(j * tall, tall), tall)
+            inner[:, span] = dot_nt(held[...], whole[span, :]).astype(BF)
+            return carry
+
+        lax.fori_loop(0, 4, towards, 0)
+        keep = jnp.where(i == 1, 0.0, 1.5)
+        take = jnp.where(i == 1, square, -0.5 * square)
+
+        def back(j, carry):
+            chunk = jnp.where(i == 3, 2 * j, j)
+            span = pl.ds(pl.multiple_of(chunk * tall, tall), tall)
+            value = keep * total[:, span] + take * dot_nn(inner[...], whole[:, span])
+            total[:, span] = value
+            held[:, span] = value.astype(BF)
+
+            @pl.when(i == 0)
+            def _():
+                first[:, span] = value
+
+            return carry
+
+        lax.fori_loop(0, jnp.where(i == 3, 2, 4), back, 0)
+        return carry
+
+    lax.fori_loop(0, 4, one_pass, 0)
+    last = scale_ref[1]
+    for k in range(2):
+        span = slice(2 * k * tall, (2 * k + 1) * tall)
+        out_ref[:, k * tall : (k + 1) * tall] = last * (
+            1.5 * first[:, span] - 0.5 * total[:, span]
+        )
+
+
+def refresh_rows(scales, slabs, rows):
+    size = rows.shape[1]
+    count = rows.shape[0]
+    return pl.pallas_call(
+        refresh_kernel,
+        out_shape=jax.ShapeDtypeStruct((count, size // 2), F32),
+        in_specs=[pl.BlockSpec(memory_space=pltpu.SMEM)]
+        + [pl.BlockSpec(memory_space=pl.ANY)] * 8
+        + [pl.BlockSpec(memory_space=pltpu.VMEM)],
+        out_specs=pl.BlockSpec(memory_space=pltpu.VMEM),
+        scratch_shapes=[
+            pltpu.VMEM((size, size), BF),
+            pltpu.VMEM((count, size), BF),
+            pltpu.VMEM((count, size), BF),
+            pltpu.VMEM((count, size), F32),
+            pltpu.VMEM((count, size), F32),
+            pltpu.SemaphoreType.DMA((8,)),
+        ],
+        compiler_params=pltpu.CompilerParams(vmem_limit_bytes=48 * 2**20),
+        cost_estimate=pl.CostEstimate(
+            flops=15 * count * size * size, bytes_accessed=2 * size * size, transcendentals=0
+        ),
+    )(scales, *[part for pair in slabs for part in pair], rows)
+
+
+def local_pattern(gradient, moment_one, moment_two, stat_left, stat_right, basis_left, basis_right):
+    rows_left = gradient.shape[0]
+    rows_right = stat_right.shape[0]
+    cols_right = stat_right.shape[1]
+    shard_pos = lax.axis_index("shard")
+    tensor_pos = lax.axis_index("tensor")
+    z, x = shard_pos // 2, shard_pos % 2
+    y, core = tensor_pos // 2, tensor_pos % 2
+
+    left_b = (basis_left / math.sqrt(D)).astype(BF)
+    right_b = (basis_right / math.sqrt(FF)).astype(BF)
+    stat_b = stat_right.astype(BF)
+
+    both = gather_rows_zx(jnp.concatenate([gradient, left_b], axis=1), z, x)
+    grad_cols, left_all = both[:, :cols_right], both[:, cols_right:]
+    right_cols = gather_rows_zx(right_b, z, x)
+    grad_whole = gather_cols(grad_cols, y, core)
+    stat_rows = gather_cols(stat_b, y, core)
+
+    share = (1.0 - beta_stat) / D
+    picked = lax.dynamic_slice_in_dim(grad_whole, shard_pos * rows_right, rows_right, 1)
+    carried = dot_nn(grad_whole, right_cols).astype(BF)
+    power_right = beta_stat * dot_nn(stat_rows, right_cols) + share * dot_tn(picked, carried)
+    new_stat_right = blend_stat(stat_right, dot_tn(picked, grad_cols), D)
+    slabs = gather_slabs(power_right.astype(BF), z)
+
+    left_cols_own = lax.dynamic_slice_in_dim(left_all, shard_pos * rows_left, rows_left, 1)
+    left_rows_own = lax.dynamic_slice_in_dim(left_all, shard_pos * rows_left, rows_left, 0)
+    rotated = dot_tn(left_cols_own, carried)
+    new_moment_one, new_moment_two, direction = adam_moments(rotated, moment_one, moment_two)
+    direction_cols = gather_rows_xz(direction, z, x)
+    back_half = dot_nn(left_rows_own, direction_cols).astype(BF)
+    back_terms = dot_nt(back_half, right_cols)
+    width = 2 * cols_right
+    away = lax.dynamic_slice_in_dim(back_terms, (1 - y) * width, width, 1).astype(BF)
+    near = lax.dynamic_slice_in_dim(back_terms, y * width, width, 1) + swap_y(away).astype(F32)
+    away = lax.dynamic_slice_in_dim(near, (1 - core) * cols_right, cols_right, 1).astype(BF)
+    near = lax.dynamic_slice_in_dim(near, core * cols_right, cols_right, 1)
+    update = (near + swap_core(away).astype(F32)).astype(BF)
+
+    grad_rows = lax.dynamic_slice_in_dim(grad_whole, shard_pos * rows_left, rows_left, 0)
+    new_stat_left = blend_stat(stat_left, dot_nt(grad_rows, grad_whole), FF)
+    power_left = dot_nn(new_stat_left.astype(BF), left_all)
+    power_all = gather_rows_xz(power_left.astype(BF), z, x)
+    total_left = jnp.sum(jnp.square(power_all.astype(F32)))
+    square_left = D / (16.0 * total_left)
+    keep = power_left
+    value = power_left
+    for turn in range(4):
+        across = dot_nt(value.astype(BF), power_all).astype(BF)
+        moved = square_left * dot_nn(across, power_all)
+        value = moved if turn == 1 else 1.5 * value - 0.5 * moved
+        if turn == 0:
+            keep = value
+    value = 1.5 * keep - 0.5 * value
+    new_basis_left = value * (math.sqrt(D) * jnp.sqrt(square_left))
+
+    total_right = sum(jnp.sum(jnp.square(part.astype(F32))) for pair in slabs for part in pair)
+    square_right = FF / (16.0 * total_right)
+    half = rows_right // 2
+    own = jnp.concatenate([part[:rows_right] for part in slabs[0]], axis=1)
+    own = lax.dynamic_slice_in_dim(own, core * half, half, 0)
+    scales = jnp.stack([square_right, math.sqrt(FF) * jnp.sqrt(square_right)])
+    fresh = refresh_rows(scales, slabs, own)
+    mine = fresh[:, :cols_right]
+    theirs = swap_core(fresh[:, cols_right:])
+    new_basis_right = jnp.where(
+        core == 0, jnp.concatenate([mine, theirs]), jnp.concatenate([theirs, mine])
+    )
+    return (
+        update,
+        new_moment_one,
+        new_moment_two,
+        new_stat_left,
+        new_stat_right,
+        new_basis_left,
+        new_basis_right,
+    )
+
+
 def solution(mesh):
+    nz, nx, ny, nc = PATTERN
+    fits = (mesh.shape["shard"], mesh.shape["tensor"]) == (nz * nx, ny * nc)
+    local = local_pattern if fits else local_general
     placed = (
         P("shard", "tensor"),
         P("shard", "tensor"),

time: 1160 us -> 413 us (0.36)
  waiting for transfers between devices: 992 us -> 69.3 us
  starting transfers between devices: 1.09 us -> 123 us
  other arithmetic: 9.29 us -> 80.2 us
  blocking collectives: 66.3 us -> 0 us
  Pallas kernels: 0 us -> 45.8 us
  local copies, waits for them, and re-layouts: 1.79 us -> 43.2 us
  matrix products: 70.6 us -> 37.1 us
    all_gather x11 -> x0, waiting for transfers between devices: 593 us -> none  [the longest x2 155 us: local(): lax.all_gather(mixing, 'shard', axis=0, tiled=True)]
    reduce_scatter x3 -> x0, waiting for transfers between devices: 214 us -> none  [the longest x2 188 us: local(): lax.psum_scatter(jnp.dot(iterate_rows.T, rounded_iterate, preferred_eleme...]
    psum x3 -> x0, waiting for transfers between devices: 183 us -> none  [the longest x2 156 us: local(): lax.psum(partial_gram.astype(jnp.bfloat16), 'shard').astype(jnp.float32)]
    ppermute x0 -> x69, starting transfers between devices: none -> 123 us  [the longest x30 73 us: step_z(): return lax.ppermute(a, AXES, full)]
    ppermute x0 -> x69, waiting for transfers between devices: none -> 69.3 us  [the longest x11 34 us: swap_y(): return lax.ppermute(a, AXES, pairs(lambda z, x, y, c: (z, x, 1 - y, c)))]
    psum x2 -> x0, blocking collectives: 55.1 us -> none  [the longest x1 40.1 us: local(): total_right = lax.psum(local_right, ('shard', 'tensor'))]
    reduce_sum x0 -> x9, other arithmetic: none -> 49.5 us  [the longest x8 48.3 us: local_pattern(): jnp.sum(jnp.square(part.astype(F32)))]
    pallas_call x0 -> x1, Pallas kernels: none -> 45.8 us  [refresh_rows(): pl.pallas_call(refresh_kernel, out_shape=jax.ShapeDtypeStruct((count, siz...]
  transfers between devices with their start and end apart: 17 -> 69, of which waited for: 17 -> 19; matrix products, arithmetic and copies ran while one was open for 4% -> 35% of each run, Pallas kernels for 0% -> 0%
where the time goes in v1:
time: 413 us; the launch traced here: 406 us
  starting transfers between devices  123 us (30%)
  other arithmetic  80.2 us (19%)
  waiting for transfers between devices  69.3 us (17%)
  Pallas kernels  45.8 us (11%)
  local copies, waits for them, and re-layouts  43.2 us (10%)
  matrix products  37.1 us (9%)
  between operations  7.56 us (2%)
    ppermute x30, starting transfers between devices, step_z(): return lax.ppermute(a, AXES, full)  73 us
    reduce_sum x8, other arithmetic, local_pattern(): jnp.sum(jnp.square(part.astype(F32)))  48.3 us
    pallas_call x1, Pallas kernels, refresh_rows(): pl.pallas_call(refresh_kernel, out_shape=jax.ShapeDtypeStruct((count, siz...  45.8 us
    ppermute x11, waiting for transfers between devices, swap_y(): return lax.ppermute(a, AXES, pairs(lambda z, x, y, c: (z, x, 1 - y, c)))  34 us
    ppermute x10, starting transfers between devices, swap_core(): return lax.ppermute(a, AXES, pairs(lambda z, x, y, c: (z, x, y, 1 - c)))  26.8 us
    dot_general x7, matrix products, dot_nn(): return jnp.dot(a, b, preferred_element_type=F32)  21.3 us
    dynamic_update_slice x14, local copies, waits for them, and re-layouts, put(): return lax.dynamic_update_slice(whole, part, (row, col))  21 us
    dynamic_update_slice x16, other arithmetic, put(): return lax.dynamic_update_slice(whole, part, (row, col))  20.7 us
  transfers between devices with their start and end apart: 69, of which 19 were waited for; matrix products, arithmetic and copies ran while one was open for 35% of the time, Pallas kernels for 0%

profile of v1, /device:TPU:9, one launch (start us, length us, event | category | flops | bytes accessed | tf_op | source)
XLA Modules:
  0.0 406.1 jit_solution(10010897491696040632)
XLA Ops:
  36.2 5.0 %collective-permute-start.15 = (bf16[384,768]{1,0:T(8,128)(2,1)}, bf16[384,768]{1,0:T(8,128)(2,1)}, u32[]{:S(2)}, u32[]{:S(2)}) collective-permute-start(bf16[384,768]{1,0:T(8,128)(2,1)} %get-tuple-element.37), channel_id=1, source_target_pairs={{0,8},{1,9},{2,10},{3,11},{4,12},{5,13},{6,14},{7,15},{8,16},{9,17... | collective-permute-start | bytes 1769480 | tf_op jit(solution)/shard_map/ppermute | solution.py:176
  54.9 4.2 %collective-permute-start.18 = (bf16[384,768]{1,0:T(8,128)(2,1)}, bf16[384,768]{1,0:T(8,128)(2,1)}, u32[]{:S(2)}, u32[]{:S(2)}) collective-permute-start(bf16[384,768]{1,0:T(8,128)(2,1)} %collective-permute-done.15), channel_id=1, source_target_pairs={{8,16},{9,17},{10,18},{11,19},{12,20},{13,21},{14,22},{15,23},{16,... | collective-permute-start | bytes 1769480 | tf_op jit(solution)/shard_map/ppermute | solution.py:176
  76.0 17.7 %collective-permute-done.40 = bf16[384,768]{1,0:T(8,128)(2,1)} collective-permute-done((bf16[384,768]{1,0:T(8,128)(2,1)}, bf16[384,768]{1,0:T(8,128)(2,1)}, u32[]{:S(2)}, u32[]{:S(2)}) %collective-permute-start.40) | collective-permute-done | bytes 589856 | tf_op jit(solution)/shard_map/ppermute | solution.py:167
  93.7 9.0 %collective-permute-start.10 = (bf16[768,768]{1,0:T(8,128)(2,1)}, bf16[768,768]{1,0:T(8,128)(2,1)}, u32[]{:S(2)}, u32[]{:S(2)}) collective-permute-start(bf16[768,768]{1,0:T(8,128)(2,1)} %get-tuple-element.40), channel_id=1, source_target_pairs={{0,1},{1,0},{2,3},{3,2},{4,5},{5,4},{6,7},{7,6},{8,9},{9,8},{10,11... | collective-permute-start | bytes 3538952 | tf_op jit(solution)/shard_map/ppermute | solution.py:171
  113.5 8.9 %collective-permute-done.22 = bf16[384,768]{1,0:T(8,128)(2,1)S(1)} collective-permute-done((bf16[384,768]{1,0:T(8,128)(2,1)}, bf16[384,768]{1,0:T(8,128)(2,1)S(1)}, u32[]{:S(2)}, u32[]{:S(2)}) %collective-permute-start.22) | collective-permute-done | bytes 589856 | tf_op jit(solution)/shard_map/ppermute | solution.py:163
  130.6 4.3 %fusion.13 = f32[96,768]{1,0:T(8,128)S(1)} fusion(bf16[768,3072]{1,0:T(8,128)(2,1)} %constant_dynamic-update-slice_fusion.14, s32[]{:T(128)S(6)} %select_n.374, f32[96,768]{1,0:T(8,128)S(1)} %copy-done.16), kind=kOutput, calls=%fused_computation.40 | convolution fusion | flops 453206016 | bytes 5898244 | tf_op jit(solution)/shard_map/dot_general | solution.py:140
  136.8 6.1 %convolution_convert_fusion = bf16[768,768]{1,0:T(8,128)(2,1)S(1)} fusion(bf16[768,3072]{1,0:T(8,128)(2,1)S(1)} %copy-done.3, bf16[3072,768]{1,0:T(8,128)(2,1)} %constant_dynamic-update-slice_fusion.6), kind=kOutput, calls=%fused_computation.16 | convolution fusion | flops 3624468480 | bytes 10616832 | tf_op jit(solution)/shard_map/dot_general | solution.py:136
  147.0 5.2 %fusion.2 = bf16[384,768]{1,0:T(8,128)(2,1)} fusion(f32[384,768]{1,0:T(8,128)S(1)} %convolution_multiply_fusion.1, bf16[384,3072]{1,0:T(8,128)(2,1)S(1)} %copy-done.10, bf16[3072,768]{1,0:T(8,128)(2,1)} %constant_dynamic-update-slice_fusion.6), kind=kOutput, calls=%fused_computation.22 | convolution fusion | flops 1812824064 | bytes 8847360 | tf_op jit(solution)/shard_map/dot_general | solution.py:136
  154.1 4.2 %collective-permute-start.47 = (bf16[384,768]{1,0:T(8,128)(2,1)}, bf16[384,768]{1,0:T(8,128)(2,1)}, u32[]{:S(2)}, u32[]{:S(2)}) collective-permute-start(bf16[384,768]{1,0:T(8,128)(2,1)} %fusion.2), channel_id=1, source_target_pairs={{8,0},{9,1},{10,2},{11,3},{12,4},{13,5},{14,6},{15,7},{16,8},{17,9... | collective-permute-start | bytes 1769480 | tf_op jit(solution)/shard_map/ppermute | solution.py:176
  168.4 7.0 %collective-permute-done.33 = bf16[192,768]{1,0:T(8,128)(2,1)} collective-permute-done((bf16[192,768]{1,0:T(8,128)(2,1)S(1)}, bf16[192,768]{1,0:T(8,128)(2,1)}, u32[]{:S(2)}, u32[]{:S(2)}) %collective-permute-start.33) | collective-permute-done | bytes 294944 | tf_op jit(solution)/shard_map/ppermute | solution.py:176
  200.4 4.8 %collective-permute-start.27 = (bf16[192,768]{1,0:T(8,128)(2,1)}, bf16[192,768]{1,0:T(8,128)(2,1)}, u32[]{:S(2)}, u32[]{:S(2)}) collective-permute-start(bf16[192,768]{1,0:T(8,128)(2,1)} %collective-permute-done.25), channel_id=1, source_target_pairs={{8,16},{9,17},{10,18},{11,19},{12,20},{13,21},{14,22},{15,23},{16,... | collective-permute-start | bytes 884744 | tf_op jit(solution)/shard_map/ppermute | solution.py:176
  222.3 7.3 %multiply_reduce_fusion.7 = (f32[]{:T(128)}, bf16[768,1536]{1,0:T(8,128)(2,1)S(1)}) fusion(bf16[192,768]{1,0:T(8,128)(2,1)S(1)} %collective-permute-done.45, bf16[192,768]{1,0:T(8,128)(2,1)S(1)} %collective-permute-done.44, bf16[384,768]{1,0:T(8,128)(2,1)} %collective-permute-done.43, bf16[384,768]{1,0:T(8,128)(2,1)} %collective-permute-done.42, ...), kind=kLoop, calls=%fused_computation.7 | loop fusion | flops 15335423 | bytes 4718596 | tf_op jit(solution)/shard_map/reduce_sum | solution.py:396
  243.1 5.3 %fusion.14 = f32[96,3072]{1,0:T(8,128)} fusion(bf16[3072,768]{1,0:T(8,128)(2,1)} %constant_dynamic-update-slice_fusion.6, bf16[768,768]{1,0:T(8,128)(2,1)} %select_dynamic-update-slice_fusion.3, bf16[768,768]{1,0:T(8,128)(2,1)} %get-tuple-element.38, s32[]{:T(128)S(6)} %select_n.374), kind=kOutput, calls=%fused_computation.46 | convolution fusion | flops 566304768 | bytes 7225348 | tf_op jit(solution)/shard_map/dot_general | solution.py:140
  250.1 8.0 %collective-permute-done.49 = bf16[384,768]{1,0:T(8,128)(2,1)} collective-permute-done((bf16[384,768]{1,0:T(8,128)(2,1)}, bf16[384,768]{1,0:T(8,128)(2,1)}, u32[]{:S(2)}, u32[]{:S(2)}) %collective-permute-start.49) | collective-permute-done | bytes 589856 | tf_op jit(solution)/shard_map/ppermute | solution.py:167
  258.2 14.1 %collective-permute-start.46 = (bf16[768,1536]{1,0:T(8,128)(2,1)S(1)}, bf16[768,1536]{1,0:T(8,128)(2,1)}, u32[]{:S(2)}, u32[]{:S(2)}) collective-permute-start(bf16[768,1536]{1,0:T(8,128)(2,1)S(1)} %get-tuple-element.14.refs_0_), channel_id=1, source_target_pairs={{0,1},{1,0},{2,3},{3,2},{4,5},{5,4},{6,7},{7,6},{8,9},{9,8},{10,11... | collective-permute-start | bytes 7077896 | tf_op jit(solution)/shard_map/ppermute | solution.py:171
  285.0 6.3 %multiply_reduce_fusion.5 = (f32[]{:T(128)}, bf16[768,1536]{1,0:T(8,128)(2,1)}) fusion(bf16[192,768]{1,0:T(8,128)(2,1)} %collective-permute-done.52, bf16[192,768]{1,0:T(8,128)(2,1)} %collective-permute-done.51, bf16[384,768]{1,0:T(8,128)(2,1)} %collective-permute-done.50, bf16[384,768]{1,0:T(8,128)(2,1)} %collective-permute-done.49, ...), kind=kLoop, calls=%fused_computation.5 | loop fusion | flops 15335423 | bytes 4718596 | tf_op jit(solution)/shard_map/reduce_sum | solution.py:396
  291.3 4.6 %collective-permute-done.58 = bf16[192,768]{1,0:T(8,128)(2,1)S(1)} collective-permute-done((bf16[192,768]{1,0:T(8,128)(2,1)S(1)}, bf16[192,768]{1,0:T(8,128)(2,1)S(1)}, u32[]{:S(2)}, u32[]{:S(2)}) %collective-permute-start.58) | collective-permute-done | bytes 294944 | tf_op jit(solution)/shard_map/ppermute | solution.py:167
  297.5 10.3 %multiply_reduce_fusion.3 = (f32[]{:T(128)}, bf16[768,1536]{1,0:T(8,128)(2,1)}) fusion(bf16[192,768]{1,0:T(8,128)(2,1)S(1)} %collective-permute-done.59, bf16[192,768]{1,0:T(8,128)(2,1)S(1)} %collective-permute-done.58, bf16[384,768]{1,0:T(8,128)(2,1)} %collective-permute-done.57, bf16[384,768]{1,0:T(8,128)(2,1)} %collective-permute-done.56, ...), kind=kLoop, calls=%fused_computation.3 | loop fusion | flops 15335423 | bytes 4718596 | tf_op jit(solution)/shard_map/reduce_sum | solution.py:396
  307.9 10.5 %multiply_reduce_fusion.1 = (f32[]{:T(128)}, bf16[768,1536]{1,0:T(8,128)(2,1)}) fusion(bf16[192,768]{1,0:T(8,128)(2,1)S(1)} %collective-permute-done.66, bf16[192,768]{1,0:T(8,128)(2,1)S(1)} %collective-permute-done.65, bf16[384,768]{1,0:T(8,128)(2,1)} %collective-permute-done.64, bf16[384,768]{1,0:T(8,128)(2,1)} %collective-permute-done.63, ...), kind=kLoop, calls=%fused_computation.1 | loop fusion | flops 15335423 | bytes 4718596 | tf_op jit(solution)/shard_map/reduce_sum | solution.py:396
  325.9 3.6 collective-permute-done.30
  339.4 3.5 multiply_reduce_fusion.4
  344.2 3.5 multiply_reduce_fusion.2
  348.9 3.5 multiply_reduce_fusion
  353.2 45.8 %shard_map.126 = f32[192,1536]{1,0:T(8,128)S(1)} custom-call(f32[2]{0:T(128)S(1)} %pad_maximum_fusion.1.scale_ref, bf16[768,1536]{1,0:T(8,128)(2,1)S(1)} %get-tuple-element.14.refs_0_, bf16[768,1536]{1,0:T(8,128)(2,1)} %collective-permute-done.46.refs_1_, bf16[768,1536]{1,0:T(8,128)(2,1)} %get-tuple-element.12.refs_2_, ...), custom_call_target="tpu_custom_call" | custom-call | flops 27179089920 | bytes 18874368 | tf_op jit(solution)/shard_map/pallas_call | solution.py:317
  (233 shorter events, 195.8 us)
Async XLA Ops:
  61.4 43.8 %collective-permute-start.11 = (bf16[768,768]{1,0:T(8,128)(2,1)}, bf16[768,768]{1,0:T(8,128)(2,1)}, u32[]{:S(2)}, u32[]{:S(2)}) collective-permute-start(bf16[768,768]{1,0:T(8,128)(2,1)} %get-tuple-element.40), channel_id=1, source_target_pairs={{0,2},{1,3},{2,0},{3,1},{4,6},{5,7},{6,4},{7,5},{8,10},{9,11},{10,... | collective-permute-start | bytes 3538952 | tf_op jit(solution)/shard_map/ppermute | solution.py:167
  65.9 27.8 %collective-permute-start.40 = (bf16[384,768]{1,0:T(8,128)(2,1)}, bf16[384,768]{1,0:T(8,128)(2,1)}, u32[]{:S(2)}, u32[]{:S(2)}) collective-permute-start(bf16[384,768]{1,0:T(8,128)(2,1)} %get-tuple-element.16), channel_id=1, source_target_pairs={{0,2},{1,3},{2,0},{3,1},{4,6},{5,7},{6,4},{7,5},{8,10},{9,11},{10,... | collective-permute-start | bytes 1769480 | tf_op jit(solution)/shard_map/ppermute | solution.py:167
  71.5 31.2 %collective-permute-start.19 = (bf16[384,768]{1,0:T(8,128)(2,1)}, bf16[384,768]{1,0:T(8,128)(2,1)}, u32[]{:S(2)}, u32[]{:S(2)}) collective-permute-start(bf16[384,768]{1,0:T(8,128)(2,1)} %get-tuple-element.33), channel_id=1, source_target_pairs={{0,4},{1,5},{2,6},{3,7},{4,0},{5,1},{6,2},{7,3},{8,12},{9,13},{10,... | collective-permute-start | bytes 1769480 | tf_op jit(solution)/shard_map/ppermute | solution.py:163
  72.0 32.8 %collective-permute-start.20 = (bf16[384,768]{1,0:T(8,128)(2,1)S(1)}, bf16[384,768]{1,0:T(8,128)(2,1)}, u32[]{:S(2)}, u32[]{:S(2)}) collective-permute-start(bf16[384,768]{1,0:T(8,128)(2,1)S(1)} %collective-permute-done.17), channel_id=1, source_target_pairs={{8,0},{9,1},{10,2},{11,3},{12,4},{13,5},{14,6},{15,7}} | collective-permute-start | bytes 1769480 | tf_op jit(solution)/shard_map/ppermute | solution.py:176
  74.1 31.2 %collective-permute-start.21 = (bf16[384,768]{1,0:T(8,128)(2,1)}, bf16[384,768]{1,0:T(8,128)(2,1)}, u32[]{:S(2)}, u32[]{:S(2)}) collective-permute-start(bf16[384,768]{1,0:T(8,128)(2,1)} %collective-permute-done.18), channel_id=1, source_target_pairs={{16,24},{17,25},{18,26},{19,27},{20,28},{21,29},{22,30},{23,31}} | collective-permute-start | bytes 1769480 | tf_op jit(solution)/shard_map/ppermute | solution.py:176
  93.7 29.5 %collective-permute-start.10 = (bf16[768,768]{1,0:T(8,128)(2,1)}, bf16[768,768]{1,0:T(8,128)(2,1)}, u32[]{:S(2)}, u32[]{:S(2)}) collective-permute-start(bf16[768,768]{1,0:T(8,128)(2,1)} %get-tuple-element.40), channel_id=1, source_target_pairs={{0,1},{1,0},{2,3},{3,2},{4,5},{5,4},{6,7},{7,6},{8,9},{9,8},{10,11... | collective-permute-start | bytes 3538952 | tf_op jit(solution)/shard_map/ppermute | solution.py:171
  105.2 23.0 %collective-permute-start.12 = (bf16[768,768]{1,0:T(8,128)(2,1)}, bf16[768,768]{1,0:T(8,128)(2,1)}, u32[]{:S(2)}, u32[]{:S(2)}) collective-permute-start(bf16[768,768]{1,0:T(8,128)(2,1)} %collective-permute-done.11), channel_id=1, source_target_pairs={{0,1},{1,0},{2,3},{3,2},{4,5},{5,4},{6,7},{7,6},{8,9},{9,8},{10,11... | collective-permute-start | bytes 3538952 | tf_op jit(solution)/shard_map/ppermute | solution.py:171
  136.0 22.4 %collective-permute-start.32 = (bf16[96,768]{1,0:T(8,128)(2,1)S(1)}, bf16[96,768]{1,0:T(8,128)(2,1)S(1)}, u32[]{:S(2)}, u32[]{:S(2)}) collective-permute-start(bf16[96,768]{1,0:T(8,128)(2,1)S(1)} %get-tuple-element.48), channel_id=1, source_target_pairs={{0,4},{1,5},{2,6},{3,7},{4,0},{5,1},{6,2},{7,3},{8,12},{9,13},{10,... | collective-permute-start | bytes 442376 | tf_op jit(solution)/shard_map/ppermute | solution.py:163
  152.2 34.7 %collective-permute-start.48 = (bf16[384,768]{1,0:T(8,128)(2,1)}, bf16[384,768]{1,0:T(8,128)(2,1)}, u32[]{:S(2)}, u32[]{:S(2)}) collective-permute-start(bf16[384,768]{1,0:T(8,128)(2,1)} %fusion.2), channel_id=1, source_target_pairs={{0,8},{1,9},{2,10},{3,11},{4,12},{5,13},{6,14},{7,15},{8,16},{9,17... | collective-permute-start | bytes 1769480 | tf_op jit(solution)/shard_map/ppermute | solution.py:176
  154.1 34.8 %collective-permute-start.47 = (bf16[384,768]{1,0:T(8,128)(2,1)}, bf16[384,768]{1,0:T(8,128)(2,1)}, u32[]{:S(2)}, u32[]{:S(2)}) collective-permute-start(bf16[384,768]{1,0:T(8,128)(2,1)} %fusion.2), channel_id=1, source_target_pairs={{8,0},{9,1},{10,2},{11,3},{12,4},{13,5},{14,6},{15,7},{16,8},{17,9... | collective-permute-start | bytes 1769480 | tf_op jit(solution)/shard_map/ppermute | solution.py:176
  186.9 25.2 %collective-permute-start.55 = (bf16[384,768]{1,0:T(8,128)(2,1)}, bf16[384,768]{1,0:T(8,128)(2,1)S(1)}, u32[]{:S(2)}, u32[]{:S(2)}) collective-permute-start(bf16[384,768]{1,0:T(8,128)(2,1)} %collective-permute-done.48), channel_id=1, source_target_pairs={{8,16},{9,17},{10,18},{11,19},{12,20},{13,21},{14,22},{15,23},{16,... | collective-permute-start | bytes 1769480 | tf_op jit(solution)/shard_map/ppermute | solution.py:176
  188.9 23.8 %collective-permute-start.54 = (bf16[384,768]{1,0:T(8,128)(2,1)}, bf16[384,768]{1,0:T(8,128)(2,1)S(1)}, u32[]{:S(2)}, u32[]{:S(2)}) collective-permute-start(bf16[384,768]{1,0:T(8,128)(2,1)} %collective-permute-done.47), channel_id=1, source_target_pairs={{8,0},{9,1},{10,2},{11,3},{12,4},{13,5},{14,6},{15,7},{16,8},{17,9... | collective-permute-start | bytes 1769480 | tf_op jit(solution)/shard_map/ppermute | solution.py:176
  212.8 18.3 %collective-permute-start.61 = (bf16[384,768]{1,0:T(8,128)(2,1)S(1)}, bf16[384,768]{1,0:T(8,128)(2,1)S(1)}, u32[]{:S(2)}, u32[]{:S(2)}) collective-permute-start(bf16[384,768]{1,0:T(8,128)(2,1)S(1)} %collective-permute-done.54), channel_id=1, source_target_pairs={{8,0},{9,1},{10,2},{11,3},{12,4},{13,5},{14,6},{15,7}} | collective-permute-start | bytes 1769480 | tf_op jit(solution)/shard_map/ppermute | solution.py:176
  236.3 37.7 %collective-permute-start.64 = (bf16[384,768]{1,0:T(8,128)(2,1)}, bf16[384,768]{1,0:T(8,128)(2,1)}, u32[]{:S(2)}, u32[]{:S(2)}) collective-permute-start(bf16[384,768]{1,0:T(8,128)(2,1)} %get-tuple-element.43), channel_id=1, source_target_pairs={{0,4},{1,5},{2,6},{3,7},{4,0},{5,1},{6,2},{7,3},{8,12},{9,13},{10,... | collective-permute-start | bytes 1769480 | tf_op jit(solution)/shard_map/ppermute | solution.py:163
  237.3 37.1 %collective-permute-start.63 = (bf16[384,768]{1,0:T(8,128)(2,1)}, bf16[384,768]{1,0:T(8,128)(2,1)}, u32[]{:S(2)}, u32[]{:S(2)}) collective-permute-start(bf16[384,768]{1,0:T(8,128)(2,1)} %get-tuple-element.43), channel_id=1, source_target_pairs={{0,2},{1,3},{2,0},{3,1},{4,6},{5,7},{6,4},{7,5},{8,10},{9,11},{10,... | collective-permute-start | bytes 1769480 | tf_op jit(solution)/shard_map/ppermute | solution.py:167
  237.7 20.5 %collective-permute-start.49 = (bf16[384,768]{1,0:T(8,128)(2,1)}, bf16[384,768]{1,0:T(8,128)(2,1)}, u32[]{:S(2)}, u32[]{:S(2)}) collective-permute-start(bf16[384,768]{1,0:T(8,128)(2,1)} %get-tuple-element.45), channel_id=1, source_target_pairs={{0,2},{1,3},{2,0},{3,1},{4,6},{5,7},{6,4},{7,5},{8,10},{9,11},{10,... | collective-permute-start | bytes 1769480 | tf_op jit(solution)/shard_map/ppermute | solution.py:167
  240.6 39.2 %collective-permute-start.57 = (bf16[384,768]{1,0:T(8,128)(2,1)}, bf16[384,768]{1,0:T(8,128)(2,1)}, u32[]{:S(2)}, u32[]{:S(2)}) collective-permute-start(bf16[384,768]{1,0:T(8,128)(2,1)} %get-tuple-element.44), channel_id=1, source_target_pairs={{0,4},{1,5},{2,6},{3,7},{4,0},{5,1},{6,2},{7,3},{8,12},{9,13},{10,... | collective-permute-start | bytes 1769480 | tf_op jit(solution)/shard_map/ppermute | solution.py:163
  242.7 38.9 %collective-permute-start.56 = (bf16[384,768]{1,0:T(8,128)(2,1)}, bf16[384,768]{1,0:T(8,128)(2,1)}, u32[]{:S(2)}, u32[]{:S(2)}) collective-permute-start(bf16[384,768]{1,0:T(8,128)(2,1)} %get-tuple-element.44), channel_id=1, source_target_pairs={{0,2},{1,3},{2,0},{3,1},{4,6},{5,7},{6,4},{7,5},{8,10},{9,11},{10,... | collective-permute-start | bytes 1769480 | tf_op jit(solution)/shard_map/ppermute | solution.py:167
  258.2 73.3 %collective-permute-start.46 = (bf16[768,1536]{1,0:T(8,128)(2,1)S(1)}, bf16[768,1536]{1,0:T(8,128)(2,1)}, u32[]{:S(2)}, u32[]{:S(2)}) collective-permute-start(bf16[768,1536]{1,0:T(8,128)(2,1)S(1)} %get-tuple-element.14.refs_0_), channel_id=1, source_target_pairs={{0,1},{1,0},{2,3},{3,2},{4,5},{5,4},{6,7},{7,6},{8,9},{9,8},{10,11... | collective-permute-start | bytes 7077896 | tf_op jit(solution)/shard_map/ppermute | solution.py:171
  279.9 27.9 %collective-permute-start.65 = (bf16[192,768]{1,0:T(8,128)(2,1)S(1)}, bf16[192,768]{1,0:T(8,128)(2,1)S(1)}, u32[]{:S(2)}, u32[]{:S(2)}) collective-permute-start(bf16[192,768]{1,0:T(8,128)(2,1)S(1)} %slice.60), channel_id=1, source_target_pairs={{0,2},{1,3},{2,0},{3,1},{4,6},{5,7},{6,4},{7,5},{8,10},{9,11},{10,... | collective-permute-start | bytes 884744 | tf_op jit(solution)/shard_map/ppermute | solution.py:167
  281.6 26.2 %collective-permute-start.66 = (bf16[192,768]{1,0:T(8,128)(2,1)S(1)}, bf16[192,768]{1,0:T(8,128)(2,1)S(1)}, u32[]{:S(2)}, u32[]{:S(2)}) collective-permute-start(bf16[192,768]{1,0:T(8,128)(2,1)S(1)} %slice.61), channel_id=1, source_target_pairs={{0,4},{1,5},{2,6},{3,7},{4,0},{5,1},{6,2},{7,3},{8,12},{9,13},{10,... | collective-permute-start | bytes 884744 | tf_op jit(solution)/shard_map/ppermute | solution.py:163
  295.9 43.5 %collective-permute-start.53 = (bf16[768,1536]{1,0:T(8,128)(2,1)}, bf16[768,1536]{1,0:T(8,128)(2,1)}, u32[]{:S(2)}, u32[]{:S(2)}) collective-permute-start(bf16[768,1536]{1,0:T(8,128)(2,1)} %get-tuple-element.12.refs_2_), channel_id=1, source_target_pairs={{0,1},{1,0},{2,3},{3,2},{4,5},{5,4},{6,7},{7,6},{8,9},{9,8},{10,11... | collective-permute-start | bytes 7077896 | tf_op jit(solution)/shard_map/ppermute | solution.py:171
  307.8 36.4 %collective-permute-start.60 = (bf16[768,1536]{1,0:T(8,128)(2,1)}, bf16[768,1536]{1,0:T(8,128)(2,1)}, u32[]{:S(2)}, u32[]{:S(2)}) collective-permute-start(bf16[768,1536]{1,0:T(8,128)(2,1)} %get-tuple-element.10.refs_4_), channel_id=1, source_target_pairs={{0,1},{1,0},{2,3},{3,2},{4,5},{5,4},{6,7},{7,6},{8,9},{9,8},{10,11... | collective-permute-start | bytes 7077896 | tf_op jit(solution)/shard_map/ppermute | solution.py:171
  318.3 30.6 %collective-permute-start.67 = (bf16[768,1536]{1,0:T(8,128)(2,1)}, bf16[768,1536]{1,0:T(8,128)(2,1)}, u32[]{:S(2)}, u32[]{:S(2)}) collective-permute-start(bf16[768,1536]{1,0:T(8,128)(2,1)} %get-tuple-element.8.refs_6_), channel_id=1, source_target_pairs={{0,1},{1,0},{2,3},{3,2},{4,5},{5,4},{6,7},{7,6},{8,9},{9,8},{10,11... | collective-permute-start | bytes 7077896 | tf_op jit(solution)/shard_map/ppermute | solution.py:171
  (65 other events, 737.3 us)

commit v2 on v0

--- a/solution.py
+++ b/solution.py
@@ -1,8 +1,11 @@
+import functools
 import math
 
 import jax
 import jax.numpy as jnp
 from jax import lax
+from jax.experimental import pallas as pl
+from jax.experimental.pallas import tpu as pltpu
 from jax.sharding import PartitionSpec as P
 
 D = 768
@@ -31,7 +34,7 @@
     return (first_moment, second_moment, direction)
 
 
-def local(gradient, moment_one, moment_two, stat_left, stat_right, basis_left, basis_right):
+def local_general(gradient, moment_one, moment_two, stat_left, stat_right, basis_left, basis_right):
     rows_left = gradient.shape[0]
     rows_right = stat_right.shape[0]
     cols_right = stat_right.shape[1]
@@ -124,7 +127,435 @@
     )
 
 
+BF = jnp.bfloat16
+F32 = jnp.float32
+AXES = ("shard", "tensor")
+PATTERN = (4, 2, 2, 2)
+
+
+def dot_nn(a, b):
+    return jnp.dot(a, b, preferred_element_type=F32)
+
+
+def dot_nt(a, b):
+    return lax.dot_general(a, b, (((1,), (1,)), ((), ())), preferred_element_type=F32)
+
+
+def dot_tn(a, b):
+    return lax.dot_general(a, b, (((0,), (0,)), ((), ())), preferred_element_type=F32)
+
+
+def pairs(move):
+    nz, nx, ny, nc = PATTERN
+    out = []
+    for z in range(nz):
+        for x in range(nx):
+            for y in range(ny):
+                for c in range(nc):
+                    to = move(z, x, y, c)
+                    if 0 <= to[0] < nz:
+                        source = ((z * nx + x) * ny + y) * nc + c
+                        target = ((to[0] * nx + to[1]) * ny + to[2]) * nc + to[3]
+                        out.append((source, target))
+    return out
+
+
+def swap_x(a):
+    return lax.ppermute(a, AXES, pairs(lambda z, x, y, c: (z, 1 - x, y, c)))
+
+
+def swap_y(a):
+    return lax.ppermute(a, AXES, pairs(lambda z, x, y, c: (z, x, 1 - y, c)))
+
+
+def swap_core(a):
+    return lax.ppermute(a, AXES, pairs(lambda z, x, y, c: (z, x, y, 1 - c)))
+
+
+def send_up(a):
+    return lax.ppermute(a, AXES, pairs(lambda z, x, y, c: (z + 1, x, y, c)))
+
+
+def send_down(a):
+    return lax.ppermute(a, AXES, pairs(lambda z, x, y, c: (z - 1, x, y, c)))
+
+
+def turn_over(a, straight):
+    crossed = pairs(lambda z, x, y, c: (z if x != c else -1, 1 - x, y, 1 - c))
+    return jnp.where(straight, a, lax.ppermute(a, AXES, crossed))
+
+
+def stage(*parts):
+    return lax.optimization_barrier(parts)
+
+
+def near_of(z, up, down):
+    return jnp.where(z % 2 == 0, down, up)
+
+
+def mid_of(z, up1, down1, up2, down2):
+    return jnp.where(z == 0, down2, jnp.where(z == 1, down1, jnp.where(z == 2, up1, up2)))
+
+
+def far_of(z, up2, down2, up3, down3):
+    return jnp.where(z == 0, down3, jnp.where(z == 1, down2, jnp.where(z == 2, up2, up3)))
+
+
+def in_order(z, own, near, mid, far):
+    places = (z, z + 1 - 2 * (z % 2), jnp.where(z < 2, 2, 1), jnp.where(z < 2, 3, 0))
+    whole = jnp.zeros((4,) + own.shape, own.dtype)
+    for block, place in zip((own, near, mid, far), places):
+        whole = lax.dynamic_update_slice(whole, block[None], (place,) + (0,) * own.ndim)
+    return whole
+
+
+def along_z(z, own, steps):
+    (up1, down1), (up2, down2), (up3, down3) = steps
+    return in_order(
+        z,
+        own,
+        near_of(z, up1, down1),
+        mid_of(z, up1, down1, up2, down2),
+        far_of(z, up2, down2, up3, down3),
+    )
+
+
+def put(whole, part, *start):
+    return lax.dynamic_update_slice(whole, part, start)
+
+
+def interleave(core, mine, theirs):
+    rows, cols = mine.shape[1:]
+    whole = jnp.zeros((4, 2, rows, cols), mine.dtype)
+    whole = put(whole, mine[:, None], 0, core, 0, 0)
+    whole = put(whole, theirs[:, None], 0, 1 - core, 0, 0)
+    return whole.reshape(8 * rows, cols)
+
+
+def pass_kernel(turn, scale_ref, *refs):
+    slabs = refs[:8]
+    if turn == 0:
+        rows_ref, out_ref, square_ref, whole, inner, held, sums, sems = refs[8:]
+    elif turn == 3:
+        rows_ref, first_ref, out_ref, whole, inner, held, sems = refs[8:]
+    else:
+        rows_ref, out_ref, whole, inner, held, sems = refs[8:]
+    size = whole.shape[0]
+    tall = size // 4
+    half = size // 8
+
+    def copy(k):
+        return pltpu.make_async_copy(
+            slabs[k], whole.at[pl.ds(k * half, half), :], sems.at[k]
+        )
+
+    for k in range(8):
+        copy(k).start()
+    held[...] = rows_ref[...].astype(BF)
+    if turn == 0:
+        sums[...] = jnp.zeros_like(sums)
+
+    def towards(j, carry):
+        for k in range(4):
+
+            @pl.when(j == k)
+            def _():
+                copy(2 * k).wait()
+                copy(2 * k + 1).wait()
+
+        span = pl.ds(pl.multiple_of(j * tall, tall), tall)
+        inner[:, span] = dot_nt(held[...], whole[span, :]).astype(BF)
+        if turn == 0:
+            for part in range(4):
+                cols = slice(part * tall, (part + 1) * tall)
+
+                def add(i, total):
+                    start = pl.multiple_of(j * tall + i * 16, 16)
+                    block = whole[pl.ds(start, 16), cols].astype(F32)
+                    return total + block * block
+
+                zero = jnp.zeros((16, tall), F32)
+                sums[...] += lax.fori_loop(0, tall // 16, add, zero)
+        return carry
+
+    lax.fori_loop(0, 4, towards, 0)
+    if turn == 0:
+        square = scale_ref[0] / jnp.sum(sums[...])
+        square_ref[0] = square
+    else:
+        square = scale_ref[0]
+
+    def back(j, carry):
+        span = pl.ds(pl.multiple_of(j * tall, tall), tall)
+        moved = square * dot_nn(inner[...], whole[:, span])
+        if turn == 1:
+            out_ref[:, span] = moved
+        else:
+            value = 1.5 * rows_ref[:, span].astype(F32) - 0.5 * moved
+            if turn == 3:
+                value = scale_ref[1] * (1.5 * first_ref[:, span] - 0.5 * value)
+            out_ref[:, span] = value
+        return carry
+
+    lax.fori_loop(0, 2 if turn == 3 else 4, back, 0)
+
+
+def refresh_pass(turn, scales, slabs, *rows):
+    count, size = rows[0].shape
+    in_vmem = pl.BlockSpec(memory_space=pltpu.VMEM)
+    in_smem = pl.BlockSpec(memory_space=pltpu.SMEM)
+    shapes = [jax.ShapeDtypeStruct((count, size // 2 if turn == 3 else size), F32)]
+    scratch = [
+        pltpu.VMEM((size, size), BF),
+        pltpu.VMEM((count, size), BF),
+        pltpu.VMEM((count, size), BF),
+    ]
+    if turn == 0:
+        shapes.append(jax.ShapeDtypeStruct((1,), F32))
+        scratch.append(pltpu.VMEM((16, size // 4), F32))
+    return pl.pallas_call(
+        functools.partial(pass_kernel, turn),
+        out_shape=shapes,
+        in_specs=[in_smem] + [pl.BlockSpec(memory_space=pl.ANY)] * 8 + [in_vmem] * len(rows),
+        out_specs=[in_vmem, in_smem][: len(shapes)],
+        scratch_shapes=scratch + [pltpu.SemaphoreType.DMA((8,))],
+        compiler_params=pltpu.CompilerParams(vmem_limit_bytes=40 * 2**20),
+        cost_estimate=pl.CostEstimate(
+            flops=4 * count * size * size, bytes_accessed=2 * size * size, transcendentals=0
+        ),
+    )(scales, *slabs, *rows)
+
+
+def local_pattern(gradient, moment_one, moment_two, stat_left, stat_right, basis_left, basis_right):
+    rows_left = gradient.shape[0]
+    rows_right = stat_right.shape[0]
+    cols_right = stat_right.shape[1]
+    shard_pos = lax.axis_index("shard")
+    tensor_pos = lax.axis_index("tensor")
+    z, x = shard_pos // 2, shard_pos % 2
+    y, core = tensor_pos // 2, tensor_pos % 2
+    straight = x == core
+    half = rows_right // 2
+
+    left_b = (basis_left / math.sqrt(D)).astype(BF)
+    right_b = (basis_right / math.sqrt(FF)).astype(BF)
+    stat_b = stat_right.astype(BF)
+    part_left = rows_left // 2
+    small = jnp.concatenate(
+        [gradient, lax.dynamic_slice_in_dim(left_b, y * part_left, part_left, 0)]
+    )
+    rows_small = small.shape[0]
+
+    turned, small_u1, small_d1 = stage(
+        turn_over(right_b, straight), send_up(small), send_down(small)
+    )
+    both_u, both_d, stat_x, stat_y = stage(
+        send_up(jnp.concatenate([turned, small_u1])),
+        send_down(jnp.concatenate([turned, small_d1])),
+        swap_x(stat_b),
+        swap_y(stat_b),
+    )
+    turned_u1, small_u2 = both_u[:rows_right], both_u[rows_right:]
+    turned_d1, small_d2 = both_d[:rows_right], both_d[rows_right:]
+    both_u, both_d, stat_hi, stat_lo = stage(
+        send_up(both_u), send_down(both_d), swap_x(stat_y[half:]), swap_y(stat_x[:half])
+    )
+    turned_u2, small_u3 = both_u[:rows_right], both_u[rows_right:]
+    turned_d2, small_d3 = both_d[:rows_right], both_d[rows_right:]
+    small_z = along_z(
+        z, small, [(small_u1, small_d1), (small_u2, small_d2), (small_u3, small_d3)]
+    ).reshape(4 * rows_small, cols_right)
+    stat_xy = jnp.concatenate([stat_lo, stat_hi])
+    stat_keep = [jnp.where(straight, stat_b, stat_x), jnp.where(straight, stat_y, stat_xy)]
+    stat_send = [jnp.where(straight, stat_x, stat_b), jnp.where(straight, stat_xy, stat_y)]
+    turned_u3, turned_d3, small_x, small_y, stat_got = stage(
+        send_up(turned_u2),
+        send_down(turned_d2),
+        swap_x(small_z),
+        swap_y(small_z),
+        swap_core(jnp.concatenate(stat_send)),
+    )
+    turned_z = along_z(
+        z,
+        turned,
+        [(turned_u1, turned_d1), (turned_u2, turned_d2), (turned_u3, turned_d3)],
+    )
+    stat_rows = jnp.zeros((rows_right, 4 * cols_right), BF)
+    stat_rows = put(stat_rows, stat_keep[0], 0, (2 * y + core) * cols_right)
+    stat_rows = put(stat_rows, stat_keep[1], 0, (2 - 2 * y + core) * cols_right)
+    stat_rows = put(stat_rows, stat_got[:rows_right], 0, (2 * y + 1 - core) * cols_right)
+    stat_rows = put(stat_rows, stat_got[rows_right:], 0, (3 - 2 * y - core) * cols_right)
+    some = 2 * rows_small
+    small_hi, small_lo, turned_got = stage(
+        swap_x(small_y[some:]), swap_y(small_x[:some]), swap_core(turned_z)
+    )
+    right_cols = interleave(core, turned_z, turned_got)
+    grad_core = jnp.zeros((4, 2, rows_left, 2 * cols_right), BF)
+    left_all = jnp.zeros((4, 2, 2, part_left, cols_right), BF)
+    small_xy = jnp.concatenate([small_lo, small_hi])
+    for block, at_x, at_y in (
+        (small_z, x, y),
+        (small_x, 1 - x, y),
+        (small_y, x, 1 - y),
+        (small_xy, 1 - x, 1 - y),
+    ):
+        block = block.reshape(4, 1, rows_small, cols_right)
+        grad_core = put(grad_core, block[:, :, :rows_left], 0, at_x, 0, at_y * cols_right)
+        left_all = put(left_all, block[:, :, None, rows_left:], 0, at_x, at_y, 0, 0)
+    grad_core = grad_core.reshape(8 * rows_left, 2 * cols_right)
+    left_all = left_all.reshape(8 * rows_left, cols_right)
+    (grad_other,) = stage(swap_core(grad_core))
+    grad_whole = jnp.zeros((8 * rows_left, 4 * cols_right), BF)
+    for k in range(2):
+        cols = slice(k * cols_right, (k + 1) * cols_right)
+        grad_whole = put(grad_whole, grad_core[:, cols], 0, (2 * k + core) * cols_right)
+        grad_whole = put(grad_whole, grad_other[:, cols], 0, (2 * k + 1 - core) * cols_right)
+
+    share = (1.0 - beta_stat) / D
+    picked = lax.dynamic_slice_in_dim(grad_whole, (2 * z + core) * rows_right, rows_right, 1)
+    carried = dot_nn(grad_whole, right_cols).astype(BF)
+    power = beta_stat * dot_nn(stat_rows, right_cols) + share * dot_tn(picked, carried)
+    power = power.astype(BF)
+
+    own_cols = lax.dynamic_slice_in_dim(grad_whole, shard_pos * rows_right, rows_right, 1)
+    own_grad = lax.dynamic_slice_in_dim(grad_whole, tensor_pos * cols_right, cols_right, 1)
+    new_stat_right = blend_stat(stat_right, dot_tn(own_cols, own_grad), D)
+    left_cols = lax.dynamic_slice_in_dim(left_all, (2 * z + core) * rows_left, rows_left, 1)
+    rotated = dot_tn(left_cols, carried).astype(BF)
+    grad_rows = lax.dynamic_slice_in_dim(grad_whole, shard_pos * rows_left, rows_left, 0)
+    new_stat_left = blend_stat(stat_left, dot_nt(grad_rows, grad_whole), FF)
+    power_left = dot_nn(new_stat_left.astype(BF), left_all)
+    power_left_b = power_left.astype(BF)
+
+    power_x, power_y, power_u1, power_d1, extra = stage(
+        swap_x(power),
+        swap_y(power),
+        send_up(power),
+        send_down(power),
+        turn_over(jnp.concatenate([rotated, power_left_b]), straight),
+    )
+    near = near_of(z, power_u1, power_d1)
+    rotated, left_t = extra[:rows_left], extra[rows_left:]
+    new_moment_one, new_moment_two, direction = adam_moments(
+        rotated.astype(F32), moment_one, moment_two
+    )
+    got_x, got_y, got_u, got_d, direction_t = stage(
+        swap_x(jnp.concatenate([power_y[half:], near])),
+        swap_y(jnp.concatenate([power_x[:half], near])),
+        send_up(jnp.concatenate([power_u1, left_t])),
+        send_down(jnp.concatenate([power_d1, left_t])),
+        turn_over(direction, straight),
+    )
+    slab0 = jnp.concatenate(
+        [power, power_x, power_y, jnp.concatenate([got_y[:half], got_x[:half]])], axis=1
+    )
+    near_x, near_y = got_x[half:], got_y[half:]
+    power_u2, left_u1 = got_u[:rows_right], got_u[rows_right:]
+    power_d2, left_d1 = got_d[:rows_right], got_d[rows_right:]
+    mid = mid_of(z, power_u1, power_d1, power_u2, power_d2)
+    got_x, got_y, got_u, got_d, slab0_other = stage(
+        swap_x(jnp.concatenate([near_y[half:], mid])),
+        swap_y(jnp.concatenate([near_x[:half], mid])),
+        send_up(jnp.concatenate([power_u2, left_u1, direction_t])),
+        send_down(jnp.concatenate([power_d2, left_d1, direction_t])),
+        swap_core(slab0),
+    )
+    slab1 = jnp.concatenate(
+        [near, near_x, near_y, jnp.concatenate([got_y[:half], got_x[:half]])], axis=1
+    )
+    mid_x, mid_y = got_x[half:], got_y[half:]
+    power_u3, rest_u = got_u[:rows_right], got_u[rows_right:]
+    power_d3, rest_d = got_d[:rows_right], got_d[rows_right:]
+    left_u2, direction_u1 = rest_u[:rows_left], rest_u[rows_left:]
+    left_d2, direction_d1 = rest_d[:rows_left], rest_d[rows_left:]
+    far = far_of(z, power_u2, power_d2, power_u3, power_d3)
+    got_x, got_y, rest_u, rest_d, slab1_other = stage(
+        swap_x(jnp.concatenate([mid_y[half:], far])),
+        swap_y(jnp.concatenate([mid_x[:half], far])),
+        send_up(rest_u),
+        send_down(rest_d),
+        swap_core(slab1),
+    )
+    slab2 = jnp.concatenate(
+        [mid, mid_x, mid_y, jnp.concatenate([got_y[:half], got_x[:half]])], axis=1
+    )
+    far_x, far_y = got_x[half:], got_y[half:]
+    left_u3, direction_u2 = rest_u[:rows_left], rest_u[rows_left:]
+    left_d3, direction_d2 = rest_d[:rows_left], rest_d[rows_left:]
+    left_z = along_z(z, left_t, [(left_u1, left_d1), (left_u2, left_d2), (left_u3, left_d3)])
+    got_x, got_y, direction_u3, direction_d3, slab2_other, left_other = stage(
+        swap_x(far_y[half:]),
+        swap_y(far_x[:half]),
+        send_up(direction_u2),
+        send_down(direction_d2),
+        swap_core(slab2),
+        swap_core(left_z),
+    )
+    slab3 = jnp.concatenate([far, far_x, far_y, jnp.concatenate([got_y, got_x])], axis=1)
+    direction_z = along_z(
+        z,
+        direction_t,
+        [
+            (direction_u1, direction_d1),
+            (direction_u2, direction_d2),
+            (direction_u3, direction_d3),
+        ],
+    )
+    slab3_other, direction_other = stage(swap_core(slab3), swap_core(direction_z))
+
+    slabs = (slab0, slab0_other, slab1, slab1_other, slab2, slab2_other, slab3, slab3_other)
+    own = lax.dynamic_slice_in_dim(jnp.where(straight, slab0, slab0_other), core * half, half, 0)
+    first, square_right = refresh_pass(0, jnp.full((1,), FF / 16.0, F32), slabs, own)
+    (second,) = refresh_pass(1, square_right, slabs, first)
+    (third,) = refresh_pass(2, square_right, slabs, second)
+    scales = jnp.concatenate([square_right, math.sqrt(FF) * jnp.sqrt(square_right)])
+    (fresh,) = refresh_pass(3, scales, slabs, third, first)
+    ahead, behind = fresh[:, :cols_right], fresh[:, cols_right:]
+    mine = jnp.where(straight, ahead, behind)
+    theirs = swap_core(jnp.where(straight, behind, ahead))
+    new_basis_right = jnp.where(
+        core == 0, jnp.concatenate([mine, theirs]), jnp.concatenate([theirs, mine])
+    )
+
+    direction_cols = interleave(core, direction_z, direction_other)
+    left_rows = lax.dynamic_slice_in_dim(left_all, (2 * z + core) * rows_left, rows_left, 0)
+    back_half = dot_nn(left_rows, direction_cols).astype(BF)
+    back_terms = dot_nt(back_half, right_cols)
+    width = 2 * cols_right
+    away = lax.dynamic_slice_in_dim(back_terms, (1 - y) * width, width, 1).astype(BF)
+    kept = lax.dynamic_slice_in_dim(back_terms, y * width, width, 1)
+    kept = kept + swap_y(away).astype(F32)
+    away = lax.dynamic_slice_in_dim(kept, (1 - x) * cols_right, cols_right, 1).astype(BF)
+    kept = lax.dynamic_slice_in_dim(kept, x * cols_right, cols_right, 1)
+    update = turn_over((kept + swap_x(away).astype(F32)).astype(BF), straight)
+
+    power_all = interleave(core, left_z, left_other)
+    square_left = D / (16.0 * jnp.sum(jnp.square(power_all.astype(F32))))
+    keep = power_left
+    value = power_left
+    for turn in range(4):
+        across = dot_nt(value.astype(BF), power_all).astype(BF)
+        moved = square_left * dot_nn(across, power_all)
+        value = moved if turn == 1 else 1.5 * value - 0.5 * moved
+        if turn == 0:
+            keep = value
+    value = 1.5 * keep - 0.5 * value
+    new_basis_left = value * (math.sqrt(D) * jnp.sqrt(square_left))
+    return (
+        update,
+        new_moment_one,
+        new_moment_two,
+        new_stat_left,
+        new_stat_right,
+        new_basis_left,
+        new_basis_right,
+    )
+
+
 def solution(mesh):
+    nz, nx, ny, nc = PATTERN
+    fits = (mesh.shape["shard"], mesh.shape["tensor"]) == (nz * nx, ny * nc)
+    local = local_pattern if fits else local_general
     placed = (
         P("shard", "tensor"),
         P("shard", "tensor"),

time: 1160 us -> 385 us (0.33)
  waiting for transfers between devices: 992 us -> 127 us
  starting transfers between devices: 1.09 us -> 86.3 us
  blocking collectives: 66.3 us -> 0 us
  Pallas kernels: 0 us -> 62 us
  matrix products: 70.6 us -> 22 us
  other arithmetic: 9.29 us -> 51.6 us
  local copies, waits for them, and re-layouts: 1.79 us -> 26.4 us
    all_gather x11 -> x0, waiting for transfers between devices: 593 us -> none  [the longest x2 155 us: local(): lax.all_gather(mixing, 'shard', axis=0, tiled=True)]
    reduce_scatter x3 -> x0, waiting for transfers between devices: 214 us -> none  [the longest x2 188 us: local(): lax.psum_scatter(jnp.dot(iterate_rows.T, rounded_iterate, preferred_eleme...]
    psum x3 -> x0, waiting for transfers between devices: 183 us -> none  [the longest x2 156 us: local(): lax.psum(partial_gram.astype(jnp.bfloat16), 'shard').astype(jnp.float32)]
    ppermute x0 -> x52, waiting for transfers between devices: none -> 127 us  [the longest x10 39.6 us: swap_y(): return lax.ppermute(a, AXES, pairs(lambda z, x, y, c: (z, x, 1 - y, c)))]
    ppermute x0 -> x52, starting transfers between devices: none -> 86.3 us  [the longest x9 30.5 us: send_up(): return lax.ppermute(a, AXES, pairs(lambda z, x, y, c: (z + 1, x, y, c)))]
    pallas_call x0 -> x4, Pallas kernels: none -> 62 us  [refresh_pass(): pl.pallas_call(functools.partial(pass_kernel, turn), out_shape=shapes, in...]
    psum x2 -> x0, blocking collectives: 55.1 us -> none  [the longest x1 40.1 us: local(): total_right = lax.psum(local_right, ('shard', 'tensor'))]
    dot_general x15 -> x12, matrix products: 70.6 us -> 22 us  [the longest x7 10.6 us: dot_nn(): return jnp.dot(a, b, preferred_element_type=F32)]
  transfers between devices with their start and end apart: 17 -> 52, of which waited for: 17 -> 30; matrix products, arithmetic and copies ran while one was open for 4% -> 9% of each run, Pallas kernels for 0% -> 16%
where the time goes in v2:
time: 385 us; the launch traced here: 380 us
  waiting for transfers between devices  127 us (33%)
  starting transfers between devices  86.3 us (22%)
  Pallas kernels  62 us (16%)
  other arithmetic  51.6 us (13%)
  local copies, waits for them, and re-layouts  26.4 us (7%)
  matrix products  22 us (6%)
  between operations  4.05 us (1%)
    pallas_call x4, Pallas kernels, refresh_pass(): pl.pallas_call(functools.partial(pass_kernel, turn), out_shape=shapes, in...  62 us
    ppermute x10, waiting for transfers between devices, swap_y(): return lax.ppermute(a, AXES, pairs(lambda z, x, y, c: (z, x, 1 - y, c)))  39.6 us
    ppermute x9, starting transfers between devices, send_up(): return lax.ppermute(a, AXES, pairs(lambda z, x, y, c: (z + 1, x, y, c)))  30.5 us
    ppermute x9, waiting for transfers between devices, send_down(): return lax.ppermute(a, AXES, pairs(lambda z, x, y, c: (z - 1, x, y, c)))  24.2 us
    ppermute x4, waiting for transfers between devices, turn_over(): return jnp.where(straight, a, lax.ppermute(a, AXES, crossed))  23.8 us
    ppermute x9, waiting for transfers between devices, send_up(): return lax.ppermute(a, AXES, pairs(lambda z, x, y, c: (z + 1, x, y, c)))  20.4 us
    ppermute x10, waiting for transfers between devices, swap_x(): return lax.ppermute(a, AXES, pairs(lambda z, x, y, c: (z, 1 - x, y, c)))  18.6 us
    ppermute x9, starting transfers between devices, send_down(): return lax.ppermute(a, AXES, pairs(lambda z, x, y, c: (z - 1, x, y, c)))  18.1 us
  transfers between devices with their start and end apart: 52, of which 30 were waited for; matrix products, arithmetic and copies ran while one was open for 9% of the time, Pallas kernels for 16%

profile of v2, /device:TPU:9, one launch (start us, length us, event | category | flops | bytes accessed | tf_op | source)
XLA Modules:
  0.0 379.7 jit_solution(16769682666418730878)
XLA Ops:
  26.7 13.3 %collective-permute-done.6 = bf16[384,768]{1,0:T(8,128)(2,1)S(1)} collective-permute-done((bf16[384,768]{1,0:T(8,128)(2,1)S(1)}, bf16[384,768]{1,0:T(8,128)(2,1)S(1)}, u32[]{:S(2)}, u32[]{:S(2)}) %collective-permute-start.6) | collective-permute-done | bytes 589856 | tf_op jit(solution)/shard_map/ppermute | solution.py:168
  52.0 5.2 %collective-permute-done.10 = bf16[192,768]{1,0:T(8,128)(2,1)S(1)} collective-permute-done((bf16[192,768]{1,0:T(8,128)(2,1)S(1)}, bf16[192,768]{1,0:T(8,128)(2,1)S(1)}, u32[]{:S(2)}, u32[]{:S(2)}) %collective-permute-start.10) | collective-permute-done | bytes 294944 | tf_op jit(solution)/shard_map/ppermute | solution.py:168
  58.2 6.1 %collective-permute-done.8 = bf16[528,768]{1,0:T(8,128)(2,1)S(1)} collective-permute-done((bf16[528,768]{1,0:T(8,128)(2,1)}, bf16[528,768]{1,0:T(8,128)(2,1)S(1)}, u32[]{:S(2)}, u32[]{:S(2)}) %collective-permute-start.8) | collective-permute-done | bytes 811040 | tf_op jit(solution)/shard_map/ppermute | solution.py:180
  81.4 7.1 %collective-permute-done.11 = bf16[384,768]{1,0:T(8,128)(2,1)S(1)} collective-permute-done((bf16[384,768]{1,0:T(8,128)(2,1)S(1)}, bf16[384,768]{1,0:T(8,128)(2,1)S(1)}, u32[]{:S(2)}, u32[]{:S(2)}) %collective-permute-start.11) | collective-permute-done | bytes 589856 | tf_op jit(solution)/shard_map/ppermute | solution.py:176
  99.6 10.4 %collective-permute-done.16 = bf16[288,768]{1,0:T(8,128)(2,1)S(1)} collective-permute-done((bf16[288,768]{1,0:T(8,128)(2,1)S(1)}, bf16[288,768]{1,0:T(8,128)(2,1)S(1)}, u32[]{:S(2)}, u32[]{:S(2)}) %collective-permute-start.16) | collective-permute-done | bytes 442400 | tf_op jit(solution)/shard_map/ppermute | solution.py:164
  118.1 3.9 %convolution_convert_fusion = bf16[768,768]{1,0:T(8,128)(2,1)S(1)} fusion(bf16[768,3072]{1,0:T(8,128)(2,1)S(1)} %slice_dynamic-update-slice_fusion, bf16[3072,768]{1,0:T(8,128)(2,1)S(1)} %bitcast.117), kind=kOutput, calls=%fused_computation.7 | convolution fusion | flops 3624468480 | bytes 10616832 | tf_op jit(solution)/shard_map/dot_general | solution.py:137
  132.0 3.9 %collective-permute-start.24 = (bf16[192,768]{1,0:T(8,128)(2,1)S(1)}, bf16[192,768]{1,0:T(8,128)(2,1)S(1)}, u32[]{:S(2)}, u32[]{:S(2)}) collective-permute-start(bf16[192,768]{1,0:T(8,128)(2,1)S(1)} %pad_maximum_fusion.14), channel_id=1, source_target_pairs={{1,4},{3,6},{4,1},{6,3},{9,12},{11,14},{12,9},{14,11},{17,20},{19,... | collective-permute-start | bytes 884744 | tf_op jit(solution)/shard_map/ppermute | solution.py:185
  135.8 10.7 %collective-permute-done.24 = bf16[192,768]{1,0:T(8,128)(2,1)S(1)} collective-permute-done((bf16[192,768]{1,0:T(8,128)(2,1)S(1)}, bf16[192,768]{1,0:T(8,128)(2,1)S(1)}, u32[]{:S(2)}, u32[]{:S(2)}) %collective-permute-start.24) | collective-permute-done | bytes 294944 | tf_op jit(solution)/shard_map/ppermute | solution.py:185
  150.3 3.8 %collective-permute-start.27 = (bf16[480,768]{1,0:T(8,128)(2,1)S(1)}, bf16[480,768]{1,0:T(8,128)(2,1)S(1)}, u32[]{:S(2)}, u32[]{:S(2)}) collective-permute-start(bf16[480,768]{1,0:T(8,128)(2,1)S(1)} %get-tuple-element.141), channel_id=1, source_target_pairs={{0,8},{1,9},{2,10},{3,11},{4,12},{5,13},{6,14},{7,15},{8,16},{9,17... | collective-permute-start | bytes 2211848 | tf_op jit(solution)/shard_map/ppermute | solution.py:176
  155.1 3.8 collective-permute-start.29
  158.9 12.3 %collective-permute-done.29 = bf16[96,768]{1,0:T(8,128)(2,1)S(1)} collective-permute-done((bf16[96,768]{1,0:T(8,128)(2,1)S(1)}, bf16[96,768]{1,0:T(8,128)(2,1)S(1)}, u32[]{:S(2)}, u32[]{:S(2)}) %collective-permute-start.29) | collective-permute-done | bytes 147488 | tf_op jit(solution)/shard_map/ppermute | solution.py:185
  171.4 7.3 %maximum_maximum_fusion.refs_0_ = bf16[384,3072]{1,0:T(8,128)(2,1)S(1)} fusion(bf16[192,768]{1,0:T(8,128)(2,1)S(1)} %get-tuple-element.128, bf16[192,768]{1,0:T(8,128)(2,1)S(1)} %get-tuple-element.126, bf16[384,768]{1,0:T(8,128)(2,1)S(1)} %collective-permute-done.21, bf16[384,768]{1,0:T(8,128)(2,1)S(1)} %collective-permute-done.20, bf16[384,768]{1,0:T(8,128)(2,1)S(1)} %fusion.2), kind=kLoop, calls=%fused_computation | loop fusion | flops 11796480 | bytes 4718592 | tf_op jit(solution)/shard_map/concatenate | solution.py:449
  186.0 13.7 %collective-permute-done.31 = bf16[576,768]{1,0:T(8,128)(2,1)S(1)} collective-permute-done((bf16[576,768]{1,0:T(8,128)(2,1)S(1)}, bf16[576,768]{1,0:T(8,128)(2,1)S(1)}, u32[]{:S(2)}, u32[]{:S(2)}) %collective-permute-start.31) | collective-permute-done | bytes 884768 | tf_op jit(solution)/shard_map/ppermute | solution.py:168
  206.6 7.2 %maximum_maximum_fusion.1.refs_2_ = bf16[384,3072]{1,0:T(8,128)(2,1)S(1)} fusion(bf16[192,768]{1,0:T(8,128)(2,1)S(1)} %get-tuple-element.124, bf16[192,768]{1,0:T(8,128)(2,1)S(1)} %get-tuple-element.122, bf16[384,768]{1,0:T(8,128)(2,1)S(1)} %slice-done, bf16[384,768]{1,0:T(8,128)(2,1)S(1)} %slice-done.1, bf16[384,768]{1,0:T(8,128)(2,1)S(1)} %broadcast_select_fusion), kind=kLoop, calls=%fused_computation.1 | loop fusion | flops 11796480 | bytes 4718592 | tf_op jit(solution)/shard_map/concatenate | solution.py:463
  229.0 6.6 %collective-permute-done.36 = bf16[576,768]{1,0:T(8,128)(2,1)S(1)} collective-permute-done((bf16[576,768]{1,0:T(8,128)(2,1)S(1)}, bf16[576,768]{1,0:T(8,128)(2,1)S(1)}, u32[]{:S(2)}, u32[]{:S(2)}) %collective-permute-start.36) | collective-permute-done | bytes 884768 | tf_op jit(solution)/shard_map/ppermute | solution.py:168
  238.0 7.2 %maximum_maximum_fusion.2.refs_4_ = bf16[384,3072]{1,0:T(8,128)(2,1)S(1)} fusion(bf16[192,768]{1,0:T(8,128)(2,1)S(1)} %get-tuple-element.120, bf16[192,768]{1,0:T(8,128)(2,1)S(1)} %get-tuple-element.118, bf16[384,768]{1,0:T(8,128)(2,1)S(1)} %slice.263, bf16[384,768]{1,0:T(8,128)(2,1)S(1)} %slice.262, bf16[384,768]{1,0:T(8,128)(2,1)S(1)} %select_select_fusion.1), kind=kLoop, calls=%fused_computation.2 | loop fusion | flops 11796480 | bytes 4718592 | tf_op jit(solution)/shard_map/concatenate | solution.py:479
  258.6 4.3 %collective-permute-done.43 = bf16[96,768]{1,0:T(8,128)(2,1)S(1)} collective-permute-done((bf16[96,768]{1,0:T(8,128)(2,1)S(1)}, bf16[96,768]{1,0:T(8,128)(2,1)S(1)}, u32[]{:S(2)}, u32[]{:S(2)}) %collective-permute-start.43) | collective-permute-done | bytes 147488 | tf_op jit(solution)/shard_map/ppermute | solution.py:180
  262.9 8.3 %maximum_maximum_fusion.3.refs_6_ = bf16[384,3072]{1,0:T(8,128)(2,1)} fusion(bf16[192,768]{1,0:T(8,128)(2,1)S(1)} %collective-permute-done.40, bf16[192,768]{1,0:T(8,128)(2,1)S(1)} %collective-permute-done.41, bf16[384,768]{1,0:T(8,128)(2,1)S(1)} %slice.273, bf16[384,768]{1,0:T(8,128)(2,1)S(1)} %slice.272, bf16[384,768]{1,0:T(8,128)(2,1)S(1)} %select_select_fusion), kind=kLoop, calls=%fused_computation.3 | loop fusion | flops 11796480 | bytes 4718592 | tf_op jit(solution)/shard_map/concatenate | solution.py:494
  281.0 5.3 %fusion.14 = f32[96,3072]{1,0:T(8,128)} fusion(bf16[3072,768]{1,0:T(8,128)(2,1)} %bitcast.118, bf16[768,768]{1,0:T(8,128)(2,1)} %bitcast.125, bf16[768,768]{1,0:T(8,128)(2,1)} %bitcast.124, s32[]{:T(128)S(6)} %select_n.444), kind=kOutput, calls=%fused_computation.46 | convolution fusion | flops 566304768 | bytes 7225348 | tf_op jit(solution)/shard_map/dot_general | solution.py:141
  293.4 20.4 %shard_map.126 = (f32[192,3072]{1,0:T(8,128)S(1)}, f32[1]{0:T(128)}) custom-call(f32[1]{0:T(128)} %constant.139.clone.1.scale_ref, bf16[384,3072]{1,0:T(8,128)(2,1)S(1)} %maximum_maximum_fusion.refs_0_, bf16[384,3072]{1,0:T(8,128)(2,1)S(1)} %copy-done.7, bf16[384,3072]{1,0:T(8,128)(2,1)S(1)} %copy-done.1, bf16[384,3072]{1,0:T(8,128)(2,1)S(1)} %copy-done.9, ...), custom_call_target="tpu_custom_call" | custom-call | flops 7247757312 | bytes 18874368 | tf_op jit(solution)/shard_map/pallas_call | solution.py:316
  316.6 14.5 %shard_map.127.refs_8_ = f32[192,3072]{1,0:T(8,128)S(1)} custom-call(f32[1]{0:T(128)} %get-tuple-element.103.scale_ref, bf16[384,3072]{1,0:T(8,128)(2,1)S(1)} %maximum_maximum_fusion.refs_0_, bf16[384,3072]{1,0:T(8,128)(2,1)S(1)} %copy-done.7, bf16[384,3072]{1,0:T(8,128)(2,1)S(1)} %copy-done.2, bf16[384,3072]{1,0:T(8,128)(2,1)S(1)} %copy-done.9, ...), custom_call_target="tpu_custom_call" | custom-call | flops 7247757312 | bytes 18874368 | tf_op jit(solution)/shard_map/pallas_call | solution.py:316
  332.4 14.7 %shard_map.128.refs_8_ = f32[192,3072]{1,0:T(8,128)S(1)} custom-call(f32[1]{0:T(128)} %get-tuple-element.103.scale_ref, bf16[384,3072]{1,0:T(8,128)(2,1)S(1)} %maximum_maximum_fusion.refs_0_, bf16[384,3072]{1,0:T(8,128)(2,1)S(1)} %copy-done.7, bf16[384,3072]{1,0:T(8,128)(2,1)S(1)} %copy-done.2, bf16[384,3072]{1,0:T(8,128)(2,1)S(1)} %copy-done.9, ...), custom_call_target="tpu_custom_call" | custom-call | flops 7247757312 | bytes 18874368 | tf_op jit(solution)/shard_map/pallas_call | solution.py:316
  348.5 12.5 %shard_map.129 = f32[192,1536]{1,0:T(8,128)S(1)} custom-call(f32[2]{0:T(128)S(1)} %pad_maximum_fusion.16.scale_ref, bf16[384,3072]{1,0:T(8,128)(2,1)S(1)} %maximum_maximum_fusion.refs_0_, bf16[384,3072]{1,0:T(8,128)(2,1)S(1)} %copy-done.7, bf16[384,3072]{1,0:T(8,128)(2,1)S(1)} %copy-done.2, bf16[384,3072]{1,0:T(8,128)(2,1)S(1)} %copy-done.9, ...), custom_call_target="tpu_custom_call" | custom-call | flops 7247757312 | bytes 18874368 | tf_op jit(solution)/shard_map/pallas_call | solution.py:316
  367.6 4.4 %collective-permute-done.49 = bf16[96,768]{1,0:T(8,128)(2,1)S(1)} collective-permute-done((bf16[96,768]{1,0:T(8,128)(2,1)S(1)}, bf16[96,768]{1,0:T(8,128)(2,1)S(1)}, u32[]{:S(2)}, u32[]{:S(2)}) %collective-permute-start.49) | collective-permute-done | bytes 147488 | tf_op jit(solution)/shard_map/ppermute | solution.py:164
  (339 shorter events, 169.0 us)
Async XLA Ops:
  20.1 21.8 %collective-permute-start.4 = (bf16[528,768]{1,0:T(8,128)(2,1)S(1)}, bf16[528,768]{1,0:T(8,128)(2,1)}, u32[]{:S(2)}, u32[]{:S(2)}) collective-permute-start(bf16[528,768]{1,0:T(8,128)(2,1)S(1)} %get-tuple-element.136), channel_id=1, source_target_pairs={{8,0},{9,1},{10,2},{11,3},{12,4},{13,5},{14,6},{15,7},{16,8},{17,9... | collective-permute-start | bytes 2433032 | tf_op jit(solution)/shard_map/ppermute | solution.py:180
  22.2 21.5 %collective-permute-start.3 = (bf16[528,768]{1,0:T(8,128)(2,1)S(1)}, bf16[528,768]{1,0:T(8,128)(2,1)}, u32[]{:S(2)}, u32[]{:S(2)}) collective-permute-start(bf16[528,768]{1,0:T(8,128)(2,1)S(1)} %get-tuple-element.137), channel_id=1, source_target_pairs={{0,8},{1,9},{2,10},{3,11},{4,12},{5,13},{6,14},{7,15},{8,16},{9,17... | collective-permute-start | bytes 2433032 | tf_op jit(solution)/shard_map/ppermute | solution.py:176
  43.6 20.6 %collective-permute-start.8 = (bf16[528,768]{1,0:T(8,128)(2,1)}, bf16[528,768]{1,0:T(8,128)(2,1)S(1)}, u32[]{:S(2)}, u32[]{:S(2)}) collective-permute-start(bf16[528,768]{1,0:T(8,128)(2,1)} %collective-permute-done.4), channel_id=1, source_target_pairs={{8,0},{9,1},{10,2},{11,3},{12,4},{13,5},{14,6},{15,7},{16,8},{17,9... | collective-permute-start | bytes 2433032 | tf_op jit(solution)/shard_map/ppermute | solution.py:180
  45.5 20.7 %collective-permute-start.7 = (bf16[528,768]{1,0:T(8,128)(2,1)}, bf16[528,768]{1,0:T(8,128)(2,1)S(1)}, u32[]{:S(2)}, u32[]{:S(2)}) collective-permute-start(bf16[528,768]{1,0:T(8,128)(2,1)} %collective-permute-done.3), channel_id=1, source_target_pairs={{0,8},{1,9},{2,10},{3,11},{4,12},{5,13},{6,14},{7,15},{8,16},{9,17... | collective-permute-start | bytes 2433032 | tf_op jit(solution)/shard_map/ppermute | solution.py:176
  66.6 26.0 %collective-permute-start.15 = (bf16[768,768]{1,0:T(8,128)(2,1)S(1)}, bf16[768,768]{1,0:T(8,128)(2,1)S(1)}, u32[]{:S(2)}, u32[]{:S(2)}) collective-permute-start(bf16[768,768]{1,0:T(8,128)(2,1)S(1)} %pad_maximum_fusion), channel_id=1, source_target_pairs={{0,1},{1,0},{2,3},{3,2},{4,5},{5,4},{6,7},{7,6},{8,9},{9,8},{10,11... | collective-permute-start | bytes 3538952 | tf_op jit(solution)/shard_map/ppermute | solution.py:172
  71.0 20.7 %collective-permute-start.14 = (bf16[576,768]{1,0:T(8,128)(2,1)S(1)}, bf16[576,768]{1,0:T(8,128)(2,1)S(1)}, u32[]{:S(2)}, u32[]{:S(2)}) collective-permute-start(bf16[576,768]{1,0:T(8,128)(2,1)S(1)} %bitcast.128), channel_id=1, source_target_pairs={{0,2},{1,3},{2,0},{3,1},{4,6},{5,7},{6,4},{7,5},{8,10},{9,11},{10,... | collective-permute-start | bytes 2654216 | tf_op jit(solution)/shard_map/ppermute | solution.py:168
  72.3 20.3 %collective-permute-start.13 = (bf16[576,768]{1,0:T(8,128)(2,1)S(1)}, bf16[576,768]{1,0:T(8,128)(2,1)S(1)}, u32[]{:S(2)}, u32[]{:S(2)}) collective-permute-start(bf16[576,768]{1,0:T(8,128)(2,1)S(1)} %bitcast.129), channel_id=1, source_target_pairs={{0,4},{1,5},{2,6},{3,7},{4,0},{5,1},{6,2},{7,3},{8,12},{9,13},{10,... | collective-permute-start | bytes 2654216 | tf_op jit(solution)/shard_map/ppermute | solution.py:164
  122.7 23.9 %collective-permute-start.23 = (bf16[384,768]{1,0:T(8,128)(2,1)S(1)}, bf16[384,768]{1,0:T(8,128)(2,1)S(1)}, u32[]{:S(2)}, u32[]{:S(2)}) collective-permute-start(bf16[384,768]{1,0:T(8,128)(2,1)S(1)} %fusion.2), channel_id=1, source_target_pairs={{8,0},{9,1},{10,2},{11,3},{12,4},{13,5},{14,6},{15,7},{16,8},{17,9... | collective-permute-start | bytes 1769480 | tf_op jit(solution)/shard_map/ppermute | solution.py:180
  124.6 22.0 %collective-permute-start.22 = (bf16[384,768]{1,0:T(8,128)(2,1)S(1)}, bf16[384,768]{1,0:T(8,128)(2,1)S(1)}, u32[]{:S(2)}, u32[]{:S(2)}) collective-permute-start(bf16[384,768]{1,0:T(8,128)(2,1)S(1)} %fusion.2), channel_id=1, source_target_pairs={{0,8},{1,9},{2,10},{3,11},{4,12},{5,13},{6,14},{7,15},{8,16},{9,17... | collective-permute-start | bytes 1769480 | tf_op jit(solution)/shard_map/ppermute | solution.py:176
  128.0 18.6 %collective-permute-start.21 = (bf16[384,768]{1,0:T(8,128)(2,1)S(1)}, bf16[384,768]{1,0:T(8,128)(2,1)S(1)}, u32[]{:S(2)}, u32[]{:S(2)}) collective-permute-start(bf16[384,768]{1,0:T(8,128)(2,1)S(1)} %fusion.2), channel_id=1, source_target_pairs={{0,2},{1,3},{2,0},{3,1},{4,6},{5,7},{6,4},{7,5},{8,10},{9,11},{10,... | collective-permute-start | bytes 1769480 | tf_op jit(solution)/shard_map/ppermute | solution.py:168
  128.3 18.3 %collective-permute-start.20 = (bf16[384,768]{1,0:T(8,128)(2,1)S(1)}, bf16[384,768]{1,0:T(8,128)(2,1)S(1)}, u32[]{:S(2)}, u32[]{:S(2)}) collective-permute-start(bf16[384,768]{1,0:T(8,128)(2,1)S(1)} %fusion.2), channel_id=1, source_target_pairs={{0,4},{1,5},{2,6},{3,7},{4,0},{5,1},{6,2},{7,3},{8,12},{9,13},{10,... | collective-permute-start | bytes 1769480 | tf_op jit(solution)/shard_map/ppermute | solution.py:164
  146.9 24.3 %collective-permute-start.26 = (bf16[576,768]{1,0:T(8,128)(2,1)S(1)}, bf16[576,768]{1,0:T(8,128)(2,1)S(1)}, u32[]{:S(2)}, u32[]{:S(2)}) collective-permute-start(bf16[576,768]{1,0:T(8,128)(2,1)S(1)} %get-tuple-element.134), channel_id=1, source_target_pairs={{0,2},{1,3},{2,0},{3,1},{4,6},{5,7},{6,4},{7,5},{8,10},{9,11},{10,... | collective-permute-start | bytes 2654216 | tf_op jit(solution)/shard_map/ppermute | solution.py:168
  148.2 23.0 %collective-permute-start.25 = (bf16[576,768]{1,0:T(8,128)(2,1)S(1)}, bf16[576,768]{1,0:T(8,128)(2,1)S(1)}, u32[]{:S(2)}, u32[]{:S(2)}) collective-permute-start(bf16[576,768]{1,0:T(8,128)(2,1)S(1)} %get-tuple-element.135), channel_id=1, source_target_pairs={{0,4},{1,5},{2,6},{3,7},{4,0},{5,1},{6,2},{7,3},{8,12},{9,13},{10,... | collective-permute-start | bytes 2654216 | tf_op jit(solution)/shard_map/ppermute | solution.py:164
  148.3 22.9 %collective-permute-start.28 = (bf16[480,768]{1,0:T(8,128)(2,1)S(1)}, bf16[480,768]{1,0:T(8,128)(2,1)S(1)}, u32[]{:S(2)}, u32[]{:S(2)}) collective-permute-start(bf16[480,768]{1,0:T(8,128)(2,1)S(1)} %get-tuple-element.140), channel_id=1, source_target_pairs={{8,0},{9,1},{10,2},{11,3},{12,4},{13,5},{14,6},{15,7},{16,8},{17,9... | collective-permute-start | bytes 2211848 | tf_op jit(solution)/shard_map/ppermute | solution.py:180
  150.3 20.9 %collective-permute-start.27 = (bf16[480,768]{1,0:T(8,128)(2,1)S(1)}, bf16[480,768]{1,0:T(8,128)(2,1)S(1)}, u32[]{:S(2)}, u32[]{:S(2)}) collective-permute-start(bf16[480,768]{1,0:T(8,128)(2,1)S(1)} %get-tuple-element.141), channel_id=1, source_target_pairs={{0,8},{1,9},{2,10},{3,11},{4,12},{5,13},{6,14},{7,15},{8,16},{9,17... | collective-permute-start | bytes 2211848 | tf_op jit(solution)/shard_map/ppermute | solution.py:176
  178.7 26.5 %collective-permute-start.34 = (bf16[384,3072]{1,0:T(8,128)(2,1)S(1)}, bf16[384,3072]{1,0:T(8,128)(2,1)S(1)}, u32[]{:S(2)}, u32[]{:S(2)}) collective-permute-start(bf16[384,3072]{1,0:T(8,128)(2,1)S(1)} %maximum_maximum_fusion.refs_0_), channel_id=1, source_target_pairs={{0,1},{1,0},{2,3},{3,2},{4,5},{5,4},{6,7},{7,6},{8,9},{9,8},{10,11... | collective-permute-start | bytes 7077896 | tf_op jit(solution)/shard_map/ppermute | solution.py:172
  179.0 20.8 %collective-permute-start.31 = (bf16[576,768]{1,0:T(8,128)(2,1)S(1)}, bf16[576,768]{1,0:T(8,128)(2,1)S(1)}, u32[]{:S(2)}, u32[]{:S(2)}) collective-permute-start(bf16[576,768]{1,0:T(8,128)(2,1)S(1)} %get-tuple-element.132), channel_id=1, source_target_pairs={{0,2},{1,3},{2,0},{3,1},{4,6},{5,7},{6,4},{7,5},{8,10},{9,11},{10,... | collective-permute-start | bytes 2654216 | tf_op jit(solution)/shard_map/ppermute | solution.py:168
  179.3 20.5 %collective-permute-start.30 = (bf16[576,768]{1,0:T(8,128)(2,1)S(1)}, bf16[576,768]{1,0:T(8,128)(2,1)S(1)}, u32[]{:S(2)}, u32[]{:S(2)}) collective-permute-start(bf16[576,768]{1,0:T(8,128)(2,1)S(1)} %get-tuple-element.133), channel_id=1, source_target_pairs={{0,4},{1,5},{2,6},{3,7},{4,0},{5,1},{6,2},{7,3},{8,12},{9,13},{10,... | collective-permute-start | bytes 2654216 | tf_op jit(solution)/shard_map/ppermute | solution.py:164
  180.7 22.5 %collective-permute-start.33 = (bf16[576,768]{1,0:T(8,128)(2,1)S(1)}, bf16[576,768]{1,0:T(8,128)(2,1)S(1)}, u32[]{:S(2)}, u32[]{:S(2)}) collective-permute-start(bf16[576,768]{1,0:T(8,128)(2,1)S(1)} %get-tuple-element.138), channel_id=1, source_target_pairs={{8,0},{9,1},{10,2},{11,3},{12,4},{13,5},{14,6},{15,7},{16,8},{17,9... | collective-permute-start | bytes 2654216 | tf_op jit(solution)/shard_map/ppermute | solution.py:180
  182.6 22.5 %collective-permute-start.32 = (bf16[576,768]{1,0:T(8,128)(2,1)S(1)}, bf16[576,768]{1,0:T(8,128)(2,1)S(1)}, u32[]{:S(2)}, u32[]{:S(2)}) collective-permute-start(bf16[576,768]{1,0:T(8,128)(2,1)S(1)} %get-tuple-element.139), channel_id=1, source_target_pairs={{0,8},{1,9},{2,10},{3,11},{4,12},{5,13},{6,14},{7,15},{8,16},{9,17... | collective-permute-start | bytes 2654216 | tf_op jit(solution)/shard_map/ppermute | solution.py:176
  213.8 22.8 %collective-permute-start.39 = (bf16[384,3072]{1,0:T(8,128)(2,1)S(1)}, bf16[384,3072]{1,0:T(8,128)(2,1)S(1)}, u32[]{:S(2)}, u32[]{:S(2)}) collective-permute-start(bf16[384,3072]{1,0:T(8,128)(2,1)S(1)} %maximum_maximum_fusion.1.refs_2_), channel_id=1, source_target_pairs={{0,1},{1,0},{2,3},{3,2},{4,5},{5,4},{6,7},{7,6},{8,9},{9,8},{10,11... | collective-permute-start | bytes 7077896 | tf_op jit(solution)/shard_map/ppermute | solution.py:172
  215.5 20.1 %collective-permute-start.36 = (bf16[576,768]{1,0:T(8,128)(2,1)S(1)}, bf16[576,768]{1,0:T(8,128)(2,1)S(1)}, u32[]{:S(2)}, u32[]{:S(2)}) collective-permute-start(bf16[576,768]{1,0:T(8,128)(2,1)S(1)} %get-tuple-element.130), channel_id=1, source_target_pairs={{0,2},{1,3},{2,0},{3,1},{4,6},{5,7},{6,4},{7,5},{8,10},{9,11},{10,... | collective-permute-start | bytes 2654216 | tf_op jit(solution)/shard_map/ppermute | solution.py:168
  216.9 19.7 %collective-permute-start.35 = (bf16[576,768]{1,0:T(8,128)(2,1)S(1)}, bf16[576,768]{1,0:T(8,128)(2,1)S(1)}, u32[]{:S(2)}, u32[]{:S(2)}) collective-permute-start(bf16[576,768]{1,0:T(8,128)(2,1)S(1)} %get-tuple-element.131), channel_id=1, source_target_pairs={{0,4},{1,5},{2,6},{3,7},{4,0},{5,1},{6,2},{7,3},{8,12},{9,13},{10,... | collective-permute-start | bytes 2654216 | tf_op jit(solution)/shard_map/ppermute | solution.py:164
  288.2 76.5 %collective-permute-start.48 = (bf16[96,1536]{1,0:T(8,128)(2,1)}, bf16[96,1536]{1,0:T(8,128)(2,1)}, u32[]{:S(2)}, u32[]{:S(2)}) collective-permute-start(bf16[96,1536]{1,0:T(8,128)(2,1)} %dynamic-slice_convert_fusion), channel_id=1, source_target_pairs={{0,2},{1,3},{2,0},{3,1},{4,6},{5,7},{6,4},{7,5},{8,10},{9,11},{10,... | collective-permute-start | bytes 884744 | tf_op jit(solution)/shard_map/ppermute | solution.py:168
  (97 other events, 820.6 us)

commit v3 on v2

--- a/solution.py
+++ b/solution.py
@@ -172,12 +172,12 @@
     return lax.ppermute(a, AXES, pairs(lambda z, x, y, c: (z, x, y, 1 - c)))
 
 
-def send_up(a):
-    return lax.ppermute(a, AXES, pairs(lambda z, x, y, c: (z + 1, x, y, c)))
-
-
-def send_down(a):
-    return lax.ppermute(a, AXES, pairs(lambda z, x, y, c: (z - 1, x, y, c)))
+def swap_outer(a):
+    return lax.ppermute(a, AXES, pairs(lambda z, x, y, c: (z + 1 - 2 * (z % 2), x, y, c)))
+
+
+def swap_inner(a):
+    return lax.ppermute(a, AXES, pairs(lambda z, x, y, c: (3 - z if 0 < z < 3 else -1, x, y, c)))
 
 
 def turn_over(a, straight):
@@ -189,35 +189,20 @@
     return lax.optimization_barrier(parts)
 
 
-def near_of(z, up, down):
-    return jnp.where(z % 2 == 0, down, up)
-
-
-def mid_of(z, up1, down1, up2, down2):
-    return jnp.where(z == 0, down2, jnp.where(z == 1, down1, jnp.where(z == 2, up1, up2)))
-
-
-def far_of(z, up2, down2, up3, down3):
-    return jnp.where(z == 0, down3, jnp.where(z == 1, down2, jnp.where(z == 2, up2, up3)))
+def places_z(z):
+    return z + 1 - 2 * (z % 2), jnp.where(z < 2, 2, 1), jnp.where(z < 2, 3, 0)
 
 
 def in_order(z, own, near, mid, far):
-    places = (z, z + 1 - 2 * (z % 2), jnp.where(z < 2, 2, 1), jnp.where(z < 2, 3, 0))
     whole = jnp.zeros((4,) + own.shape, own.dtype)
-    for block, place in zip((own, near, mid, far), places):
+    for block, place in zip((own, near, mid, far), (z,) + places_z(z)):
         whole = lax.dynamic_update_slice(whole, block[None], (place,) + (0,) * own.ndim)
     return whole
 
 
-def along_z(z, own, steps):
-    (up1, down1), (up2, down2), (up3, down3) = steps
-    return in_order(
-        z,
-        own,
-        near_of(z, up1, down1),
-        mid_of(z, up1, down1, up2, down2),
-        far_of(z, up2, down2, up3, down3),
-    )
+def ordered_pair(ahead, first, second):
+    both = jnp.concatenate([first[None], second[None]])
+    return jnp.where(ahead, both, jnp.concatenate([second[None], first[None]]))
 
 
 def put(whole, part, *start):
@@ -232,98 +217,122 @@
     return whole.reshape(8 * rows, cols)
 
 
-def pass_kernel(turn, scale_ref, *refs):
+def refresh_kernel(part, scale_ref, place_ref, *refs):
     slabs = refs[:8]
-    if turn == 0:
-        rows_ref, out_ref, square_ref, whole, inner, held, sums, sems = refs[8:]
-    elif turn == 3:
-        rows_ref, first_ref, out_ref, whole, inner, held, sems = refs[8:]
+    if part == 0:
+        first_ref, second_ref, whole, inner, held, sems = refs[8:]
     else:
-        rows_ref, out_ref, whole, inner, held, sems = refs[8:]
+        second_ref, first_ref, out_ref, whole, inner, held, third, sems = refs[8:]
     size = whole.shape[0]
+    count = held.shape[0]
     tall = size // 4
     half = size // 8
-
-    def copy(k):
+    square = scale_ref[0]
+
+    def copy(k, i):
         return pltpu.make_async_copy(
-            slabs[k], whole.at[pl.ds(k * half, half), :], sems.at[k]
+            slabs[k].at[pl.ds(i * half, half), :],
+            whole.at[pl.ds(k * half, half), pl.ds(i * tall, tall)],
+            sems.at[k, i],
         )
 
+    def arrived(j):
+        for k in (2 * j, 2 * j + 1):
+            for i in range(4):
+                copy(k, i).wait()
+
+    def span_of(j):
+        return pl.ds(pl.multiple_of(j * tall, tall), tall)
+
+    def towards(fresh):
+        def step(j, carry):
+            if fresh:
+                for k in range(1 - part, 4):
+                    pl.when(j == k)(functools.partial(arrived, k))
+            span = span_of(j)
+            inner[:, span] = dot_nt(held[...], whole[span, :]).astype(BF)
+            return carry
+
+        lax.fori_loop(0, 4, step, 0)
+
+    def back(chunks, use):
+        def step(j, carry):
+            use(j, span_of(j), square * dot_nn(inner[...], whole[:, span_of(j)]))
+            return carry
+
+        lax.fori_loop(0, chunks, step, 0)
+
     for k in range(8):
-        copy(k).start()
-    held[...] = rows_ref[...].astype(BF)
-    if turn == 0:
-        sums[...] = jnp.zeros_like(sums)
-
-    def towards(j, carry):
-        for k in range(4):
-
-            @pl.when(j == k)
-            def _():
-                copy(2 * k).wait()
-                copy(2 * k + 1).wait()
-
-        span = pl.ds(pl.multiple_of(j * tall, tall), tall)
-        inner[:, span] = dot_nt(held[...], whole[span, :]).astype(BF)
-        if turn == 0:
-            for part in range(4):
-                cols = slice(part * tall, (part + 1) * tall)
-
-                def add(i, total):
-                    start = pl.multiple_of(j * tall + i * 16, 16)
-                    block = whole[pl.ds(start, 16), cols].astype(F32)
-                    return total + block * block
-
-                zero = jnp.zeros((16, tall), F32)
-                sums[...] += lax.fori_loop(0, tall // 16, add, zero)
-        return carry
-
-    lax.fori_loop(0, 4, towards, 0)
-    if turn == 0:
-        square = scale_ref[0] / jnp.sum(sums[...])
-        square_ref[0] = square
+        for i in range(4):
+            copy(k, i).start()
+    if part == 0:
+        arrived(0)
+        held[...] = whole[pl.ds(pl.multiple_of(place_ref[0], 16), count), :]
+        towards(True)
+
+        def use_first(j, span, moved):
+            value = 1.5 * held[:, span].astype(F32) - 0.5 * moved
+            first_ref[:, span] = value
+            held[:, span] = value.astype(BF)
+
+        back(4, use_first)
+        towards(False)
+
+        def use_second(j, span, moved):
+            second_ref[:, span] = moved
+
+        back(4, use_second)
     else:
-        square = scale_ref[0]
-
-    def back(j, carry):
-        span = pl.ds(pl.multiple_of(j * tall, tall), tall)
-        moved = square * dot_nn(inner[...], whole[:, span])
-        if turn == 1:
-            out_ref[:, span] = moved
-        else:
-            value = 1.5 * rows_ref[:, span].astype(F32) - 0.5 * moved
-            if turn == 3:
-                value = scale_ref[1] * (1.5 * first_ref[:, span] - 0.5 * value)
-            out_ref[:, span] = value
-        return carry
-
-    lax.fori_loop(0, 2 if turn == 3 else 4, back, 0)
-
-
-def refresh_pass(turn, scales, slabs, *rows):
-    count, size = rows[0].shape
+        held[...] = second_ref[...].astype(BF)
+        towards(True)
+
+        def use_third(j, span, moved):
+            value = 1.5 * second_ref[:, span] - 0.5 * moved
+            third[:, span] = value
+            held[:, span] = value.astype(BF)
+
+        back(4, use_third)
+        towards(False)
+
+        def use_last(j, span, moved):
+            value = 1.5 * third[:, span] - 0.5 * moved
+            value = scale_ref[1] * (1.5 * first_ref[:, span] - 0.5 * value)
+            out_ref[jnp.where(place_ref[1] == 1, j, 1 - j)] = value
+
+        back(2, use_last)
+
+
+def refresh_part(part, scales, places, slabs, *rows):
+    size = slabs[0].shape[0] * 2
+    count = size // 16
     in_vmem = pl.BlockSpec(memory_space=pltpu.VMEM)
     in_smem = pl.BlockSpec(memory_space=pltpu.SMEM)
-    shapes = [jax.ShapeDtypeStruct((count, size // 2 if turn == 3 else size), F32)]
+    state = jax.ShapeDtypeStruct((count, size), F32)
     scratch = [
         pltpu.VMEM((size, size), BF),
         pltpu.VMEM((count, size), BF),
         pltpu.VMEM((count, size), BF),
     ]
-    if turn == 0:
-        shapes.append(jax.ShapeDtypeStruct((1,), F32))
-        scratch.append(pltpu.VMEM((16, size // 4), F32))
+    if part == 0:
+        shapes = [state, state]
+    else:
+        shapes = [jax.ShapeDtypeStruct((2, count, size // 4), F32)]
+        scratch.append(pltpu.VMEM((count, size), F32))
     return pl.pallas_call(
-        functools.partial(pass_kernel, turn),
+        functools.partial(refresh_kernel, part),
         out_shape=shapes,
-        in_specs=[in_smem] + [pl.BlockSpec(memory_space=pl.ANY)] * 8 + [in_vmem] * len(rows),
-        out_specs=[in_vmem, in_smem][: len(shapes)],
-        scratch_shapes=scratch + [pltpu.SemaphoreType.DMA((8,))],
-        compiler_params=pltpu.CompilerParams(vmem_limit_bytes=40 * 2**20),
+        in_specs=[in_smem] * 2 + [pl.BlockSpec(memory_space=pl.ANY)] * 8 + [in_vmem] * len(rows),
+        out_specs=[in_vmem] * len(shapes),
+        scratch_shapes=scratch + [pltpu.SemaphoreType.DMA((8, 4))],
+        compiler_params=pltpu.CompilerParams(vmem_limit_bytes=36 * 2**20),
         cost_estimate=pl.CostEstimate(
-            flops=4 * count * size * size, bytes_accessed=2 * size * size, transcendentals=0
+            flops=8 * count * size * size, bytes_accessed=2 * size * size, transcendentals=0
         ),
-    )(scales, *slabs, *rows)
+    )(scales, places, *slabs, *rows)
+
+
+def squares(tiles):
+    return jnp.sum(jnp.square(tiles.astype(F32)))
 
 
 def local_pattern(gradient, moment_one, moment_two, stat_left, stat_right, basis_left, basis_right):
@@ -335,6 +344,7 @@
     z, x = shard_pos // 2, shard_pos % 2
     y, core = tensor_pos // 2, tensor_pos % 2
     straight = x == core
+    inner = (z == 1) | (z == 2)
     half = rows_right // 2
 
     left_b = (basis_left / math.sqrt(D)).astype(BF)
@@ -346,74 +356,89 @@
     )
     rows_small = small.shape[0]
 
-    turned, small_u1, small_d1 = stage(
-        turn_over(right_b, straight), send_up(small), send_down(small)
-    )
-    both_u, both_d, stat_x, stat_y = stage(
-        send_up(jnp.concatenate([turned, small_u1])),
-        send_down(jnp.concatenate([turned, small_d1])),
+    turned, small_o1, small_i1 = stage(
+        turn_over(right_b, straight), swap_outer(small), swap_inner(small)
+    )
+    got_o, got_i, stat_x, stat_y = stage(
+        swap_outer(jnp.concatenate([turned, small_i1])),
+        swap_inner(jnp.concatenate([turned, small_o1])),
         swap_x(stat_b),
         swap_y(stat_b),
     )
-    turned_u1, small_u2 = both_u[:rows_right], both_u[rows_right:]
-    turned_d1, small_d2 = both_d[:rows_right], both_d[rows_right:]
-    both_u, both_d, stat_hi, stat_lo = stage(
-        send_up(both_u), send_down(both_d), swap_x(stat_y[half:]), swap_y(stat_x[:half])
-    )
-    turned_u2, small_u3 = both_u[:rows_right], both_u[rows_right:]
-    turned_d2, small_d3 = both_d[:rows_right], both_d[rows_right:]
-    small_z = along_z(
-        z, small, [(small_u1, small_d1), (small_u2, small_d2), (small_u3, small_d3)]
-    ).reshape(4 * rows_small, cols_right)
-    stat_xy = jnp.concatenate([stat_lo, stat_hi])
+    turned_o1, small_o2 = got_o[:rows_right], got_o[rows_right:]
+    turned_i1, small_i2 = got_i[:rows_right], got_i[rows_right:]
+    small_1 = ordered_pair(z % 2 == 0, small, small_o1).reshape(2 * rows_small, cols_right)
+    got_o, turned_i2, got_x, got_y = stage(
+        swap_outer(jnp.concatenate([turned_i1, small_i2])),
+        swap_inner(turned_o1),
+        swap_x(jnp.concatenate([stat_y[half:], small_1])),
+        swap_y(jnp.concatenate([stat_x[:half], small_1])),
+    )
+    turned_o2, small_o3 = got_o[:rows_right], got_o[rows_right:]
+    small_2 = ordered_pair(
+        z < 2, jnp.where(inner, small_i1, small_o2), jnp.where(inner, small_i2, small_o3)
+    ).reshape(2 * rows_small, cols_right)
+    stat_xy = jnp.concatenate([got_y[:half], got_x[:half]])
+    small_1x, small_1y = got_x[half:], got_y[half:]
     stat_keep = [jnp.where(straight, stat_b, stat_x), jnp.where(straight, stat_y, stat_xy)]
     stat_send = [jnp.where(straight, stat_x, stat_b), jnp.where(straight, stat_xy, stat_y)]
-    turned_u3, turned_d3, small_x, small_y, stat_got = stage(
-        send_up(turned_u2),
-        send_down(turned_d2),
-        swap_x(small_z),
-        swap_y(small_z),
+    turned_o3, got_x, got_y, stat_got = stage(
+        swap_outer(turned_i2),
+        swap_x(jnp.concatenate([small_1y[rows_small:], small_2])),
+        swap_y(jnp.concatenate([small_1x[:rows_small], small_2])),
         swap_core(jnp.concatenate(stat_send)),
     )
-    turned_z = along_z(
+    small_1xy = jnp.concatenate([got_y[:rows_small], got_x[:rows_small]])
+    small_2x, small_2y = got_x[rows_small:], got_y[rows_small:]
+    turned_z = in_order(
         z,
         turned,
-        [(turned_u1, turned_d1), (turned_u2, turned_d2), (turned_u3, turned_d3)],
+        turned_o1,
+        jnp.where(inner, turned_i1, turned_o2),
+        jnp.where(inner, turned_i2, turned_o3),
     )
     stat_rows = jnp.zeros((rows_right, 4 * cols_right), BF)
     stat_rows = put(stat_rows, stat_keep[0], 0, (2 * y + core) * cols_right)
     stat_rows = put(stat_rows, stat_keep[1], 0, (2 - 2 * y + core) * cols_right)
     stat_rows = put(stat_rows, stat_got[:rows_right], 0, (2 * y + 1 - core) * cols_right)
     stat_rows = put(stat_rows, stat_got[rows_right:], 0, (3 - 2 * y - core) * cols_right)
-    some = 2 * rows_small
-    small_hi, small_lo, turned_got = stage(
-        swap_x(small_y[some:]), swap_y(small_x[:some]), swap_core(turned_z)
+    small_2hi, small_2lo, turned_got = stage(
+        swap_x(small_2y[rows_small:]), swap_y(small_2x[:rows_small]), swap_core(turned_z)
     )
     right_cols = interleave(core, turned_z, turned_got)
     grad_core = jnp.zeros((4, 2, rows_left, 2 * cols_right), BF)
     left_all = jnp.zeros((4, 2, 2, part_left, cols_right), BF)
-    small_xy = jnp.concatenate([small_lo, small_hi])
-    for block, at_x, at_y in (
-        (small_z, x, y),
-        (small_x, 1 - x, y),
-        (small_y, x, 1 - y),
-        (small_xy, 1 - x, 1 - y),
+    small_2xy = jnp.concatenate([small_2lo, small_2hi])
+    low = 2 * (z // 2)
+    for block, at_z, at_x, at_y in (
+        (small_1, low, x, y),
+        (small_1x, low, 1 - x, y),
+        (small_1y, low, x, 1 - y),
+        (small_1xy, low, 1 - x, 1 - y),
+        (small_2, 2 - low, x, y),
+        (small_2x, 2 - low, 1 - x, y),
+        (small_2y, 2 - low, x, 1 - y),
+        (small_2xy, 2 - low, 1 - x, 1 - y),
     ):
-        block = block.reshape(4, 1, rows_small, cols_right)
-        grad_core = put(grad_core, block[:, :, :rows_left], 0, at_x, 0, at_y * cols_right)
-        left_all = put(left_all, block[:, :, None, rows_left:], 0, at_x, at_y, 0, 0)
+        block = block.reshape(2, 1, rows_small, cols_right)
+        grad_core = put(grad_core, block[:, :, :rows_left], at_z, at_x, 0, at_y * cols_right)
+        left_all = put(left_all, block[:, :, None, rows_left:], at_z, at_x, at_y, 0, 0)
     grad_core = grad_core.reshape(8 * rows_left, 2 * cols_right)
     left_all = left_all.reshape(8 * rows_left, cols_right)
-    (grad_other,) = stage(swap_core(grad_core))
+
+    grad_other = swap_core(grad_core)
+    rows_core = lax.dynamic_slice_in_dim(
+        right_cols.reshape(2, 2, cols_right, cols_right), core, 1, 1
+    ).reshape(2 * cols_right, cols_right)
+    carried = dot_nn(grad_core, rows_core)
+    carried = (carried + swap_core(carried.astype(BF)).astype(F32)).astype(BF)
     grad_whole = jnp.zeros((8 * rows_left, 4 * cols_right), BF)
     for k in range(2):
         cols = slice(k * cols_right, (k + 1) * cols_right)
         grad_whole = put(grad_whole, grad_core[:, cols], 0, (2 * k + core) * cols_right)
         grad_whole = put(grad_whole, grad_other[:, cols], 0, (2 * k + 1 - core) * cols_right)
-
     share = (1.0 - beta_stat) / D
     picked = lax.dynamic_slice_in_dim(grad_whole, (2 * z + core) * rows_right, rows_right, 1)
-    carried = dot_nn(grad_whole, right_cols).astype(BF)
     power = beta_stat * dot_nn(stat_rows, right_cols) + share * dot_tn(picked, carried)
     power = power.astype(BF)
 
@@ -427,95 +452,95 @@
     power_left = dot_nn(new_stat_left.astype(BF), left_all)
     power_left_b = power_left.astype(BF)
 
-    power_x, power_y, power_u1, power_d1, extra = stage(
+    power_x, power_y, near, power_i1, extra = stage(
         swap_x(power),
         swap_y(power),
-        send_up(power),
-        send_down(power),
+        swap_outer(power),
+        swap_inner(power),
         turn_over(jnp.concatenate([rotated, power_left_b]), straight),
     )
-    near = near_of(z, power_u1, power_d1)
     rotated, left_t = extra[:rows_left], extra[rows_left:]
     new_moment_one, new_moment_two, direction = adam_moments(
         rotated.astype(F32), moment_one, moment_two
     )
-    got_x, got_y, got_u, got_d, direction_t = stage(
+    got_x, got_y, got_o, got_i, direction_t = stage(
         swap_x(jnp.concatenate([power_y[half:], near])),
         swap_y(jnp.concatenate([power_x[:half], near])),
-        send_up(jnp.concatenate([power_u1, left_t])),
-        send_down(jnp.concatenate([power_d1, left_t])),
+        swap_outer(jnp.concatenate([power_i1, left_t])),
+        swap_inner(jnp.concatenate([near, left_t])),
         turn_over(direction, straight),
     )
-    slab0 = jnp.concatenate(
-        [power, power_x, power_y, jnp.concatenate([got_y[:half], got_x[:half]])], axis=1
-    )
+    slab0 = jnp.concatenate([power, power_x, power_y, got_y[:half], got_x[:half]])
     near_x, near_y = got_x[half:], got_y[half:]
-    power_u2, left_u1 = got_u[:rows_right], got_u[rows_right:]
-    power_d2, left_d1 = got_d[:rows_right], got_d[rows_right:]
-    mid = mid_of(z, power_u1, power_d1, power_u2, power_d2)
-    got_x, got_y, got_u, got_d, slab0_other = stage(
+    power_o2, left_o1 = got_o[:rows_right], got_o[rows_right:]
+    power_i2, left_i1 = got_i[:rows_right], got_i[rows_right:]
+    mid = jnp.where(inner, power_i1, power_o2)
+    got_x, got_y, got_o, got_i, slab0_other = stage(
         swap_x(jnp.concatenate([near_y[half:], mid])),
         swap_y(jnp.concatenate([near_x[:half], mid])),
-        send_up(jnp.concatenate([power_u2, left_u1, direction_t])),
-        send_down(jnp.concatenate([power_d2, left_d1, direction_t])),
+        swap_outer(jnp.concatenate([power_i2, left_i1, direction_t])),
+        swap_inner(jnp.concatenate([left_o1, direction_t])),
         swap_core(slab0),
     )
-    slab1 = jnp.concatenate(
-        [near, near_x, near_y, jnp.concatenate([got_y[:half], got_x[:half]])], axis=1
-    )
+    slab1 = jnp.concatenate([near, near_x, near_y, got_y[:half], got_x[:half]])
     mid_x, mid_y = got_x[half:], got_y[half:]
-    power_u3, rest_u = got_u[:rows_right], got_u[rows_right:]
-    power_d3, rest_d = got_d[:rows_right], got_d[rows_right:]
-    left_u2, direction_u1 = rest_u[:rows_left], rest_u[rows_left:]
-    left_d2, direction_d1 = rest_d[:rows_left], rest_d[rows_left:]
-    far = far_of(z, power_u2, power_d2, power_u3, power_d3)
-    got_x, got_y, rest_u, rest_d, slab1_other = stage(
+    power_o3, left_o2, direction_o1 = (
+        got_o[:rows_right],
+        got_o[rows_right:-rows_left],
+        got_o[-rows_left:],
+    )
+    left_i2, direction_i1 = got_i[:rows_left], got_i[rows_left:]
+    far = jnp.where(inner, power_i2, power_o3)
+    got_x, got_y, got_o, direction_i2, slab1_other = stage(
         swap_x(jnp.concatenate([mid_y[half:], far])),
         swap_y(jnp.concatenate([mid_x[:half], far])),
-        send_up(rest_u),
-        send_down(rest_d),
+        swap_outer(jnp.concatenate([left_i2, direction_i1])),
+        swap_inner(direction_o1),
         swap_core(slab1),
     )
-    slab2 = jnp.concatenate(
-        [mid, mid_x, mid_y, jnp.concatenate([got_y[:half], got_x[:half]])], axis=1
-    )
+    slab2 = jnp.concatenate([mid, mid_x, mid_y, got_y[:half], got_x[:half]])
     far_x, far_y = got_x[half:], got_y[half:]
-    left_u3, direction_u2 = rest_u[:rows_left], rest_u[rows_left:]
-    left_d3, direction_d2 = rest_d[:rows_left], rest_d[rows_left:]
-    left_z = along_z(z, left_t, [(left_u1, left_d1), (left_u2, left_d2), (left_u3, left_d3)])
-    got_x, got_y, direction_u3, direction_d3, slab2_other, left_other = stage(
+    left_o3, direction_o2 = got_o[:rows_left], got_o[rows_left:]
+    left_z = in_order(
+        z,
+        left_t,
+        left_o1,
+        jnp.where(inner, left_i1, left_o2),
+        jnp.where(inner, left_i2, left_o3),
+    )
+    got_x, got_y, direction_o3, slab2_other, left_other = stage(
         swap_x(far_y[half:]),
         swap_y(far_x[:half]),
-        send_up(direction_u2),
-        send_down(direction_d2),
+        swap_outer(direction_i2),
         swap_core(slab2),
         swap_core(left_z),
     )
-    slab3 = jnp.concatenate([far, far_x, far_y, jnp.concatenate([got_y, got_x])], axis=1)
-    direction_z = along_z(
+    slab3 = jnp.concatenate([far, far_x, far_y, got_y, got_x])
+    direction_z = in_order(
         z,
         direction_t,
-        [
-            (direction_u1, direction_d1),
-            (direction_u2, direction_d2),
-            (direction_u3, direction_d3),
-        ],
-    )
-    slab3_other, direction_other = stage(swap_core(slab3), swap_core(direction_z))
+        direction_o1,
+        jnp.where(inner, direction_i1, direction_o2),
+        jnp.where(inner, direction_i2, direction_o3),
+    )
+    sum_core = squares(slab0) + squares(slab1) + squares(slab2) + squares(slab3)
+    sum_core = jnp.full((8, 128), sum_core)
+    slab3_other, direction_other, sum_other = stage(
+        swap_core(slab3), swap_core(direction_z), swap_core(sum_core)
+    )
+    square_right = FF / (16.0 * (sum_core[0, 0] + sum_other[0, 0]))
 
     slabs = (slab0, slab0_other, slab1, slab1_other, slab2, slab2_other, slab3, slab3_other)
-    own = lax.dynamic_slice_in_dim(jnp.where(straight, slab0, slab0_other), core * half, half, 0)
-    first, square_right = refresh_pass(0, jnp.full((1,), FF / 16.0, F32), slabs, own)
-    (second,) = refresh_pass(1, square_right, slabs, first)
-    (third,) = refresh_pass(2, square_right, slabs, second)
-    scales = jnp.concatenate([square_right, math.sqrt(FF) * jnp.sqrt(square_right)])
-    (fresh,) = refresh_pass(3, scales, slabs, third, first)
-    ahead, behind = fresh[:, :cols_right], fresh[:, cols_right:]
-    mine = jnp.where(straight, ahead, behind)
-    theirs = swap_core(jnp.where(straight, behind, ahead))
-    new_basis_right = jnp.where(
-        core == 0, jnp.concatenate([mine, theirs]), jnp.concatenate([theirs, mine])
-    )
+    scales = jnp.stack([square_right, math.sqrt(FF) * jnp.sqrt(square_right)])
+    places = jnp.stack(
+        [jnp.where(straight, 0, rows_right) + core * half, straight.astype(jnp.int32)]
+    )
+    first, second = refresh_part(0, scales, places, slabs)
+    (fresh,) = refresh_part(1, scales, places, slabs, second, first)
+    theirs = swap_core(fresh[1])
+    new_basis_right = jnp.zeros((rows_right, cols_right), F32)
+    new_basis_right = put(new_basis_right, fresh[0], core * half, 0)
+    new_basis_right = put(new_basis_right, theirs, (1 - core) * half, 0)
 
     direction_cols = interleave(core, direction_z, direction_other)
     left_rows = lax.dynamic_slice_in_dim(left_all, (2 * z + core) * rows_left, rows_left, 0)
@@ -530,7 +555,7 @@
     update = turn_over((kept + swap_x(away).astype(F32)).astype(BF), straight)
 
     power_all = interleave(core, left_z, left_other)
-    square_left = D / (16.0 * jnp.sum(jnp.square(power_all.astype(F32))))
+    square_left = D / (16.0 * squares(power_all))
     keep = power_left
     value = power_left
     for turn in range(4):

time: 385 us -> 329 us (0.85)
  other arithmetic: 51.6 us -> 27 us
  starting transfers between devices: 86.3 us -> 67.7 us
  Pallas kernels: 62 us -> 49.7 us
  waiting for transfers between devices: 127 us -> 119 us
  matrix products: 22 us -> 26.7 us
    concatenate x10 -> x11, other arithmetic: 32 us -> 2.26 us  [the longest x3 1.73 us: ordered_pair(): both = jnp.concatenate([first[None], second[None]])]
    ppermute x18 -> x16, starting transfers between devices: 48.6 us -> 24.2 us  [the longest x7 20 us: swap_inner(): lax.ppermute(a, AXES, pairs(lambda z, x, y, c: (3 - z if 0 < z < 3 else -...]
    ppermute x10, waiting for transfers between devices: 39.6 us -> 27.3 us  [swap_y(): return lax.ppermute(a, AXES, pairs(lambda z, x, y, c: (z, x, 1 - y, c)))]
    pallas_call x4 -> x2, Pallas kernels: 62 us -> 49.7 us  [refresh_part(): pl.pallas_call(functools.partial(refresh_kernel, part), out_shape=shapes,...]
    ppermute x10, waiting for transfers between devices: 18.6 us -> 6.43 us  [swap_x(): return lax.ppermute(a, AXES, pairs(lambda z, x, y, c: (z, 1 - x, y, c)))]
    ppermute x18 -> x16, waiting for transfers between devices: 44.6 us -> 53.8 us  [the longest x7 33.2 us: swap_inner(): lax.ppermute(a, AXES, pairs(lambda z, x, y, c: (3 - z if 0 < z < 3 else -...]
    reduce_sum x1 -> x5, other arithmetic: 1.2 us -> 10.3 us  [squares(): return jnp.sum(jnp.square(tiles.astype(F32)))]
    dot_general x7, matrix products: 10.6 us -> 15.1 us  [dot_nn(): return jnp.dot(a, b, preferred_element_type=F32)]
  transfers between devices with their start and end apart: 52 -> 52, of which waited for: 30 -> 28; matrix products, arithmetic and copies ran while one was open for 9% -> 15% of each run, Pallas kernels for 16% -> 15%
where the time goes in v3:
time: 329 us; the launch traced here: 326 us
  waiting for transfers between devices  119 us (36%)
  starting transfers between devices  67.7 us (21%)
  Pallas kernels  49.7 us (15%)
  local copies, waits for them, and re-layouts  29.4 us (9%)
  other arithmetic  27 us (8%)
  matrix products  26.7 us (8%)
  between operations  6.14 us (2%)
    pallas_call x2, Pallas kernels, refresh_part(): pl.pallas_call(functools.partial(refresh_kernel, part), out_shape=shapes,...  49.7 us
    ppermute x7, waiting for transfers between devices, swap_inner(): lax.ppermute(a, AXES, pairs(lambda z, x, y, c: (3 - z if 0 < z < 3 else -...  33.2 us
    ppermute x4, waiting for transfers between devices, turn_over(): return jnp.where(straight, a, lax.ppermute(a, AXES, crossed))  27.8 us
    ppermute x10, waiting for transfers between devices, swap_y(): return lax.ppermute(a, AXES, pairs(lambda z, x, y, c: (z, x, 1 - y, c)))  27.3 us
    ppermute x9, waiting for transfers between devices, swap_outer(): lax.ppermute(a, AXES, pairs(lambda z, x, y, c: (z + 1 - 2 * (z % 2), x, y...  20.6 us
    ppermute x7, starting transfers between devices, swap_inner(): lax.ppermute(a, AXES, pairs(lambda z, x, y, c: (3 - z if 0 < z < 3 else -...  20 us
    ppermute x12, starting transfers between devices, swap_core(): return lax.ppermute(a, AXES, pairs(lambda z, x, y, c: (z, x, y, 1 - c)))  15.4 us
    dot_general x7, matrix products, dot_nn(): return jnp.dot(a, b, preferred_element_type=F32)  15.1 us
  transfers between devices with their start and end apart: 52, of which 28 were waited for; matrix products, arithmetic and copies ran while one was open for 15% of the time, Pallas kernels for 15%

profile of v3, /device:TPU:9, one launch (start us, length us, event | category | flops | bytes accessed | tf_op | source)
XLA Modules:
  0.0 325.6 jit_solution(2586521164640023794)
XLA Ops:
  3.0 3.7 %collective-permute-start = (bf16[384,768]{1,0:T(8,128)(2,1)}, bf16[384,768]{1,0:T(8,128)(2,1)}, u32[]{:S(2)}, u32[]{:S(2)}) collective-permute-start(bf16[384,768]{1,0:T(8,128)(2,1)} %multiply_convert_fusion), channel_id=1, source_target_pairs={{1,4},{3,6},{4,1},{6,3},{9,12},{11,14},{12,9},{14,11},{17,20},{19,... | collective-permute-start | bytes 1769480 | tf_op jit(solution)/shard_map/ppermute | solution.py:185
  9.4 4.3 %collective-permute-start.2 = (bf16[144,768]{1,0:T(8,128)(2,1)S(1)}, bf16[144,768]{1,0:T(8,128)(2,1)S(1)}, u32[]{:S(2)}, u32[]{:S(2)}) collective-permute-start(bf16[144,768]{1,0:T(8,128)(2,1)S(1)} %get-tuple-element.152), channel_id=1, source_target_pairs={{8,16},{9,17},{10,18},{11,19},{12,20},{13,21},{14,22},{15,23},{16,... | collective-permute-start | bytes 663560 | tf_op jit(solution)/shard_map/ppermute | solution.py:180
  18.9 3.6 %collective-permute-start.4 = (bf16[528,768]{1,0:T(8,128)(2,1)S(1)}, bf16[528,768]{1,0:T(8,128)(2,1)S(1)}, u32[]{:S(2)}, u32[]{:S(2)}) collective-permute-start(bf16[528,768]{1,0:T(8,128)(2,1)S(1)} %get-tuple-element.144), channel_id=1, source_target_pairs={{8,16},{9,17},{10,18},{11,19},{12,20},{13,21},{14,22},{15,23},{16,... | collective-permute-start | bytes 2433032 | tf_op jit(solution)/shard_map/ppermute | solution.py:180
  23.3 6.4 %collective-permute-done.6 = bf16[384,768]{1,0:T(8,128)(2,1)} collective-permute-done((bf16[384,768]{1,0:T(8,128)(2,1)}, bf16[384,768]{1,0:T(8,128)(2,1)}, u32[]{:S(2)}, u32[]{:S(2)}) %collective-permute-start.6) | collective-permute-done | bytes 589856 | tf_op jit(solution)/shard_map/ppermute | solution.py:168
  31.2 9.6 %collective-permute-done.4 = bf16[528,768]{1,0:T(8,128)(2,1)S(1)} collective-permute-done((bf16[528,768]{1,0:T(8,128)(2,1)S(1)}, bf16[528,768]{1,0:T(8,128)(2,1)S(1)}, u32[]{:S(2)}, u32[]{:S(2)}) %collective-permute-start.4) | collective-permute-done | bytes 811040 | tf_op jit(solution)/shard_map/ppermute | solution.py:180
  49.7 10.8 %collective-permute-done.8 = bf16[384,768]{1,0:T(8,128)(2,1)S(1)} collective-permute-done((bf16[384,768]{1,0:T(8,128)(2,1)S(1)}, bf16[384,768]{1,0:T(8,128)(2,1)S(1)}, u32[]{:S(2)}, u32[]{:S(2)}) %collective-permute-start.8) | collective-permute-done | bytes 589856 | tf_op jit(solution)/shard_map/ppermute | solution.py:180
  60.5 3.7 %collective-permute-done.10 = bf16[480,768]{1,0:T(8,128)(2,1)S(1)} collective-permute-done((bf16[480,768]{1,0:T(8,128)(2,1)S(1)}, bf16[480,768]{1,0:T(8,128)(2,1)S(1)}, u32[]{:S(2)}, u32[]{:S(2)}) %collective-permute-start.10) | collective-permute-done | bytes 737312 | tf_op jit(solution)/shard_map/ppermute | solution.py:168
  72.5 6.5 %collective-permute-done.11 = bf16[384,768]{1,0:T(8,128)(2,1)S(1)} collective-permute-done((bf16[384,768]{1,0:T(8,128)(2,1)S(1)}, bf16[384,768]{1,0:T(8,128)(2,1)S(1)}, u32[]{:S(2)}, u32[]{:S(2)}) %collective-permute-start.11) | collective-permute-done | bytes 589856 | tf_op jit(solution)/shard_map/ppermute | solution.py:176
  83.5 4.0 %collective-permute-start.17 = (bf16[4,384,768]{2,1,0:T(8,128)(2,1)S(1)}, bf16[4,384,768]{2,1,0:T(8,128)(2,1)S(1)}, u32[]{:S(2)}, u32[]{:S(2)}) collective-permute-start(bf16[4,384,768]{2,1,0:T(8,128)(2,1)S(1)} %bitcast_dynamic-update-slice_fusion.6), channel_id=1, source_target_pairs={{0,1},{1,0},{2,3},{3,2},{4,5},{5,4},{6,7},{7,6},{8,9},{9,8},{10,11... | collective-permute-start | bytes 7077896 | tf_op jit(solution)/shard_map/ppermute | solution.py:172
  111.2 11.0 %collective-permute-done.24 = bf16[192,768]{1,0:T(8,128)(2,1)S(1)} collective-permute-done((bf16[192,768]{1,0:T(8,128)(2,1)S(1)}, bf16[192,768]{1,0:T(8,128)(2,1)S(1)}, u32[]{:S(2)}, u32[]{:S(2)}) %collective-permute-start.24) | collective-permute-done | bytes 294944 | tf_op jit(solution)/shard_map/ppermute | solution.py:185
  126.6 4.4 %collective-permute-start.29 = (bf16[96,768]{1,0:T(8,128)(2,1)S(1)}, bf16[96,768]{1,0:T(8,128)(2,1)S(1)}, u32[]{:S(2)}, u32[]{:S(2)}) collective-permute-start(bf16[96,768]{1,0:T(8,128)(2,1)S(1)} %get-tuple-element.107), channel_id=1, source_target_pairs={{1,4},{3,6},{4,1},{6,3},{9,12},{11,14},{12,9},{14,11},{17,20},{19,... | collective-permute-start | bytes 442376 | tf_op jit(solution)/shard_map/ppermute | solution.py:185
  131.2 15.0 %collective-permute-done.29 = bf16[96,768]{1,0:T(8,128)(2,1)S(1)} collective-permute-done((bf16[96,768]{1,0:T(8,128)(2,1)S(1)}, bf16[96,768]{1,0:T(8,128)(2,1)S(1)}, u32[]{:S(2)}, u32[]{:S(2)}) %collective-permute-start.29) | collective-permute-done | bytes 147488 | tf_op jit(solution)/shard_map/ppermute | solution.py:185
  152.2 7.3 %collective-permute-done.33 = bf16[192,768]{1,0:T(8,128)(2,1)S(1)} collective-permute-done((bf16[192,768]{1,0:T(8,128)(2,1)S(1)}, bf16[192,768]{1,0:T(8,128)(2,1)S(1)}, u32[]{:S(2)}, u32[]{:S(2)}) %collective-permute-start.33) | collective-permute-done | bytes 294944 | tf_op jit(solution)/shard_map/ppermute | solution.py:180
  159.5 7.8 %collective-permute-done.32 = bf16[576,768]{1,0:T(8,128)(2,1)S(1)} collective-permute-done((bf16[576,768]{1,0:T(8,128)(2,1)S(1)}, bf16[576,768]{1,0:T(8,128)(2,1)S(1)}, u32[]{:S(2)}, u32[]{:S(2)}) %collective-permute-start.32) | collective-permute-done | bytes 884768 | tf_op jit(solution)/shard_map/ppermute | solution.py:176
  176.0 3.9 %collective-permute-done.38 = bf16[96,768]{1,0:T(8,128)(2,1)S(1)} collective-permute-done((bf16[96,768]{1,0:T(8,128)(2,1)S(1)}, bf16[96,768]{1,0:T(8,128)(2,1)S(1)}, u32[]{:S(2)}, u32[]{:S(2)}) %collective-permute-start.38) | collective-permute-done | bytes 147488 | tf_op jit(solution)/shard_map/ppermute | solution.py:180
  179.9 11.4 %collective-permute-done.36 = bf16[576,768]{1,0:T(8,128)(2,1)S(1)} collective-permute-done((bf16[576,768]{1,0:T(8,128)(2,1)S(1)}, bf16[576,768]{1,0:T(8,128)(2,1)S(1)}, u32[]{:S(2)}, u32[]{:S(2)}) %collective-permute-start.36) | collective-permute-done | bytes 884768 | tf_op jit(solution)/shard_map/ppermute | solution.py:168
  200.7 4.2 %collective-permute-done.42 = bf16[96,768]{1,0:T(8,128)(2,1)S(1)} collective-permute-done((bf16[96,768]{1,0:T(8,128)(2,1)S(1)}, bf16[96,768]{1,0:T(8,128)(2,1)S(1)}, u32[]{:S(2)}, u32[]{:S(2)}) %collective-permute-start.42) | collective-permute-done | bytes 147488 | tf_op jit(solution)/shard_map/ppermute | solution.py:176
  210.3 3.3 %fusion = f32[384,768]{1,0:T(8,128)} fusion(bf16[768,3072]{1,0:T(8,128)(2,1)} %copy-done.22, s32[]{:T(128)S(6)} %select_n.404, f32[384,768]{1,0:T(8,128)S(1)} %copy-done.23, s32[]{:T(128)S(6)} %select_n.403), kind=kOutput, calls=%fused_computation.10 | convolution fusion | flops 453869568 | bytes 4128776 | tf_op jit(solution)/shard_map/dot_general | solution.py:145
  218.7 3.6 %multiply_reduce_fusion.1 = f32[]{:T(128)} fusion(bf16[1536,768]{1,0:T(8,128)(2,1)} %copy-done.5), kind=kLoop, calls=%fused_computation.1 | loop fusion | flops 3538943 | bytes 2359300 | tf_op jit(solution)/shard_map/reduce_sum | solution.py:335
  234.6 5.5 %fusion.14 = f32[96,3072]{1,0:T(8,128)} fusion(bf16[3072,768]{1,0:T(8,128)(2,1)} %bitcast.166, bf16[768,768]{1,0:T(8,128)(2,1)} %bitcast.174, bf16[768,768]{1,0:T(8,128)(2,1)} %bitcast.173, s32[]{:T(128)S(6)} %select_n.371), kind=kOutput, calls=%fused_computation.42 | convolution fusion | flops 566304768 | bytes 7225348 | tf_op jit(solution)/shard_map/dot_general | solution.py:141
  253.3 24.9 %shard_map.126 = (f32[192,3072]{1,0:T(8,128)S(1)}, f32[192,3072]{1,0:T(8,128)S(1)}) custom-call(f32[2]{0:T(128)S(1)} %pad_maximum_fusion.22.scale_ref, s32[2]{0:T(128)S(1)} %pad_add_fusion.place_ref, bf16[1536,768]{1,0:T(8,128)(2,1)S(1)} %copy-done.4, bf16[1536,768]{1,0:T(8,128)(2,1)S(1)} %copy-done.12, bf16[1536,768]{1,0:T(8,128)(2,1)S(1)} %copy-done.10, ...), custom_call_target="tpu_custom_call" | custom-call | flops 14495514624 | bytes 18874368 | tf_op jit(solution)/shard_map/pallas_call | solution.py:321
  281.0 24.8 %shard_map.127 = f32[2,192,768]{2,1,0:T(8,128)S(1)} custom-call(f32[2]{0:T(128)S(1)} %pad_maximum_fusion.22.scale_ref, s32[2]{0:T(128)S(1)} %pad_add_fusion.place_ref, bf16[1536,768]{1,0:T(8,128)(2,1)S(1)} %copy-done.4, bf16[1536,768]{1,0:T(8,128)(2,1)S(1)} %copy-done.12, bf16[1536,768]{1,0:T(8,128)(2,1)S(1)} %copy-done.10, ...), custom_call_target="tpu_custom_call" | custom-call | flops 14495514624 | bytes 18874368 | tf_op jit(solution)/shard_map/pallas_call | solution.py:321
  307.5 3.4 %fusion.10 = f32[96,768]{1,0:T(8,128)} fusion(bf16[768,768]{1,0:T(8,128)(2,1)} %bitcast.162, f32[96,768]{1,0:T(8,128)} %convolution_multiply_fusion.5, f32[]{:T(128)S(6)} %div.69), kind=kOutput, calls=%fused_computation.29 | convolution fusion | flops 226934784 | bytes 1769476 | tf_op jit(solution)/shard_map/dot_general | solution.py:137
  318.4 3.3 %collective-permute-start.50 = (bf16[96,768]{1,0:T(8,128)(2,1)S(1)}, bf16[96,768]{1,0:T(8,128)(2,1)S(1)}, u32[]{:S(2)}, u32[]{:S(2)}) collective-permute-start(bf16[96,768]{1,0:T(8,128)(2,1)S(1)} %add_convert_fusion.1), channel_id=1, source_target_pairs={{1,4},{3,6},{4,1},{6,3},{9,12},{11,14},{12,9},{14,11},{17,20},{19,... | collective-permute-start | bytes 442376 | tf_op jit(solution)/shard_map/ppermute | solution.py:185
  (324 shorter events, 132.8 us)
Async XLA Ops:
  18.9 22.0 %collective-permute-start.4 = (bf16[528,768]{1,0:T(8,128)(2,1)S(1)}, bf16[528,768]{1,0:T(8,128)(2,1)S(1)}, u32[]{:S(2)}, u32[]{:S(2)}) collective-permute-start(bf16[528,768]{1,0:T(8,128)(2,1)S(1)} %get-tuple-element.144), channel_id=1, source_target_pairs={{8,16},{9,17},{10,18},{11,19},{12,20},{13,21},{14,22},{15,23},{16,... | collective-permute-start | bytes 2433032 | tf_op jit(solution)/shard_map/ppermute | solution.py:180
  22.5 19.9 %collective-permute-start.3 = (bf16[528,768]{1,0:T(8,128)(2,1)S(1)}, bf16[528,768]{1,0:T(8,128)(2,1)S(1)}, u32[]{:S(2)}, u32[]{:S(2)}) collective-permute-start(bf16[528,768]{1,0:T(8,128)(2,1)S(1)} %get-tuple-element.145), channel_id=1, source_target_pairs={{0,8},{1,9},{2,10},{3,11},{4,12},{5,13},{6,14},{7,15},{8,0},{9,1},... | collective-permute-start | bytes 2433032 | tf_op jit(solution)/shard_map/ppermute | solution.py:176
  44.4 16.1 %collective-permute-start.8 = (bf16[384,768]{1,0:T(8,128)(2,1)S(1)}, bf16[384,768]{1,0:T(8,128)(2,1)S(1)}, u32[]{:S(2)}, u32[]{:S(2)}) collective-permute-start(bf16[384,768]{1,0:T(8,128)(2,1)S(1)} %slice.249), channel_id=1, source_target_pairs={{8,16},{9,17},{10,18},{11,19},{12,20},{13,21},{14,22},{15,23},{16,... | collective-permute-start | bytes 1769480 | tf_op jit(solution)/shard_map/ppermute | solution.py:180
  46.6 19.0 %collective-permute-start.7 = (bf16[528,768]{1,0:T(8,128)(2,1)S(1)}, bf16[528,768]{1,0:T(8,128)(2,1)S(1)}, u32[]{:S(2)}, u32[]{:S(2)}) collective-permute-start(bf16[528,768]{1,0:T(8,128)(2,1)S(1)} %collective-permute-done.4), channel_id=1, source_target_pairs={{0,8},{1,9},{2,10},{3,11},{4,12},{5,13},{6,14},{7,15},{8,0},{9,1},... | collective-permute-start | bytes 2433032 | tf_op jit(solution)/shard_map/ppermute | solution.py:176
  46.8 17.4 %collective-permute-start.10 = (bf16[480,768]{1,0:T(8,128)(2,1)S(1)}, bf16[480,768]{1,0:T(8,128)(2,1)S(1)}, u32[]{:S(2)}, u32[]{:S(2)}) collective-permute-start(bf16[480,768]{1,0:T(8,128)(2,1)S(1)} %get-tuple-element.148), channel_id=1, source_target_pairs={{0,2},{1,3},{2,0},{3,1},{4,6},{5,7},{6,4},{7,5},{8,10},{9,11},{10,... | collective-permute-start | bytes 2211848 | tf_op jit(solution)/shard_map/ppermute | solution.py:168
  48.1 17.0 %collective-permute-start.9 = (bf16[480,768]{1,0:T(8,128)(2,1)S(1)}, bf16[480,768]{1,0:T(8,128)(2,1)S(1)}, u32[]{:S(2)}, u32[]{:S(2)}) collective-permute-start(bf16[480,768]{1,0:T(8,128)(2,1)S(1)} %get-tuple-element.149), channel_id=1, source_target_pairs={{0,4},{1,5},{2,6},{3,7},{4,0},{5,1},{6,2},{7,3},{8,12},{9,13},{10,... | collective-permute-start | bytes 2211848 | tf_op jit(solution)/shard_map/ppermute | solution.py:164
  99.7 22.6 %collective-permute-start.23 = (bf16[384,768]{1,0:T(8,128)(2,1)S(1)}, bf16[384,768]{1,0:T(8,128)(2,1)S(1)}, u32[]{:S(2)}, u32[]{:S(2)}) collective-permute-start(bf16[384,768]{1,0:T(8,128)(2,1)S(1)} %get-tuple-element.160), channel_id=1, source_target_pairs={{8,16},{9,17},{10,18},{11,19},{12,20},{13,21},{14,22},{15,23},{16,... | collective-permute-start | bytes 1769480 | tf_op jit(solution)/shard_map/ppermute | solution.py:180
  103.0 19.3 %collective-permute-start.22 = (bf16[384,768]{1,0:T(8,128)(2,1)S(1)}, bf16[384,768]{1,0:T(8,128)(2,1)S(1)}, u32[]{:S(2)}, u32[]{:S(2)}) collective-permute-start(bf16[384,768]{1,0:T(8,128)(2,1)S(1)} %get-tuple-element.160), channel_id=1, source_target_pairs={{0,8},{1,9},{2,10},{3,11},{4,12},{5,13},{6,14},{7,15},{8,0},{9,1},... | collective-permute-start | bytes 1769480 | tf_op jit(solution)/shard_map/ppermute | solution.py:176
  103.1 19.3 %collective-permute-start.21 = (bf16[384,768]{1,0:T(8,128)(2,1)S(1)}, bf16[384,768]{1,0:T(8,128)(2,1)S(1)}, u32[]{:S(2)}, u32[]{:S(2)}) collective-permute-start(bf16[384,768]{1,0:T(8,128)(2,1)S(1)} %get-tuple-element.160), channel_id=1, source_target_pairs={{0,2},{1,3},{2,0},{3,1},{4,6},{5,7},{6,4},{7,5},{8,10},{9,11},{10,... | collective-permute-start | bytes 1769480 | tf_op jit(solution)/shard_map/ppermute | solution.py:168
  104.0 18.3 %collective-permute-start.20 = (bf16[384,768]{1,0:T(8,128)(2,1)S(1)}, bf16[384,768]{1,0:T(8,128)(2,1)S(1)}, u32[]{:S(2)}, u32[]{:S(2)}) collective-permute-start(bf16[384,768]{1,0:T(8,128)(2,1)S(1)} %get-tuple-element.160), channel_id=1, source_target_pairs={{0,4},{1,5},{2,6},{3,7},{4,0},{5,1},{6,2},{7,3},{8,12},{9,13},{10,... | collective-permute-start | bytes 1769480 | tf_op jit(solution)/shard_map/ppermute | solution.py:164
  122.6 23.6 %collective-permute-start.26 = (bf16[576,768]{1,0:T(8,128)(2,1)S(1)}, bf16[576,768]{1,0:T(8,128)(2,1)S(1)}, u32[]{:S(2)}, u32[]{:S(2)}) collective-permute-start(bf16[576,768]{1,0:T(8,128)(2,1)S(1)} %get-tuple-element.142), channel_id=1, source_target_pairs={{0,2},{1,3},{2,0},{3,1},{4,6},{5,7},{6,4},{7,5},{8,10},{9,11},{10,... | collective-permute-start | bytes 2654216 | tf_op jit(solution)/shard_map/ppermute | solution.py:168
  123.2 23.0 %collective-permute-start.25 = (bf16[576,768]{1,0:T(8,128)(2,1)S(1)}, bf16[576,768]{1,0:T(8,128)(2,1)S(1)}, u32[]{:S(2)}, u32[]{:S(2)}) collective-permute-start(bf16[576,768]{1,0:T(8,128)(2,1)S(1)} %get-tuple-element.143), channel_id=1, source_target_pairs={{0,4},{1,5},{2,6},{3,7},{4,0},{5,1},{6,2},{7,3},{8,12},{9,13},{10,... | collective-permute-start | bytes 2654216 | tf_op jit(solution)/shard_map/ppermute | solution.py:164
  123.3 22.9 %collective-permute-start.28 = (bf16[480,768]{1,0:T(8,128)(2,1)S(1)}, bf16[480,768]{1,0:T(8,128)(2,1)S(1)}, u32[]{:S(2)}, u32[]{:S(2)}) collective-permute-start(bf16[480,768]{1,0:T(8,128)(2,1)S(1)} %get-tuple-element.153), channel_id=1, source_target_pairs={{8,16},{9,17},{10,18},{11,19},{12,20},{13,21},{14,22},{15,23},{16,... | collective-permute-start | bytes 2211848 | tf_op jit(solution)/shard_map/ppermute | solution.py:180
  125.5 20.7 %collective-permute-start.27 = (bf16[480,768]{1,0:T(8,128)(2,1)S(1)}, bf16[480,768]{1,0:T(8,128)(2,1)S(1)}, u32[]{:S(2)}, u32[]{:S(2)}) collective-permute-start(bf16[480,768]{1,0:T(8,128)(2,1)S(1)} %get-tuple-element.154), channel_id=1, source_target_pairs={{0,8},{1,9},{2,10},{3,11},{4,12},{5,13},{6,14},{7,15},{8,0},{9,1},... | collective-permute-start | bytes 2211848 | tf_op jit(solution)/shard_map/ppermute | solution.py:176
  126.6 19.6 %collective-permute-start.29 = (bf16[96,768]{1,0:T(8,128)(2,1)S(1)}, bf16[96,768]{1,0:T(8,128)(2,1)S(1)}, u32[]{:S(2)}, u32[]{:S(2)}) collective-permute-start(bf16[96,768]{1,0:T(8,128)(2,1)S(1)} %get-tuple-element.107), channel_id=1, source_target_pairs={{1,4},{3,6},{4,1},{6,3},{9,12},{11,14},{12,9},{14,11},{17,20},{19,... | collective-permute-start | bytes 442376 | tf_op jit(solution)/shard_map/ppermute | solution.py:185
  146.4 22.9 %collective-permute-start.34 = (bf16[1536,768]{1,0:T(8,128)(2,1)S(1)}, bf16[1536,768]{1,0:T(8,128)(2,1)S(1)}, u32[]{:S(2)}, u32[]{:S(2)}) collective-permute-start(bf16[1536,768]{1,0:T(8,128)(2,1)S(1)} %get-tuple-element.128.refs_0_), channel_id=1, source_target_pairs={{0,1},{1,0},{2,3},{3,2},{4,5},{5,4},{6,7},{7,6},{8,9},{9,8},{10,11... | collective-permute-start | bytes 7077896 | tf_op jit(solution)/shard_map/ppermute | solution.py:172
  146.5 20.8 %collective-permute-start.32 = (bf16[576,768]{1,0:T(8,128)(2,1)S(1)}, bf16[576,768]{1,0:T(8,128)(2,1)S(1)}, u32[]{:S(2)}, u32[]{:S(2)}) collective-permute-start(bf16[576,768]{1,0:T(8,128)(2,1)S(1)} %pad_maximum_fusion.9), channel_id=1, source_target_pairs={{0,8},{1,9},{2,10},{3,11},{4,12},{5,13},{6,14},{7,15},{8,0},{9,1},... | collective-permute-start | bytes 2654216 | tf_op jit(solution)/shard_map/ppermute | solution.py:176
  148.2 20.5 %collective-permute-start.31 = (bf16[576,768]{1,0:T(8,128)(2,1)S(1)}, bf16[576,768]{1,0:T(8,128)(2,1)S(1)}, u32[]{:S(2)}, u32[]{:S(2)}) collective-permute-start(bf16[576,768]{1,0:T(8,128)(2,1)S(1)} %get-tuple-element.140), channel_id=1, source_target_pairs={{0,2},{1,3},{2,0},{3,1},{4,6},{5,7},{6,4},{7,5},{8,10},{9,11},{10,... | collective-permute-start | bytes 2654216 | tf_op jit(solution)/shard_map/ppermute | solution.py:168
  149.2 20.1 %collective-permute-start.30 = (bf16[576,768]{1,0:T(8,128)(2,1)S(1)}, bf16[576,768]{1,0:T(8,128)(2,1)S(1)}, u32[]{:S(2)}, u32[]{:S(2)}) collective-permute-start(bf16[576,768]{1,0:T(8,128)(2,1)S(1)} %get-tuple-element.141), channel_id=1, source_target_pairs={{0,4},{1,5},{2,6},{3,7},{4,0},{5,1},{6,2},{7,3},{8,12},{9,13},{10,... | collective-permute-start | bytes 2654216 | tf_op jit(solution)/shard_map/ppermute | solution.py:164
  169.4 22.2 %collective-permute-start.39 = (bf16[1536,768]{1,0:T(8,128)(2,1)S(1)}, bf16[1536,768]{1,0:T(8,128)(2,1)S(1)}, u32[]{:S(2)}, u32[]{:S(2)}) collective-permute-start(bf16[1536,768]{1,0:T(8,128)(2,1)S(1)} %get-tuple-element.124.refs_2_), channel_id=1, source_target_pairs={{0,1},{1,0},{2,3},{3,2},{4,5},{5,4},{6,7},{7,6},{8,9},{9,8},{10,11... | collective-permute-start | bytes 7077896 | tf_op jit(solution)/shard_map/ppermute | solution.py:172
  171.7 19.6 %collective-permute-start.36 = (bf16[576,768]{1,0:T(8,128)(2,1)S(1)}, bf16[576,768]{1,0:T(8,128)(2,1)S(1)}, u32[]{:S(2)}, u32[]{:S(2)}) collective-permute-start(bf16[576,768]{1,0:T(8,128)(2,1)S(1)} %get-tuple-element.138), channel_id=1, source_target_pairs={{0,2},{1,3},{2,0},{3,1},{4,6},{5,7},{6,4},{7,5},{8,10},{9,11},{10,... | collective-permute-start | bytes 2654216 | tf_op jit(solution)/shard_map/ppermute | solution.py:168
  172.4 19.2 %collective-permute-start.35 = (bf16[576,768]{1,0:T(8,128)(2,1)S(1)}, bf16[576,768]{1,0:T(8,128)(2,1)S(1)}, u32[]{:S(2)}, u32[]{:S(2)}) collective-permute-start(bf16[576,768]{1,0:T(8,128)(2,1)S(1)} %get-tuple-element.139), channel_id=1, source_target_pairs={{0,4},{1,5},{2,6},{3,7},{4,0},{5,1},{6,2},{7,3},{8,12},{9,13},{10,... | collective-permute-start | bytes 2654216 | tf_op jit(solution)/shard_map/ppermute | solution.py:164
  209.2 19.1 %collective-permute-start.45 = (bf16[1536,768]{1,0:T(8,128)(2,1)S(1)}, bf16[1536,768]{1,0:T(8,128)(2,1)}, u32[]{:S(2)}, u32[]{:S(2)}) collective-permute-start(bf16[1536,768]{1,0:T(8,128)(2,1)S(1)} %constant_dynamic-update-slice_fusion.5.refs_6_), channel_id=1, source_target_pairs={{0,1},{1,0},{2,3},{3,2},{4,5},{5,4},{6,7},{7,6},{8,9},{9,8},{10,11... | collective-permute-start | bytes 7077896 | tf_op jit(solution)/shard_map/ppermute | solution.py:172
  246.0 65.0 %collective-permute-start.48 = (bf16[96,1536]{1,0:T(8,128)(2,1)}, bf16[96,1536]{1,0:T(8,128)(2,1)}, u32[]{:S(2)}, u32[]{:S(2)}) collective-permute-start(bf16[96,1536]{1,0:T(8,128)(2,1)} %dynamic-slice_convert_fusion), channel_id=1, source_target_pairs={{0,2},{1,3},{2,0},{3,1},{4,6},{5,7},{6,4},{7,5},{8,10},{9,11},{10,... | collective-permute-start | bytes 884744 | tf_op jit(solution)/shard_map/ppermute | solution.py:168
  (78 other events, 613.2 us)

commit v4 on v3

--- a/solution.py
+++ b/solution.py
@@ -189,6 +189,12 @@
     return lax.optimization_barrier(parts)
 
 
+def swap_to(across, along):
+    return lambda a: lax.ppermute(
+        a, AXES, pairs(lambda z, x, y, c: (z, c, (y + along) % 2, (x + across) % 2))
+    )
+
+
 def places_z(z):
     return z + 1 - 2 * (z % 2), jnp.where(z < 2, 2, 1), jnp.where(z < 2, 3, 0)
 
@@ -217,24 +223,17 @@
     return whole.reshape(8 * rows, cols)
 
 
-def refresh_kernel(part, scale_ref, place_ref, *refs):
+def refresh_kernel(place_ref, sum_ref, more_ref, *refs):
     slabs = refs[:8]
-    if part == 0:
-        first_ref, second_ref, whole, inner, held, sems = refs[8:]
-    else:
-        second_ref, first_ref, out_ref, whole, inner, held, third, sems = refs[8:]
-    size = whole.shape[0]
-    count = held.shape[0]
+    out_ref, whole, inner, held, total, first, sems = refs[8:]
+    count, size = held.shape
     tall = size // 4
     half = size // 8
-    square = scale_ref[0]
 
     def copy(k, i):
-        return pltpu.make_async_copy(
-            slabs[k].at[pl.ds(i * half, half), :],
-            whole.at[pl.ds(k * half, half), pl.ds(i * tall, tall)],
-            sems.at[k, i],
-        )
+        source = slabs[k].at[pl.ds(i * half, half), :]
+        target = whole.at[pl.ds(k * half, half), pl.ds(i * tall, tall)]
+        return pltpu.make_async_copy(source, target, sems.at[k, i])
 
     def arrived(j):
         for k in (2 * j, 2 * j + 1):
@@ -244,91 +243,124 @@
     def span_of(j):
         return pl.ds(pl.multiple_of(j * tall, tall), tall)
 
-    def towards(fresh):
-        def step(j, carry):
-            if fresh:
-                for k in range(1 - part, 4):
-                    pl.when(j == k)(functools.partial(arrived, k))
-            span = span_of(j)
-            inner[:, span] = dot_nt(held[...], whole[span, :]).astype(BF)
-            return carry
-
-        lax.fori_loop(0, 4, step, 0)
-
-    def back(chunks, use):
-        def step(j, carry):
-            use(j, span_of(j), square * dot_nn(inner[...], whole[:, span_of(j)]))
-            return carry
-
-        lax.fori_loop(0, chunks, step, 0)
-
     for k in range(8):
         for i in range(4):
             copy(k, i).start()
-    if part == 0:
-        arrived(0)
-        held[...] = whole[pl.ds(pl.multiple_of(place_ref[0], 16), count), :]
-        towards(True)
-
-        def use_first(j, span, moved):
-            value = 1.5 * held[:, span].astype(F32) - 0.5 * moved
-            first_ref[:, span] = value
+    squares = size / (16.0 * (sum_ref[...] + more_ref[...]))
+    square = squares[0, 0]
+    last = (math.sqrt(size) * jnp.sqrt(squares))[0, 0]
+    arrived(0)
+    held[...] = whole[pl.ds(pl.multiple_of(place_ref[0], 16), count), :]
+    total[...] = held[...].astype(F32)
+
+    def one_pass(i, carry):
+        def towards(j, carry):
+            @pl.when(i == 0)
+            def _():
+                for k in range(1, 4):
+                    pl.when(j == k)(functools.partial(arrived, k))
+
+            inner[:, span_of(j)] = dot_nt(held[...], whole[span_of(j), :]).astype(BF)
+            return carry
+
+        lax.fori_loop(0, 4, towards, 0)
+        keep = jnp.where(i == 1, 0.0, 1.5)
+        take = jnp.where(i == 1, square, -0.5 * square)
+
+        def back(j, carry):
+            span = span_of(j)
+            value = keep * total[:, span] + take * dot_nn(inner[...], whole[:, span])
+            total[:, span] = value
             held[:, span] = value.astype(BF)
 
-        back(4, use_first)
-        towards(False)
-
-        def use_second(j, span, moved):
-            second_ref[:, span] = moved
-
-        back(4, use_second)
-    else:
-        held[...] = second_ref[...].astype(BF)
-        towards(True)
-
-        def use_third(j, span, moved):
-            value = 1.5 * second_ref[:, span] - 0.5 * moved
-            third[:, span] = value
-            held[:, span] = value.astype(BF)
-
-        back(4, use_third)
-        towards(False)
-
-        def use_last(j, span, moved):
-            value = 1.5 * third[:, span] - 0.5 * moved
-            value = scale_ref[1] * (1.5 * first_ref[:, span] - 0.5 * value)
-            out_ref[jnp.where(place_ref[1] == 1, j, 1 - j)] = value
-
-        back(2, use_last)
-
-
-def refresh_part(part, scales, places, slabs, *rows):
-    size = slabs[0].shape[0] * 2
+            @pl.when(i == 0)
+            def _():
+                first[:, span] = value
+
+            return carry
+
+        lax.fori_loop(0, jnp.where(i == 3, 2, 4), back, 0)
+        return carry
+
+    lax.fori_loop(0, 4, one_pass, 0)
+    for k in range(2):
+        span = slice(k * tall, (k + 1) * tall)
+        place = jnp.where(place_ref[1] == 1, k, 1 - k)
+        out_ref[place] = last * (1.5 * first[:, span] - 0.5 * total[:, span])
+
+
+def refresh(places, sums, slabs):
+    size, tall = 2 * slabs[0].shape[0], slabs[0].shape[1]
     count = size // 16
     in_vmem = pl.BlockSpec(memory_space=pltpu.VMEM)
     in_smem = pl.BlockSpec(memory_space=pltpu.SMEM)
-    state = jax.ShapeDtypeStruct((count, size), F32)
-    scratch = [
-        pltpu.VMEM((size, size), BF),
-        pltpu.VMEM((count, size), BF),
-        pltpu.VMEM((count, size), BF),
-    ]
-    if part == 0:
-        shapes = [state, state]
-    else:
-        shapes = [jax.ShapeDtypeStruct((2, count, size // 4), F32)]
-        scratch.append(pltpu.VMEM((count, size), F32))
+    mine = pl.BlockSpec(memory_space=pl.ANY)
+    theirs = pl.BlockSpec(memory_space=pltpu.HBM)
     return pl.pallas_call(
-        functools.partial(refresh_kernel, part),
-        out_shape=shapes,
-        in_specs=[in_smem] * 2 + [pl.BlockSpec(memory_space=pl.ANY)] * 8 + [in_vmem] * len(rows),
-        out_specs=[in_vmem] * len(shapes),
-        scratch_shapes=scratch + [pltpu.SemaphoreType.DMA((8, 4))],
-        compiler_params=pltpu.CompilerParams(vmem_limit_bytes=36 * 2**20),
+        refresh_kernel,
+        out_shape=jax.ShapeDtypeStruct((2, count, tall), F32),
+        in_specs=[in_smem] + [in_vmem] * 2 + [mine, theirs] * 4,
+        out_specs=in_vmem,
+        scratch_shapes=[
+            pltpu.VMEM((size, size), BF),
+            pltpu.VMEM((count, size), BF),
+            pltpu.VMEM((count, size), BF),
+            pltpu.VMEM((count, size), F32),
+            pltpu.VMEM((count, size), F32),
+            pltpu.SemaphoreType.DMA((8, 4)),
+        ],
+        compiler_params=pltpu.CompilerParams(vmem_limit_bytes=34 * 2**20),
         cost_estimate=pl.CostEstimate(
-            flops=8 * count * size * size, bytes_accessed=2 * size * size, transcendentals=0
+            flops=15 * count * size * size, bytes_accessed=2 * size * size, transcendentals=0
         ),
-    )(scales, places, *slabs, *rows)
+    )(places, *sums, *slabs)
+
+
+def side_kernel(place_ref, core_ref, other_ref, cols_ref, rows_ref, power_ref, *refs):
+    basis_ref, terms, power, direction = refs[0], refs[1:5], refs[5], refs[6]
+    rows = power_ref.shape[0]
+    size = power.shape[0]
+    for k in range(8):
+        source = (core_ref, other_ref)[k // 4]
+        start = (k % 4) * 2 * rows
+        place = pl.ds(pl.multiple_of(place_ref[k], 16), rows)
+        direction[place, :] = source[start : start + rows, :]
+        power[k * rows : (k + 1) * rows, :] = source[start + rows : start + 2 * rows, :]
+    back_half = dot_nn(rows_ref[...], direction[...]).astype(BF)
+    for k in range(4):
+        block = pl.ds(pl.multiple_of(place_ref[8 + k], 16), size)
+        terms[k][...] = dot_nt(back_half, cols_ref[block, :]).astype(BF)
+    total = jnp.zeros((rows, size), F32)
+    for k in range(8):
+        total += jnp.square(power[k * rows : (k + 1) * rows, :].astype(F32))
+    square = size / (16.0 * jnp.sum(total))
+    keep = power_ref[...]
+    value = keep
+    for turn in range(4):
+        across = dot_nt(value.astype(BF), power[...]).astype(BF)
+        moved = square * dot_nn(across, power[...])
+        value = moved if turn == 1 else 1.5 * value - 0.5 * moved
+        if turn == 0:
+            keep = value
+    scale = math.sqrt(size) * jnp.sqrt(jnp.full((rows, size), square))
+    basis_ref[...] = scale * (1.5 * keep - 0.5 * value)
+
+
+def side(places, extra_core, extra_other, right_cols, left_rows, power_left):
+    rows, size = power_left.shape
+    in_vmem = pl.BlockSpec(memory_space=pltpu.VMEM)
+    term = jax.ShapeDtypeStruct((rows, size), BF)
+    return pl.pallas_call(
+        side_kernel,
+        out_shape=[jax.ShapeDtypeStruct((rows, size), F32)] + [term] * 4,
+        in_specs=[pl.BlockSpec(memory_space=pltpu.SMEM)] + [in_vmem] * 5,
+        out_specs=[in_vmem] * 5,
+        scratch_shapes=[pltpu.VMEM((size, size), BF), pltpu.VMEM((size, size), BF)],
+        compiler_params=pltpu.CompilerParams(vmem_limit_bytes=12 * 2**20),
+        cost_estimate=pl.CostEstimate(
+            flops=26 * rows * size * size, bytes_accessed=12 * size * size, transcendentals=0
+        ),
+    )(places, extra_core, extra_other, right_cols, left_rows, power_left)
 
 
 def squares(tiles):
@@ -359,20 +391,20 @@
     turned, small_o1, small_i1 = stage(
         turn_over(right_b, straight), swap_outer(small), swap_inner(small)
     )
-    got_o, got_i, stat_x, stat_y = stage(
+    got_i, got_o, stat_y, stat_x = stage(
+        swap_inner(jnp.concatenate([turned, small_o1])),
         swap_outer(jnp.concatenate([turned, small_i1])),
-        swap_inner(jnp.concatenate([turned, small_o1])),
+        swap_y(stat_b),
         swap_x(stat_b),
-        swap_y(stat_b),
     )
     turned_o1, small_o2 = got_o[:rows_right], got_o[rows_right:]
     turned_i1, small_i2 = got_i[:rows_right], got_i[rows_right:]
     small_1 = ordered_pair(z % 2 == 0, small, small_o1).reshape(2 * rows_small, cols_right)
-    got_o, turned_i2, got_x, got_y = stage(
+    turned_i2, got_o, got_y, got_x = stage(
+        swap_inner(turned_o1),
         swap_outer(jnp.concatenate([turned_i1, small_i2])),
-        swap_inner(turned_o1),
+        swap_y(jnp.concatenate([stat_x[:half], small_1])),
         swap_x(jnp.concatenate([stat_y[half:], small_1])),
-        swap_y(jnp.concatenate([stat_x[:half], small_1])),
     )
     turned_o2, small_o3 = got_o[:rows_right], got_o[rows_right:]
     small_2 = ordered_pair(
@@ -452,120 +484,103 @@
     power_left = dot_nn(new_stat_left.astype(BF), left_all)
     power_left_b = power_left.astype(BF)
 
-    power_x, power_y, near, power_i1, extra = stage(
-        swap_x(power),
-        swap_y(power),
-        swap_outer(power),
-        swap_inner(power),
-        turn_over(jnp.concatenate([rotated, power_left_b]), straight),
-    )
-    rotated, left_t = extra[:rows_left], extra[rows_left:]
+    rotated = turn_over(rotated, straight)
     new_moment_one, new_moment_two, direction = adam_moments(
         rotated.astype(F32), moment_one, moment_two
     )
-    got_x, got_y, got_o, got_i, direction_t = stage(
+    extra = turn_over(jnp.concatenate([direction, power_left_b]), straight)
+    power_i1, near, power_y, power_x, extra, new_stat_right = stage(
+        swap_inner(power),
+        swap_outer(power),
+        swap_y(power),
+        swap_x(power),
+        extra,
+        new_stat_right,
+    )
+    got_i, got_o, got_y, got_x = stage(
+        swap_inner(jnp.concatenate([near, extra])),
+        swap_outer(jnp.concatenate([power_i1, extra])),
+        swap_y(jnp.concatenate([power_x[:half], near])),
         swap_x(jnp.concatenate([power_y[half:], near])),
-        swap_y(jnp.concatenate([power_x[:half], near])),
-        swap_outer(jnp.concatenate([power_i1, left_t])),
-        swap_inner(jnp.concatenate([near, left_t])),
-        turn_over(direction, straight),
     )
     slab0 = jnp.concatenate([power, power_x, power_y, got_y[:half], got_x[:half]])
     near_x, near_y = got_x[half:], got_y[half:]
-    power_o2, left_o1 = got_o[:rows_right], got_o[rows_right:]
-    power_i2, left_i1 = got_i[:rows_right], got_i[rows_right:]
+    power_o2, extra_o1 = got_o[:rows_right], got_o[rows_right:]
+    power_i2, extra_i1 = got_i[:rows_right], got_i[rows_right:]
     mid = jnp.where(inner, power_i1, power_o2)
-    got_x, got_y, got_o, got_i, slab0_other = stage(
+    slab0_other = swap_core(slab0)
+    extra_i2, got_o, got_y, got_x, slab0_other, sum0 = stage(
+        swap_inner(extra_o1),
+        swap_outer(jnp.concatenate([power_i2, extra_i1])),
+        swap_y(jnp.concatenate([near_x[:half], mid])),
         swap_x(jnp.concatenate([near_y[half:], mid])),
-        swap_y(jnp.concatenate([near_x[:half], mid])),
-        swap_outer(jnp.concatenate([power_i2, left_i1, direction_t])),
-        swap_inner(jnp.concatenate([left_o1, direction_t])),
-        swap_core(slab0),
+        slab0_other,
+        squares(slab0_other),
     )
     slab1 = jnp.concatenate([near, near_x, near_y, got_y[:half], got_x[:half]])
     mid_x, mid_y = got_x[half:], got_y[half:]
-    power_o3, left_o2, direction_o1 = (
-        got_o[:rows_right],
-        got_o[rows_right:-rows_left],
-        got_o[-rows_left:],
-    )
-    left_i2, direction_i1 = got_i[:rows_left], got_i[rows_left:]
+    power_o3, extra_o2 = got_o[:rows_right], got_o[rows_right:]
     far = jnp.where(inner, power_i2, power_o3)
-    got_x, got_y, got_o, direction_i2, slab1_other = stage(
+    slab1_other = swap_core(slab1)
+    extra_o3, got_y, got_x, slab1_other, sum1 = stage(
+        swap_outer(extra_i2),
+        swap_y(jnp.concatenate([mid_x[:half], far])),
         swap_x(jnp.concatenate([mid_y[half:], far])),
-        swap_y(jnp.concatenate([mid_x[:half], far])),
-        swap_outer(jnp.concatenate([left_i2, direction_i1])),
-        swap_inner(direction_o1),
-        swap_core(slab1),
+        slab1_other,
+        squares(slab1_other),
     )
     slab2 = jnp.concatenate([mid, mid_x, mid_y, got_y[:half], got_x[:half]])
     far_x, far_y = got_x[half:], got_y[half:]
-    left_o3, direction_o2 = got_o[:rows_left], got_o[rows_left:]
-    left_z = in_order(
-        z,
-        left_t,
-        left_o1,
-        jnp.where(inner, left_i1, left_o2),
-        jnp.where(inner, left_i2, left_o3),
-    )
-    got_x, got_y, direction_o3, slab2_other, left_other = stage(
+    extra_core = jnp.concatenate(
+        [extra, extra_o1, jnp.where(inner, extra_i1, extra_o2), jnp.where(inner, extra_i2, extra_o3)]
+    )
+    slab2_other = swap_core(slab2)
+    extra_other = swap_core(extra_core)
+    near_place, mid_place, far_place = places_z(z)
+    side_places = [
+        (2 * at_z + at_x) * rows_left
+        for at_x in (core, 1 - core)
+        for at_z in (z, near_place, mid_place, far_place)
+    ] + [
+        ((y + along) % 2 * 2 + (x + across) % 2) * cols_right
+        for along in range(2)
+        for across in range(2)
+    ]
+    new_basis_left, *terms = side(
+        jnp.stack(side_places),
+        extra_core,
+        extra_other,
+        right_cols,
+        lax.dynamic_slice_in_dim(left_all, (2 * z + core) * rows_left, rows_left, 0),
+        power_left,
+    )
+    got_y, got_x, slab2_other, sum2, new_basis_left = stage(
+        swap_y(far_x[:half]),
         swap_x(far_y[half:]),
-        swap_y(far_x[:half]),
-        swap_outer(direction_i2),
-        swap_core(slab2),
-        swap_core(left_z),
+        slab2_other,
+        squares(slab2_other),
+        new_basis_left,
     )
     slab3 = jnp.concatenate([far, far_x, far_y, got_y, got_x])
-    direction_z = in_order(
-        z,
-        direction_t,
-        direction_o1,
-        jnp.where(inner, direction_i1, direction_o2),
-        jnp.where(inner, direction_i2, direction_o3),
-    )
-    sum_core = squares(slab0) + squares(slab1) + squares(slab2) + squares(slab3)
-    sum_core = jnp.full((8, 128), sum_core)
-    slab3_other, direction_other, sum_other = stage(
-        swap_core(slab3), swap_core(direction_z), swap_core(sum_core)
-    )
-    square_right = FF / (16.0 * (sum_core[0, 0] + sum_other[0, 0]))
-
-    slabs = (slab0, slab0_other, slab1, slab1_other, slab2, slab2_other, slab3, slab3_other)
-    scales = jnp.stack([square_right, math.sqrt(FF) * jnp.sqrt(square_right)])
+    slab3_other = swap_core(slab3)
+    sum_core = jnp.full((8, 128), sum0 + sum1 + sum2 + squares(slab3))
+
+    terms = [
+        swap_to(across, along)(terms[2 * along + across])
+        for along in range(2)
+        for across in range(2)
+    ]
+    update = sum(term.astype(F32) for term in terms).astype(BF)
+
     places = jnp.stack(
         [jnp.where(straight, 0, rows_right) + core * half, straight.astype(jnp.int32)]
     )
-    first, second = refresh_part(0, scales, places, slabs)
-    (fresh,) = refresh_part(1, scales, places, slabs, second, first)
+    slabs = (slab0, slab0_other, slab1, slab1_other, slab2, slab2_other, slab3, slab3_other)
+    fresh = refresh(places, (sum_core, swap_core(sum_core)), slabs)
     theirs = swap_core(fresh[1])
     new_basis_right = jnp.zeros((rows_right, cols_right), F32)
     new_basis_right = put(new_basis_right, fresh[0], core * half, 0)
     new_basis_right = put(new_basis_right, theirs, (1 - core) * half, 0)
-
-    direction_cols = interleave(core, direction_z, direction_other)
-    left_rows = lax.dynamic_slice_in_dim(left_all, (2 * z + core) * rows_left, rows_left, 0)
-    back_half = dot_nn(left_rows, direction_cols).astype(BF)
-    back_terms = dot_nt(back_half, right_cols)
-    width = 2 * cols_right
-    away = lax.dynamic_slice_in_dim(back_terms, (1 - y) * width, width, 1).astype(BF)
-    kept = lax.dynamic_slice_in_dim(back_terms, y * width, width, 1)
-    kept = kept + swap_y(away).astype(F32)
-    away = lax.dynamic_slice_in_dim(kept, (1 - x) * cols_right, cols_right, 1).astype(BF)
-    kept = lax.dynamic_slice_in_dim(kept, x * cols_right, cols_right, 1)
-    update = turn_over((kept + swap_x(away).astype(F32)).astype(BF), straight)
-
-    power_all = interleave(core, left_z, left_other)
-    square_left = D / (16.0 * squares(power_all))
-    keep = power_left
-    value = power_left
-    for turn in range(4):
-        across = dot_nt(value.astype(BF), power_all).astype(BF)
-        moved = square_left * dot_nn(across, power_all)
-        value = moved if turn == 1 else 1.5 * value - 0.5 * moved
-        if turn == 0:
-            keep = value
-    value = 1.5 * keep - 0.5 * value
-    new_basis_left = value * (math.sqrt(D) * jnp.sqrt(square_left))
     return (
         update,
         new_moment_one,

time: 329 us -> 298 us (0.906)
  matrix products: 26.7 us -> 12.3 us
  waiting for transfers between devices: 119 us -> 107 us
  starting transfers between devices: 67.7 us -> 63.7 us
    ppermute x10 -> x9, waiting for transfers between devices: 6.43 us -> 38.1 us  [swap_x(): return lax.ppermute(a, AXES, pairs(lambda z, x, y, c: (z, 1 - x, y, c)))]
    ppermute x4 -> x3, waiting for transfers between devices: 27.8 us -> 6.8 us  [turn_over(): return jnp.where(straight, a, lax.ppermute(a, AXES, crossed))]
    ppermute x10 -> x9, waiting for transfers between devices: 27.3 us -> 8.96 us  [swap_y(): return lax.ppermute(a, AXES, pairs(lambda z, x, y, c: (z, x, 1 - y, c)))]
    ppermute x7 -> x6, waiting for transfers between devices: 33.2 us -> 18.8 us  [swap_inner(): lax.ppermute(a, AXES, pairs(lambda z, x, y, c: (3 - z if 0 < z < 3 else -...]
    ppermute x9 -> x8, waiting for transfers between devices: 20.6 us -> 32.6 us  [swap_outer(): lax.ppermute(a, AXES, pairs(lambda z, x, y, c: (z + 1 - 2 * (z % 2), x, y...]
    dot_general x7 -> x3, matrix products: 15.1 us -> 5.02 us  [dot_nn(): return jnp.dot(a, b, preferred_element_type=F32)]
    dot_general x2 -> x1, matrix products: 7.08 us -> 1.6 us  [dot_nt(): lax.dot_general(a, b, (((1,), (1,)), ((), ())), preferred_element_type=F32)]
    ppermute x0 -> x4, starting transfers between devices: none -> 5.17 us  [swap_to(): lax.ppermute(a, AXES, pairs(lambda z, x, y, c: (z, c, (y + along) % 2, (x...]
  transfers between devices with their start and end apart: 52 -> 50, of which waited for: 28 -> 27; matrix products, arithmetic and copies ran while one was open for 15% -> 16% of each run, Pallas kernels for 15% -> 18%
where the time goes in v4:
time: 298 us; the launch traced here: 296 us
  waiting for transfers between devices  107 us (36%)
  starting transfers between devices  63.7 us (21%)
  Pallas kernels  52 us (17%)
  other arithmetic  29.6 us (10%)
  local copies, waits for them, and re-layouts  26.7 us (9%)
  matrix products  12.3 us (4%)
  between operations  4.31 us (1%)
    pallas_call x1, Pallas kernels, refresh(): pl.pallas_call(refresh_kernel, out_shape=jax.ShapeDtypeStruct((2, count,...  45.8 us
    ppermute x9, waiting for transfers between devices, swap_x(): return lax.ppermute(a, AXES, pairs(lambda z, x, y, c: (z, 1 - x, y, c)))  38.1 us
    ppermute x8, waiting for transfers between devices, swap_outer(): lax.ppermute(a, AXES, pairs(lambda z, x, y, c: (z + 1 - 2 * (z % 2), x, y...  32.6 us
    ppermute x6, waiting for transfers between devices, swap_inner(): lax.ppermute(a, AXES, pairs(lambda z, x, y, c: (3 - z if 0 < z < 3 else -...  18.8 us
    ppermute x11, starting transfers between devices, swap_core(): return lax.ppermute(a, AXES, pairs(lambda z, x, y, c: (z, x, y, 1 - c)))  18.1 us
    unnamed x70, local copies, waits for them, and re-layouts  17.6 us
    ppermute x6, starting transfers between devices, swap_inner(): lax.ppermute(a, AXES, pairs(lambda z, x, y, c: (3 - z if 0 < z < 3 else -...  16 us
    ppermute x3, starting transfers between devices, turn_over(): return jnp.where(straight, a, lax.ppermute(a, AXES, crossed))  10.4 us
  transfers between devices with their start and end apart: 50, of which 27 were waited for; matrix products, arithmetic and copies ran while one was open for 16% of the time, Pallas kernels for 18%

profile of v4, /device:TPU:9, one launch (start us, length us, event | category | flops | bytes accessed | tf_op | source)
XLA Modules:
  0.0 295.8 jit_solution(2193194332028663738)
XLA Ops:
  3.0 3.7 %collective-permute-start = (bf16[384,768]{1,0:T(8,128)(2,1)}, bf16[384,768]{1,0:T(8,128)(2,1)}, u32[]{:S(2)}, u32[]{:S(2)}) collective-permute-start(bf16[384,768]{1,0:T(8,128)(2,1)} %multiply_convert_fusion), channel_id=1, source_target_pairs={{1,4},{3,6},{4,1},{6,3},{9,12},{11,14},{12,9},{14,11},{17,20},{19,... | collective-permute-start | bytes 1769480 | tf_op jit(solution)/shard_map/ppermute | solution.py:185
  9.3 3.2 %collective-permute-start.2 = (bf16[144,768]{1,0:T(8,128)(2,1)}, bf16[144,768]{1,0:T(8,128)(2,1)}, u32[]{:S(2)}, u32[]{:S(2)}) collective-permute-start(bf16[144,768]{1,0:T(8,128)(2,1)} %get-tuple-element.152), channel_id=1, source_target_pairs={{8,16},{9,17},{10,18},{11,19},{12,20},{13,21},{14,22},{15,23},{16,... | collective-permute-start | bytes 663560 | tf_op jit(solution)/shard_map/ppermute | solution.py:180
  23.7 4.6 %collective-permute-done.6 = bf16[384,768]{1,0:T(8,128)(2,1)} collective-permute-done((bf16[384,768]{1,0:T(8,128)(2,1)}, bf16[384,768]{1,0:T(8,128)(2,1)}, u32[]{:S(2)}, u32[]{:S(2)}) %collective-permute-start.6) | collective-permute-done | bytes 589856 | tf_op jit(solution)/shard_map/ppermute | solution.py:164
  28.2 12.5 %collective-permute-done.4 = bf16[528,768]{1,0:T(8,128)(2,1)S(1)} collective-permute-done((bf16[528,768]{1,0:T(8,128)(2,1)S(1)}, bf16[528,768]{1,0:T(8,128)(2,1)S(1)}, u32[]{:S(2)}, u32[]{:S(2)}) %collective-permute-start.4) | collective-permute-done | bytes 811040 | tf_op jit(solution)/shard_map/ppermute | solution.py:176
  50.0 10.0 %collective-permute-done.7 = bf16[384,768]{1,0:T(8,128)(2,1)S(1)} collective-permute-done((bf16[384,768]{1,0:T(8,128)(2,1)S(1)}, bf16[384,768]{1,0:T(8,128)(2,1)S(1)}, u32[]{:S(2)}, u32[]{:S(2)}) %collective-permute-start.7) | collective-permute-done | bytes 589856 | tf_op jit(solution)/shard_map/ppermute | solution.py:180
  60.1 3.4 %collective-permute-done.10 = bf16[480,768]{1,0:T(8,128)(2,1)S(1)} collective-permute-done((bf16[480,768]{1,0:T(8,128)(2,1)S(1)}, bf16[480,768]{1,0:T(8,128)(2,1)S(1)}, u32[]{:S(2)}, u32[]{:S(2)}) %collective-permute-start.10) | collective-permute-done | bytes 737312 | tf_op jit(solution)/shard_map/ppermute | solution.py:164
  68.5 3.1 %collective-permute-start.14 = (bf16[768,768]{1,0:T(8,128)(2,1)S(1)}, bf16[768,768]{1,0:T(8,128)(2,1)S(1)}, u32[]{:S(2)}, u32[]{:S(2)}) collective-permute-start(bf16[768,768]{1,0:T(8,128)(2,1)S(1)} %pad_maximum_fusion), channel_id=1, source_target_pairs={{0,1},{1,0},{2,3},{3,2},{4,5},{5,4},{6,7},{7,6},{8,9},{9,8},{10,11... | collective-permute-start | bytes 3538952 | tf_op jit(solution)/shard_map/ppermute | solution.py:172
  71.9 6.5 %collective-permute-done.11 = bf16[384,768]{1,0:T(8,128)(2,1)S(1)} collective-permute-done((bf16[384,768]{1,0:T(8,128)(2,1)S(1)}, bf16[384,768]{1,0:T(8,128)(2,1)S(1)}, u32[]{:S(2)}, u32[]{:S(2)}) %collective-permute-start.11) | collective-permute-done | bytes 589856 | tf_op jit(solution)/shard_map/ppermute | solution.py:176
  82.2 4.2 %collective-permute-start.17 = (bf16[4,384,768]{2,1,0:T(8,128)(2,1)S(1)}, bf16[4,384,768]{2,1,0:T(8,128)(2,1)S(1)}, u32[]{:S(2)}, u32[]{:S(2)}) collective-permute-start(bf16[4,384,768]{2,1,0:T(8,128)(2,1)S(1)} %bitcast_dynamic-update-slice_fusion.2), channel_id=1, source_target_pairs={{0,1},{1,0},{2,3},{3,2},{4,5},{5,4},{6,7},{7,6},{8,9},{9,8},{10,11... | collective-permute-start | bytes 7077896 | tf_op jit(solution)/shard_map/ppermute | solution.py:172
  87.7 6.0 %collective-permute-done.16 = bf16[144,768]{1,0:T(8,128)(2,1)S(1)} collective-permute-done((bf16[144,768]{1,0:T(8,128)(2,1)S(1)}, bf16[144,768]{1,0:T(8,128)(2,1)S(1)}, u32[]{:S(2)}, u32[]{:S(2)}) %collective-permute-start.16) | collective-permute-done | bytes 221216 | tf_op jit(solution)/shard_map/ppermute | solution.py:168
  104.3 3.0 %collective-permute-done.24 = bf16[96,768]{1,0:T(8,128)(2,1)S(1)} collective-permute-done((bf16[96,768]{1,0:T(8,128)(2,1)S(1)}, bf16[96,768]{1,0:T(8,128)(2,1)S(1)}, u32[]{:S(2)}, u32[]{:S(2)}) %collective-permute-start.24) | collective-permute-done | bytes 147488 | tf_op jit(solution)/shard_map/ppermute | solution.py:185
  111.3 3.1 %collective-permute-start.20 = (bf16[384,768]{1,0:T(8,128)(2,1)}, bf16[384,768]{1,0:T(8,128)(2,1)}, u32[]{:S(2)}, u32[]{:S(2)}) collective-permute-start(bf16[384,768]{1,0:T(8,128)(2,1)} %get-tuple-element.158), channel_id=1, source_target_pairs={{8,16},{9,17},{10,18},{11,19},{12,20},{13,21},{14,22},{15,23},{16,... | collective-permute-start | bytes 1769480 | tf_op jit(solution)/shard_map/ppermute | solution.py:180
  117.8 4.1 %collective-permute-start.25 = (bf16[192,768]{1,0:T(8,128)(2,1)}, bf16[192,768]{1,0:T(8,128)(2,1)}, u32[]{:S(2)}, u32[]{:S(2)}) collective-permute-start(bf16[192,768]{1,0:T(8,128)(2,1)} %pad_maximum_fusion.19), channel_id=1, source_target_pairs={{1,4},{3,6},{4,1},{6,3},{9,12},{11,14},{12,9},{14,11},{17,20},{19,... | collective-permute-start | bytes 884744 | tf_op jit(solution)/shard_map/ppermute | solution.py:185
  122.0 3.3 %fusion = f32[384,768]{1,0:T(8,128)} fusion(bf16[768,3072]{1,0:T(8,128)(2,1)} %copy-done.11, s32[]{:T(128)S(6)} %select_n.380, f32[384,768]{1,0:T(8,128)S(1)} %copy-done.12, s32[]{:T(128)S(6)} %select_n.379), kind=kOutput, calls=%fused_computation.9 | convolution fusion | flops 453869568 | bytes 4128776 | tf_op jit(solution)/shard_map/dot_general | solution.py:145
  125.2 3.7 %collective-permute-done.25 = bf16[192,768]{1,0:T(8,128)(2,1)} collective-permute-done((bf16[192,768]{1,0:T(8,128)(2,1)}, bf16[192,768]{1,0:T(8,128)(2,1)}, u32[]{:S(2)}, u32[]{:S(2)}) %collective-permute-start.25) | collective-permute-done | bytes 294944 | tf_op jit(solution)/shard_map/ppermute | solution.py:185
  134.3 3.0 %collective-permute-start.26 = (bf16[576,768]{1,0:T(8,128)(2,1)S(1)}, bf16[576,768]{1,0:T(8,128)(2,1)S(1)}, u32[]{:S(2)}, u32[]{:S(2)}) collective-permute-start(bf16[576,768]{1,0:T(8,128)(2,1)S(1)} %get-tuple-element.142), channel_id=1, source_target_pairs={{8,16},{9,17},{10,18},{11,19},{12,20},{13,21},{14,22},{15,23},{16,... | collective-permute-start | bytes 2654216 | tf_op jit(solution)/shard_map/ppermute | solution.py:180
  139.9 15.5 %collective-permute-done.29 = bf16[576,768]{1,0:T(8,128)(2,1)S(1)} collective-permute-done((bf16[576,768]{1,0:T(8,128)(2,1)S(1)}, bf16[576,768]{1,0:T(8,128)(2,1)S(1)}, u32[]{:S(2)}, u32[]{:S(2)}) %collective-permute-start.29) | collective-permute-done | bytes 884768 | tf_op jit(solution)/shard_map/ppermute | solution.py:164
  156.5 3.2 %collective-permute-start.34 = (bf16[1536,768]{1,0:T(8,128)(2,1)S(1)}, bf16[1536,768]{1,0:T(8,128)(2,1)S(1)}, u32[]{:S(2)}, u32[]{:S(2)}) collective-permute-start(bf16[1536,768]{1,0:T(8,128)(2,1)S(1)} %get-tuple-element.128.refs_0_), channel_id=1, source_target_pairs={{0,1},{1,0},{2,3},{3,2},{4,5},{5,4},{6,7},{7,6},{8,9},{9,8},{10,11... | collective-permute-start | bytes 7077896 | tf_op jit(solution)/shard_map/ppermute | solution.py:172
  168.4 5.0 %collective-permute-done.30 = bf16[192,768]{1,0:T(8,128)(2,1)S(1)} collective-permute-done((bf16[192,768]{1,0:T(8,128)(2,1)S(1)}, bf16[192,768]{1,0:T(8,128)(2,1)S(1)}, u32[]{:S(2)}, u32[]{:S(2)}) %collective-permute-start.30) | collective-permute-done | bytes 294944 | tf_op jit(solution)/shard_map/ppermute | solution.py:180
  173.4 7.5 %collective-permute-done.31 = bf16[576,768]{1,0:T(8,128)(2,1)S(1)} collective-permute-done((bf16[576,768]{1,0:T(8,128)(2,1)S(1)}, bf16[576,768]{1,0:T(8,128)(2,1)S(1)}, u32[]{:S(2)}, u32[]{:S(2)}) %collective-permute-start.31) | collective-permute-done | bytes 884768 | tf_op jit(solution)/shard_map/ppermute | solution.py:176
  193.8 12.2 %collective-permute-done.37 = bf16[576,768]{1,0:T(8,128)(2,1)S(1)} collective-permute-done((bf16[576,768]{1,0:T(8,128)(2,1)S(1)}, bf16[576,768]{1,0:T(8,128)(2,1)S(1)}, u32[]{:S(2)}, u32[]{:S(2)}) %collective-permute-start.37) | collective-permute-done | bytes 884768 | tf_op jit(solution)/shard_map/ppermute | solution.py:164
  218.2 6.3 %shard_map.126 = (f32[96,768]{1,0:T(8,128)}, bf16[96,768]{1,0:T(8,128)(2,1)}, bf16[96,768]{1,0:T(8,128)(2,1)}, bf16[96,768]{1,0:T(8,128)(2,1)}, bf16[96,768]{1,0:T(8,128)(2,1)}) custom-call(s32[12]{0:T(128)S(1)} %stack.63.place_ref, bf16[768,768]{1,0:T(8,128)(2,1)S(1)} %pad_maximum_fusion.1.core_ref, bf16[768,768]{1,0:T(8,128)(2,1)} %collective-permute-done.39.other_ref, ...), custom_call_target="tpu_custom_call" | custom-call | flops 1472200704 | bytes 7077888 | tf_op jit(solution)/shard_map/pallas_call | solution.py:353
  224.5 3.5 %multiply_reduce_fusion.1 = f32[]{:T(128)} fusion(bf16[1536,768]{1,0:T(8,128)(2,1)} %collective-permute-done.46.refs_5_), kind=kLoop, calls=%fused_computation.1 | loop fusion | flops 3538943 | bytes 2359300 | tf_op jit(solution)/shard_map/reduce_sum | solution.py:367
  245.4 45.8 %shard_map.127 = f32[2,192,768]{2,1,0:T(8,128)S(1)} custom-call(s32[2]{0:T(128)S(1)} %pad_add_fusion.place_ref, f32[8,128]{1,0:T(8,128)S(1)} %broadcast_in_dim.107.sum_ref, f32[8,128]{1,0:T(8,128)S(1)} %collective-permute-done.47.more_ref, bf16[1536,768]{1,0:T(8,128)(2,1)S(1)} %copy-done.8, bf16[1536,768]{1,0:T(8,128)(2,1)S(1)} %copy-done.3, ...), custom_call_target="tpu_custom_call" | custom-call | flops 27179089920 | bytes 18874368 | tf_op jit(solution)/shard_map/pallas_call | solution.py:299
  (256 shorter events, 115.3 us)
Async XLA Ops:
  20.6 20.1 %collective-permute-start.4 = (bf16[528,768]{1,0:T(8,128)(2,1)S(1)}, bf16[528,768]{1,0:T(8,128)(2,1)S(1)}, u32[]{:S(2)}, u32[]{:S(2)}) collective-permute-start(bf16[528,768]{1,0:T(8,128)(2,1)S(1)} %get-tuple-element.143), channel_id=1, source_target_pairs={{0,8},{1,9},{2,10},{3,11},{4,12},{5,13},{6,14},{7,15},{8,0},{9,1},... | collective-permute-start | bytes 2433032 | tf_op jit(solution)/shard_map/ppermute | solution.py:176
  20.7 21.9 %collective-permute-start.3 = (bf16[528,768]{1,0:T(8,128)(2,1)S(1)}, bf16[528,768]{1,0:T(8,128)(2,1)S(1)}, u32[]{:S(2)}, u32[]{:S(2)}) collective-permute-start(bf16[528,768]{1,0:T(8,128)(2,1)S(1)} %get-tuple-element.144), channel_id=1, source_target_pairs={{8,16},{9,17},{10,18},{11,19},{12,20},{13,21},{14,22},{15,23},{16,... | collective-permute-start | bytes 2433032 | tf_op jit(solution)/shard_map/ppermute | solution.py:180
  45.9 19.0 %collective-permute-start.8 = (bf16[528,768]{1,0:T(8,128)(2,1)S(1)}, bf16[528,768]{1,0:T(8,128)(2,1)S(1)}, u32[]{:S(2)}, u32[]{:S(2)}) collective-permute-start(bf16[528,768]{1,0:T(8,128)(2,1)S(1)} %collective-permute-done.3), channel_id=1, source_target_pairs={{0,8},{1,9},{2,10},{3,11},{4,12},{5,13},{6,14},{7,15},{8,0},{9,1},... | collective-permute-start | bytes 2433032 | tf_op jit(solution)/shard_map/ppermute | solution.py:176
  46.0 17.4 %collective-permute-start.10 = (bf16[480,768]{1,0:T(8,128)(2,1)S(1)}, bf16[480,768]{1,0:T(8,128)(2,1)S(1)}, u32[]{:S(2)}, u32[]{:S(2)}) collective-permute-start(bf16[480,768]{1,0:T(8,128)(2,1)S(1)} %get-tuple-element.147), channel_id=1, source_target_pairs={{0,4},{1,5},{2,6},{3,7},{4,0},{5,1},{6,2},{7,3},{8,12},{9,13},{10,... | collective-permute-start | bytes 2211848 | tf_op jit(solution)/shard_map/ppermute | solution.py:164
  46.1 17.4 %collective-permute-start.9 = (bf16[480,768]{1,0:T(8,128)(2,1)S(1)}, bf16[480,768]{1,0:T(8,128)(2,1)S(1)}, u32[]{:S(2)}, u32[]{:S(2)}) collective-permute-start(bf16[480,768]{1,0:T(8,128)(2,1)S(1)} %get-tuple-element.148), channel_id=1, source_target_pairs={{0,2},{1,3},{2,0},{3,1},{4,6},{5,7},{6,4},{7,5},{8,10},{9,11},{10,... | collective-permute-start | bytes 2211848 | tf_op jit(solution)/shard_map/ppermute | solution.py:168
  111.0 19.0 %collective-permute-start.23 = (bf16[384,768]{1,0:T(8,128)(2,1)}, bf16[384,768]{1,0:T(8,128)(2,1)}, u32[]{:S(2)}, u32[]{:S(2)}) collective-permute-start(bf16[384,768]{1,0:T(8,128)(2,1)} %get-tuple-element.158), channel_id=1, source_target_pairs={{0,4},{1,5},{2,6},{3,7},{4,0},{5,1},{6,2},{7,3},{8,12},{9,13},{10,... | collective-permute-start | bytes 1769480 | tf_op jit(solution)/shard_map/ppermute | solution.py:164
  111.0 19.0 %collective-permute-start.22 = (bf16[384,768]{1,0:T(8,128)(2,1)}, bf16[384,768]{1,0:T(8,128)(2,1)}, u32[]{:S(2)}, u32[]{:S(2)}) collective-permute-start(bf16[384,768]{1,0:T(8,128)(2,1)} %get-tuple-element.158), channel_id=1, source_target_pairs={{0,2},{1,3},{2,0},{3,1},{4,6},{5,7},{6,4},{7,5},{8,10},{9,11},{10,... | collective-permute-start | bytes 1769480 | tf_op jit(solution)/shard_map/ppermute | solution.py:168
  111.1 18.8 %collective-permute-start.21 = (bf16[384,768]{1,0:T(8,128)(2,1)}, bf16[384,768]{1,0:T(8,128)(2,1)}, u32[]{:S(2)}, u32[]{:S(2)}) collective-permute-start(bf16[384,768]{1,0:T(8,128)(2,1)} %get-tuple-element.158), channel_id=1, source_target_pairs={{0,8},{1,9},{2,10},{3,11},{4,12},{5,13},{6,14},{7,15},{8,0},{9,1},... | collective-permute-start | bytes 1769480 | tf_op jit(solution)/shard_map/ppermute | solution.py:176
  111.3 18.7 %collective-permute-start.20 = (bf16[384,768]{1,0:T(8,128)(2,1)}, bf16[384,768]{1,0:T(8,128)(2,1)}, u32[]{:S(2)}, u32[]{:S(2)}) collective-permute-start(bf16[384,768]{1,0:T(8,128)(2,1)} %get-tuple-element.158), channel_id=1, source_target_pairs={{8,16},{9,17},{10,18},{11,19},{12,20},{13,21},{14,22},{15,23},{16,... | collective-permute-start | bytes 1769480 | tf_op jit(solution)/shard_map/ppermute | solution.py:180
  133.6 21.7 %collective-permute-start.29 = (bf16[576,768]{1,0:T(8,128)(2,1)S(1)}, bf16[576,768]{1,0:T(8,128)(2,1)S(1)}, u32[]{:S(2)}, u32[]{:S(2)}) collective-permute-start(bf16[576,768]{1,0:T(8,128)(2,1)S(1)} %get-tuple-element.140), channel_id=1, source_target_pairs={{0,4},{1,5},{2,6},{3,7},{4,0},{5,1},{6,2},{7,3},{8,12},{9,13},{10,... | collective-permute-start | bytes 2654216 | tf_op jit(solution)/shard_map/ppermute | solution.py:164
  133.7 21.6 %collective-permute-start.28 = (bf16[576,768]{1,0:T(8,128)(2,1)S(1)}, bf16[576,768]{1,0:T(8,128)(2,1)S(1)}, u32[]{:S(2)}, u32[]{:S(2)}) collective-permute-start(bf16[576,768]{1,0:T(8,128)(2,1)S(1)} %get-tuple-element.141), channel_id=1, source_target_pairs={{0,2},{1,3},{2,0},{3,1},{4,6},{5,7},{6,4},{7,5},{8,10},{9,11},{10,... | collective-permute-start | bytes 2654216 | tf_op jit(solution)/shard_map/ppermute | solution.py:168
  134.3 21.1 %collective-permute-start.26 = (bf16[576,768]{1,0:T(8,128)(2,1)S(1)}, bf16[576,768]{1,0:T(8,128)(2,1)S(1)}, u32[]{:S(2)}, u32[]{:S(2)}) collective-permute-start(bf16[576,768]{1,0:T(8,128)(2,1)S(1)} %get-tuple-element.142), channel_id=1, source_target_pairs={{8,16},{9,17},{10,18},{11,19},{12,20},{13,21},{14,22},{15,23},{16,... | collective-permute-start | bytes 2654216 | tf_op jit(solution)/shard_map/ppermute | solution.py:180
  137.4 19.0 %collective-permute-start.27 = (bf16[576,768]{1,0:T(8,128)(2,1)S(1)}, bf16[576,768]{1,0:T(8,128)(2,1)S(1)}, u32[]{:S(2)}, u32[]{:S(2)}) collective-permute-start(bf16[576,768]{1,0:T(8,128)(2,1)S(1)} %get-tuple-element.149), channel_id=1, source_target_pairs={{0,8},{1,9},{2,10},{3,11},{4,12},{5,13},{6,14},{7,15},{8,0},{9,1},... | collective-permute-start | bytes 2654216 | tf_op jit(solution)/shard_map/ppermute | solution.py:176
  159.7 21.2 %collective-permute-start.31 = (bf16[576,768]{1,0:T(8,128)(2,1)S(1)}, bf16[576,768]{1,0:T(8,128)(2,1)S(1)}, u32[]{:S(2)}, u32[]{:S(2)}) collective-permute-start(bf16[576,768]{1,0:T(8,128)(2,1)S(1)} %collective-permute-done.26), channel_id=1, source_target_pairs={{0,8},{1,9},{2,10},{3,11},{4,12},{5,13},{6,14},{7,15},{8,0},{9,1},... | collective-permute-start | bytes 2654216 | tf_op jit(solution)/shard_map/ppermute | solution.py:176
  161.9 20.5 %collective-permute-start.33 = (bf16[576,768]{1,0:T(8,128)(2,1)S(1)}, bf16[576,768]{1,0:T(8,128)(2,1)S(1)}, u32[]{:S(2)}, u32[]{:S(2)}) collective-permute-start(bf16[576,768]{1,0:T(8,128)(2,1)S(1)} %get-tuple-element.138), channel_id=1, source_target_pairs={{0,4},{1,5},{2,6},{3,7},{4,0},{5,1},{6,2},{7,3},{8,12},{9,13},{10,... | collective-permute-start | bytes 2654216 | tf_op jit(solution)/shard_map/ppermute | solution.py:164
  163.3 20.1 %collective-permute-start.32 = (bf16[576,768]{1,0:T(8,128)(2,1)S(1)}, bf16[576,768]{1,0:T(8,128)(2,1)S(1)}, u32[]{:S(2)}, u32[]{:S(2)}) collective-permute-start(bf16[576,768]{1,0:T(8,128)(2,1)S(1)} %get-tuple-element.139), channel_id=1, source_target_pairs={{0,2},{1,3},{2,0},{3,1},{4,6},{5,7},{6,4},{7,5},{8,10},{9,11},{10,... | collective-permute-start | bytes 2654216 | tf_op jit(solution)/shard_map/ppermute | solution.py:168
  185.8 20.1 %collective-permute-start.37 = (bf16[576,768]{1,0:T(8,128)(2,1)S(1)}, bf16[576,768]{1,0:T(8,128)(2,1)S(1)}, u32[]{:S(2)}, u32[]{:S(2)}) collective-permute-start(bf16[576,768]{1,0:T(8,128)(2,1)S(1)} %get-tuple-element.136), channel_id=1, source_target_pairs={{0,4},{1,5},{2,6},{3,7},{4,0},{5,1},{6,2},{7,3},{8,12},{9,13},{10,... | collective-permute-start | bytes 2654216 | tf_op jit(solution)/shard_map/ppermute | solution.py:164
  186.0 20.0 %collective-permute-start.36 = (bf16[576,768]{1,0:T(8,128)(2,1)S(1)}, bf16[576,768]{1,0:T(8,128)(2,1)S(1)}, u32[]{:S(2)}, u32[]{:S(2)}) collective-permute-start(bf16[576,768]{1,0:T(8,128)(2,1)S(1)} %get-tuple-element.137), channel_id=1, source_target_pairs={{0,2},{1,3},{2,0},{3,1},{4,6},{5,7},{6,4},{7,5},{8,10},{9,11},{10,... | collective-permute-start | bytes 2654216 | tf_op jit(solution)/shard_map/ppermute | solution.py:168
  207.8 16.7 %collective-permute-start.46 = (bf16[1536,768]{1,0:T(8,128)(2,1)}, bf16[1536,768]{1,0:T(8,128)(2,1)}, u32[]{:S(2)}, u32[]{:S(2)}) collective-permute-start(bf16[1536,768]{1,0:T(8,128)(2,1)} %get-tuple-element.120.refs_4_), channel_id=1, source_target_pairs={{0,1},{1,0},{2,3},{3,2},{4,5},{5,4},{6,7},{7,6},{8,9},{9,8},{10,11... | collective-permute-start | bytes 7077896 | tf_op jit(solution)/shard_map/ppermute | solution.py:172
  211.3 16.7 %collective-permute-start.44 = (bf16[192,768]{1,0:T(8,128)(2,1)}, bf16[192,768]{1,0:T(8,128)(2,1)S(1)}, u32[]{:S(2)}, u32[]{:S(2)}) collective-permute-start(bf16[192,768]{1,0:T(8,128)(2,1)} %get-tuple-element.121), channel_id=1, source_target_pairs={{0,2},{1,3},{2,0},{3,1},{4,6},{5,7},{6,4},{7,5},{8,10},{9,11},{10,... | collective-permute-start | bytes 884744 | tf_op jit(solution)/shard_map/ppermute | solution.py:168
  233.6 59.1 %collective-permute-start.40 = (bf16[96,768]{1,0:T(8,128)(2,1)}, bf16[96,768]{1,0:T(8,128)(2,1)}, u32[]{:S(2)}, u32[]{:S(2)}) collective-permute-start(bf16[96,768]{1,0:T(8,128)(2,1)} %get-tuple-element.88), channel_id=1, source_target_pairs={{0,0},{1,4},{2,2},{3,6},{4,1},{5,5},{6,3},{7,7},{8,8},{9,12},{10,1... | collective-permute-start | bytes 442376 | tf_op jit(solution)/shard_map/ppermute | solution.py:193
  236.6 56.1 %collective-permute-start.41 = (bf16[96,768]{1,0:T(8,128)(2,1)}, bf16[96,768]{1,0:T(8,128)(2,1)}, u32[]{:S(2)}, u32[]{:S(2)}) collective-permute-start(bf16[96,768]{1,0:T(8,128)(2,1)} %get-tuple-element.89), channel_id=1, source_target_pairs={{0,1},{1,5},{2,3},{3,7},{4,0},{5,4},{6,2},{7,6},{8,9},{9,13},{10,1... | collective-permute-start | bytes 442376 | tf_op jit(solution)/shard_map/ppermute | solution.py:193
  237.2 55.5 %collective-permute-start.42 = (bf16[96,768]{1,0:T(8,128)(2,1)}, bf16[96,768]{1,0:T(8,128)(2,1)}, u32[]{:S(2)}, u32[]{:S(2)}) collective-permute-start(bf16[96,768]{1,0:T(8,128)(2,1)} %get-tuple-element.90), channel_id=1, source_target_pairs={{0,2},{1,6},{2,0},{3,4},{4,3},{5,7},{6,1},{7,5},{8,10},{9,14},{10,... | collective-permute-start | bytes 442376 | tf_op jit(solution)/shard_map/ppermute | solution.py:193
  238.8 53.9 %collective-permute-start.43 = (bf16[96,768]{1,0:T(8,128)(2,1)}, bf16[96,768]{1,0:T(8,128)(2,1)}, u32[]{:S(2)}, u32[]{:S(2)}) collective-permute-start(bf16[96,768]{1,0:T(8,128)(2,1)} %get-tuple-element.91), channel_id=1, source_target_pairs={{0,3},{1,7},{2,1},{3,5},{4,2},{5,6},{6,0},{7,4},{8,11},{9,15},{10,... | collective-permute-start | bytes 442376 | tf_op jit(solution)/shard_map/ppermute | solution.py:193
  (57 other events, 433.7 us)

commit v5 on v4

--- a/solution.py
+++ b/solution.py
@@ -189,6 +189,10 @@
     return lax.optimization_barrier(parts)
 
 
+def swap_diagonal(a):
+    return lax.ppermute(a, AXES, pairs(lambda z, x, y, c: (z, 1 - x, 1 - y, c)))
+
+
 def swap_to(across, along):
     return lambda a: lax.ppermute(
         a, AXES, pairs(lambda z, x, y, c: (z, c, (y + along) % 2, (x + across) % 2))
@@ -223,7 +227,7 @@
     return whole.reshape(8 * rows, cols)
 
 
-def refresh_kernel(place_ref, sum_ref, more_ref, *refs):
+def refresh_kernel(place_ref, sum_ref, *refs):
     slabs = refs[:8]
     out_ref, whole, inner, held, total, first, sems = refs[8:]
     count, size = held.shape
@@ -246,7 +250,7 @@
     for k in range(8):
         for i in range(4):
             copy(k, i).start()
-    squares = size / (16.0 * (sum_ref[...] + more_ref[...]))
+    squares = size / (16.0 * sum_ref[...])
     square = squares[0, 0]
     last = (math.sqrt(size) * jnp.sqrt(squares))[0, 0]
     arrived(0)
@@ -299,7 +303,7 @@
     return pl.pallas_call(
         refresh_kernel,
         out_shape=jax.ShapeDtypeStruct((2, count, tall), F32),
-        in_specs=[in_smem] + [in_vmem] * 2 + [mine, theirs] * 4,
+        in_specs=[in_smem] + [in_vmem] + [mine, theirs] * 4,
         out_specs=in_vmem,
         scratch_shapes=[
             pltpu.VMEM((size, size), BF),
@@ -309,31 +313,39 @@
             pltpu.VMEM((count, size), F32),
             pltpu.SemaphoreType.DMA((8, 4)),
         ],
-        compiler_params=pltpu.CompilerParams(vmem_limit_bytes=34 * 2**20),
+        compiler_params=pltpu.CompilerParams(vmem_limit_bytes=56 * 2**20),
         cost_estimate=pl.CostEstimate(
             flops=15 * count * size * size, bytes_accessed=2 * size * size, transcendentals=0
         ),
-    )(places, *sums, *slabs)
+    )(places, sums, *slabs)
 
 
 def side_kernel(place_ref, core_ref, other_ref, cols_ref, rows_ref, power_ref, *refs):
-    basis_ref, terms, power, direction = refs[0], refs[1:5], refs[5], refs[6]
-    rows = power_ref.shape[0]
-    size = power.shape[0]
+    basis_ref, sum_ref, terms = refs[0], refs[1], refs[2:6]
+    power, direction, cols, sems = refs[6:]
+    rows, size = power_ref.shape
+    step = core_ref.shape[0] // 4
+
+    def copy(k):
+        block = pl.ds(pl.multiple_of(place_ref[8 + k], 16), size)
+        return pltpu.make_async_copy(cols_ref.at[block, :], cols.at[k], sems.at[k])
+
+    for k in range(4):
+        copy(k).start()
+    total = jnp.zeros((8, 128), F32)
     for k in range(8):
         source = (core_ref, other_ref)[k // 4]
-        start = (k % 4) * 2 * rows
+        start = (k % 4) * step
         place = pl.ds(pl.multiple_of(place_ref[k], 16), rows)
         direction[place, :] = source[start : start + rows, :]
         power[k * rows : (k + 1) * rows, :] = source[start + rows : start + 2 * rows, :]
-    back_half = dot_nn(rows_ref[...], direction[...]).astype(BF)
-    for k in range(4):
-        block = pl.ds(pl.multiple_of(place_ref[8 + k], 16), size)
-        terms[k][...] = dot_nt(back_half, cols_ref[block, :]).astype(BF)
-    total = jnp.zeros((rows, size), F32)
+        part = source[start + 2 * rows : start + step, :128].astype(F32)
+        total += jnp.sum(part, axis=0, keepdims=True)
+    sum_ref[...] = total
+    squares = jnp.zeros((rows, size), F32)
     for k in range(8):
-        total += jnp.square(power[k * rows : (k + 1) * rows, :].astype(F32))
-    square = size / (16.0 * jnp.sum(total))
+        squares += jnp.square(power[k * rows : (k + 1) * rows, :].astype(F32))
+    square = size / (16.0 * jnp.sum(squares))
     keep = power_ref[...]
     value = keep
     for turn in range(4):
@@ -344,27 +356,46 @@
             keep = value
     scale = math.sqrt(size) * jnp.sqrt(jnp.full((rows, size), square))
     basis_ref[...] = scale * (1.5 * keep - 0.5 * value)
+    back_half = dot_nn(rows_ref[...], direction[...]).astype(BF)
+    for k in range(4):
+        copy(k).wait()
+        terms[k][...] = dot_nt(back_half, cols[k]).astype(BF)
 
 
 def side(places, extra_core, extra_other, right_cols, left_rows, power_left):
     rows, size = power_left.shape
     in_vmem = pl.BlockSpec(memory_space=pltpu.VMEM)
     term = jax.ShapeDtypeStruct((rows, size), BF)
+    sums = jax.ShapeDtypeStruct((8, 128), F32)
     return pl.pallas_call(
         side_kernel,
-        out_shape=[jax.ShapeDtypeStruct((rows, size), F32)] + [term] * 4,
-        in_specs=[pl.BlockSpec(memory_space=pltpu.SMEM)] + [in_vmem] * 5,
-        out_specs=[in_vmem] * 5,
-        scratch_shapes=[pltpu.VMEM((size, size), BF), pltpu.VMEM((size, size), BF)],
-        compiler_params=pltpu.CompilerParams(vmem_limit_bytes=12 * 2**20),
+        out_shape=[jax.ShapeDtypeStruct((rows, size), F32), sums] + [term] * 4,
+        in_specs=[pl.BlockSpec(memory_space=pltpu.SMEM)]
+        + [in_vmem] * 2
+        + [pl.BlockSpec(memory_space=pl.ANY)]
+        + [in_vmem] * 2,
+        out_specs=[in_vmem] * 6,
+        scratch_shapes=[
+            pltpu.VMEM((size, size), BF),
+            pltpu.VMEM((size, size), BF),
+            pltpu.VMEM((4, size, size), BF),
+            pltpu.SemaphoreType.DMA((4,)),
+        ],
+        compiler_params=pltpu.CompilerParams(vmem_limit_bytes=56 * 2**20),
         cost_estimate=pl.CostEstimate(
             flops=26 * rows * size * size, bytes_accessed=12 * size * size, transcendentals=0
         ),
     )(places, extra_core, extra_other, right_cols, left_rows, power_left)
 
 
-def squares(tiles):
-    return jnp.sum(jnp.square(tiles.astype(F32)))
+def split_sum(total, cols):
+    row = lax.broadcasted_iota(jnp.int32, (16, cols), 0)
+    block = jnp.zeros((16, cols), F32)
+    for k in range(3):
+        head = lax.reduce_precision(total, 8, 7)
+        block = jnp.where(row == k, head, block)
+        total = total - head
+    return block.astype(BF)
 
 
 def local_pattern(gradient, moment_one, moment_two, stat_left, stat_right, basis_left, basis_right):
@@ -388,14 +419,21 @@
     )
     rows_small = small.shape[0]
 
-    turned, small_o1, small_i1 = stage(
-        turn_over(right_b, straight), swap_outer(small), swap_inner(small)
-    )
-    got_i, got_o, stat_y, stat_x = stage(
+    turned, small_o1, small_i1, moment_one, moment_two, stat_left = stage(
+        turn_over(right_b, straight),
+        swap_outer(small),
+        swap_inner(small),
+        moment_one,
+        moment_two,
+        stat_left,
+    )
+    early = jnp.concatenate([moment_one, moment_two, stat_left]).astype(BF)
+    got_i, got_o, stat_y, stat_x, early = stage(
         swap_inner(jnp.concatenate([turned, small_o1])),
         swap_outer(jnp.concatenate([turned, small_i1])),
         swap_y(stat_b),
         swap_x(stat_b),
+        turn_over(early, straight),
     )
     turned_o1, small_o2 = got_o[:rows_right], got_o[rows_right:]
     turned_i1, small_i2 = got_i[:rows_right], got_i[rows_right:]
@@ -464,77 +502,83 @@
     ).reshape(2 * cols_right, cols_right)
     carried = dot_nn(grad_core, rows_core)
     carried = (carried + swap_core(carried.astype(BF)).astype(F32)).astype(BF)
-    grad_whole = jnp.zeros((8 * rows_left, 4 * cols_right), BF)
-    for k in range(2):
-        cols = slice(k * cols_right, (k + 1) * cols_right)
-        grad_whole = put(grad_whole, grad_core[:, cols], 0, (2 * k + core) * cols_right)
-        grad_whole = put(grad_whole, grad_other[:, cols], 0, (2 * k + 1 - core) * cols_right)
+
+    def grad_block(at_x):
+        start = (z // 2) * cols_right + at_x * rows_right
+        ours = lax.dynamic_slice_in_dim(grad_core, start, rows_right, 1)
+        other = lax.dynamic_slice_in_dim(grad_other, start, rows_right, 1)
+        return jnp.where(z % 2 == core, ours, other)
+
+    def grad_gram(start):
+        total = 0.0
+        for part in (grad_core, grad_other):
+            rows = lax.dynamic_slice_in_dim(part, start, rows_left, 0)
+            total = total + dot_nt(rows, part)
+        return total
+
     share = (1.0 - beta_stat) / D
-    picked = lax.dynamic_slice_in_dim(grad_whole, (2 * z + core) * rows_right, rows_right, 1)
+    picked = grad_block(core)
     power = beta_stat * dot_nn(stat_rows, right_cols) + share * dot_tn(picked, carried)
-    power = power.astype(BF)
-
-    own_cols = lax.dynamic_slice_in_dim(grad_whole, shard_pos * rows_right, rows_right, 1)
-    own_grad = lax.dynamic_slice_in_dim(grad_whole, tensor_pos * cols_right, cols_right, 1)
-    new_stat_right = blend_stat(stat_right, dot_tn(own_cols, own_grad), D)
-    left_cols = lax.dynamic_slice_in_dim(left_all, (2 * z + core) * rows_left, rows_left, 1)
-    rotated = dot_tn(left_cols, carried).astype(BF)
-    grad_rows = lax.dynamic_slice_in_dim(grad_whole, shard_pos * rows_left, rows_left, 0)
-    new_stat_left = blend_stat(stat_left, dot_nt(grad_rows, grad_whole), FF)
+    power, carried = stage(power.astype(BF), carried)
+
+    here = (2 * z + core) * rows_left
+    early = early.astype(F32)
+    left_cols = lax.dynamic_slice_in_dim(left_all, here, rows_left, 1)
+    rotated = dot_tn(left_cols, carried)
+    _, _, direction = adam_moments(rotated, early[:rows_left], early[rows_left : 2 * rows_left])
+    stat_t = blend_stat(early[2 * rows_left :], grad_gram(here), FF)
+    left_t = dot_nn(stat_t.astype(BF), left_all).astype(BF)
+    square = jnp.sum(jnp.square(power.astype(F32)), keepdims=True)
+    extra = jnp.concatenate([direction, left_t, split_sum(square, cols_right)])
+
+    own_grad = lax.dynamic_slice_in_dim(grad_core, y * cols_right, cols_right, 1)
+    new_stat_right = blend_stat(stat_right, dot_tn(grad_block(x), own_grad), D)
+    new_stat_left = blend_stat(stat_left, grad_gram(shard_pos * rows_left), FF)
     power_left = dot_nn(new_stat_left.astype(BF), left_all)
-    power_left_b = power_left.astype(BF)
-
-    rotated = turn_over(rotated, straight)
-    new_moment_one, new_moment_two, direction = adam_moments(
-        rotated.astype(F32), moment_one, moment_two
-    )
-    extra = turn_over(jnp.concatenate([direction, power_left_b]), straight)
-    power_i1, near, power_y, power_x, extra, new_stat_right = stage(
+
+    power_i1, near, power_y, power_x, extra = stage(
         swap_inner(power),
         swap_outer(power),
         swap_y(power),
         swap_x(power),
         extra,
-        new_stat_right,
-    )
-    got_i, got_o, got_y, got_x = stage(
+    )
+    got_i, got_o, got_y, got_x, new_stat_right, new_stat_left, power_left = stage(
         swap_inner(jnp.concatenate([near, extra])),
         swap_outer(jnp.concatenate([power_i1, extra])),
         swap_y(jnp.concatenate([power_x[:half], near])),
         swap_x(jnp.concatenate([power_y[half:], near])),
+        new_stat_right,
+        new_stat_left,
+        power_left,
     )
     slab0 = jnp.concatenate([power, power_x, power_y, got_y[:half], got_x[:half]])
     near_x, near_y = got_x[half:], got_y[half:]
     power_o2, extra_o1 = got_o[:rows_right], got_o[rows_right:]
     power_i2, extra_i1 = got_i[:rows_right], got_i[rows_right:]
     mid = jnp.where(inner, power_i1, power_o2)
-    slab0_other = swap_core(slab0)
-    extra_i2, got_o, got_y, got_x, slab0_other, sum0 = stage(
+    extra_i2, got_o, got_y, got_x, slab0_other = stage(
         swap_inner(extra_o1),
         swap_outer(jnp.concatenate([power_i2, extra_i1])),
         swap_y(jnp.concatenate([near_x[:half], mid])),
         swap_x(jnp.concatenate([near_y[half:], mid])),
-        slab0_other,
-        squares(slab0_other),
+        swap_core(slab0),
     )
     slab1 = jnp.concatenate([near, near_x, near_y, got_y[:half], got_x[:half]])
     mid_x, mid_y = got_x[half:], got_y[half:]
     power_o3, extra_o2 = got_o[:rows_right], got_o[rows_right:]
     far = jnp.where(inner, power_i2, power_o3)
-    slab1_other = swap_core(slab1)
-    extra_o3, got_y, got_x, slab1_other, sum1 = stage(
+    extra_o3, got_y, got_x, slab1_other = stage(
         swap_outer(extra_i2),
         swap_y(jnp.concatenate([mid_x[:half], far])),
         swap_x(jnp.concatenate([mid_y[half:], far])),
-        slab1_other,
-        squares(slab1_other),
+        swap_core(slab1),
     )
     slab2 = jnp.concatenate([mid, mid_x, mid_y, got_y[:half], got_x[:half]])
     far_x, far_y = got_x[half:], got_y[half:]
     extra_core = jnp.concatenate(
         [extra, extra_o1, jnp.where(inner, extra_i1, extra_o2), jnp.where(inner, extra_i2, extra_o3)]
     )
-    slab2_other = swap_core(slab2)
     extra_other = swap_core(extra_core)
     near_place, mid_place, far_place = places_z(z)
     side_places = [
@@ -546,7 +590,7 @@
         for along in range(2)
         for across in range(2)
     ]
-    new_basis_left, *terms = side(
+    new_basis_left, sums, *terms = side(
         jnp.stack(side_places),
         extra_core,
         extra_other,
@@ -554,16 +598,21 @@
         lax.dynamic_slice_in_dim(left_all, (2 * z + core) * rows_left, rows_left, 0),
         power_left,
     )
-    got_y, got_x, slab2_other, sum2, new_basis_left = stage(
+    got_y, got_x, slab2_other, rotated, new_basis_left, sums = stage(
         swap_y(far_x[:half]),
         swap_x(far_y[half:]),
-        slab2_other,
-        squares(slab2_other),
+        swap_core(slab2),
+        rotated.astype(BF),
         new_basis_left,
+        sums,
     )
     slab3 = jnp.concatenate([far, far_x, far_y, got_y, got_x])
+    rotated = turn_over(rotated, straight)
+    new_moment_one, new_moment_two, _ = adam_moments(
+        rotated.astype(F32), moment_one, moment_two
+    )
     slab3_other = swap_core(slab3)
-    sum_core = jnp.full((8, 128), sum0 + sum1 + sum2 + squares(slab3))
+    sums = sums + swap_x(sums) + swap_y(sums) + swap_diagonal(sums)
 
     terms = [
         swap_to(across, along)(terms[2 * along + across])
@@ -576,7 +625,7 @@
         [jnp.where(straight, 0, rows_right) + core * half, straight.astype(jnp.int32)]
     )
     slabs = (slab0, slab0_other, slab1, slab1_other, slab2, slab2_other, slab3, slab3_other)
-    fresh = refresh(places, (sum_core, swap_core(sum_core)), slabs)
+    fresh = refresh(places, sums, slabs)
     theirs = swap_core(fresh[1])
     new_basis_right = jnp.zeros((rows_right, cols_right), F32)
     new_basis_right = put(new_basis_right, fresh[0], core * half, 0)

time: 298 us -> 295 us (0.990)
  waiting for transfers between devices: 107 us -> 93.2 us
  matrix products: 12.3 us -> 20.3 us
  Pallas kernels: 52 us -> 56.8 us
    reduce_sum x4 -> x1, other arithmetic: 9.03 us -> 1.97 us  [local_pattern(): square = jnp.sum(jnp.square(power.astype(F32)), keepdims=True)]
    ppermute x9 -> x10, waiting for transfers between devices: 38.1 us -> 31.3 us  [swap_x(): return lax.ppermute(a, AXES, pairs(lambda z, x, y, c: (z, 1 - x, y, c)))]
    ppermute x8, waiting for transfers between devices: 32.6 us -> 26.2 us  [swap_outer(): lax.ppermute(a, AXES, pairs(lambda z, x, y, c: (z + 1 - 2 * (z % 2), x, y...]
    ppermute x11 -> x10, starting transfers between devices: 18.1 us -> 13.5 us  [swap_core(): return lax.ppermute(a, AXES, pairs(lambda z, x, y, c: (z, x, y, 1 - c)))]
    dot_general x1 -> x3, matrix products: 1.6 us -> 5.83 us  [dot_nt(): lax.dot_general(a, b, (((1,), (1,)), ((), ())), preferred_element_type=F32)]
    ppermute x9 -> x10, waiting for transfers between devices: 8.96 us -> 4.75 us  [swap_y(): return lax.ppermute(a, AXES, pairs(lambda z, x, y, c: (z, x, 1 - y, c)))]
    unnamed x70 -> x72, local copies, waits for them, and re-layouts: 17.6 us -> 13.7 us
    dot_general x3 -> x4, matrix products: 5.02 us -> 8.83 us  [dot_nn(): return jnp.dot(a, b, preferred_element_type=F32)]
  transfers between devices with their start and end apart: 50 -> 52, of which waited for: 27 -> 25; matrix products, arithmetic and copies ran while one was open for 16% -> 19% of each run, Pallas kernels for 18% -> 19%
where the time goes in v5:
time: 295 us; the launch traced here: 292 us
  waiting for transfers between devices  93.2 us (32%)
  starting transfers between devices  62.7 us (21%)
  Pallas kernels  56.8 us (19%)
  other arithmetic  27.8 us (9%)
  local copies, waits for them, and re-layouts  25.2 us (9%)
  matrix products  20.3 us (7%)
  between operations  6.1 us (2%)
    pallas_call x1, Pallas kernels, refresh(): pl.pallas_call(refresh_kernel, out_shape=jax.ShapeDtypeStruct((2, count,...  48.1 us
    ppermute x10, waiting for transfers between devices, swap_x(): return lax.ppermute(a, AXES, pairs(lambda z, x, y, c: (z, 1 - x, y, c)))  31.3 us
    ppermute x8, waiting for transfers between devices, swap_outer(): lax.ppermute(a, AXES, pairs(lambda z, x, y, c: (z + 1 - 2 * (z % 2), x, y...  26.2 us
    ppermute x6, waiting for transfers between devices, swap_inner(): lax.ppermute(a, AXES, pairs(lambda z, x, y, c: (3 - z if 0 < z < 3 else -...  22.2 us
    ppermute x6, starting transfers between devices, swap_inner(): lax.ppermute(a, AXES, pairs(lambda z, x, y, c: (3 - z if 0 < z < 3 else -...  16.6 us
    unnamed x72, local copies, waits for them, and re-layouts  13.7 us
    ppermute x10, starting transfers between devices, swap_core(): return lax.ppermute(a, AXES, pairs(lambda z, x, y, c: (z, x, y, 1 - c)))  13.5 us
    ppermute x3, starting transfers between devices, turn_over(): return jnp.where(straight, a, lax.ppermute(a, AXES, crossed))  9.42 us
  transfers between devices with their start and end apart: 52, of which 25 were waited for; matrix products, arithmetic and copies ran while one was open for 19% of the time, Pallas kernels for 19%

profile of v5, /device:TPU:9, one launch (start us, length us, event | category | flops | bytes accessed | tf_op | source)
XLA Modules:
  0.0 292.0 jit_solution(6869736613580268360)
XLA Ops:
  3.0 3.7 %collective-permute-start = (bf16[384,768]{1,0:T(8,128)(2,1)}, bf16[384,768]{1,0:T(8,128)(2,1)}, u32[]{:S(2)}, u32[]{:S(2)}) collective-permute-start(bf16[384,768]{1,0:T(8,128)(2,1)} %multiply_convert_fusion), channel_id=1, source_target_pairs={{1,4},{3,6},{4,1},{6,3},{9,12},{11,14},{12,9},{14,11},{17,20},{19,... | collective-permute-start | bytes 1769480 | tf_op jit(solution)/shard_map/ppermute | solution.py:185
  9.4 3.3 %collective-permute-start.2 = (bf16[144,768]{1,0:T(8,128)(2,1)}, bf16[144,768]{1,0:T(8,128)(2,1)}, u32[]{:S(2)}, u32[]{:S(2)}) collective-permute-start(bf16[144,768]{1,0:T(8,128)(2,1)} %get-tuple-element.169), channel_id=1, source_target_pairs={{8,16},{9,17},{10,18},{11,19},{12,20},{13,21},{14,22},{15,23},{16,... | collective-permute-start | bytes 663560 | tf_op jit(solution)/shard_map/ppermute | solution.py:180
  26.9 6.3 %collective-permute-done.7 = bf16[288,768]{1,0:T(8,128)(2,1)S(1)} collective-permute-done((bf16[288,768]{1,0:T(8,128)(2,1)S(1)}, bf16[288,768]{1,0:T(8,128)(2,1)S(1)}, u32[]{:S(2)}, u32[]{:S(2)}) %collective-permute-start.7) | collective-permute-done | bytes 442400 | tf_op jit(solution)/shard_map/ppermute | solution.py:185
  33.3 8.4 %collective-permute-done.4 = bf16[528,768]{1,0:T(8,128)(2,1)S(1)} collective-permute-done((bf16[528,768]{1,0:T(8,128)(2,1)S(1)}, bf16[528,768]{1,0:T(8,128)(2,1)S(1)}, u32[]{:S(2)}, u32[]{:S(2)}) %collective-permute-start.4) | collective-permute-done | bytes 811040 | tf_op jit(solution)/shard_map/ppermute | solution.py:176
  53.2 9.2 %collective-permute-done.8 = bf16[384,768]{1,0:T(8,128)(2,1)S(1)} collective-permute-done((bf16[384,768]{1,0:T(8,128)(2,1)S(1)}, bf16[384,768]{1,0:T(8,128)(2,1)S(1)}, u32[]{:S(2)}, u32[]{:S(2)}) %collective-permute-start.8) | collective-permute-done | bytes 589856 | tf_op jit(solution)/shard_map/ppermute | solution.py:180
  62.4 3.9 %collective-permute-done.11 = bf16[480,768]{1,0:T(8,128)(2,1)S(1)} collective-permute-done((bf16[480,768]{1,0:T(8,128)(2,1)S(1)}, bf16[480,768]{1,0:T(8,128)(2,1)S(1)}, u32[]{:S(2)}, u32[]{:S(2)}) %collective-permute-start.11) | collective-permute-done | bytes 737312 | tf_op jit(solution)/shard_map/ppermute | solution.py:164
  74.9 7.4 %collective-permute-done.12 = bf16[384,768]{1,0:T(8,128)(2,1)S(1)} collective-permute-done((bf16[384,768]{1,0:T(8,128)(2,1)S(1)}, bf16[384,768]{1,0:T(8,128)(2,1)S(1)}, u32[]{:S(2)}, u32[]{:S(2)}) %collective-permute-start.12) | collective-permute-done | bytes 589856 | tf_op jit(solution)/shard_map/ppermute | solution.py:176
  82.3 2.6 collective-permute-done.14
  87.5 2.7 collective-permute-start.18
  108.6 3.3 %collective-permute-start.21 = (bf16[384,768]{1,0:T(8,128)(2,1)}, bf16[384,768]{1,0:T(8,128)(2,1)}, u32[]{:S(2)}, u32[]{:S(2)}) collective-permute-start(bf16[384,768]{1,0:T(8,128)(2,1)} %fusion.2), channel_id=1, source_target_pairs={{8,16},{9,17},{10,18},{11,19},{12,20},{13,21},{14,22},{15,23},{16,... | collective-permute-start | bytes 1769480 | tf_op jit(solution)/shard_map/ppermute | solution.py:180
  118.0 3.8 %convolution_convert_fusion = bf16[96,768]{1,0:T(8,128)(2,1)} fusion(bf16[768,768]{1,0:T(8,128)(2,1)S(1)} %bitcast.149, f32[96,768]{1,0:T(8,128)} %fusion.38, bf16[768,1536]{1,0:T(8,128)(2,1)} %copy-done.1, f32[288,768]{1,0:T(8,128)} %copy-done.9, s32[]{:T(128)S(6)} %select_n.395), kind=kOutput, calls=%fused_computation.19 | convolution fusion | flops 340180992 | bytes 4571140 | tf_op jit(solution)/shard_map/dot_general | solution.py:137
  124.2 2.7 multiply_add_fusion
  133.0 2.8 collective-permute-start.25
  138.0 2.8 fusion
  143.0 6.9 %collective-permute-done.28 = bf16[576,768]{1,0:T(8,128)(2,1)S(1)} collective-permute-done((bf16[576,768]{1,0:T(8,128)(2,1)S(1)}, bf16[576,768]{1,0:T(8,128)(2,1)S(1)}, u32[]{:S(2)}, u32[]{:S(2)}) %collective-permute-start.28) | collective-permute-done | bytes 884768 | tf_op jit(solution)/shard_map/ppermute | solution.py:164
  154.5 3.1 %collective-permute-start.33 = (bf16[1536,768]{1,0:T(8,128)(2,1)S(1)}, bf16[1536,768]{1,0:T(8,128)(2,1)S(1)}, u32[]{:S(2)}, u32[]{:S(2)}) collective-permute-start(bf16[1536,768]{1,0:T(8,128)(2,1)S(1)} %get-tuple-element.141.refs_0_), channel_id=1, source_target_pairs={{0,1},{1,0},{2,3},{3,2},{4,5},{5,4},{6,7},{7,6},{8,9},{9,8},{10,11... | collective-permute-start | bytes 7077896 | tf_op jit(solution)/shard_map/ppermute | solution.py:172
  165.0 7.5 %collective-permute-done.29 = bf16[208,768]{1,0:T(8,128)(2,1)S(1)} collective-permute-done((bf16[208,768]{1,0:T(8,128)(2,1)S(1)}, bf16[208,768]{1,0:T(8,128)(2,1)S(1)}, u32[]{:S(2)}, u32[]{:S(2)}) %collective-permute-start.29) | collective-permute-done | bytes 319520 | tf_op jit(solution)/shard_map/ppermute | solution.py:180
  172.5 8.1 %collective-permute-done.32 = bf16[576,768]{1,0:T(8,128)(2,1)S(1)} collective-permute-done((bf16[576,768]{1,0:T(8,128)(2,1)S(1)}, bf16[576,768]{1,0:T(8,128)(2,1)S(1)}, u32[]{:S(2)}, u32[]{:S(2)}) %collective-permute-start.32) | collective-permute-done | bytes 884768 | tf_op jit(solution)/shard_map/ppermute | solution.py:164
  187.6 5.3 %collective-permute-done.34 = bf16[208,768]{1,0:T(8,128)(2,1)S(1)} collective-permute-done((bf16[208,768]{1,0:T(8,128)(2,1)S(1)}, bf16[208,768]{1,0:T(8,128)(2,1)S(1)}, u32[]{:S(2)}, u32[]{:S(2)}) %collective-permute-start.34) | collective-permute-done | bytes 319520 | tf_op jit(solution)/shard_map/ppermute | solution.py:176
  192.9 11.5 %collective-permute-done.36 = bf16[576,768]{1,0:T(8,128)(2,1)S(1)} collective-permute-done((bf16[576,768]{1,0:T(8,128)(2,1)S(1)}, bf16[576,768]{1,0:T(8,128)(2,1)S(1)}, u32[]{:S(2)}, u32[]{:S(2)}) %collective-permute-start.36) | collective-permute-done | bytes 884768 | tf_op jit(solution)/shard_map/ppermute | solution.py:164
  215.2 8.7 %shard_map.126 = (f32[96,768]{1,0:T(8,128)}, f32[8,128]{1,0:T(8,128)}, bf16[96,768]{1,0:T(8,128)(2,1)}, bf16[96,768]{1,0:T(8,128)(2,1)}, bf16[96,768]{1,0:T(8,128)(2,1)}, /*index=5*/bf16[96,768]{1,0:T(8,128)(2,1)}) custom-call(s32[12]{0:T(128)} %stack.63.place_ref, bf16[832,768]{1,0:T(8,128)(2,1)} %copy-done.2, ...), custom_call_target="tpu_custom_call" | custom-call | flops 1472200704 | bytes 7077888 | tf_op jit(solution)/shard_map/pallas_call | solution.py:370
  229.4 3.1 %collective-permute-start.39 = (bf16[96,768]{1,0:T(8,128)(2,1)}, bf16[96,768]{1,0:T(8,128)(2,1)S(1)}, u32[]{:S(2)}, u32[]{:S(2)}) collective-permute-start(bf16[96,768]{1,0:T(8,128)(2,1)} %get-tuple-element.103), channel_id=1, source_target_pairs={{0,0},{1,4},{2,2},{3,6},{4,1},{5,5},{6,3},{7,7},{8,8},{9,12},{10,1... | collective-permute-start | bytes 442376 | tf_op jit(solution)/shard_map/ppermute | solution.py:197
  235.7 3.8 %collective-permute-start.46 = (bf16[96,768]{1,0:T(8,128)(2,1)S(1)}, bf16[96,768]{1,0:T(8,128)(2,1)S(1)}, u32[]{:S(2)}, u32[]{:S(2)}) collective-permute-start(bf16[96,768]{1,0:T(8,128)(2,1)S(1)} %copy-done.25), channel_id=1, source_target_pairs={{1,4},{3,6},{4,1},{6,3},{9,12},{11,14},{12,9},{14,11},{17,20},{19,... | collective-permute-start | bytes 442376 | tf_op jit(solution)/shard_map/ppermute | solution.py:185
  239.6 48.1 %shard_map.127 = f32[2,192,768]{2,1,0:T(8,128)} custom-call(s32[2]{0:T(128)} %pad_add_fusion.place_ref, f32[8,128]{1,0:T(8,128)} %add_add_fusion.sum_ref, bf16[1536,768]{1,0:T(8,128)(2,1)} %copy-done.23, bf16[1536,768]{1,0:T(8,128)(2,1)} %copy-done.26, bf16[1536,768]{1,0:T(8,128)(2,1)} %copy-done.24, bf16[1536,768]{1,0:T(8,128)(2,1)} %copy-done.27, ...), custom_call_target="tpu_custom_call" | custom-call | flops 27179089920 | bytes 18874368 | tf_op jit(solution)/shard_map/pallas_call | solution.py:303
  (267 shorter events, 116.7 us)
Async XLA Ops:
  13.7 19.6 %collective-permute-start.6 = (bf16[384,768]{1,0:T(8,128)(2,1)}, bf16[384,768]{1,0:T(8,128)(2,1)}, u32[]{:S(2)}, u32[]{:S(2)}) collective-permute-start(bf16[384,768]{1,0:T(8,128)(2,1)} %convert_element_type.65), channel_id=1, source_target_pairs={{0,4},{1,5},{2,6},{3,7},{4,0},{5,1},{6,2},{7,3},{8,12},{9,13},{10,... | collective-permute-start | bytes 1769480 | tf_op jit(solution)/shard_map/ppermute | solution.py:164
  13.7 19.6 %collective-permute-start.5 = (bf16[384,768]{1,0:T(8,128)(2,1)}, bf16[384,768]{1,0:T(8,128)(2,1)}, u32[]{:S(2)}, u32[]{:S(2)}) collective-permute-start(bf16[384,768]{1,0:T(8,128)(2,1)} %convert_element_type.65), channel_id=1, source_target_pairs={{0,2},{1,3},{2,0},{3,1},{4,6},{5,7},{6,4},{7,5},{8,10},{9,11},{10,... | collective-permute-start | bytes 1769480 | tf_op jit(solution)/shard_map/ppermute | solution.py:168
  22.9 18.9 %collective-permute-start.4 = (bf16[528,768]{1,0:T(8,128)(2,1)S(1)}, bf16[528,768]{1,0:T(8,128)(2,1)S(1)}, u32[]{:S(2)}, u32[]{:S(2)}) collective-permute-start(bf16[528,768]{1,0:T(8,128)(2,1)S(1)} %get-tuple-element.155), channel_id=1, source_target_pairs={{0,8},{1,9},{2,10},{3,11},{4,12},{5,13},{6,14},{7,15},{8,0},{9,1},... | collective-permute-start | bytes 2433032 | tf_op jit(solution)/shard_map/ppermute | solution.py:176
  22.9 20.4 %collective-permute-start.3 = (bf16[528,768]{1,0:T(8,128)(2,1)S(1)}, bf16[528,768]{1,0:T(8,128)(2,1)S(1)}, u32[]{:S(2)}, u32[]{:S(2)}) collective-permute-start(bf16[528,768]{1,0:T(8,128)(2,1)S(1)} %get-tuple-element.156), channel_id=1, source_target_pairs={{8,16},{9,17},{10,18},{11,19},{12,20},{13,21},{14,22},{15,23},{16,... | collective-permute-start | bytes 2433032 | tf_op jit(solution)/shard_map/ppermute | solution.py:180
  47.8 19.8 %collective-permute-start.9 = (bf16[528,768]{1,0:T(8,128)(2,1)S(1)}, bf16[528,768]{1,0:T(8,128)(2,1)S(1)}, u32[]{:S(2)}, u32[]{:S(2)}) collective-permute-start(bf16[528,768]{1,0:T(8,128)(2,1)S(1)} %collective-permute-done.3), channel_id=1, source_target_pairs={{0,8},{1,9},{2,10},{3,11},{4,12},{5,13},{6,14},{7,15},{8,0},{9,1},... | collective-permute-start | bytes 2433032 | tf_op jit(solution)/shard_map/ppermute | solution.py:176
  107.2 19.7 %collective-permute-start.24 = (bf16[384,768]{1,0:T(8,128)(2,1)}, bf16[384,768]{1,0:T(8,128)(2,1)}, u32[]{:S(2)}, u32[]{:S(2)}) collective-permute-start(bf16[384,768]{1,0:T(8,128)(2,1)} %fusion.2), channel_id=1, source_target_pairs={{0,4},{1,5},{2,6},{3,7},{4,0},{5,1},{6,2},{7,3},{8,12},{9,13},{10,... | collective-permute-start | bytes 1769480 | tf_op jit(solution)/shard_map/ppermute | solution.py:164
  107.6 19.3 %collective-permute-start.23 = (bf16[384,768]{1,0:T(8,128)(2,1)}, bf16[384,768]{1,0:T(8,128)(2,1)}, u32[]{:S(2)}, u32[]{:S(2)}) collective-permute-start(bf16[384,768]{1,0:T(8,128)(2,1)} %fusion.2), channel_id=1, source_target_pairs={{0,2},{1,3},{2,0},{3,1},{4,6},{5,7},{6,4},{7,5},{8,10},{9,11},{10,... | collective-permute-start | bytes 1769480 | tf_op jit(solution)/shard_map/ppermute | solution.py:168
  108.3 18.6 %collective-permute-start.22 = (bf16[384,768]{1,0:T(8,128)(2,1)}, bf16[384,768]{1,0:T(8,128)(2,1)}, u32[]{:S(2)}, u32[]{:S(2)}) collective-permute-start(bf16[384,768]{1,0:T(8,128)(2,1)} %fusion.2), channel_id=1, source_target_pairs={{0,8},{1,9},{2,10},{3,11},{4,12},{5,13},{6,14},{7,15},{8,0},{9,1},... | collective-permute-start | bytes 1769480 | tf_op jit(solution)/shard_map/ppermute | solution.py:176
  130.2 19.7 %collective-permute-start.28 = (bf16[576,768]{1,0:T(8,128)(2,1)S(1)}, bf16[576,768]{1,0:T(8,128)(2,1)S(1)}, u32[]{:S(2)}, u32[]{:S(2)}) collective-permute-start(bf16[576,768]{1,0:T(8,128)(2,1)S(1)} %get-tuple-element.153), channel_id=1, source_target_pairs={{0,4},{1,5},{2,6},{3,7},{4,0},{5,1},{6,2},{7,3},{8,12},{9,13},{10,... | collective-permute-start | bytes 2654216 | tf_op jit(solution)/shard_map/ppermute | solution.py:164
  130.7 19.4 %collective-permute-start.27 = (bf16[576,768]{1,0:T(8,128)(2,1)S(1)}, bf16[576,768]{1,0:T(8,128)(2,1)S(1)}, u32[]{:S(2)}, u32[]{:S(2)}) collective-permute-start(bf16[576,768]{1,0:T(8,128)(2,1)S(1)} %get-tuple-element.154), channel_id=1, source_target_pairs={{0,2},{1,3},{2,0},{3,1},{4,6},{5,7},{6,4},{7,5},{8,10},{9,11},{10,... | collective-permute-start | bytes 2654216 | tf_op jit(solution)/shard_map/ppermute | solution.py:168
  132.9 19.6 %collective-permute-start.26 = (bf16[592,768]{1,0:T(8,128)(2,1)S(1)}, bf16[592,768]{1,0:T(8,128)(2,1)S(1)}, u32[]{:S(2)}, u32[]{:S(2)}) collective-permute-start(bf16[592,768]{1,0:T(8,128)(2,1)S(1)} %get-tuple-element.161), channel_id=1, source_target_pairs={{0,8},{1,9},{2,10},{3,11},{4,12},{5,13},{6,14},{7,15},{8,0},{9,1},... | collective-permute-start | bytes 2727944 | tf_op jit(solution)/shard_map/ppermute | solution.py:176
  133.0 21.4 %collective-permute-start.25 = (bf16[592,768]{1,0:T(8,128)(2,1)S(1)}, bf16[592,768]{1,0:T(8,128)(2,1)S(1)}, u32[]{:S(2)}, u32[]{:S(2)}) collective-permute-start(bf16[592,768]{1,0:T(8,128)(2,1)S(1)} %get-tuple-element.162), channel_id=1, source_target_pairs={{8,16},{9,17},{10,18},{11,19},{12,20},{13,21},{14,22},{15,23},{16,... | collective-permute-start | bytes 2727944 | tf_op jit(solution)/shard_map/ppermute | solution.py:180
  154.5 26.7 %collective-permute-start.33 = (bf16[1536,768]{1,0:T(8,128)(2,1)S(1)}, bf16[1536,768]{1,0:T(8,128)(2,1)S(1)}, u32[]{:S(2)}, u32[]{:S(2)}) collective-permute-start(bf16[1536,768]{1,0:T(8,128)(2,1)S(1)} %get-tuple-element.141.refs_0_), channel_id=1, source_target_pairs={{0,1},{1,0},{2,3},{3,2},{4,5},{5,4},{6,7},{7,6},{8,9},{9,8},{10,11... | collective-permute-start | bytes 7077896 | tf_op jit(solution)/shard_map/ppermute | solution.py:172
  157.6 23.6 %collective-permute-start.30 = (bf16[592,768]{1,0:T(8,128)(2,1)S(1)}, bf16[592,768]{1,0:T(8,128)(2,1)S(1)}, u32[]{:S(2)}, u32[]{:S(2)}) collective-permute-start(bf16[592,768]{1,0:T(8,128)(2,1)S(1)} %collective-permute-done.25), channel_id=1, source_target_pairs={{0,8},{1,9},{2,10},{3,11},{4,12},{5,13},{6,14},{7,15},{8,0},{9,1},... | collective-permute-start | bytes 2727944 | tf_op jit(solution)/shard_map/ppermute | solution.py:176
  159.8 20.7 %collective-permute-start.32 = (bf16[576,768]{1,0:T(8,128)(2,1)S(1)}, bf16[576,768]{1,0:T(8,128)(2,1)S(1)}, u32[]{:S(2)}, u32[]{:S(2)}) collective-permute-start(bf16[576,768]{1,0:T(8,128)(2,1)S(1)} %get-tuple-element.151), channel_id=1, source_target_pairs={{0,4},{1,5},{2,6},{3,7},{4,0},{5,1},{6,2},{7,3},{8,12},{9,13},{10,... | collective-permute-start | bytes 2654216 | tf_op jit(solution)/shard_map/ppermute | solution.py:164
  160.8 20.3 %collective-permute-start.31 = (bf16[576,768]{1,0:T(8,128)(2,1)S(1)}, bf16[576,768]{1,0:T(8,128)(2,1)S(1)}, u32[]{:S(2)}, u32[]{:S(2)}) collective-permute-start(bf16[576,768]{1,0:T(8,128)(2,1)S(1)} %get-tuple-element.152), channel_id=1, source_target_pairs={{0,2},{1,3},{2,0},{3,1},{4,6},{5,7},{6,4},{7,5},{8,10},{9,11},{10,... | collective-permute-start | bytes 2654216 | tf_op jit(solution)/shard_map/ppermute | solution.py:168
  181.3 23.3 %collective-permute-start.37 = (bf16[1536,768]{1,0:T(8,128)(2,1)S(1)}, bf16[1536,768]{1,0:T(8,128)(2,1)S(1)}, u32[]{:S(2)}, u32[]{:S(2)}) collective-permute-start(bf16[1536,768]{1,0:T(8,128)(2,1)S(1)} %get-tuple-element.137.refs_2_), channel_id=1, source_target_pairs={{0,1},{1,0},{2,3},{3,2},{4,5},{5,4},{6,7},{7,6},{8,9},{9,8},{10,11... | collective-permute-start | bytes 7077896 | tf_op jit(solution)/shard_map/ppermute | solution.py:172
  184.2 20.2 %collective-permute-start.36 = (bf16[576,768]{1,0:T(8,128)(2,1)S(1)}, bf16[576,768]{1,0:T(8,128)(2,1)S(1)}, u32[]{:S(2)}, u32[]{:S(2)}) collective-permute-start(bf16[576,768]{1,0:T(8,128)(2,1)S(1)} %get-tuple-element.149), channel_id=1, source_target_pairs={{0,4},{1,5},{2,6},{3,7},{4,0},{5,1},{6,2},{7,3},{8,12},{9,13},{10,... | collective-permute-start | bytes 2654216 | tf_op jit(solution)/shard_map/ppermute | solution.py:164
  184.8 19.9 %collective-permute-start.35 = (bf16[576,768]{1,0:T(8,128)(2,1)S(1)}, bf16[576,768]{1,0:T(8,128)(2,1)S(1)}, u32[]{:S(2)}, u32[]{:S(2)}) collective-permute-start(bf16[576,768]{1,0:T(8,128)(2,1)S(1)} %get-tuple-element.150), channel_id=1, source_target_pairs={{0,2},{1,3},{2,0},{3,1},{4,6},{5,7},{6,4},{7,5},{8,10},{9,11},{10,... | collective-permute-start | bytes 2654216 | tf_op jit(solution)/shard_map/ppermute | solution.py:168
  229.4 59.4 %collective-permute-start.39 = (bf16[96,768]{1,0:T(8,128)(2,1)}, bf16[96,768]{1,0:T(8,128)(2,1)S(1)}, u32[]{:S(2)}, u32[]{:S(2)}) collective-permute-start(bf16[96,768]{1,0:T(8,128)(2,1)} %get-tuple-element.103), channel_id=1, source_target_pairs={{0,0},{1,4},{2,2},{3,6},{4,1},{5,5},{6,3},{7,7},{8,8},{9,12},{10,1... | collective-permute-start | bytes 442376 | tf_op jit(solution)/shard_map/ppermute | solution.py:197
  232.6 56.4 %collective-permute-start.40 = (bf16[96,768]{1,0:T(8,128)(2,1)}, bf16[96,768]{1,0:T(8,128)(2,1)S(1)}, u32[]{:S(2)}, u32[]{:S(2)}) collective-permute-start(bf16[96,768]{1,0:T(8,128)(2,1)} %get-tuple-element.104), channel_id=1, source_target_pairs={{0,1},{1,5},{2,3},{3,7},{4,0},{5,4},{6,2},{7,6},{8,9},{9,13},{10,1... | collective-permute-start | bytes 442376 | tf_op jit(solution)/shard_map/ppermute | solution.py:197
  232.6 56.3 %collective-permute-start.41 = (bf16[96,768]{1,0:T(8,128)(2,1)}, bf16[96,768]{1,0:T(8,128)(2,1)S(1)}, u32[]{:S(2)}, u32[]{:S(2)}) collective-permute-start(bf16[96,768]{1,0:T(8,128)(2,1)} %get-tuple-element.105), channel_id=1, source_target_pairs={{0,2},{1,6},{2,0},{3,4},{4,3},{5,7},{6,1},{7,5},{8,10},{9,14},{10,... | collective-permute-start | bytes 442376 | tf_op jit(solution)/shard_map/ppermute | solution.py:197
  234.0 55.0 %collective-permute-start.42 = (bf16[96,768]{1,0:T(8,128)(2,1)}, bf16[96,768]{1,0:T(8,128)(2,1)S(1)}, u32[]{:S(2)}, u32[]{:S(2)}) collective-permute-start(bf16[96,768]{1,0:T(8,128)(2,1)} %get-tuple-element.106), channel_id=1, source_target_pairs={{0,3},{1,7},{2,1},{3,5},{4,2},{5,6},{6,0},{7,4},{8,11},{9,15},{10,... | collective-permute-start | bytes 442376 | tf_op jit(solution)/shard_map/ppermute | solution.py:197
  235.7 54.0 %collective-permute-start.46 = (bf16[96,768]{1,0:T(8,128)(2,1)S(1)}, bf16[96,768]{1,0:T(8,128)(2,1)S(1)}, u32[]{:S(2)}, u32[]{:S(2)}) collective-permute-start(bf16[96,768]{1,0:T(8,128)(2,1)S(1)} %copy-done.25), channel_id=1, source_target_pairs={{1,4},{3,6},{4,1},{6,3},{9,12},{11,14},{12,9},{14,11},{17,20},{19,... | collective-permute-start | bytes 442376 | tf_op jit(solution)/shard_map/ppermute | solution.py:185
  (59 other events, 636.9 us)

commit v6 on v5

--- a/solution.py
+++ b/solution.py
@@ -228,27 +228,38 @@
 
 
 def refresh_kernel(place_ref, sum_ref, *refs):
-    slabs = refs[:8]
-    out_ref, whole, inner, held, total, first, sems = refs[8:]
+    stacks = refs[:10]
+    out_ref, whole, inner, held, total, first, sems = refs[10:]
     count, size = held.shape
     tall = size // 4
     half = size // 8
 
     def copy(k, i):
-        source = slabs[k].at[pl.ds(i * half, half), :]
-        target = whole.at[pl.ds(k * half, half), pl.ds(i * tall, tall)]
+        slot, other = k // 2, k % 2
+        stack, row = slot, 0
+        rows = half if i < 3 else half // 2
+        if 0 < i < 3:
+            row = i * half if slot == 0 else (1 + i) * half + (i - 2) * (half // 2)
+        if i >= 3:
+            stack = slot + 1
+            row = (i - 3) * (half // 2)
+            if slot < 3:
+                row = half if i == 4 else 2 * half + half // 2
+        source = stacks[2 * stack + other].at[pl.ds(row, rows), :]
+        start = k * half + (half // 2 if i == 4 else 0)
+        target = whole.at[pl.ds(start, rows), pl.ds(min(i, 3) * tall, tall)]
         return pltpu.make_async_copy(source, target, sems.at[k, i])
 
     def arrived(j):
         for k in (2 * j, 2 * j + 1):
-            for i in range(4):
+            for i in range(5):
                 copy(k, i).wait()
 
     def span_of(j):
         return pl.ds(pl.multiple_of(j * tall, tall), tall)
 
     for k in range(8):
-        for i in range(4):
+        for i in range(5):
             copy(k, i).start()
     squares = size / (16.0 * sum_ref[...])
     square = squares[0, 0]
@@ -293,17 +304,16 @@
         out_ref[place] = last * (1.5 * first[:, span] - 0.5 * total[:, span])
 
 
-def refresh(places, sums, slabs):
-    size, tall = 2 * slabs[0].shape[0], slabs[0].shape[1]
+def refresh(places, sums, stacks):
+    tall = stacks[0].shape[1]
+    size = 4 * tall
     count = size // 16
     in_vmem = pl.BlockSpec(memory_space=pltpu.VMEM)
     in_smem = pl.BlockSpec(memory_space=pltpu.SMEM)
-    mine = pl.BlockSpec(memory_space=pl.ANY)
-    theirs = pl.BlockSpec(memory_space=pltpu.HBM)
     return pl.pallas_call(
         refresh_kernel,
         out_shape=jax.ShapeDtypeStruct((2, count, tall), F32),
-        in_specs=[in_smem] + [in_vmem] + [mine, theirs] * 4,
+        in_specs=[in_smem] + [in_vmem] + [pl.BlockSpec(memory_space=pl.ANY)] * 10,
         out_specs=in_vmem,
         scratch_shapes=[
             pltpu.VMEM((size, size), BF),
@@ -311,13 +321,13 @@
             pltpu.VMEM((count, size), BF),
             pltpu.VMEM((count, size), F32),
             pltpu.VMEM((count, size), F32),
-            pltpu.SemaphoreType.DMA((8, 4)),
+            pltpu.SemaphoreType.DMA((8, 5)),
         ],
         compiler_params=pltpu.CompilerParams(vmem_limit_bytes=56 * 2**20),
         cost_estimate=pl.CostEstimate(
             flops=15 * count * size * size, bytes_accessed=2 * size * size, transcendentals=0
         ),
-    )(places, sums, *slabs)
+    )(places, sums, *stacks)
 
 
 def side_kernel(place_ref, core_ref, other_ref, cols_ref, rows_ref, power_ref, *refs):
@@ -332,16 +342,15 @@
 
     for k in range(4):
         copy(k).start()
-    total = jnp.zeros((8, 128), F32)
+    total = jnp.zeros((step - 2 * rows, size), F32)
     for k in range(8):
         source = (core_ref, other_ref)[k // 4]
         start = (k % 4) * step
         place = pl.ds(pl.multiple_of(place_ref[k], 16), rows)
         direction[place, :] = source[start : start + rows, :]
         power[k * rows : (k + 1) * rows, :] = source[start + rows : start + 2 * rows, :]
-        part = source[start + 2 * rows : start + step, :128].astype(F32)
-        total += jnp.sum(part, axis=0, keepdims=True)
-    sum_ref[...] = total
+        total += source[start + 2 * rows : start + step, :].astype(F32)
+    sum_ref[...] = jnp.full(sum_ref.shape, jnp.sum(total))
     squares = jnp.zeros((rows, size), F32)
     for k in range(8):
         squares += jnp.square(power[k * rows : (k + 1) * rows, :].astype(F32))
@@ -388,14 +397,13 @@
     )(places, extra_core, extra_other, right_cols, left_rows, power_left)
 
 
-def split_sum(total, cols):
-    row = lax.broadcasted_iota(jnp.int32, (16, cols), 0)
-    block = jnp.zeros((16, cols), F32)
-    for k in range(3):
-        head = lax.reduce_precision(total, 8, 7)
-        block = jnp.where(row == k, head, block)
-        total = total - head
-    return block.astype(BF)
+def partial_squares(a):
+    squares = jnp.square(a.astype(F32)).reshape(-1, 16, a.shape[1])
+    return jnp.sum(squares, axis=0).astype(BF)
+
+
+def after(block, *others):
+    return lax.optimization_barrier((block, *others))[0]
 
 
 def local_pattern(gradient, moment_one, moment_two, stat_left, stat_right, basis_left, basis_right):
@@ -438,11 +446,13 @@
     turned_o1, small_o2 = got_o[:rows_right], got_o[rows_right:]
     turned_i1, small_i2 = got_i[:rows_right], got_i[rows_right:]
     small_1 = ordered_pair(z % 2 == 0, small, small_o1).reshape(2 * rows_small, cols_right)
-    turned_i2, got_o, got_y, got_x = stage(
-        swap_inner(turned_o1),
-        swap_outer(jnp.concatenate([turned_i1, small_i2])),
-        swap_y(jnp.concatenate([stat_x[:half], small_1])),
-        swap_x(jnp.concatenate([stat_y[half:], small_1])),
+    to_x = jnp.concatenate([stat_y[half:], small_1])
+    to_y = jnp.concatenate([stat_x[:half], small_1])
+    got_x, got_y, got_o, turned_i2 = stage(
+        swap_x(to_x),
+        swap_y(to_y),
+        swap_outer(after(jnp.concatenate([turned_i1, small_i2]), to_x, to_y)),
+        swap_inner(after(turned_o1, to_x, to_y)),
     )
     turned_o2, small_o3 = got_o[:rows_right], got_o[rows_right:]
     small_2 = ordered_pair(
@@ -509,13 +519,13 @@
         other = lax.dynamic_slice_in_dim(grad_other, start, rows_right, 1)
         return jnp.where(z % 2 == core, ours, other)
 
-    def grad_gram(start):
-        total = 0.0
-        for part in (grad_core, grad_other):
-            rows = lax.dynamic_slice_in_dim(part, start, rows_left, 0)
-            total = total + dot_nt(rows, part)
-        return total
-
+    gram = 0.0
+    for part in (grad_core, grad_other):
+        rows = lax.dynamic_slice_in_dim(part, 2 * z * rows_left, 2 * rows_left, 0)
+        gram = gram + dot_nt(rows, part)
+    gram = gram.reshape(2, rows_left, cols_right)
+    gram_own = lax.dynamic_index_in_dim(gram, x, 0, False)
+    gram_here = lax.dynamic_index_in_dim(gram, core, 0, False)
     share = (1.0 - beta_stat) / D
     picked = grad_block(core)
     power = beta_stat * dot_nn(stat_rows, right_cols) + share * dot_tn(picked, carried)
@@ -526,60 +536,68 @@
     left_cols = lax.dynamic_slice_in_dim(left_all, here, rows_left, 1)
     rotated = dot_tn(left_cols, carried)
     _, _, direction = adam_moments(rotated, early[:rows_left], early[rows_left : 2 * rows_left])
-    stat_t = blend_stat(early[2 * rows_left :], grad_gram(here), FF)
+    stat_t = blend_stat(early[2 * rows_left :], gram_here, FF)
     left_t = dot_nn(stat_t.astype(BF), left_all).astype(BF)
-    square = jnp.sum(jnp.square(power.astype(F32)), keepdims=True)
-    extra = jnp.concatenate([direction, left_t, split_sum(square, cols_right)])
+    extra = jnp.concatenate([direction, left_t, partial_squares(power)])
 
     own_grad = lax.dynamic_slice_in_dim(grad_core, y * cols_right, cols_right, 1)
     new_stat_right = blend_stat(stat_right, dot_tn(grad_block(x), own_grad), D)
-    new_stat_left = blend_stat(stat_left, grad_gram(shard_pos * rows_left), FF)
+    new_stat_left = blend_stat(stat_left, gram_own, FF)
     power_left = dot_nn(new_stat_left.astype(BF), left_all)
 
-    power_i1, near, power_y, power_x, extra = stage(
+    power_x, power_y, near, power_i1, extra = stage(
+        swap_x(power),
+        swap_y(power),
+        swap_outer(power),
         swap_inner(power),
-        swap_outer(power),
-        swap_y(power),
-        swap_x(power),
         extra,
     )
-    got_i, got_o, got_y, got_x, new_stat_right, new_stat_left, power_left = stage(
-        swap_inner(jnp.concatenate([near, extra])),
-        swap_outer(jnp.concatenate([power_i1, extra])),
-        swap_y(jnp.concatenate([power_x[:half], near])),
-        swap_x(jnp.concatenate([power_y[half:], near])),
+    left_rows = lax.dynamic_slice_in_dim(left_all, here, rows_left, 0)
+    to_x = jnp.concatenate([power_y[half:], near])
+    to_y = jnp.concatenate([power_x[:half], near])
+    got_x, got_y, got_o, got_i, new_stat_right, new_stat_left, power_left, left_rows = stage(
+        swap_x(to_x),
+        swap_y(to_y),
+        swap_outer(after(jnp.concatenate([power_i1, extra]), to_x, to_y)),
+        swap_inner(after(jnp.concatenate([near, extra]), to_x, to_y)),
         new_stat_right,
         new_stat_left,
         power_left,
-    )
-    slab0 = jnp.concatenate([power, power_x, power_y, got_y[:half], got_x[:half]])
+        left_rows,
+    )
+    stack0 = jnp.concatenate([power, power_x, power_y])
+    stack1 = jnp.concatenate([near, got_x, got_y])
     near_x, near_y = got_x[half:], got_y[half:]
     power_o2, extra_o1 = got_o[:rows_right], got_o[rows_right:]
     power_i2, extra_i1 = got_i[:rows_right], got_i[rows_right:]
     mid = jnp.where(inner, power_i1, power_o2)
-    extra_i2, got_o, got_y, got_x, slab0_other = stage(
-        swap_inner(extra_o1),
-        swap_outer(jnp.concatenate([power_i2, extra_i1])),
-        swap_y(jnp.concatenate([near_x[:half], mid])),
-        swap_x(jnp.concatenate([near_y[half:], mid])),
-        swap_core(slab0),
-    )
-    slab1 = jnp.concatenate([near, near_x, near_y, got_y[:half], got_x[:half]])
+    to_x = jnp.concatenate([near_y[half:], mid])
+    to_y = jnp.concatenate([near_x[:half], mid])
+    got_x, got_y, got_o, extra_i2, other0 = stage(
+        swap_x(to_x),
+        swap_y(to_y),
+        swap_outer(after(jnp.concatenate([power_i2, extra_i1]), to_x, to_y)),
+        swap_inner(after(extra_o1, to_x, to_y)),
+        swap_core(stack0),
+    )
+    stack2 = jnp.concatenate([mid, got_x, got_y])
     mid_x, mid_y = got_x[half:], got_y[half:]
     power_o3, extra_o2 = got_o[:rows_right], got_o[rows_right:]
     far = jnp.where(inner, power_i2, power_o3)
-    extra_o3, got_y, got_x, slab1_other = stage(
-        swap_outer(extra_i2),
-        swap_y(jnp.concatenate([mid_x[:half], far])),
-        swap_x(jnp.concatenate([mid_y[half:], far])),
-        swap_core(slab1),
-    )
-    slab2 = jnp.concatenate([mid, mid_x, mid_y, got_y[:half], got_x[:half]])
+    to_x = jnp.concatenate([mid_y[half:], far])
+    to_y = jnp.concatenate([mid_x[:half], far])
+    got_x, got_y, extra_o3, other1, rotated = stage(
+        swap_x(to_x),
+        swap_y(to_y),
+        swap_outer(after(extra_i2, to_x, to_y)),
+        swap_core(stack1),
+        turn_over(rotated.astype(BF), straight),
+    )
+    stack3 = jnp.concatenate([far, got_x, got_y])
     far_x, far_y = got_x[half:], got_y[half:]
     extra_core = jnp.concatenate(
         [extra, extra_o1, jnp.where(inner, extra_i1, extra_o2), jnp.where(inner, extra_i2, extra_o3)]
     )
-    extra_other = swap_core(extra_core)
     near_place, mid_place, far_place = places_z(z)
     side_places = [
         (2 * at_z + at_x) * rows_left
@@ -593,26 +611,24 @@
     new_basis_left, sums, *terms = side(
         jnp.stack(side_places),
         extra_core,
-        extra_other,
+        swap_core(extra_core),
         right_cols,
-        lax.dynamic_slice_in_dim(left_all, (2 * z + core) * rows_left, rows_left, 0),
+        left_rows,
         power_left,
     )
-    got_y, got_x, slab2_other, rotated, new_basis_left, sums = stage(
+    got_y, got_x, other2, new_basis_left, sums = stage(
         swap_y(far_x[:half]),
         swap_x(far_y[half:]),
-        swap_core(slab2),
-        rotated.astype(BF),
+        swap_core(stack2),
         new_basis_left,
         sums,
     )
-    slab3 = jnp.concatenate([far, far_x, far_y, got_y, got_x])
-    rotated = turn_over(rotated, straight)
+    stack4 = jnp.concatenate([got_y, got_x])
+    other3, other4 = swap_core(stack3), swap_core(stack4)
+    sums = sums + swap_x(sums) + swap_y(sums) + swap_diagonal(sums)
     new_moment_one, new_moment_two, _ = adam_moments(
         rotated.astype(F32), moment_one, moment_two
     )
-    slab3_other = swap_core(slab3)
-    sums = sums + swap_x(sums) + swap_y(sums) + swap_diagonal(sums)
 
     terms = [
         swap_to(across, along)(terms[2 * along + across])
@@ -624,8 +640,10 @@
     places = jnp.stack(
         [jnp.where(straight, 0, rows_right) + core * half, straight.astype(jnp.int32)]
     )
-    slabs = (slab0, slab0_other, slab1, slab1_other, slab2, slab2_other, slab3, slab3_other)
-    fresh = refresh(places, sums, slabs)
+    stacks = (
+        stack0, other0, stack1, other1, stack2, other2, stack3, other3, stack4, other4
+    )
+    fresh = refresh(places, sums, stacks)
     theirs = swap_core(fresh[1])
     new_basis_right = jnp.zeros((rows_right, cols_right), F32)
     new_basis_right = put(new_basis_right, fresh[0], core * half, 0)

time: 295 us -> 278 us (0.942)
  starting transfers between devices: 62.7 us -> 78.5 us
  local copies, waits for them, and re-layouts: 25.2 us -> 14.3 us
  matrix products: 20.3 us -> 12.6 us
  waiting for transfers between devices: 93.2 us -> 87 us
  between operations: 6.1 us -> 1.84 us
  other arithmetic: 27.8 us -> 24.3 us
    ppermute x8, waiting for transfers between devices: 26.2 us -> 13.1 us  [swap_outer(): lax.ppermute(a, AXES, pairs(lambda z, x, y, c: (z + 1 - 2 * (z % 2), x, y...]
    unnamed x72 -> x65, local copies, waits for them, and re-layouts: 13.7 us -> 3.82 us
    ppermute x10 -> x11, starting transfers between devices: 13.5 us -> 20.4 us  [swap_core(): return lax.ppermute(a, AXES, pairs(lambda z, x, y, c: (z, x, y, 1 - c)))]
    ppermute x10 -> x11, waiting for transfers between devices: 2.41 us -> 6.54 us  [swap_core(): return lax.ppermute(a, AXES, pairs(lambda z, x, y, c: (z, x, y, 1 - c)))]
    ppermute x3, starting transfers between devices: 9.42 us -> 13.5 us  [turn_over(): return jnp.where(straight, a, lax.ppermute(a, AXES, crossed))]
    dot_general x3 -> x2, matrix products: 5.83 us -> 1.81 us  [dot_nt(): lax.dot_general(a, b, (((1,), (1,)), ((), ())), preferred_element_type=F32)]
    ppermute x3, waiting for transfers between devices: 6.32 us -> 9.79 us  [turn_over(): return jnp.where(straight, a, lax.ppermute(a, AXES, crossed))]
    unnamed x2 -> x0, other arithmetic: 3.06 us -> none
  transfers between devices with their start and end apart: 52 -> 53, of which waited for: 25 -> 30; matrix products, arithmetic and copies ran while one was open for 19% -> 15% of each run, Pallas kernels for 19% -> 21%
where the time goes in v6:
time: 278 us; the launch traced here: 275 us
  waiting for transfers between devices  87 us (31%)
  starting transfers between devices  78.5 us (28%)
  Pallas kernels  56.8 us (20%)
  other arithmetic  24.3 us (9%)
  local copies, waits for them, and re-layouts  14.3 us (5%)
  matrix products  12.6 us (5%)
    pallas_call x1, Pallas kernels, refresh(): pl.pallas_call(refresh_kernel, out_shape=jax.ShapeDtypeStruct((2, count,...  48.2 us
    ppermute x10, waiting for transfers between devices, swap_x(): return lax.ppermute(a, AXES, pairs(lambda z, x, y, c: (z, 1 - x, y, c)))  32.4 us
    ppermute x6, waiting for transfers between devices, swap_inner(): lax.ppermute(a, AXES, pairs(lambda z, x, y, c: (3 - z if 0 < z < 3 else -...  23 us
    ppermute x11, starting transfers between devices, swap_core(): return lax.ppermute(a, AXES, pairs(lambda z, x, y, c: (z, x, y, 1 - c)))  20.4 us
    ppermute x6, starting transfers between devices, swap_inner(): lax.ppermute(a, AXES, pairs(lambda z, x, y, c: (3 - z if 0 < z < 3 else -...  17 us
    ppermute x3, starting transfers between devices, turn_over(): return jnp.where(straight, a, lax.ppermute(a, AXES, crossed))  13.5 us
    ppermute x8, waiting for transfers between devices, swap_outer(): lax.ppermute(a, AXES, pairs(lambda z, x, y, c: (z + 1 - 2 * (z % 2), x, y...  13.1 us
    ppermute x3, waiting for transfers between devices, turn_over(): return jnp.where(straight, a, lax.ppermute(a, AXES, crossed))  9.79 us
  transfers between devices with their start and end apart: 53, of which 30 were waited for; matrix products, arithmetic and copies ran while one was open for 15% of the time, Pallas kernels for 21%

profile of v6, /device:TPU:9, one launch (start us, length us, event | category | flops | bytes accessed | tf_op | source)
XLA Modules:
  0.0 275.2 jit_solution(1258853098848570070)
XLA Ops:
  3.0 3.8 %collective-permute-start = (bf16[384,768]{1,0:T(8,128)(2,1)}, bf16[384,768]{1,0:T(8,128)(2,1)}, u32[]{:S(2)}, u32[]{:S(2)}) collective-permute-start(bf16[384,768]{1,0:T(8,128)(2,1)} %multiply_convert_fusion), channel_id=1, source_target_pairs={{1,4},{3,6},{4,1},{6,3},{9,12},{11,14},{12,9},{14,11},{17,20},{19,... | collective-permute-start | bytes 1769480 | tf_op jit(solution)/shard_map/ppermute | solution.py:185
  7.8 4.3 %collective-permute-start.2 = (bf16[144,768]{1,0:T(8,128)(2,1)}, bf16[144,768]{1,0:T(8,128)(2,1)}, u32[]{:S(2)}, u32[]{:S(2)}) collective-permute-start(bf16[144,768]{1,0:T(8,128)(2,1)} %get-tuple-element.167), channel_id=1, source_target_pairs={{8,16},{9,17},{10,18},{11,19},{12,20},{13,21},{14,22},{15,23},{16,... | collective-permute-start | bytes 663560 | tf_op jit(solution)/shard_map/ppermute | solution.py:180
  18.4 3.6 %collective-permute-start.3 = (bf16[528,768]{1,0:T(8,128)(2,1)S(1)}, bf16[528,768]{1,0:T(8,128)(2,1)S(1)}, u32[]{:S(2)}, u32[]{:S(2)}) collective-permute-start(bf16[528,768]{1,0:T(8,128)(2,1)S(1)} %get-tuple-element.156), channel_id=1, source_target_pairs={{8,16},{9,17},{10,18},{11,19},{12,20},{13,21},{14,22},{15,23},{16,... | collective-permute-start | bytes 2433032 | tf_op jit(solution)/shard_map/ppermute | solution.py:180
  25.2 9.1 %collective-permute-done.7 = bf16[288,768]{1,0:T(8,128)(2,1)S(1)} collective-permute-done((bf16[288,768]{1,0:T(8,128)(2,1)S(1)}, bf16[288,768]{1,0:T(8,128)(2,1)S(1)}, u32[]{:S(2)}, u32[]{:S(2)}) %collective-permute-start.7) | collective-permute-done | bytes 442400 | tf_op jit(solution)/shard_map/ppermute | solution.py:185
  34.5 6.0 %collective-permute-done.3 = bf16[528,768]{1,0:T(8,128)(2,1)S(1)} collective-permute-done((bf16[528,768]{1,0:T(8,128)(2,1)S(1)}, bf16[528,768]{1,0:T(8,128)(2,1)S(1)}, u32[]{:S(2)}, u32[]{:S(2)}) %collective-permute-start.3) | collective-permute-done | bytes 811040 | tf_op jit(solution)/shard_map/ppermute | solution.py:180
  49.5 11.1 %collective-permute-done.11 = bf16[384,768]{1,0:T(8,128)(2,1)S(1)} collective-permute-done((bf16[384,768]{1,0:T(8,128)(2,1)S(1)}, bf16[384,768]{1,0:T(8,128)(2,1)S(1)}, u32[]{:S(2)}, u32[]{:S(2)}) %collective-permute-start.11) | collective-permute-done | bytes 589856 | tf_op jit(solution)/shard_map/ppermute | solution.py:180
  66.7 3.0 %collective-permute-start.15 = (bf16[768,768]{1,0:T(8,128)(2,1)S(1)}, bf16[768,768]{1,0:T(8,128)(2,1)S(1)}, u32[]{:S(2)}, u32[]{:S(2)}) collective-permute-start(bf16[768,768]{1,0:T(8,128)(2,1)S(1)} %pad_maximum_fusion.3), channel_id=1, source_target_pairs={{0,1},{1,0},{2,3},{3,2},{4,5},{5,4},{6,7},{7,6},{8,9},{9,8},{10,11... | collective-permute-start | bytes 3538952 | tf_op jit(solution)/shard_map/ppermute | solution.py:172
  70.1 5.5 %collective-permute-done.12 = bf16[384,768]{1,0:T(8,128)(2,1)S(1)} collective-permute-done((bf16[384,768]{1,0:T(8,128)(2,1)S(1)}, bf16[384,768]{1,0:T(8,128)(2,1)S(1)}, u32[]{:S(2)}, u32[]{:S(2)}) %collective-permute-start.12) | collective-permute-done | bytes 589856 | tf_op jit(solution)/shard_map/ppermute | solution.py:176
  75.5 2.9 %collective-permute-done.13 = bf16[432,768]{1,0:T(8,128)(2,1)S(1)} collective-permute-done((bf16[432,768]{1,0:T(8,128)(2,1)S(1)}, bf16[432,768]{1,0:T(8,128)(2,1)S(1)}, u32[]{:S(2)}, u32[]{:S(2)}) %collective-permute-start.13) | collective-permute-done | bytes 663584 | tf_op jit(solution)/shard_map/ppermute | solution.py:164
  81.2 3.9 %collective-permute-start.18 = (bf16[4,384,768]{2,1,0:T(8,128)(2,1)S(1)}, bf16[4,384,768]{2,1,0:T(8,128)(2,1)S(1)}, u32[]{:S(2)}, u32[]{:S(2)}) collective-permute-start(bf16[4,384,768]{2,1,0:T(8,128)(2,1)S(1)} %bitcast_dynamic-update-slice_fusion.2), channel_id=1, source_target_pairs={{0,1},{1,0},{2,3},{3,2},{4,5},{5,4},{6,7},{7,6},{8,9},{9,8},{10,11... | collective-permute-start | bytes 7077896 | tf_op jit(solution)/shard_map/ppermute | solution.py:172
  86.4 3.0 %collective-permute-done.18 = bf16[4,384,768]{2,1,0:T(8,128)(2,1)S(1)} collective-permute-done((bf16[4,384,768]{2,1,0:T(8,128)(2,1)S(1)}, bf16[4,384,768]{2,1,0:T(8,128)(2,1)S(1)}, u32[]{:S(2)}, u32[]{:S(2)}) %collective-permute-start.18) | collective-permute-done | bytes 2359328 | tf_op jit(solution)/shard_map/ppermute | solution.py:172
  123.3 2.8 %fusion = f32[384,768]{1,0:T(8,128)} fusion(bf16[768,1536]{1,0:T(8,128)(2,1)S(1)} %bitcast.152, s32[]{:T(128)S(6)} %select_n.375, f32[384,768]{1,0:T(8,128)S(1)} %copy-done.3, bf16[768,1536]{1,0:T(8,128)(2,1)} %copy-done.6, s32[]{:T(128)S(6)} %select_n.387, pred[]{:T(512)S(6)} %eq.36), kind=kOutput, calls=%fused_computation.7 | convolution fusion | flops 454164480 | bytes 4718601 | tf_op jit(solution)/shard_map/dot_general | solution.py:145
  128.3 3.0 %collective-permute-start.33 = (bf16[1152,768]{1,0:T(8,128)(2,1)S(1)}, bf16[1152,768]{1,0:T(8,128)(2,1)S(1)}, u32[]{:S(2)}, u32[]{:S(2)}) collective-permute-start(bf16[1152,768]{1,0:T(8,128)(2,1)S(1)} %constant_dynamic-update-slice_fusion.refs_0_), channel_id=1, source_target_pairs={{0,1},{1,0},{2,3},{3,2},{4,5},{5,4},{6,7},{7,6},{8,9},{9,8},{10,11... | collective-permute-start | bytes 5308424 | tf_op jit(solution)/shard_map/ppermute | solution.py:172
  131.4 4.5 %collective-permute-done.25 = bf16[576,768]{1,0:T(8,128)(2,1)S(1)} collective-permute-done((bf16[576,768]{1,0:T(8,128)(2,1)S(1)}, bf16[576,768]{1,0:T(8,128)(2,1)S(1)}, u32[]{:S(2)}, u32[]{:S(2)}) %collective-permute-start.25) | collective-permute-done | bytes 884768 | tf_op jit(solution)/shard_map/ppermute | solution.py:164
  136.5 2.4 collective-permute-done.27
  144.8 3.9 %collective-permute-start.37 = (bf16[1536,768]{1,0:T(8,128)(2,1)S(1)}, bf16[1536,768]{1,0:T(8,128)(2,1)S(1)}, u32[]{:S(2)}, u32[]{:S(2)}) collective-permute-start(bf16[1536,768]{1,0:T(8,128)(2,1)S(1)} %constant_dynamic-update-slice_fusion.3.refs_2_), channel_id=1, source_target_pairs={{0,1},{1,0},{2,3},{3,2},{4,5},{5,4},{6,7},{7,6},{8,9},{9,8},{10,11... | collective-permute-start | bytes 7077896 | tf_op jit(solution)/shard_map/ppermute | solution.py:172
  150.8 7.4 %collective-permute-start.38 = (bf16[96,768]{1,0:T(8,128)(2,1)S(1)}, bf16[96,768]{1,0:T(8,128)(2,1)S(1)}, u32[]{:S(2)}, u32[]{:S(2)}) collective-permute-start(bf16[96,768]{1,0:T(8,128)(2,1)S(1)} %copy-done.25), channel_id=1, source_target_pairs={{1,4},{3,6},{4,1},{6,3},{9,12},{11,14},{12,9},{14,11},{17,20},{19,... | collective-permute-start | bytes 442376 | tf_op jit(solution)/shard_map/ppermute | solution.py:185
  158.2 11.7 %collective-permute-done.29 = bf16[576,768]{1,0:T(8,128)(2,1)S(1)} collective-permute-done((bf16[576,768]{1,0:T(8,128)(2,1)S(1)}, bf16[576,768]{1,0:T(8,128)(2,1)S(1)}, u32[]{:S(2)}, u32[]{:S(2)}) %collective-permute-start.29) | collective-permute-done | bytes 884768 | tf_op jit(solution)/shard_map/ppermute | solution.py:164
  179.0 11.4 %collective-permute-done.34 = bf16[576,768]{1,0:T(8,128)(2,1)S(1)} collective-permute-done((bf16[576,768]{1,0:T(8,128)(2,1)S(1)}, bf16[576,768]{1,0:T(8,128)(2,1)S(1)}, u32[]{:S(2)}, u32[]{:S(2)}) %collective-permute-start.34) | collective-permute-done | bytes 884768 | tf_op jit(solution)/shard_map/ppermute | solution.py:164
  192.6 2.9 %collective-permute-start.50 = (bf16[1536,768]{1,0:T(8,128)(2,1)}, bf16[1536,768]{1,0:T(8,128)(2,1)}, u32[]{:S(2)}, u32[]{:S(2)}) collective-permute-start(bf16[1536,768]{1,0:T(8,128)(2,1)} %pad_maximum_fusion.1.refs_6_), channel_id=1, source_target_pairs={{0,1},{1,0},{2,3},{3,2},{4,5},{5,4},{6,7},{7,6},{8,9},{9,8},{10,11... | collective-permute-start | bytes 7077896 | tf_op jit(solution)/shard_map/ppermute | solution.py:172
  198.3 3.4 %collective-permute-done.39.other_ref = bf16[832,768]{1,0:T(8,128)(2,1)} collective-permute-done((bf16[832,768]{1,0:T(8,128)(2,1)S(1)}, bf16[832,768]{1,0:T(8,128)(2,1)}, u32[]{:S(2)}, u32[]{:S(2)}) %collective-permute-start.39) | collective-permute-done | bytes 1277984 | tf_op jit(solution)/shard_map/ppermute | solution.py:172
  201.7 8.6 %shard_map.126 = (f32[96,768]{1,0:T(8,128)}, f32[8,128]{1,0:T(8,128)}, bf16[96,768]{1,0:T(8,128)(2,1)}, bf16[96,768]{1,0:T(8,128)(2,1)}, bf16[96,768]{1,0:T(8,128)(2,1)}, /*index=5*/bf16[96,768]{1,0:T(8,128)(2,1)}) custom-call(s32[12]{0:T(128)} %stack.63.place_ref, bf16[832,768]{1,0:T(8,128)(2,1)} %copy-done.1, ...), custom_call_target="tpu_custom_call" | custom-call | flops 1472200704 | bytes 7077888 | tf_op jit(solution)/shard_map/pallas_call | solution.py:379
  219.6 3.2 %collective-permute-start.40 = (bf16[96,768]{1,0:T(8,128)(2,1)}, bf16[96,768]{1,0:T(8,128)(2,1)S(1)}, u32[]{:S(2)}, u32[]{:S(2)}) collective-permute-start(bf16[96,768]{1,0:T(8,128)(2,1)} %get-tuple-element.119), channel_id=1, source_target_pairs={{0,0},{1,4},{2,2},{3,6},{4,1},{5,5},{6,3},{7,7},{8,8},{9,12},{10,1... | collective-permute-start | bytes 442376 | tf_op jit(solution)/shard_map/ppermute | solution.py:197
  222.8 48.2 %shard_map.127 = f32[2,192,768]{2,1,0:T(8,128)} custom-call(s32[2]{0:T(128)} %pad_add_fusion.place_ref, f32[8,128]{1,0:T(8,128)} %add_add_fusion.sum_ref, bf16[1152,768]{1,0:T(8,128)(2,1)} %copy-done.21, bf16[1152,768]{1,0:T(8,128)(2,1)} %copy-done.28, bf16[1536,768]{1,0:T(8,128)(2,1)} %copy-done.23, bf16[1536,768]{1,0:T(8,128)(2,1)} %copy-done.27, ...), custom_call_target="tpu_custom_call" | custom-call | flops 27179089920 | bytes 18874368 | tf_op jit(solution)/shard_map/pallas_call | solution.py:313
  (270 shorter events, 103.7 us)
Async XLA Ops:
  13.0 21.4 %collective-permute-start.5 = (bf16[384,768]{1,0:T(8,128)(2,1)}, bf16[384,768]{1,0:T(8,128)(2,1)S(1)}, u32[]{:S(2)}, u32[]{:S(2)}) collective-permute-start(bf16[384,768]{1,0:T(8,128)(2,1)} %convert_element_type.65), channel_id=1, source_target_pairs={{0,2},{1,3},{2,0},{3,1},{4,6},{5,7},{6,4},{7,5},{8,10},{9,11},{10,... | collective-permute-start | bytes 1769480 | tf_op jit(solution)/shard_map/ppermute | solution.py:168
  14.3 20.2 %collective-permute-start.6 = (bf16[384,768]{1,0:T(8,128)(2,1)}, bf16[384,768]{1,0:T(8,128)(2,1)}, u32[]{:S(2)}, u32[]{:S(2)}) collective-permute-start(bf16[384,768]{1,0:T(8,128)(2,1)} %convert_element_type.65), channel_id=1, source_target_pairs={{0,4},{1,5},{2,6},{3,7},{4,0},{5,1},{6,2},{7,3},{8,12},{9,13},{10,... | collective-permute-start | bytes 1769480 | tf_op jit(solution)/shard_map/ppermute | solution.py:164
  18.4 22.1 %collective-permute-start.3 = (bf16[528,768]{1,0:T(8,128)(2,1)S(1)}, bf16[528,768]{1,0:T(8,128)(2,1)S(1)}, u32[]{:S(2)}, u32[]{:S(2)}) collective-permute-start(bf16[528,768]{1,0:T(8,128)(2,1)S(1)} %get-tuple-element.156), channel_id=1, source_target_pairs={{8,16},{9,17},{10,18},{11,19},{12,20},{13,21},{14,22},{15,23},{16,... | collective-permute-start | bytes 2433032 | tf_op jit(solution)/shard_map/ppermute | solution.py:180
  22.0 19.9 %collective-permute-start.4 = (bf16[528,768]{1,0:T(8,128)(2,1)S(1)}, bf16[528,768]{1,0:T(8,128)(2,1)S(1)}, u32[]{:S(2)}, u32[]{:S(2)}) collective-permute-start(bf16[528,768]{1,0:T(8,128)(2,1)S(1)} %get-tuple-element.155), channel_id=1, source_target_pairs={{0,8},{1,9},{2,10},{3,11},{4,12},{5,13},{6,14},{7,15},{8,0},{9,1},... | collective-permute-start | bytes 2433032 | tf_op jit(solution)/shard_map/ppermute | solution.py:176
  43.1 19.0 %collective-permute-start.10 = (bf16[528,768]{1,0:T(8,128)(2,1)S(1)}, bf16[528,768]{1,0:T(8,128)(2,1)S(1)}, u32[]{:S(2)}, u32[]{:S(2)}) collective-permute-start(bf16[528,768]{1,0:T(8,128)(2,1)S(1)} %collective-permute-done.3), channel_id=1, source_target_pairs={{0,8},{1,9},{2,10},{3,11},{4,12},{5,13},{6,14},{7,15},{8,0},{9,1},... | collective-permute-start | bytes 2433032 | tf_op jit(solution)/shard_map/ppermute | solution.py:176
  43.4 17.3 %collective-permute-start.8 = (bf16[480,768]{1,0:T(8,128)(2,1)S(1)}, bf16[480,768]{1,0:T(8,128)(2,1)S(1)}, u32[]{:S(2)}, u32[]{:S(2)}) collective-permute-start(bf16[480,768]{1,0:T(8,128)(2,1)S(1)} %get-tuple-element.160), channel_id=1, source_target_pairs={{0,4},{1,5},{2,6},{3,7},{4,0},{5,1},{6,2},{7,3},{8,12},{9,13},{10,... | collective-permute-start | bytes 2211848 | tf_op jit(solution)/shard_map/ppermute | solution.py:164
  116.9 19.0 %collective-permute-start.25 = (bf16[576,768]{1,0:T(8,128)(2,1)S(1)}, bf16[576,768]{1,0:T(8,128)(2,1)S(1)}, u32[]{:S(2)}, u32[]{:S(2)}) collective-permute-start(bf16[576,768]{1,0:T(8,128)(2,1)S(1)} %get-tuple-element.154), channel_id=1, source_target_pairs={{0,4},{1,5},{2,6},{3,7},{4,0},{5,1},{6,2},{7,3},{8,12},{9,13},{10,... | collective-permute-start | bytes 2654216 | tf_op jit(solution)/shard_map/ppermute | solution.py:164
  117.9 18.6 %collective-permute-start.26 = (bf16[576,768]{1,0:T(8,128)(2,1)S(1)}, bf16[576,768]{1,0:T(8,128)(2,1)S(1)}, u32[]{:S(2)}, u32[]{:S(2)}) collective-permute-start(bf16[576,768]{1,0:T(8,128)(2,1)S(1)} %get-tuple-element.153), channel_id=1, source_target_pairs={{0,2},{1,3},{2,0},{3,1},{4,6},{5,7},{6,4},{7,5},{8,10},{9,11},{10,... | collective-permute-start | bytes 2654216 | tf_op jit(solution)/shard_map/ppermute | solution.py:168
  119.9 19.1 %collective-permute-start.27 = (bf16[592,768]{1,0:T(8,128)(2,1)S(1)}, bf16[592,768]{1,0:T(8,128)(2,1)S(1)}, u32[]{:S(2)}, u32[]{:S(2)}) collective-permute-start(bf16[592,768]{1,0:T(8,128)(2,1)S(1)} %get-tuple-element.103), channel_id=1, source_target_pairs={{0,8},{1,9},{2,10},{3,11},{4,12},{5,13},{6,14},{7,15},{8,0},{9,1},... | collective-permute-start | bytes 2727944 | tf_op jit(solution)/shard_map/ppermute | solution.py:176
  120.0 20.9 %collective-permute-start.28 = (bf16[592,768]{1,0:T(8,128)(2,1)S(1)}, bf16[592,768]{1,0:T(8,128)(2,1)S(1)}, u32[]{:S(2)}, u32[]{:S(2)}) collective-permute-start(bf16[592,768]{1,0:T(8,128)(2,1)S(1)} %get-tuple-element.104), channel_id=1, source_target_pairs={{8,16},{9,17},{10,18},{11,19},{12,20},{13,21},{14,22},{15,23},{16,... | collective-permute-start | bytes 2727944 | tf_op jit(solution)/shard_map/ppermute | solution.py:180
  128.3 22.4 %collective-permute-start.33 = (bf16[1152,768]{1,0:T(8,128)(2,1)S(1)}, bf16[1152,768]{1,0:T(8,128)(2,1)S(1)}, u32[]{:S(2)}, u32[]{:S(2)}) collective-permute-start(bf16[1152,768]{1,0:T(8,128)(2,1)S(1)} %constant_dynamic-update-slice_fusion.refs_0_), channel_id=1, source_target_pairs={{0,1},{1,0},{2,3},{3,2},{4,5},{5,4},{6,7},{7,6},{8,9},{9,8},{10,11... | collective-permute-start | bytes 5308424 | tf_op jit(solution)/shard_map/ppermute | solution.py:172
  144.8 45.6 %collective-permute-start.37 = (bf16[1536,768]{1,0:T(8,128)(2,1)S(1)}, bf16[1536,768]{1,0:T(8,128)(2,1)S(1)}, u32[]{:S(2)}, u32[]{:S(2)}) collective-permute-start(bf16[1536,768]{1,0:T(8,128)(2,1)S(1)} %constant_dynamic-update-slice_fusion.3.refs_2_), channel_id=1, source_target_pairs={{0,1},{1,0},{2,3},{3,2},{4,5},{5,4},{6,7},{7,6},{8,9},{9,8},{10,11... | collective-permute-start | bytes 7077896 | tf_op jit(solution)/shard_map/ppermute | solution.py:172
  148.8 21.8 %collective-permute-start.31 = (bf16[592,768]{1,0:T(8,128)(2,1)S(1)}, bf16[592,768]{1,0:T(8,128)(2,1)S(1)}, u32[]{:S(2)}, u32[]{:S(2)}) collective-permute-start(bf16[592,768]{1,0:T(8,128)(2,1)S(1)} %collective-permute-done.28), channel_id=1, source_target_pairs={{0,8},{1,9},{2,10},{3,11},{4,12},{5,13},{6,14},{7,15},{8,0},{9,1},... | collective-permute-start | bytes 2727944 | tf_op jit(solution)/shard_map/ppermute | solution.py:176
  148.8 21.1 %collective-permute-start.29 = (bf16[576,768]{1,0:T(8,128)(2,1)S(1)}, bf16[576,768]{1,0:T(8,128)(2,1)S(1)}, u32[]{:S(2)}, u32[]{:S(2)}) collective-permute-start(bf16[576,768]{1,0:T(8,128)(2,1)S(1)} %get-tuple-element.152), channel_id=1, source_target_pairs={{0,4},{1,5},{2,6},{3,7},{4,0},{5,1},{6,2},{7,3},{8,12},{9,13},{10,... | collective-permute-start | bytes 2654216 | tf_op jit(solution)/shard_map/ppermute | solution.py:164
  150.1 19.8 %collective-permute-start.30 = (bf16[576,768]{1,0:T(8,128)(2,1)S(1)}, bf16[576,768]{1,0:T(8,128)(2,1)S(1)}, u32[]{:S(2)}, u32[]{:S(2)}) collective-permute-start(bf16[576,768]{1,0:T(8,128)(2,1)S(1)} %get-tuple-element.151), channel_id=1, source_target_pairs={{0,2},{1,3},{2,0},{3,1},{4,6},{5,7},{6,4},{7,5},{8,10},{9,11},{10,... | collective-permute-start | bytes 2654216 | tf_op jit(solution)/shard_map/ppermute | solution.py:168
  150.8 21.3 %collective-permute-start.38 = (bf16[96,768]{1,0:T(8,128)(2,1)S(1)}, bf16[96,768]{1,0:T(8,128)(2,1)S(1)}, u32[]{:S(2)}, u32[]{:S(2)}) collective-permute-start(bf16[96,768]{1,0:T(8,128)(2,1)S(1)} %copy-done.25), channel_id=1, source_target_pairs={{1,4},{3,6},{4,1},{6,3},{9,12},{11,14},{12,9},{14,11},{17,20},{19,... | collective-permute-start | bytes 442376 | tf_op jit(solution)/shard_map/ppermute | solution.py:185
  170.8 19.5 %collective-permute-start.34 = (bf16[576,768]{1,0:T(8,128)(2,1)S(1)}, bf16[576,768]{1,0:T(8,128)(2,1)S(1)}, u32[]{:S(2)}, u32[]{:S(2)}) collective-permute-start(bf16[576,768]{1,0:T(8,128)(2,1)S(1)} %get-tuple-element.150), channel_id=1, source_target_pairs={{0,4},{1,5},{2,6},{3,7},{4,0},{5,1},{6,2},{7,3},{8,12},{9,13},{10,... | collective-permute-start | bytes 2654216 | tf_op jit(solution)/shard_map/ppermute | solution.py:164
  171.3 19.1 %collective-permute-start.35 = (bf16[576,768]{1,0:T(8,128)(2,1)S(1)}, bf16[576,768]{1,0:T(8,128)(2,1)S(1)}, u32[]{:S(2)}, u32[]{:S(2)}) collective-permute-start(bf16[576,768]{1,0:T(8,128)(2,1)S(1)} %get-tuple-element.149), channel_id=1, source_target_pairs={{0,2},{1,3},{2,0},{3,1},{4,6},{5,7},{6,4},{7,5},{8,10},{9,11},{10,... | collective-permute-start | bytes 2654216 | tf_op jit(solution)/shard_map/ppermute | solution.py:168
  175.1 35.3 %collective-permute-start.46 = (bf16[1536,768]{1,0:T(8,128)(2,1)}, bf16[1536,768]{1,0:T(8,128)(2,1)}, u32[]{:S(2)}, u32[]{:S(2)}) collective-permute-start(bf16[1536,768]{1,0:T(8,128)(2,1)} %pad_maximum_fusion.refs_4_), channel_id=1, source_target_pairs={{0,1},{1,0},{2,3},{3,2},{4,5},{5,4},{6,7},{7,6},{8,9},{9,8},{10,11... | collective-permute-start | bytes 7077896 | tf_op jit(solution)/shard_map/ppermute | solution.py:172
  192.6 30.2 %collective-permute-start.50 = (bf16[1536,768]{1,0:T(8,128)(2,1)}, bf16[1536,768]{1,0:T(8,128)(2,1)}, u32[]{:S(2)}, u32[]{:S(2)}) collective-permute-start(bf16[1536,768]{1,0:T(8,128)(2,1)} %pad_maximum_fusion.1.refs_6_), channel_id=1, source_target_pairs={{0,1},{1,0},{2,3},{3,2},{4,5},{5,4},{6,7},{7,6},{8,9},{9,8},{10,11... | collective-permute-start | bytes 7077896 | tf_op jit(solution)/shard_map/ppermute | solution.py:172
  214.4 58.7 %collective-permute-start.43 = (bf16[96,768]{1,0:T(8,128)(2,1)}, bf16[96,768]{1,0:T(8,128)(2,1)S(1)}, u32[]{:S(2)}, u32[]{:S(2)}) collective-permute-start(bf16[96,768]{1,0:T(8,128)(2,1)} %get-tuple-element.122), channel_id=1, source_target_pairs={{0,3},{1,7},{2,1},{3,5},{4,2},{5,6},{6,0},{7,4},{8,11},{9,15},{10,... | collective-permute-start | bytes 442376 | tf_op jit(solution)/shard_map/ppermute | solution.py:197
  215.9 57.2 %collective-permute-start.42 = (bf16[96,768]{1,0:T(8,128)(2,1)}, bf16[96,768]{1,0:T(8,128)(2,1)S(1)}, u32[]{:S(2)}, u32[]{:S(2)}) collective-permute-start(bf16[96,768]{1,0:T(8,128)(2,1)} %get-tuple-element.121), channel_id=1, source_target_pairs={{0,2},{1,6},{2,0},{3,4},{4,3},{5,7},{6,1},{7,5},{8,10},{9,14},{10,... | collective-permute-start | bytes 442376 | tf_op jit(solution)/shard_map/ppermute | solution.py:197
  218.3 54.8 %collective-permute-start.41 = (bf16[96,768]{1,0:T(8,128)(2,1)}, bf16[96,768]{1,0:T(8,128)(2,1)S(1)}, u32[]{:S(2)}, u32[]{:S(2)}) collective-permute-start(bf16[96,768]{1,0:T(8,128)(2,1)} %get-tuple-element.120), channel_id=1, source_target_pairs={{0,1},{1,5},{2,3},{3,7},{4,0},{5,4},{6,2},{7,6},{8,9},{9,13},{10,1... | collective-permute-start | bytes 442376 | tf_op jit(solution)/shard_map/ppermute | solution.py:197
  219.6 53.5 %collective-permute-start.40 = (bf16[96,768]{1,0:T(8,128)(2,1)}, bf16[96,768]{1,0:T(8,128)(2,1)S(1)}, u32[]{:S(2)}, u32[]{:S(2)}) collective-permute-start(bf16[96,768]{1,0:T(8,128)(2,1)} %get-tuple-element.119), channel_id=1, source_target_pairs={{0,0},{1,4},{2,2},{3,6},{4,1},{5,5},{6,3},{7,7},{8,8},{9,12},{10,1... | collective-permute-start | bytes 442376 | tf_op jit(solution)/shard_map/ppermute | solution.py:197
  (63 other events, 606.1 us)

commit v7 on v6

--- a/solution.py
+++ b/solution.py
@@ -189,6 +189,11 @@
     return lax.optimization_barrier(parts)
 
 
+def exchange(*pairs_of):
+    blocks = lax.optimization_barrier(tuple(block for _, block in pairs_of))
+    return [send(block) for (send, _), block in zip(pairs_of, blocks)]
+
+
 def swap_diagonal(a):
     return lax.ppermute(a, AXES, pairs(lambda z, x, y, c: (z, 1 - x, 1 - y, c)))
 
@@ -227,24 +232,26 @@
     return whole.reshape(8 * rows, cols)
 
 
-def refresh_kernel(place_ref, sum_ref, *refs):
-    stacks = refs[:10]
-    out_ref, whole, inner, held, total, first, sems = refs[10:]
+def refresh_kernel(place_ref, *refs):
+    sums, stacks, (mine_ref, theirs_ref) = refs[:4], refs[4:14], refs[14:16]
+    whole, inner, held, total, first, sems = refs[16:]
     count, size = held.shape
     tall = size // 4
+    wide = size // 2
     half = size // 8
 
     def copy(k, i):
         slot, other = k // 2, k % 2
-        stack, row = slot, 0
         rows = half if i < 3 else half // 2
-        if 0 < i < 3:
-            row = i * half if slot == 0 else (1 + i) * half + (i - 2) * (half // 2)
-        if i >= 3:
+        if i < 3:
+            stack = slot
+            row = i * half + (i * (half // 2) if slot in (1, 2) else 0)
+        elif slot < 2:
             stack = slot + 1
-            row = (i - 3) * (half // 2)
-            if slot < 3:
-                row = half if i == 4 else 2 * half + half // 2
+            row = half if i == 4 else 2 * half + half // 2
+        else:
+            stack = 4
+            row = (i - 3) * half + (slot - 2) * (half // 2)
         source = stacks[2 * stack + other].at[pl.ds(row, rows), :]
         start = k * half + (half // 2 if i == 4 else 0)
         target = whole.at[pl.ds(start, rows), pl.ds(min(i, 3) * tall, tall)]
@@ -255,35 +262,34 @@
             for i in range(5):
                 copy(k, i).wait()
 
-    def span_of(j):
-        return pl.ds(pl.multiple_of(j * tall, tall), tall)
+    spans = [slice(0, wide), slice(wide, size)]
 
     for k in range(8):
         for i in range(5):
             copy(k, i).start()
-    squares = size / (16.0 * sum_ref[...])
+    squares = size / (16.0 * sum(part[...] for part in sums))
     square = squares[0, 0]
     last = (math.sqrt(size) * jnp.sqrt(squares))[0, 0]
     arrived(0)
     held[...] = whole[pl.ds(pl.multiple_of(place_ref[0], 16), count), :]
     total[...] = held[...].astype(F32)
 
+    for j in range(4):
+        if j:
+            arrived(j)
+        rows = slice(j * tall, (j + 1) * tall)
+        inner[:, rows] = dot_nt(held[...], whole[rows, :]).astype(BF)
+
     def one_pass(i, carry):
-        def towards(j, carry):
-            @pl.when(i == 0)
-            def _():
-                for k in range(1, 4):
-                    pl.when(j == k)(functools.partial(arrived, k))
-
-            inner[:, span_of(j)] = dot_nt(held[...], whole[span_of(j), :]).astype(BF)
-            return carry
-
-        lax.fori_loop(0, 4, towards, 0)
+        @pl.when(i > 0)
+        def _():
+            for span in spans:
+                inner[:, span] = dot_nt(held[...], whole[span, :]).astype(BF)
+
         keep = jnp.where(i == 1, 0.0, 1.5)
         take = jnp.where(i == 1, square, -0.5 * square)
 
-        def back(j, carry):
-            span = span_of(j)
+        def back(span):
             value = keep * total[:, span] + take * dot_nn(inner[...], whole[:, span])
             total[:, span] = value
             held[:, span] = value.astype(BF)
@@ -292,16 +298,22 @@
             def _():
                 first[:, span] = value
 
-            return carry
-
-        lax.fori_loop(0, jnp.where(i == 3, 2, 4), back, 0)
+        back(spans[0])
+        pl.when(i < 3)(functools.partial(back, spans[1]))
         return carry
 
     lax.fori_loop(0, 4, one_pass, 0)
-    for k in range(2):
+    for k, flag in ((0, 1), (1, 0)):
         span = slice(k * tall, (k + 1) * tall)
-        place = jnp.where(place_ref[1] == 1, k, 1 - k)
-        out_ref[place] = last * (1.5 * first[:, span] - 0.5 * total[:, span])
+        value = last * (1.5 * first[:, span] - 0.5 * total[:, span])
+
+        @pl.when(place_ref[1] == flag)
+        def _():
+            mine_ref[...] = value
+
+        @pl.when(place_ref[1] != flag)
+        def _():
+            theirs_ref[...] = value
 
 
 def refresh(places, sums, stacks):
@@ -312,9 +324,9 @@
     in_smem = pl.BlockSpec(memory_space=pltpu.SMEM)
     return pl.pallas_call(
         refresh_kernel,
-        out_shape=jax.ShapeDtypeStruct((2, count, tall), F32),
-        in_specs=[in_smem] + [in_vmem] + [pl.BlockSpec(memory_space=pl.ANY)] * 10,
-        out_specs=in_vmem,
+        out_shape=[jax.ShapeDtypeStruct((count, tall), F32)] * 2,
+        in_specs=[in_smem] + [in_vmem] * 4 + [pl.BlockSpec(memory_space=pl.ANY)] * 10,
+        out_specs=[in_vmem] * 2,
         scratch_shapes=[
             pltpu.VMEM((size, size), BF),
             pltpu.VMEM((count, size), BF),
@@ -327,7 +339,7 @@
         cost_estimate=pl.CostEstimate(
             flops=15 * count * size * size, bytes_accessed=2 * size * size, transcendentals=0
         ),
-    )(places, sums, *stacks)
+    )(places, *sums, *stacks)
 
 
 def side_kernel(place_ref, core_ref, other_ref, cols_ref, rows_ref, power_ref, *refs):
@@ -552,10 +564,37 @@
         swap_inner(power),
         extra,
     )
+    near_place, mid_place, far_place = places_z(z)
+    side_places = jnp.stack(
+        [
+            (2 * at_z + at_x) * rows_left
+            for at_x in (core, 1 - core)
+            for at_z in (z, near_place, mid_place, far_place)
+        ]
+        + [
+            ((y + along) % 2 * 2 + (x + across) % 2) * cols_right
+            for along in range(2)
+            for across in range(2)
+        ]
+    )
+    places = jnp.stack(
+        [jnp.where(straight, 0, rows_right) + core * half, straight.astype(jnp.int32)]
+    )
     left_rows = lax.dynamic_slice_in_dim(left_all, here, rows_left, 0)
     to_x = jnp.concatenate([power_y[half:], near])
     to_y = jnp.concatenate([power_x[:half], near])
-    got_x, got_y, got_o, got_i, new_stat_right, new_stat_left, power_left, left_rows = stage(
+    (
+        got_x,
+        got_y,
+        got_o,
+        got_i,
+        new_stat_right,
+        new_stat_left,
+        power_left,
+        left_rows,
+        side_places,
+        places,
+    ) = stage(
         swap_x(to_x),
         swap_y(to_y),
         swap_outer(after(jnp.concatenate([power_i1, extra]), to_x, to_y)),
@@ -564,6 +603,8 @@
         new_stat_left,
         power_left,
         left_rows,
+        side_places,
+        places,
     )
     stack0 = jnp.concatenate([power, power_x, power_y])
     stack1 = jnp.concatenate([near, got_x, got_y])
@@ -574,58 +615,50 @@
     to_x = jnp.concatenate([near_y[half:], mid])
     to_y = jnp.concatenate([near_x[:half], mid])
     got_x, got_y, got_o, extra_i2, other0 = stage(
-        swap_x(to_x),
-        swap_y(to_y),
-        swap_outer(after(jnp.concatenate([power_i2, extra_i1]), to_x, to_y)),
-        swap_inner(after(extra_o1, to_x, to_y)),
+        *exchange(
+            (swap_x, to_x),
+            (swap_y, to_y),
+            (swap_outer, jnp.concatenate([power_i2, extra_i1])),
+            (swap_inner, extra_o1),
+        ),
         swap_core(stack0),
     )
     stack2 = jnp.concatenate([mid, got_x, got_y])
     mid_x, mid_y = got_x[half:], got_y[half:]
     power_o3, extra_o2 = got_o[:rows_right], got_o[rows_right:]
     far = jnp.where(inner, power_i2, power_o3)
-    to_x = jnp.concatenate([mid_y[half:], far])
-    to_y = jnp.concatenate([mid_x[:half], far])
     got_x, got_y, extra_o3, other1, rotated = stage(
-        swap_x(to_x),
-        swap_y(to_y),
-        swap_outer(after(extra_i2, to_x, to_y)),
+        swap_x(far),
+        swap_y(far),
+        swap_outer(extra_i2),
         swap_core(stack1),
         turn_over(rotated.astype(BF), straight),
     )
-    stack3 = jnp.concatenate([far, got_x, got_y])
-    far_x, far_y = got_x[half:], got_y[half:]
+    far_x, far_y = got_x, got_y
+    stack3 = jnp.concatenate([far, far_x, far_y])
     extra_core = jnp.concatenate(
         [extra, extra_o1, jnp.where(inner, extra_i1, extra_o2), jnp.where(inner, extra_i2, extra_o3)]
     )
-    near_place, mid_place, far_place = places_z(z)
-    side_places = [
-        (2 * at_z + at_x) * rows_left
-        for at_x in (core, 1 - core)
-        for at_z in (z, near_place, mid_place, far_place)
-    ] + [
-        ((y + along) % 2 * 2 + (x + across) % 2) * cols_right
-        for along in range(2)
-        for across in range(2)
-    ]
+    extra_other = swap_core(extra_core)
+    stack3 = after(stack3, extra_other)
     new_basis_left, sums, *terms = side(
-        jnp.stack(side_places),
+        side_places,
         extra_core,
-        swap_core(extra_core),
+        extra_other,
         right_cols,
         left_rows,
         power_left,
     )
     got_y, got_x, other2, new_basis_left, sums = stage(
-        swap_y(far_x[:half]),
-        swap_x(far_y[half:]),
+        swap_y(jnp.concatenate([mid_x[:half], far_x[:half]])),
+        swap_x(jnp.concatenate([mid_y[half:], far_y[half:]])),
         swap_core(stack2),
         new_basis_left,
         sums,
     )
     stack4 = jnp.concatenate([got_y, got_x])
     other3, other4 = swap_core(stack3), swap_core(stack4)
-    sums = sums + swap_x(sums) + swap_y(sums) + swap_diagonal(sums)
+    sums = (sums, swap_x(sums), swap_y(sums), swap_diagonal(sums))
     new_moment_one, new_moment_two, _ = adam_moments(
         rotated.astype(F32), moment_one, moment_two
     )
@@ -637,16 +670,13 @@
     ]
     update = sum(term.astype(F32) for term in terms).astype(BF)
 
-    places = jnp.stack(
-        [jnp.where(straight, 0, rows_right) + core * half, straight.astype(jnp.int32)]
-    )
     stacks = (
         stack0, other0, stack1, other1, stack2, other2, stack3, other3, stack4, other4
     )
-    fresh = refresh(places, sums, stacks)
-    theirs = swap_core(fresh[1])
+    mine, theirs = refresh(places, sums, stacks)
+    theirs = swap_core(theirs)
     new_basis_right = jnp.zeros((rows_right, cols_right), F32)
-    new_basis_right = put(new_basis_right, fresh[0], core * half, 0)
+    new_basis_right = put(new_basis_right, mine, core * half, 0)
     new_basis_right = put(new_basis_right, theirs, (1 - core) * half, 0)
     return (
         update,

time: 278 us -> 270 us (0.971)
  starting transfers between devices: 78.5 us -> 81.5 us
  waiting for transfers between devices: 87 us -> 84.1 us
    ppermute x10, waiting for transfers between devices: 32.4 us -> 21.6 us  [swap_x(): return lax.ppermute(a, AXES, pairs(lambda z, x, y, c: (z, 1 - x, y, c)))]
    ppermute x10, waiting for transfers between devices: 1.82 us -> 9.05 us  [swap_y(): return lax.ppermute(a, AXES, pairs(lambda z, x, y, c: (z, x, 1 - y, c)))]
    ppermute x6, waiting for transfers between devices: 23 us -> 28.8 us  [swap_inner(): lax.ppermute(a, AXES, pairs(lambda z, x, y, c: (3 - z if 0 < z < 3 else -...]
    ppermute x11, starting transfers between devices: 20.4 us -> 25.9 us  [swap_core(): return lax.ppermute(a, AXES, pairs(lambda z, x, y, c: (z, x, y, 1 - c)))]
    ppermute x11, waiting for transfers between devices: 6.54 us -> 3.36 us  [swap_core(): return lax.ppermute(a, AXES, pairs(lambda z, x, y, c: (z, x, y, 1 - c)))]
    ppermute x3, starting transfers between devices: 13.5 us -> 10.7 us  [turn_over(): return jnp.where(straight, a, lax.ppermute(a, AXES, crossed))]
  transfers between devices with their start and end apart: 53 -> 53, of which waited for: 30 -> 29; matrix products, arithmetic and copies ran while one was open for 15% -> 14% of each run, Pallas kernels for 21% -> 20%
where the time goes in v7:
time: 270 us; the launch traced here: 269 us
  waiting for transfers between devices  84.1 us (31%)
  starting transfers between devices  81.5 us (30%)
  Pallas kernels  54.6 us (20%)
  other arithmetic  21.8 us (8%)
  local copies, waits for them, and re-layouts  12.7 us (5%)
  matrix products  12.6 us (5%)
    pallas_call x1, Pallas kernels, refresh(): pl.pallas_call(refresh_kernel, out_shape=[jax.ShapeDtypeStruct((count, ta...  45.9 us
    ppermute x6, waiting for transfers between devices, swap_inner(): lax.ppermute(a, AXES, pairs(lambda z, x, y, c: (3 - z if 0 < z < 3 else -...  28.8 us
    ppermute x11, starting transfers between devices, swap_core(): return lax.ppermute(a, AXES, pairs(lambda z, x, y, c: (z, x, y, 1 - c)))  25.9 us
    ppermute x10, waiting for transfers between devices, swap_x(): return lax.ppermute(a, AXES, pairs(lambda z, x, y, c: (z, 1 - x, y, c)))  21.6 us
    ppermute x6, starting transfers between devices, swap_inner(): lax.ppermute(a, AXES, pairs(lambda z, x, y, c: (3 - z if 0 < z < 3 else -...  17.4 us
    ppermute x8, waiting for transfers between devices, swap_outer(): lax.ppermute(a, AXES, pairs(lambda z, x, y, c: (z + 1 - 2 * (z % 2), x, y...  12.2 us
    ppermute x3, starting transfers between devices, turn_over(): return jnp.where(straight, a, lax.ppermute(a, AXES, crossed))  10.7 us
    ppermute x10, starting transfers between devices, swap_y(): return lax.ppermute(a, AXES, pairs(lambda z, x, y, c: (z, x, 1 - y, c)))  9.59 us
  transfers between devices with their start and end apart: 53, of which 29 were waited for; matrix products, arithmetic and copies ran while one was open for 14% of the time, Pallas kernels for 20%

profile of v7, /device:TPU:9, one launch (start us, length us, event | category | flops | bytes accessed | tf_op | source)
XLA Modules:
  0.0 269.3 jit_solution(4786266542844085960)
XLA Ops:
  3.0 3.8 %collective-permute-start = (bf16[384,768]{1,0:T(8,128)(2,1)}, bf16[384,768]{1,0:T(8,128)(2,1)}, u32[]{:S(2)}, u32[]{:S(2)}) collective-permute-start(bf16[384,768]{1,0:T(8,128)(2,1)} %multiply_convert_fusion), channel_id=1, source_target_pairs={{1,4},{3,6},{4,1},{6,3},{9,12},{11,14},{12,9},{14,11},{17,20},{19,... | collective-permute-start | bytes 1769480 | tf_op jit(solution)/shard_map/ppermute | solution.py:185
  7.8 4.3 %collective-permute-start.2 = (bf16[144,768]{1,0:T(8,128)(2,1)}, bf16[144,768]{1,0:T(8,128)(2,1)}, u32[]{:S(2)}, u32[]{:S(2)}) collective-permute-start(bf16[144,768]{1,0:T(8,128)(2,1)} %get-tuple-element.177), channel_id=1, source_target_pairs={{8,16},{9,17},{10,18},{11,19},{12,20},{13,21},{14,22},{15,23},{16,... | collective-permute-start | bytes 663560 | tf_op jit(solution)/shard_map/ppermute | solution.py:180
  18.4 3.8 %collective-permute-start.3 = (bf16[528,768]{1,0:T(8,128)(2,1)S(1)}, bf16[528,768]{1,0:T(8,128)(2,1)S(1)}, u32[]{:S(2)}, u32[]{:S(2)}) collective-permute-start(bf16[528,768]{1,0:T(8,128)(2,1)S(1)} %get-tuple-element.166), channel_id=1, source_target_pairs={{8,16},{9,17},{10,18},{11,19},{12,20},{13,21},{14,22},{15,23},{16,... | collective-permute-start | bytes 2433032 | tf_op jit(solution)/shard_map/ppermute | solution.py:180
  25.3 9.0 %collective-permute-done.7 = bf16[288,768]{1,0:T(8,128)(2,1)S(1)} collective-permute-done((bf16[288,768]{1,0:T(8,128)(2,1)S(1)}, bf16[288,768]{1,0:T(8,128)(2,1)S(1)}, u32[]{:S(2)}, u32[]{:S(2)}) %collective-permute-start.7) | collective-permute-done | bytes 442400 | tf_op jit(solution)/shard_map/ppermute | solution.py:185
  34.5 6.2 %collective-permute-done.3 = bf16[528,768]{1,0:T(8,128)(2,1)S(1)} collective-permute-done((bf16[528,768]{1,0:T(8,128)(2,1)S(1)}, bf16[528,768]{1,0:T(8,128)(2,1)S(1)}, u32[]{:S(2)}, u32[]{:S(2)}) %collective-permute-start.3) | collective-permute-done | bytes 811040 | tf_op jit(solution)/shard_map/ppermute | solution.py:180
  49.6 11.1 %collective-permute-done.11 = bf16[384,768]{1,0:T(8,128)(2,1)S(1)} collective-permute-done((bf16[384,768]{1,0:T(8,128)(2,1)S(1)}, bf16[384,768]{1,0:T(8,128)(2,1)S(1)}, u32[]{:S(2)}, u32[]{:S(2)}) %collective-permute-start.11) | collective-permute-done | bytes 589856 | tf_op jit(solution)/shard_map/ppermute | solution.py:180
  66.6 3.1 %collective-permute-start.15 = (bf16[768,768]{1,0:T(8,128)(2,1)S(1)}, bf16[768,768]{1,0:T(8,128)(2,1)S(1)}, u32[]{:S(2)}, u32[]{:S(2)}) collective-permute-start(bf16[768,768]{1,0:T(8,128)(2,1)S(1)} %pad_maximum_fusion.3), channel_id=1, source_target_pairs={{0,1},{1,0},{2,3},{3,2},{4,5},{5,4},{6,7},{7,6},{8,9},{9,8},{10,11... | collective-permute-start | bytes 3538952 | tf_op jit(solution)/shard_map/ppermute | solution.py:172
  70.1 5.3 %collective-permute-done.12 = bf16[384,768]{1,0:T(8,128)(2,1)S(1)} collective-permute-done((bf16[384,768]{1,0:T(8,128)(2,1)S(1)}, bf16[384,768]{1,0:T(8,128)(2,1)S(1)}, u32[]{:S(2)}, u32[]{:S(2)}) %collective-permute-start.12) | collective-permute-done | bytes 589856 | tf_op jit(solution)/shard_map/ppermute | solution.py:176
  75.4 2.9 %collective-permute-done.13 = bf16[432,768]{1,0:T(8,128)(2,1)S(1)} collective-permute-done((bf16[432,768]{1,0:T(8,128)(2,1)S(1)}, bf16[432,768]{1,0:T(8,128)(2,1)S(1)}, u32[]{:S(2)}, u32[]{:S(2)}) %collective-permute-start.13) | collective-permute-done | bytes 663584 | tf_op jit(solution)/shard_map/ppermute | solution.py:164
  81.1 4.0 %collective-permute-start.18 = (bf16[4,384,768]{2,1,0:T(8,128)(2,1)S(1)}, bf16[4,384,768]{2,1,0:T(8,128)(2,1)S(1)}, u32[]{:S(2)}, u32[]{:S(2)}) collective-permute-start(bf16[4,384,768]{2,1,0:T(8,128)(2,1)S(1)} %bitcast_dynamic-update-slice_fusion.2), channel_id=1, source_target_pairs={{0,1},{1,0},{2,3},{3,2},{4,5},{5,4},{6,7},{7,6},{8,9},{9,8},{10,11... | collective-permute-start | bytes 7077896 | tf_op jit(solution)/shard_map/ppermute | solution.py:172
  86.3 3.0 %collective-permute-done.18 = bf16[4,384,768]{2,1,0:T(8,128)(2,1)S(1)} collective-permute-done((bf16[4,384,768]{2,1,0:T(8,128)(2,1)S(1)}, bf16[4,384,768]{2,1,0:T(8,128)(2,1)S(1)}, u32[]{:S(2)}, u32[]{:S(2)}) %collective-permute-start.18) | collective-permute-done | bytes 2359328 | tf_op jit(solution)/shard_map/ppermute | solution.py:172
  128.5 3.0 %collective-permute-start.33 = (bf16[1152,768]{1,0:T(8,128)(2,1)S(1)}, bf16[1152,768]{1,0:T(8,128)(2,1)S(1)}, u32[]{:S(2)}, u32[]{:S(2)}) collective-permute-start(bf16[1152,768]{1,0:T(8,128)(2,1)S(1)} %constant_dynamic-update-slice_fusion.refs_4_), channel_id=1, source_target_pairs={{0,1},{1,0},{2,3},{3,2},{4,5},{5,4},{6,7},{7,6},{8,9},{9,8},{10,11... | collective-permute-start | bytes 5308424 | tf_op jit(solution)/shard_map/ppermute | solution.py:172
  131.6 4.5 %collective-permute-done.25 = bf16[576,768]{1,0:T(8,128)(2,1)S(1)} collective-permute-done((bf16[576,768]{1,0:T(8,128)(2,1)S(1)}, bf16[576,768]{1,0:T(8,128)(2,1)S(1)}, u32[]{:S(2)}, u32[]{:S(2)}) %collective-permute-start.25) | collective-permute-done | bytes 884768 | tf_op jit(solution)/shard_map/ppermute | solution.py:164
  141.1 3.7 %collective-permute-start.37 = (bf16[1536,768]{1,0:T(8,128)(2,1)S(1)}, bf16[1536,768]{1,0:T(8,128)(2,1)S(1)}, u32[]{:S(2)}, u32[]{:S(2)}) collective-permute-start(bf16[1536,768]{1,0:T(8,128)(2,1)S(1)} %constant_dynamic-update-slice_fusion.3.refs_6_), channel_id=1, source_target_pairs={{0,1},{1,0},{2,3},{3,2},{4,5},{5,4},{6,7},{7,6},{8,9},{9,8},{10,11... | collective-permute-start | bytes 7077896 | tf_op jit(solution)/shard_map/ppermute | solution.py:172
  149.2 6.9 %collective-permute-done.32 = bf16[208,768]{1,0:T(8,128)(2,1)S(1)} collective-permute-done((bf16[208,768]{1,0:T(8,128)(2,1)S(1)}, bf16[208,768]{1,0:T(8,128)(2,1)S(1)}, u32[]{:S(2)}, u32[]{:S(2)}) %collective-permute-start.32) | collective-permute-done | bytes 319520 | tf_op jit(solution)/shard_map/ppermute | solution.py:180
  156.8 4.6 %collective-permute-start.38 = (bf16[96,768]{1,0:T(8,128)(2,1)S(1)}, bf16[96,768]{1,0:T(8,128)(2,1)S(1)}, u32[]{:S(2)}, u32[]{:S(2)}) collective-permute-start(bf16[96,768]{1,0:T(8,128)(2,1)S(1)} %copy-done.31), channel_id=1, source_target_pairs={{1,4},{3,6},{4,1},{6,3},{9,12},{11,14},{12,9},{14,11},{17,20},{19,... | collective-permute-start | bytes 442376 | tf_op jit(solution)/shard_map/ppermute | solution.py:185
  161.4 7.2 %collective-permute-done.29 = bf16[576,768]{1,0:T(8,128)(2,1)S(1)} collective-permute-done((bf16[576,768]{1,0:T(8,128)(2,1)S(1)}, bf16[576,768]{1,0:T(8,128)(2,1)S(1)}, u32[]{:S(2)}, u32[]{:S(2)}) %collective-permute-start.29) | collective-permute-done | bytes 884768 | tf_op jit(solution)/shard_map/ppermute | solution.py:164
  168.6 6.8 %collective-permute-done.30 = bf16[576,768]{1,0:T(8,128)(2,1)S(1)} collective-permute-done((bf16[576,768]{1,0:T(8,128)(2,1)S(1)}, bf16[576,768]{1,0:T(8,128)(2,1)S(1)}, u32[]{:S(2)}, u32[]{:S(2)}) %collective-permute-start.30) | collective-permute-done | bytes 884768 | tf_op jit(solution)/shard_map/ppermute | solution.py:168
  177.2 3.4 %collective-permute-start.46 = (bf16[1536,768]{1,0:T(8,128)(2,1)S(1)}, bf16[1536,768]{1,0:T(8,128)(2,1)}, u32[]{:S(2)}, u32[]{:S(2)}) collective-permute-start(bf16[1536,768]{1,0:T(8,128)(2,1)S(1)} %pad_maximum_fusion.refs_8_), channel_id=1, source_target_pairs={{0,1},{1,0},{2,3},{3,2},{4,5},{5,4},{6,7},{7,6},{8,9},{9,8},{10,11... | collective-permute-start | bytes 7077896 | tf_op jit(solution)/shard_map/ppermute | solution.py:172
  183.1 4.5 %collective-permute-done.34 = bf16[384,768]{1,0:T(8,128)(2,1)S(1)} collective-permute-done((bf16[384,768]{1,0:T(8,128)(2,1)S(1)}, bf16[384,768]{1,0:T(8,128)(2,1)S(1)}, u32[]{:S(2)}, u32[]{:S(2)}) %collective-permute-start.34) | collective-permute-done | bytes 589856 | tf_op jit(solution)/shard_map/ppermute | solution.py:164
  188.2 4.0 %collective-permute-start.39 = (bf16[832,768]{1,0:T(8,128)(2,1)S(1)}, bf16[832,768]{1,0:T(8,128)(2,1)S(1)}, u32[]{:S(2)}, u32[]{:S(2)}) collective-permute-start(bf16[832,768]{1,0:T(8,128)(2,1)S(1)} %pad_maximum_fusion.2.core_ref), channel_id=1, source_target_pairs={{0,1},{1,0},{2,3},{3,2},{4,5},{5,4},{6,7},{7,6},{8,9},{9,8},{10,11... | collective-permute-start | bytes 3833864 | tf_op jit(solution)/shard_map/ppermute | solution.py:172
  197.1 8.7 %shard_map.126 = (f32[96,768]{1,0:T(8,128)}, f32[8,128]{1,0:T(8,128)}, bf16[96,768]{1,0:T(8,128)(2,1)}, bf16[96,768]{1,0:T(8,128)(2,1)}, bf16[96,768]{1,0:T(8,128)(2,1)}, /*index=5*/bf16[96,768]{1,0:T(8,128)(2,1)}) custom-call(s32[12]{0:T(128)} %stack.63.place_ref, bf16[832,768]{1,0:T(8,128)(2,1)} %copy-done.1, bf16[832,768]{1,0:T(8,128)(2,1)} %copy-done.13, ...), custom_call_target="tpu_custom_call" | custom-call | flops 1472200704 | bytes 7077888 | tf_op jit(solution)/shard_map/pallas_call | solution.py:391
  215.6 4.3 %collective-permute-start.40 = (bf16[96,768]{1,0:T(8,128)(2,1)}, bf16[96,768]{1,0:T(8,128)(2,1)S(1)}, u32[]{:S(2)}, u32[]{:S(2)}) collective-permute-start(bf16[96,768]{1,0:T(8,128)(2,1)} %get-tuple-element.125), channel_id=1, source_target_pairs={{0,0},{1,4},{2,2},{3,6},{4,1},{5,5},{6,3},{7,7},{8,8},{9,12},{10,1... | collective-permute-start | bytes 442376 | tf_op jit(solution)/shard_map/ppermute | solution.py:202
  220.0 45.9 %shard_map.127 = (f32[192,768]{1,0:T(8,128)}, f32[192,768]{1,0:T(8,128)}) custom-call(s32[2]{0:T(128)} %pad_add_fusion.place_ref, f32[8,128]{1,0:T(8,128)} %get-tuple-element.140.refs_0_, f32[8,128]{1,0:T(8,128)} %copy-done.37, f32[8,128]{1,0:T(8,128)} %copy-done.38, f32[8,128]{1,0:T(8,128)} %copy-done.39, bf16[1152,768]{1,0:T(8,128)(2,1)} %copy-done.28, ...), custom_call_target="tpu_custom_call" | custom-call | flops 27179089920 | bytes 18874368 | tf_op jit(solution)/shard_map/pallas_call | solution.py:325
  (292 shorter events, 103.3 us)
Async XLA Ops:
  13.0 21.4 %collective-permute-start.5 = (bf16[384,768]{1,0:T(8,128)(2,1)}, bf16[384,768]{1,0:T(8,128)(2,1)S(1)}, u32[]{:S(2)}, u32[]{:S(2)}) collective-permute-start(bf16[384,768]{1,0:T(8,128)(2,1)} %convert_element_type.65), channel_id=1, source_target_pairs={{0,2},{1,3},{2,0},{3,1},{4,6},{5,7},{6,4},{7,5},{8,10},{9,11},{10,... | collective-permute-start | bytes 1769480 | tf_op jit(solution)/shard_map/ppermute | solution.py:168
  14.3 20.2 %collective-permute-start.6 = (bf16[384,768]{1,0:T(8,128)(2,1)}, bf16[384,768]{1,0:T(8,128)(2,1)}, u32[]{:S(2)}, u32[]{:S(2)}) collective-permute-start(bf16[384,768]{1,0:T(8,128)(2,1)} %convert_element_type.65), channel_id=1, source_target_pairs={{0,4},{1,5},{2,6},{3,7},{4,0},{5,1},{6,2},{7,3},{8,12},{9,13},{10,... | collective-permute-start | bytes 1769480 | tf_op jit(solution)/shard_map/ppermute | solution.py:164
  18.4 22.3 %collective-permute-start.3 = (bf16[528,768]{1,0:T(8,128)(2,1)S(1)}, bf16[528,768]{1,0:T(8,128)(2,1)S(1)}, u32[]{:S(2)}, u32[]{:S(2)}) collective-permute-start(bf16[528,768]{1,0:T(8,128)(2,1)S(1)} %get-tuple-element.166), channel_id=1, source_target_pairs={{8,16},{9,17},{10,18},{11,19},{12,20},{13,21},{14,22},{15,23},{16,... | collective-permute-start | bytes 2433032 | tf_op jit(solution)/shard_map/ppermute | solution.py:180
  22.2 19.8 %collective-permute-start.4 = (bf16[528,768]{1,0:T(8,128)(2,1)S(1)}, bf16[528,768]{1,0:T(8,128)(2,1)S(1)}, u32[]{:S(2)}, u32[]{:S(2)}) collective-permute-start(bf16[528,768]{1,0:T(8,128)(2,1)S(1)} %get-tuple-element.165), channel_id=1, source_target_pairs={{0,8},{1,9},{2,10},{3,11},{4,12},{5,13},{6,14},{7,15},{8,0},{9,1},... | collective-permute-start | bytes 2433032 | tf_op jit(solution)/shard_map/ppermute | solution.py:176
  43.1 18.9 %collective-permute-start.10 = (bf16[528,768]{1,0:T(8,128)(2,1)S(1)}, bf16[528,768]{1,0:T(8,128)(2,1)S(1)}, u32[]{:S(2)}, u32[]{:S(2)}) collective-permute-start(bf16[528,768]{1,0:T(8,128)(2,1)S(1)} %collective-permute-done.3), channel_id=1, source_target_pairs={{0,8},{1,9},{2,10},{3,11},{4,12},{5,13},{6,14},{7,15},{8,0},{9,1},... | collective-permute-start | bytes 2433032 | tf_op jit(solution)/shard_map/ppermute | solution.py:176
  43.6 17.4 %collective-permute-start.8 = (bf16[480,768]{1,0:T(8,128)(2,1)S(1)}, bf16[480,768]{1,0:T(8,128)(2,1)S(1)}, u32[]{:S(2)}, u32[]{:S(2)}) collective-permute-start(bf16[480,768]{1,0:T(8,128)(2,1)S(1)} %get-tuple-element.170), channel_id=1, source_target_pairs={{0,4},{1,5},{2,6},{3,7},{4,0},{5,1},{6,2},{7,3},{8,12},{9,13},{10,... | collective-permute-start | bytes 2211848 | tf_op jit(solution)/shard_map/ppermute | solution.py:164
  43.6 17.4 %collective-permute-start.9 = (bf16[480,768]{1,0:T(8,128)(2,1)S(1)}, bf16[480,768]{1,0:T(8,128)(2,1)S(1)}, u32[]{:S(2)}, u32[]{:S(2)}) collective-permute-start(bf16[480,768]{1,0:T(8,128)(2,1)S(1)} %get-tuple-element.169), channel_id=1, source_target_pairs={{0,2},{1,3},{2,0},{3,1},{4,6},{5,7},{6,4},{7,5},{8,10},{9,11},{10,... | collective-permute-start | bytes 2211848 | tf_op jit(solution)/shard_map/ppermute | solution.py:168
  45.0 15.7 %collective-permute-start.11 = (bf16[384,768]{1,0:T(8,128)(2,1)S(1)}, bf16[384,768]{1,0:T(8,128)(2,1)S(1)}, u32[]{:S(2)}, u32[]{:S(2)}) collective-permute-start(bf16[384,768]{1,0:T(8,128)(2,1)S(1)} %slice.181), channel_id=1, source_target_pairs={{8,16},{9,17},{10,18},{11,19},{12,20},{13,21},{14,22},{15,23},{16,... | collective-permute-start | bytes 1769480 | tf_op jit(solution)/shard_map/ppermute | solution.py:180
  117.1 19.0 %collective-permute-start.25 = (bf16[576,768]{1,0:T(8,128)(2,1)S(1)}, bf16[576,768]{1,0:T(8,128)(2,1)S(1)}, u32[]{:S(2)}, u32[]{:S(2)}) collective-permute-start(bf16[576,768]{1,0:T(8,128)(2,1)S(1)} %get-tuple-element.164), channel_id=1, source_target_pairs={{0,4},{1,5},{2,6},{3,7},{4,0},{5,1},{6,2},{7,3},{8,12},{9,13},{10,... | collective-permute-start | bytes 2654216 | tf_op jit(solution)/shard_map/ppermute | solution.py:164
  117.9 18.6 %collective-permute-start.26 = (bf16[576,768]{1,0:T(8,128)(2,1)S(1)}, bf16[576,768]{1,0:T(8,128)(2,1)S(1)}, u32[]{:S(2)}, u32[]{:S(2)}) collective-permute-start(bf16[576,768]{1,0:T(8,128)(2,1)S(1)} %get-tuple-element.163), channel_id=1, source_target_pairs={{0,2},{1,3},{2,0},{3,1},{4,6},{5,7},{6,4},{7,5},{8,10},{9,11},{10,... | collective-permute-start | bytes 2654216 | tf_op jit(solution)/shard_map/ppermute | solution.py:168
  119.9 19.1 %collective-permute-start.27 = (bf16[592,768]{1,0:T(8,128)(2,1)S(1)}, bf16[592,768]{1,0:T(8,128)(2,1)S(1)}, u32[]{:S(2)}, u32[]{:S(2)}) collective-permute-start(bf16[592,768]{1,0:T(8,128)(2,1)S(1)} %get-tuple-element.109), channel_id=1, source_target_pairs={{0,8},{1,9},{2,10},{3,11},{4,12},{5,13},{6,14},{7,15},{8,0},{9,1},... | collective-permute-start | bytes 2727944 | tf_op jit(solution)/shard_map/ppermute | solution.py:176
  119.9 20.9 %collective-permute-start.28 = (bf16[592,768]{1,0:T(8,128)(2,1)S(1)}, bf16[592,768]{1,0:T(8,128)(2,1)S(1)}, u32[]{:S(2)}, u32[]{:S(2)}) collective-permute-start(bf16[592,768]{1,0:T(8,128)(2,1)S(1)} %get-tuple-element.110), channel_id=1, source_target_pairs={{8,16},{9,17},{10,18},{11,19},{12,20},{13,21},{14,22},{15,23},{16,... | collective-permute-start | bytes 2727944 | tf_op jit(solution)/shard_map/ppermute | solution.py:180
  128.5 28.3 %collective-permute-start.33 = (bf16[1152,768]{1,0:T(8,128)(2,1)S(1)}, bf16[1152,768]{1,0:T(8,128)(2,1)S(1)}, u32[]{:S(2)}, u32[]{:S(2)}) collective-permute-start(bf16[1152,768]{1,0:T(8,128)(2,1)S(1)} %constant_dynamic-update-slice_fusion.refs_4_), channel_id=1, source_target_pairs={{0,1},{1,0},{2,3},{3,2},{4,5},{5,4},{6,7},{7,6},{8,9},{9,8},{10,11... | collective-permute-start | bytes 5308424 | tf_op jit(solution)/shard_map/ppermute | solution.py:172
  141.1 47.0 %collective-permute-start.37 = (bf16[1536,768]{1,0:T(8,128)(2,1)S(1)}, bf16[1536,768]{1,0:T(8,128)(2,1)S(1)}, u32[]{:S(2)}, u32[]{:S(2)}) collective-permute-start(bf16[1536,768]{1,0:T(8,128)(2,1)S(1)} %constant_dynamic-update-slice_fusion.3.refs_6_), channel_id=1, source_target_pairs={{0,1},{1,0},{2,3},{3,2},{4,5},{5,4},{6,7},{7,6},{8,9},{9,8},{10,11... | collective-permute-start | bytes 7077896 | tf_op jit(solution)/shard_map/ppermute | solution.py:172
  148.5 26.9 %collective-permute-start.31 = (bf16[592,768]{1,0:T(8,128)(2,1)S(1)}, bf16[592,768]{1,0:T(8,128)(2,1)S(1)}, u32[]{:S(2)}, u32[]{:S(2)}) collective-permute-start(bf16[592,768]{1,0:T(8,128)(2,1)S(1)} %collective-permute-done.28), channel_id=1, source_target_pairs={{0,8},{1,9},{2,10},{3,11},{4,12},{5,13},{6,14},{7,15},{8,0},{9,1},... | collective-permute-start | bytes 2727944 | tf_op jit(solution)/shard_map/ppermute | solution.py:176
  148.6 20.0 %collective-permute-start.29 = (bf16[576,768]{1,0:T(8,128)(2,1)S(1)}, bf16[576,768]{1,0:T(8,128)(2,1)S(1)}, u32[]{:S(2)}, u32[]{:S(2)}) collective-permute-start(bf16[576,768]{1,0:T(8,128)(2,1)S(1)} %get-tuple-element.116), channel_id=1, source_target_pairs={{0,4},{1,5},{2,6},{3,7},{4,0},{5,1},{6,2},{7,3},{8,12},{9,13},{10,... | collective-permute-start | bytes 2654216 | tf_op jit(solution)/shard_map/ppermute | solution.py:164
  156.1 19.3 %collective-permute-start.30 = (bf16[576,768]{1,0:T(8,128)(2,1)S(1)}, bf16[576,768]{1,0:T(8,128)(2,1)S(1)}, u32[]{:S(2)}, u32[]{:S(2)}) collective-permute-start(bf16[576,768]{1,0:T(8,128)(2,1)S(1)} %get-tuple-element.117), channel_id=1, source_target_pairs={{0,2},{1,3},{2,0},{3,1},{4,6},{5,7},{6,4},{7,5},{8,10},{9,11},{10,... | collective-permute-start | bytes 2654216 | tf_op jit(solution)/shard_map/ppermute | solution.py:168
  156.8 20.4 %collective-permute-start.38 = (bf16[96,768]{1,0:T(8,128)(2,1)S(1)}, bf16[96,768]{1,0:T(8,128)(2,1)S(1)}, u32[]{:S(2)}, u32[]{:S(2)}) collective-permute-start(bf16[96,768]{1,0:T(8,128)(2,1)S(1)} %copy-done.31), channel_id=1, source_target_pairs={{1,4},{3,6},{4,1},{6,3},{9,12},{11,14},{12,9},{14,11},{17,20},{19,... | collective-permute-start | bytes 442376 | tf_op jit(solution)/shard_map/ppermute | solution.py:185
  177.2 29.6 %collective-permute-start.46 = (bf16[1536,768]{1,0:T(8,128)(2,1)S(1)}, bf16[1536,768]{1,0:T(8,128)(2,1)}, u32[]{:S(2)}, u32[]{:S(2)}) collective-permute-start(bf16[1536,768]{1,0:T(8,128)(2,1)S(1)} %pad_maximum_fusion.refs_8_), channel_id=1, source_target_pairs={{0,1},{1,0},{2,3},{3,2},{4,5},{5,4},{6,7},{7,6},{8,9},{9,8},{10,11... | collective-permute-start | bytes 7077896 | tf_op jit(solution)/shard_map/ppermute | solution.py:172
  195.4 24.5 %collective-permute-start.50 = (bf16[1152,768]{1,0:T(8,128)(2,1)}, bf16[1152,768]{1,0:T(8,128)(2,1)}, u32[]{:S(2)}, u32[]{:S(2)}) collective-permute-start(bf16[1152,768]{1,0:T(8,128)(2,1)} %pad_maximum_fusion.1.refs_10_), channel_id=1, source_target_pairs={{0,1},{1,0},{2,3},{3,2},{4,5},{5,4},{6,7},{7,6},{8,9},{9,8},{10,11... | collective-permute-start | bytes 5308424 | tf_op jit(solution)/shard_map/ppermute | solution.py:172
  211.9 55.0 %collective-permute-start.43 = (bf16[96,768]{1,0:T(8,128)(2,1)}, bf16[96,768]{1,0:T(8,128)(2,1)S(1)}, u32[]{:S(2)}, u32[]{:S(2)}) collective-permute-start(bf16[96,768]{1,0:T(8,128)(2,1)} %get-tuple-element.128), channel_id=1, source_target_pairs={{0,3},{1,7},{2,1},{3,5},{4,2},{5,6},{6,0},{7,4},{8,11},{9,15},{10,... | collective-permute-start | bytes 442376 | tf_op jit(solution)/shard_map/ppermute | solution.py:202
  213.1 53.8 %collective-permute-start.42 = (bf16[96,768]{1,0:T(8,128)(2,1)}, bf16[96,768]{1,0:T(8,128)(2,1)S(1)}, u32[]{:S(2)}, u32[]{:S(2)}) collective-permute-start(bf16[96,768]{1,0:T(8,128)(2,1)} %get-tuple-element.127), channel_id=1, source_target_pairs={{0,2},{1,6},{2,0},{3,4},{4,3},{5,7},{6,1},{7,5},{8,10},{9,14},{10,... | collective-permute-start | bytes 442376 | tf_op jit(solution)/shard_map/ppermute | solution.py:202
  215.5 51.4 %collective-permute-start.41 = (bf16[96,768]{1,0:T(8,128)(2,1)}, bf16[96,768]{1,0:T(8,128)(2,1)S(1)}, u32[]{:S(2)}, u32[]{:S(2)}) collective-permute-start(bf16[96,768]{1,0:T(8,128)(2,1)} %get-tuple-element.126), channel_id=1, source_target_pairs={{0,1},{1,5},{2,3},{3,7},{4,0},{5,4},{6,2},{7,6},{8,9},{9,13},{10,1... | collective-permute-start | bytes 442376 | tf_op jit(solution)/shard_map/ppermute | solution.py:202
  215.6 51.4 %collective-permute-start.40 = (bf16[96,768]{1,0:T(8,128)(2,1)}, bf16[96,768]{1,0:T(8,128)(2,1)S(1)}, u32[]{:S(2)}, u32[]{:S(2)}) collective-permute-start(bf16[96,768]{1,0:T(8,128)(2,1)} %get-tuple-element.125), channel_id=1, source_target_pairs={{0,0},{1,4},{2,2},{3,6},{4,1},{5,5},{6,3},{7,7},{8,8},{9,12},{10,1... | collective-permute-start | bytes 442376 | tf_op jit(solution)/shard_map/ppermute | solution.py:202
  (76 other events, 696.1 us)

commit v8 on v7

--- a/solution.py
+++ b/solution.py
@@ -189,11 +189,6 @@
     return lax.optimization_barrier(parts)
 
 
-def exchange(*pairs_of):
-    blocks = lax.optimization_barrier(tuple(block for _, block in pairs_of))
-    return [send(block) for (send, _), block in zip(pairs_of, blocks)]
-
-
 def swap_diagonal(a):
     return lax.ppermute(a, AXES, pairs(lambda z, x, y, c: (z, 1 - x, 1 - y, c)))
 
@@ -584,10 +579,10 @@
     to_x = jnp.concatenate([power_y[half:], near])
     to_y = jnp.concatenate([power_x[:half], near])
     (
+        got_o,
+        got_i,
         got_x,
         got_y,
-        got_o,
-        got_i,
         new_stat_right,
         new_stat_left,
         power_left,
@@ -595,10 +590,10 @@
         side_places,
         places,
     ) = stage(
+        swap_outer(jnp.concatenate([power_i1, extra])),
+        swap_inner(jnp.concatenate([near, extra])),
         swap_x(to_x),
         swap_y(to_y),
-        swap_outer(after(jnp.concatenate([power_i1, extra]), to_x, to_y)),
-        swap_inner(after(jnp.concatenate([near, extra]), to_x, to_y)),
         new_stat_right,
         new_stat_left,
         power_left,
@@ -615,12 +610,10 @@
     to_x = jnp.concatenate([near_y[half:], mid])
     to_y = jnp.concatenate([near_x[:half], mid])
     got_x, got_y, got_o, extra_i2, other0 = stage(
-        *exchange(
-            (swap_x, to_x),
-            (swap_y, to_y),
-            (swap_outer, jnp.concatenate([power_i2, extra_i1])),
-            (swap_inner, extra_o1),
-        ),
+        swap_x(to_x),
+        swap_y(to_y),
+        swap_outer(jnp.concatenate([power_i2, extra_i1])),
+        swap_inner(extra_o1),
         swap_core(stack0),
     )
     stack2 = jnp.concatenate([mid, got_x, got_y])

time: 270 us -> 265 us (0.981)
  waiting for transfers between devices: 84.1 us -> 75.2 us
  local copies, waits for them, and re-layouts: 12.7 us -> 15.5 us
    ppermute x10, waiting for transfers between devices: 21.6 us -> 31.5 us  [swap_x(): return lax.ppermute(a, AXES, pairs(lambda z, x, y, c: (z, 1 - x, y, c)))]
    ppermute x6, waiting for transfers between devices: 28.8 us -> 19.4 us  [swap_inner(): lax.ppermute(a, AXES, pairs(lambda z, x, y, c: (3 - z if 0 < z < 3 else -...]
    ppermute x10, waiting for transfers between devices: 9.05 us -> 1.37 us  [swap_y(): return lax.ppermute(a, AXES, pairs(lambda z, x, y, c: (z, x, 1 - y, c)))]
    ppermute x8, waiting for transfers between devices: 12.2 us -> 9.02 us  [swap_outer(): lax.ppermute(a, AXES, pairs(lambda z, x, y, c: (z + 1 - 2 * (z % 2), x, y...]
  transfers between devices with their start and end apart: 53 -> 53, of which waited for: 29 -> 23; matrix products, arithmetic and copies ran while one was open for 14% -> 15% of each run, Pallas kernels for 20% -> 21%
where the time goes in v8:
time: 265 us; the launch traced here: 264 us
  starting transfers between devices  83.2 us (31%)
  waiting for transfers between devices  75.2 us (28%)
  Pallas kernels  54.6 us (21%)
  other arithmetic  20.5 us (8%)
  local copies, waits for them, and re-layouts  15.5 us (6%)
  matrix products  13.2 us (5%)
    pallas_call x1, Pallas kernels, refresh(): pl.pallas_call(refresh_kernel, out_shape=[jax.ShapeDtypeStruct((count, ta...  45.9 us
    ppermute x10, waiting for transfers between devices, swap_x(): return lax.ppermute(a, AXES, pairs(lambda z, x, y, c: (z, 1 - x, y, c)))  31.5 us
    ppermute x11, starting transfers between devices, swap_core(): return lax.ppermute(a, AXES, pairs(lambda z, x, y, c: (z, x, y, 1 - c)))  25.5 us
    ppermute x6, waiting for transfers between devices, swap_inner(): lax.ppermute(a, AXES, pairs(lambda z, x, y, c: (3 - z if 0 < z < 3 else -...  19.4 us
    ppermute x6, starting transfers between devices, swap_inner(): lax.ppermute(a, AXES, pairs(lambda z, x, y, c: (3 - z if 0 < z < 3 else -...  17.5 us
    ppermute x3, starting transfers between devices, turn_over(): return jnp.where(straight, a, lax.ppermute(a, AXES, crossed))  12.3 us
    ppermute x3, waiting for transfers between devices, turn_over(): return jnp.where(straight, a, lax.ppermute(a, AXES, crossed))  9.93 us
    ppermute x10, starting transfers between devices, swap_y(): return lax.ppermute(a, AXES, pairs(lambda z, x, y, c: (z, x, 1 - y, c)))  9.92 us
  transfers between devices with their start and end apart: 53, of which 23 were waited for; matrix products, arithmetic and copies ran while one was open for 15% of the time, Pallas kernels for 21%

profile of v8, /device:TPU:9, one launch (start us, length us, event | category | flops | bytes accessed | tf_op | source)
XLA Modules:
  0.0 264.2 jit_solution(13391498023002510338)
XLA Ops:
  3.0 3.8 %collective-permute-start = (bf16[384,768]{1,0:T(8,128)(2,1)}, bf16[384,768]{1,0:T(8,128)(2,1)}, u32[]{:S(2)}, u32[]{:S(2)}) collective-permute-start(bf16[384,768]{1,0:T(8,128)(2,1)} %multiply_convert_fusion), channel_id=1, source_target_pairs={{1,4},{3,6},{4,1},{6,3},{9,12},{11,14},{12,9},{14,11},{17,20},{19,... | collective-permute-start | bytes 1769480 | tf_op jit(solution)/shard_map/ppermute | solution.py:185
  7.8 4.3 %collective-permute-start.2 = (bf16[144,768]{1,0:T(8,128)(2,1)}, bf16[144,768]{1,0:T(8,128)(2,1)}, u32[]{:S(2)}, u32[]{:S(2)}) collective-permute-start(bf16[144,768]{1,0:T(8,128)(2,1)} %get-tuple-element.165), channel_id=1, source_target_pairs={{8,16},{9,17},{10,18},{11,19},{12,20},{13,21},{14,22},{15,23},{16,... | collective-permute-start | bytes 663560 | tf_op jit(solution)/shard_map/ppermute | solution.py:180
  18.4 3.8 %collective-permute-start.3 = (bf16[528,768]{1,0:T(8,128)(2,1)S(1)}, bf16[528,768]{1,0:T(8,128)(2,1)S(1)}, u32[]{:S(2)}, u32[]{:S(2)}) collective-permute-start(bf16[528,768]{1,0:T(8,128)(2,1)S(1)} %get-tuple-element.154), channel_id=1, source_target_pairs={{8,16},{9,17},{10,18},{11,19},{12,20},{13,21},{14,22},{15,23},{16,... | collective-permute-start | bytes 2433032 | tf_op jit(solution)/shard_map/ppermute | solution.py:180
  25.3 9.0 %collective-permute-done.7 = bf16[288,768]{1,0:T(8,128)(2,1)S(1)} collective-permute-done((bf16[288,768]{1,0:T(8,128)(2,1)S(1)}, bf16[288,768]{1,0:T(8,128)(2,1)S(1)}, u32[]{:S(2)}, u32[]{:S(2)}) %collective-permute-start.7) | collective-permute-done | bytes 442400 | tf_op jit(solution)/shard_map/ppermute | solution.py:185
  34.5 6.2 %collective-permute-done.3 = bf16[528,768]{1,0:T(8,128)(2,1)S(1)} collective-permute-done((bf16[528,768]{1,0:T(8,128)(2,1)S(1)}, bf16[528,768]{1,0:T(8,128)(2,1)S(1)}, u32[]{:S(2)}, u32[]{:S(2)}) %collective-permute-start.3) | collective-permute-done | bytes 811040 | tf_op jit(solution)/shard_map/ppermute | solution.py:180
  49.6 11.1 %collective-permute-done.11 = bf16[384,768]{1,0:T(8,128)(2,1)S(1)} collective-permute-done((bf16[384,768]{1,0:T(8,128)(2,1)S(1)}, bf16[384,768]{1,0:T(8,128)(2,1)S(1)}, u32[]{:S(2)}, u32[]{:S(2)}) %collective-permute-start.11) | collective-permute-done | bytes 589856 | tf_op jit(solution)/shard_map/ppermute | solution.py:180
  66.6 3.1 %collective-permute-start.15 = (bf16[768,768]{1,0:T(8,128)(2,1)S(1)}, bf16[768,768]{1,0:T(8,128)(2,1)S(1)}, u32[]{:S(2)}, u32[]{:S(2)}) collective-permute-start(bf16[768,768]{1,0:T(8,128)(2,1)S(1)} %pad_maximum_fusion.3), channel_id=1, source_target_pairs={{0,1},{1,0},{2,3},{3,2},{4,5},{5,4},{6,7},{7,6},{8,9},{9,8},{10,11... | collective-permute-start | bytes 3538952 | tf_op jit(solution)/shard_map/ppermute | solution.py:172
  70.1 5.3 %collective-permute-done.12 = bf16[384,768]{1,0:T(8,128)(2,1)S(1)} collective-permute-done((bf16[384,768]{1,0:T(8,128)(2,1)S(1)}, bf16[384,768]{1,0:T(8,128)(2,1)S(1)}, u32[]{:S(2)}, u32[]{:S(2)}) %collective-permute-start.12) | collective-permute-done | bytes 589856 | tf_op jit(solution)/shard_map/ppermute | solution.py:176
  75.4 2.9 %collective-permute-done.13 = bf16[432,768]{1,0:T(8,128)(2,1)S(1)} collective-permute-done((bf16[432,768]{1,0:T(8,128)(2,1)S(1)}, bf16[432,768]{1,0:T(8,128)(2,1)S(1)}, u32[]{:S(2)}, u32[]{:S(2)}) %collective-permute-start.13) | collective-permute-done | bytes 663584 | tf_op jit(solution)/shard_map/ppermute | solution.py:164
  81.1 4.0 %collective-permute-start.18 = (bf16[4,384,768]{2,1,0:T(8,128)(2,1)S(1)}, bf16[4,384,768]{2,1,0:T(8,128)(2,1)S(1)}, u32[]{:S(2)}, u32[]{:S(2)}) collective-permute-start(bf16[4,384,768]{2,1,0:T(8,128)(2,1)S(1)} %bitcast_dynamic-update-slice_fusion.2), channel_id=1, source_target_pairs={{0,1},{1,0},{2,3},{3,2},{4,5},{5,4},{6,7},{7,6},{8,9},{9,8},{10,11... | collective-permute-start | bytes 7077896 | tf_op jit(solution)/shard_map/ppermute | solution.py:172
  86.3 3.0 %collective-permute-done.18 = bf16[4,384,768]{2,1,0:T(8,128)(2,1)S(1)} collective-permute-done((bf16[4,384,768]{2,1,0:T(8,128)(2,1)S(1)}, bf16[4,384,768]{2,1,0:T(8,128)(2,1)S(1)}, u32[]{:S(2)}, u32[]{:S(2)}) %collective-permute-start.18) | collective-permute-done | bytes 2359328 | tf_op jit(solution)/shard_map/ppermute | solution.py:172
  110.1 3.3 %fusion = f32[384,768]{1,0:T(8,128)} fusion(bf16[768,1536]{1,0:T(8,128)(2,1)} %bitcast.146, s32[]{:T(128)S(6)} %select_n.371, f32[384,768]{1,0:T(8,128)S(1)} %copy-done.3, bf16[768,1536]{1,0:T(8,128)(2,1)} %copy-done.6, s32[]{:T(128)S(6)} %select_n.383, pred[]{:T(512)S(6)} %eq.36), kind=kOutput, calls=%fused_computation.7 | convolution fusion | flops 454164480 | bytes 4718601 | tf_op jit(solution)/shard_map/dot_general | solution.py:145
  125.0 3.0 %collective-permute-start.33 = (bf16[1152,768]{1,0:T(8,128)(2,1)S(1)}, bf16[1152,768]{1,0:T(8,128)(2,1)S(1)}, u32[]{:S(2)}, u32[]{:S(2)}) collective-permute-start(bf16[1152,768]{1,0:T(8,128)(2,1)S(1)} %constant_dynamic-update-slice_fusion.refs_4_), channel_id=1, source_target_pairs={{0,1},{1,0},{2,3},{3,2},{4,5},{5,4},{6,7},{7,6},{8,9},{9,8},{10,11... | collective-permute-start | bytes 5308424 | tf_op jit(solution)/shard_map/ppermute | solution.py:172
  129.1 10.3 %collective-permute-done.27 = bf16[576,768]{1,0:T(8,128)(2,1)S(1)} collective-permute-done((bf16[576,768]{1,0:T(8,128)(2,1)S(1)}, bf16[576,768]{1,0:T(8,128)(2,1)S(1)}, u32[]{:S(2)}, u32[]{:S(2)}) %collective-permute-start.27) | collective-permute-done | bytes 884768 | tf_op jit(solution)/shard_map/ppermute | solution.py:164
  140.2 2.8 %collective-permute-start.32 = (bf16[208,768]{1,0:T(8,128)(2,1)S(1)}, bf16[208,768]{1,0:T(8,128)(2,1)S(1)}, u32[]{:S(2)}, u32[]{:S(2)}) collective-permute-start(bf16[208,768]{1,0:T(8,128)(2,1)S(1)} %slice.222), channel_id=1, source_target_pairs={{8,16},{9,17},{10,18},{11,19},{12,20},{13,21},{14,22},{15,23},{16,... | collective-permute-start | bytes 958472 | tf_op jit(solution)/shard_map/ppermute | solution.py:180
  143.2 4.1 %collective-permute-start.37 = (bf16[1536,768]{1,0:T(8,128)(2,1)S(1)}, bf16[1536,768]{1,0:T(8,128)(2,1)S(1)}, u32[]{:S(2)}, u32[]{:S(2)}) collective-permute-start(bf16[1536,768]{1,0:T(8,128)(2,1)S(1)} %constant_dynamic-update-slice_fusion.3.refs_6_), channel_id=1, source_target_pairs={{0,1},{1,0},{2,3},{3,2},{4,5},{5,4},{6,7},{7,6},{8,9},{9,8},{10,11... | collective-permute-start | bytes 7077896 | tf_op jit(solution)/shard_map/ppermute | solution.py:172
  150.2 6.2 %collective-permute-start.38 = (bf16[96,768]{1,0:T(8,128)(2,1)S(1)}, bf16[96,768]{1,0:T(8,128)(2,1)S(1)}, u32[]{:S(2)}, u32[]{:S(2)}) collective-permute-start(bf16[96,768]{1,0:T(8,128)(2,1)S(1)} %copy-done.30), channel_id=1, source_target_pairs={{1,4},{3,6},{4,1},{6,3},{9,12},{11,14},{12,9},{14,11},{17,20},{19,... | collective-permute-start | bytes 442376 | tf_op jit(solution)/shard_map/ppermute | solution.py:185
  156.3 12.5 %collective-permute-done.29 = bf16[576,768]{1,0:T(8,128)(2,1)S(1)} collective-permute-done((bf16[576,768]{1,0:T(8,128)(2,1)S(1)}, bf16[576,768]{1,0:T(8,128)(2,1)S(1)}, u32[]{:S(2)}, u32[]{:S(2)}) %collective-permute-start.29) | collective-permute-done | bytes 884768 | tf_op jit(solution)/shard_map/ppermute | solution.py:164
  171.7 2.9 %collective-permute-start.46 = (bf16[1536,768]{1,0:T(8,128)(2,1)S(1)}, bf16[1536,768]{1,0:T(8,128)(2,1)}, u32[]{:S(2)}, u32[]{:S(2)}) collective-permute-start(bf16[1536,768]{1,0:T(8,128)(2,1)S(1)} %pad_maximum_fusion.refs_8_), channel_id=1, source_target_pairs={{0,1},{1,0},{2,3},{3,2},{4,5},{5,4},{6,7},{7,6},{8,9},{9,8},{10,11... | collective-permute-start | bytes 7077896 | tf_op jit(solution)/shard_map/ppermute | solution.py:172
  176.7 4.9 %collective-permute-done.34 = bf16[384,768]{1,0:T(8,128)(2,1)S(1)} collective-permute-done((bf16[384,768]{1,0:T(8,128)(2,1)S(1)}, bf16[384,768]{1,0:T(8,128)(2,1)S(1)}, u32[]{:S(2)}, u32[]{:S(2)}) %collective-permute-start.34) | collective-permute-done | bytes 589856 | tf_op jit(solution)/shard_map/ppermute | solution.py:164
  181.8 4.0 %collective-permute-start.39 = (bf16[832,768]{1,0:T(8,128)(2,1)S(1)}, bf16[832,768]{1,0:T(8,128)(2,1)S(1)}, u32[]{:S(2)}, u32[]{:S(2)}) collective-permute-start(bf16[832,768]{1,0:T(8,128)(2,1)S(1)} %pad_maximum_fusion.2.core_ref), channel_id=1, source_target_pairs={{0,1},{1,0},{2,3},{3,2},{4,5},{5,4},{6,7},{7,6},{8,9},{9,8},{10,11... | collective-permute-start | bytes 3833864 | tf_op jit(solution)/shard_map/ppermute | solution.py:172
  190.7 8.7 %shard_map.126 = (f32[96,768]{1,0:T(8,128)}, f32[8,128]{1,0:T(8,128)}, bf16[96,768]{1,0:T(8,128)(2,1)}, bf16[96,768]{1,0:T(8,128)(2,1)}, bf16[96,768]{1,0:T(8,128)(2,1)}, /*index=5*/bf16[96,768]{1,0:T(8,128)(2,1)}) custom-call(s32[12]{0:T(128)} %stack.63.place_ref, bf16[832,768]{1,0:T(8,128)(2,1)} %copy-done.1, bf16[832,768]{1,0:T(8,128)(2,1)} %copy-done.13, ...), custom_call_target="tpu_custom_call" | custom-call | flops 1472200704 | bytes 7077888 | tf_op jit(solution)/shard_map/pallas_call | solution.py:386
  210.6 4.3 %collective-permute-start.40 = (bf16[96,768]{1,0:T(8,128)(2,1)S(1)}, bf16[96,768]{1,0:T(8,128)(2,1)S(1)}, u32[]{:S(2)}, u32[]{:S(2)}) collective-permute-start(bf16[96,768]{1,0:T(8,128)(2,1)S(1)} %copy-done.34), channel_id=1, source_target_pairs={{0,0},{1,4},{2,2},{3,6},{4,1},{5,5},{6,3},{7,7},{8,8},{9,12},{10,1... | collective-permute-start | bytes 442376 | tf_op jit(solution)/shard_map/ppermute | solution.py:197
  214.9 45.9 %shard_map.127 = (f32[192,768]{1,0:T(8,128)}, f32[192,768]{1,0:T(8,128)}) custom-call(s32[2]{0:T(128)} %pad_add_fusion.place_ref, f32[8,128]{1,0:T(8,128)} %get-tuple-element.128.refs_0_, f32[8,128]{1,0:T(8,128)} %copy-done.36, f32[8,128]{1,0:T(8,128)} %copy-done.37, f32[8,128]{1,0:T(8,128)} %copy-done.38, bf16[1152,768]{1,0:T(8,128)(2,1)} %copy-done.27, ...), custom_call_target="tpu_custom_call" | custom-call | flops 27179089920 | bytes 18874368 | tf_op jit(solution)/shard_map/pallas_call | solution.py:320
  (290 shorter events, 92.9 us)
Async XLA Ops:
  13.0 21.4 %collective-permute-start.5 = (bf16[384,768]{1,0:T(8,128)(2,1)}, bf16[384,768]{1,0:T(8,128)(2,1)S(1)}, u32[]{:S(2)}, u32[]{:S(2)}) collective-permute-start(bf16[384,768]{1,0:T(8,128)(2,1)} %convert_element_type.65), channel_id=1, source_target_pairs={{0,2},{1,3},{2,0},{3,1},{4,6},{5,7},{6,4},{7,5},{8,10},{9,11},{10,... | collective-permute-start | bytes 1769480 | tf_op jit(solution)/shard_map/ppermute | solution.py:168
  14.3 20.2 %collective-permute-start.6 = (bf16[384,768]{1,0:T(8,128)(2,1)}, bf16[384,768]{1,0:T(8,128)(2,1)}, u32[]{:S(2)}, u32[]{:S(2)}) collective-permute-start(bf16[384,768]{1,0:T(8,128)(2,1)} %convert_element_type.65), channel_id=1, source_target_pairs={{0,4},{1,5},{2,6},{3,7},{4,0},{5,1},{6,2},{7,3},{8,12},{9,13},{10,... | collective-permute-start | bytes 1769480 | tf_op jit(solution)/shard_map/ppermute | solution.py:164
  18.4 22.3 %collective-permute-start.3 = (bf16[528,768]{1,0:T(8,128)(2,1)S(1)}, bf16[528,768]{1,0:T(8,128)(2,1)S(1)}, u32[]{:S(2)}, u32[]{:S(2)}) collective-permute-start(bf16[528,768]{1,0:T(8,128)(2,1)S(1)} %get-tuple-element.154), channel_id=1, source_target_pairs={{8,16},{9,17},{10,18},{11,19},{12,20},{13,21},{14,22},{15,23},{16,... | collective-permute-start | bytes 2433032 | tf_op jit(solution)/shard_map/ppermute | solution.py:180
  22.2 19.8 %collective-permute-start.4 = (bf16[528,768]{1,0:T(8,128)(2,1)S(1)}, bf16[528,768]{1,0:T(8,128)(2,1)S(1)}, u32[]{:S(2)}, u32[]{:S(2)}) collective-permute-start(bf16[528,768]{1,0:T(8,128)(2,1)S(1)} %get-tuple-element.153), channel_id=1, source_target_pairs={{0,8},{1,9},{2,10},{3,11},{4,12},{5,13},{6,14},{7,15},{8,0},{9,1},... | collective-permute-start | bytes 2433032 | tf_op jit(solution)/shard_map/ppermute | solution.py:176
  43.1 18.9 %collective-permute-start.10 = (bf16[528,768]{1,0:T(8,128)(2,1)S(1)}, bf16[528,768]{1,0:T(8,128)(2,1)S(1)}, u32[]{:S(2)}, u32[]{:S(2)}) collective-permute-start(bf16[528,768]{1,0:T(8,128)(2,1)S(1)} %collective-permute-done.3), channel_id=1, source_target_pairs={{0,8},{1,9},{2,10},{3,11},{4,12},{5,13},{6,14},{7,15},{8,0},{9,1},... | collective-permute-start | bytes 2433032 | tf_op jit(solution)/shard_map/ppermute | solution.py:176
  43.6 17.3 %collective-permute-start.8 = (bf16[480,768]{1,0:T(8,128)(2,1)S(1)}, bf16[480,768]{1,0:T(8,128)(2,1)S(1)}, u32[]{:S(2)}, u32[]{:S(2)}) collective-permute-start(bf16[480,768]{1,0:T(8,128)(2,1)S(1)} %get-tuple-element.158), channel_id=1, source_target_pairs={{0,4},{1,5},{2,6},{3,7},{4,0},{5,1},{6,2},{7,3},{8,12},{9,13},{10,... | collective-permute-start | bytes 2211848 | tf_op jit(solution)/shard_map/ppermute | solution.py:164
  43.6 17.3 %collective-permute-start.9 = (bf16[480,768]{1,0:T(8,128)(2,1)S(1)}, bf16[480,768]{1,0:T(8,128)(2,1)S(1)}, u32[]{:S(2)}, u32[]{:S(2)}) collective-permute-start(bf16[480,768]{1,0:T(8,128)(2,1)S(1)} %get-tuple-element.157), channel_id=1, source_target_pairs={{0,2},{1,3},{2,0},{3,1},{4,6},{5,7},{6,4},{7,5},{8,10},{9,11},{10,... | collective-permute-start | bytes 2211848 | tf_op jit(solution)/shard_map/ppermute | solution.py:168
  97.1 16.3 %collective-permute-start.21 = (bf16[384,768]{1,0:T(8,128)(2,1)S(1)}, bf16[384,768]{1,0:T(8,128)(2,1)}, u32[]{:S(2)}, u32[]{:S(2)}) collective-permute-start(bf16[384,768]{1,0:T(8,128)(2,1)S(1)} %fusion.2), channel_id=1, source_target_pairs={{0,4},{1,5},{2,6},{3,7},{4,0},{5,1},{6,2},{7,3},{8,12},{9,13},{10,... | collective-permute-start | bytes 1769480 | tf_op jit(solution)/shard_map/ppermute | solution.py:164
  116.1 23.9 %collective-permute-start.25 = (bf16[592,768]{1,0:T(8,128)(2,1)S(1)}, bf16[592,768]{1,0:T(8,128)(2,1)S(1)}, u32[]{:S(2)}, u32[]{:S(2)}) collective-permute-start(bf16[592,768]{1,0:T(8,128)(2,1)S(1)} %get-tuple-element.160), channel_id=1, source_target_pairs={{0,8},{1,9},{2,10},{3,11},{4,12},{5,13},{6,14},{7,15},{8,0},{9,1},... | collective-permute-start | bytes 2727944 | tf_op jit(solution)/shard_map/ppermute | solution.py:176
  116.2 23.9 %collective-permute-start.26 = (bf16[592,768]{1,0:T(8,128)(2,1)S(1)}, bf16[592,768]{1,0:T(8,128)(2,1)S(1)}, u32[]{:S(2)}, u32[]{:S(2)}) collective-permute-start(bf16[592,768]{1,0:T(8,128)(2,1)S(1)} %get-tuple-element.159), channel_id=1, source_target_pairs={{8,16},{9,17},{10,18},{11,19},{12,20},{13,21},{14,22},{15,23},{16,... | collective-permute-start | bytes 2727944 | tf_op jit(solution)/shard_map/ppermute | solution.py:180
  120.7 18.7 %collective-permute-start.27 = (bf16[576,768]{1,0:T(8,128)(2,1)S(1)}, bf16[576,768]{1,0:T(8,128)(2,1)S(1)}, u32[]{:S(2)}, u32[]{:S(2)}) collective-permute-start(bf16[576,768]{1,0:T(8,128)(2,1)S(1)} %get-tuple-element.152), channel_id=1, source_target_pairs={{0,4},{1,5},{2,6},{3,7},{4,0},{5,1},{6,2},{7,3},{8,12},{9,13},{10,... | collective-permute-start | bytes 2654216 | tf_op jit(solution)/shard_map/ppermute | solution.py:164
  121.7 18.3 %collective-permute-start.28 = (bf16[576,768]{1,0:T(8,128)(2,1)S(1)}, bf16[576,768]{1,0:T(8,128)(2,1)S(1)}, u32[]{:S(2)}, u32[]{:S(2)}) collective-permute-start(bf16[576,768]{1,0:T(8,128)(2,1)S(1)} %get-tuple-element.151), channel_id=1, source_target_pairs={{0,2},{1,3},{2,0},{3,1},{4,6},{5,7},{6,4},{7,5},{8,10},{9,11},{10,... | collective-permute-start | bytes 2654216 | tf_op jit(solution)/shard_map/ppermute | solution.py:168
  125.0 25.2 %collective-permute-start.33 = (bf16[1152,768]{1,0:T(8,128)(2,1)S(1)}, bf16[1152,768]{1,0:T(8,128)(2,1)S(1)}, u32[]{:S(2)}, u32[]{:S(2)}) collective-permute-start(bf16[1152,768]{1,0:T(8,128)(2,1)S(1)} %constant_dynamic-update-slice_fusion.refs_4_), channel_id=1, source_target_pairs={{0,1},{1,0},{2,3},{3,2},{4,5},{5,4},{6,7},{7,6},{8,9},{9,8},{10,11... | collective-permute-start | bytes 5308424 | tf_op jit(solution)/shard_map/ppermute | solution.py:172
  140.1 28.8 %collective-permute-start.31 = (bf16[592,768]{1,0:T(8,128)(2,1)S(1)}, bf16[592,768]{1,0:T(8,128)(2,1)S(1)}, u32[]{:S(2)}, u32[]{:S(2)}) collective-permute-start(bf16[592,768]{1,0:T(8,128)(2,1)S(1)} %collective-permute-done.26), channel_id=1, source_target_pairs={{0,8},{1,9},{2,10},{3,11},{4,12},{5,13},{6,14},{7,15},{8,0},{9,1},... | collective-permute-start | bytes 2727944 | tf_op jit(solution)/shard_map/ppermute | solution.py:176
  143.2 38.4 %collective-permute-start.37 = (bf16[1536,768]{1,0:T(8,128)(2,1)S(1)}, bf16[1536,768]{1,0:T(8,128)(2,1)S(1)}, u32[]{:S(2)}, u32[]{:S(2)}) collective-permute-start(bf16[1536,768]{1,0:T(8,128)(2,1)S(1)} %constant_dynamic-update-slice_fusion.3.refs_6_), channel_id=1, source_target_pairs={{0,1},{1,0},{2,3},{3,2},{4,5},{5,4},{6,7},{7,6},{8,9},{9,8},{10,11... | collective-permute-start | bytes 7077896 | tf_op jit(solution)/shard_map/ppermute | solution.py:172
  148.6 20.3 %collective-permute-start.29 = (bf16[576,768]{1,0:T(8,128)(2,1)S(1)}, bf16[576,768]{1,0:T(8,128)(2,1)S(1)}, u32[]{:S(2)}, u32[]{:S(2)}) collective-permute-start(bf16[576,768]{1,0:T(8,128)(2,1)S(1)} %get-tuple-element.150), channel_id=1, source_target_pairs={{0,4},{1,5},{2,6},{3,7},{4,0},{5,1},{6,2},{7,3},{8,12},{9,13},{10,... | collective-permute-start | bytes 2654216 | tf_op jit(solution)/shard_map/ppermute | solution.py:164
  149.4 19.5 %collective-permute-start.30 = (bf16[576,768]{1,0:T(8,128)(2,1)S(1)}, bf16[576,768]{1,0:T(8,128)(2,1)S(1)}, u32[]{:S(2)}, u32[]{:S(2)}) collective-permute-start(bf16[576,768]{1,0:T(8,128)(2,1)S(1)} %get-tuple-element.149), channel_id=1, source_target_pairs={{0,2},{1,3},{2,0},{3,1},{4,6},{5,7},{6,4},{7,5},{8,10},{9,11},{10,... | collective-permute-start | bytes 2654216 | tf_op jit(solution)/shard_map/ppermute | solution.py:168
  150.2 21.5 %collective-permute-start.38 = (bf16[96,768]{1,0:T(8,128)(2,1)S(1)}, bf16[96,768]{1,0:T(8,128)(2,1)S(1)}, u32[]{:S(2)}, u32[]{:S(2)}) collective-permute-start(bf16[96,768]{1,0:T(8,128)(2,1)S(1)} %copy-done.30), channel_id=1, source_target_pairs={{1,4},{3,6},{4,1},{6,3},{9,12},{11,14},{12,9},{14,11},{17,20},{19,... | collective-permute-start | bytes 442376 | tf_op jit(solution)/shard_map/ppermute | solution.py:185
  171.7 28.6 %collective-permute-start.46 = (bf16[1536,768]{1,0:T(8,128)(2,1)S(1)}, bf16[1536,768]{1,0:T(8,128)(2,1)}, u32[]{:S(2)}, u32[]{:S(2)}) collective-permute-start(bf16[1536,768]{1,0:T(8,128)(2,1)S(1)} %pad_maximum_fusion.refs_8_), channel_id=1, source_target_pairs={{0,1},{1,0},{2,3},{3,2},{4,5},{5,4},{6,7},{7,6},{8,9},{9,8},{10,11... | collective-permute-start | bytes 7077896 | tf_op jit(solution)/shard_map/ppermute | solution.py:172
  189.5 25.4 %collective-permute-start.50 = (bf16[1152,768]{1,0:T(8,128)(2,1)S(1)}, bf16[1152,768]{1,0:T(8,128)(2,1)}, u32[]{:S(2)}, u32[]{:S(2)}) collective-permute-start(bf16[1152,768]{1,0:T(8,128)(2,1)S(1)} %pad_maximum_fusion.1.refs_10_), channel_id=1, source_target_pairs={{0,1},{1,0},{2,3},{3,2},{4,5},{5,4},{6,7},{7,6},{8,9},{9,8},{10,11... | collective-permute-start | bytes 5308424 | tf_op jit(solution)/shard_map/ppermute | solution.py:172
  207.0 54.9 %collective-permute-start.43 = (bf16[96,768]{1,0:T(8,128)(2,1)}, bf16[96,768]{1,0:T(8,128)(2,1)S(1)}, u32[]{:S(2)}, u32[]{:S(2)}) collective-permute-start(bf16[96,768]{1,0:T(8,128)(2,1)} %get-tuple-element.116), channel_id=1, source_target_pairs={{0,3},{1,7},{2,1},{3,5},{4,2},{5,6},{6,0},{7,4},{8,11},{9,15},{10,... | collective-permute-start | bytes 442376 | tf_op jit(solution)/shard_map/ppermute | solution.py:197
  208.2 53.6 %collective-permute-start.42 = (bf16[96,768]{1,0:T(8,128)(2,1)}, bf16[96,768]{1,0:T(8,128)(2,1)S(1)}, u32[]{:S(2)}, u32[]{:S(2)}) collective-permute-start(bf16[96,768]{1,0:T(8,128)(2,1)} %get-tuple-element.115), channel_id=1, source_target_pairs={{0,2},{1,6},{2,0},{3,4},{4,3},{5,7},{6,1},{7,5},{8,10},{9,14},{10,... | collective-permute-start | bytes 442376 | tf_op jit(solution)/shard_map/ppermute | solution.py:197
  210.5 51.4 %collective-permute-start.41 = (bf16[96,768]{1,0:T(8,128)(2,1)}, bf16[96,768]{1,0:T(8,128)(2,1)S(1)}, u32[]{:S(2)}, u32[]{:S(2)}) collective-permute-start(bf16[96,768]{1,0:T(8,128)(2,1)} %get-tuple-element.114), channel_id=1, source_target_pairs={{0,1},{1,5},{2,3},{3,7},{4,0},{5,4},{6,2},{7,6},{8,9},{9,13},{10,1... | collective-permute-start | bytes 442376 | tf_op jit(solution)/shard_map/ppermute | solution.py:197
  210.6 51.3 %collective-permute-start.40 = (bf16[96,768]{1,0:T(8,128)(2,1)S(1)}, bf16[96,768]{1,0:T(8,128)(2,1)S(1)}, u32[]{:S(2)}, u32[]{:S(2)}) collective-permute-start(bf16[96,768]{1,0:T(8,128)(2,1)S(1)} %copy-done.34), channel_id=1, source_target_pairs={{0,0},{1,4},{2,2},{3,6},{4,1},{5,5},{6,3},{7,7},{8,8},{9,12},{10,1... | collective-permute-start | bytes 442376 | tf_op jit(solution)/shard_map/ppermute | solution.py:197
  (75 other events, 686.9 us)

commit v9 on v8

--- a/solution.py
+++ b/solution.py
@@ -458,8 +458,8 @@
     got_x, got_y, got_o, turned_i2 = stage(
         swap_x(to_x),
         swap_y(to_y),
-        swap_outer(after(jnp.concatenate([turned_i1, small_i2]), to_x, to_y)),
-        swap_inner(after(turned_o1, to_x, to_y)),
+        swap_outer(jnp.concatenate([turned_i1, small_i2])),
+        swap_inner(turned_o1),
     )
     turned_o2, small_o3 = got_o[:rows_right], got_o[rows_right:]
     small_2 = ordered_pair(

time: 265 us -> 265 us (level)
  no operation moved by 1% of the time
where the time goes in v9:
time: 265 us; the launch traced here: 264 us
  starting transfers between devices  83.2 us (31%)
  waiting for transfers between devices  75.1 us (28%)
  Pallas kernels  54.6 us (21%)
  other arithmetic  20.5 us (8%)
  local copies, waits for them, and re-layouts  15.5 us (6%)
  matrix products  13.2 us (5%)
    pallas_call x1, Pallas kernels, refresh(): pl.pallas_call(refresh_kernel, out_shape=[jax.ShapeDtypeStruct((count, ta...  45.9 us
    ppermute x10, waiting for transfers between devices, swap_x(): return lax.ppermute(a, AXES, pairs(lambda z, x, y, c: (z, 1 - x, y, c)))  31.5 us
    ppermute x11, starting transfers between devices, swap_core(): return lax.ppermute(a, AXES, pairs(lambda z, x, y, c: (z, x, y, 1 - c)))  25.5 us
    ppermute x6, waiting for transfers between devices, swap_inner(): lax.ppermute(a, AXES, pairs(lambda z, x, y, c: (3 - z if 0 < z < 3 else -...  19.4 us
    ppermute x6, starting transfers between devices, swap_inner(): lax.ppermute(a, AXES, pairs(lambda z, x, y, c: (3 - z if 0 < z < 3 else -...  17.5 us
    ppermute x3, starting transfers between devices, turn_over(): return jnp.where(straight, a, lax.ppermute(a, AXES, crossed))  12.3 us
    ppermute x10, starting transfers between devices, swap_y(): return lax.ppermute(a, AXES, pairs(lambda z, x, y, c: (z, x, 1 - y, c)))  9.96 us
    ppermute x3, waiting for transfers between devices, turn_over(): return jnp.where(straight, a, lax.ppermute(a, AXES, crossed))  9.81 us
  transfers between devices with their start and end apart: 53, of which 23 were waited for; matrix products, arithmetic and copies ran while one was open for 15% of the time, Pallas kernels for 21%

profile of v9, /device:TPU:9, one launch (start us, length us, event | category | flops | bytes accessed | tf_op | source)
XLA Modules:
  0.0 264.1 jit_solution(17603332867993046305)
XLA Ops:
  3.0 3.8 %collective-permute-start = (bf16[384,768]{1,0:T(8,128)(2,1)}, bf16[384,768]{1,0:T(8,128)(2,1)}, u32[]{:S(2)}, u32[]{:S(2)}) collective-permute-start(bf16[384,768]{1,0:T(8,128)(2,1)} %multiply_convert_fusion), channel_id=1, source_target_pairs={{1,4},{3,6},{4,1},{6,3},{9,12},{11,14},{12,9},{14,11},{17,20},{19,... | collective-permute-start | bytes 1769480 | tf_op jit(solution)/shard_map/ppermute | solution.py:185
  7.8 4.3 %collective-permute-start.2 = (bf16[144,768]{1,0:T(8,128)(2,1)}, bf16[144,768]{1,0:T(8,128)(2,1)}, u32[]{:S(2)}, u32[]{:S(2)}) collective-permute-start(bf16[144,768]{1,0:T(8,128)(2,1)} %get-tuple-element.161), channel_id=1, source_target_pairs={{8,16},{9,17},{10,18},{11,19},{12,20},{13,21},{14,22},{15,23},{16,... | collective-permute-start | bytes 663560 | tf_op jit(solution)/shard_map/ppermute | solution.py:180
  18.4 3.8 %collective-permute-start.3 = (bf16[528,768]{1,0:T(8,128)(2,1)S(1)}, bf16[528,768]{1,0:T(8,128)(2,1)S(1)}, u32[]{:S(2)}, u32[]{:S(2)}) collective-permute-start(bf16[528,768]{1,0:T(8,128)(2,1)S(1)} %get-tuple-element.150), channel_id=1, source_target_pairs={{8,16},{9,17},{10,18},{11,19},{12,20},{13,21},{14,22},{15,23},{16,... | collective-permute-start | bytes 2433032 | tf_op jit(solution)/shard_map/ppermute | solution.py:180
  25.4 8.9 %collective-permute-done.7 = bf16[288,768]{1,0:T(8,128)(2,1)S(1)} collective-permute-done((bf16[288,768]{1,0:T(8,128)(2,1)S(1)}, bf16[288,768]{1,0:T(8,128)(2,1)S(1)}, u32[]{:S(2)}, u32[]{:S(2)}) %collective-permute-start.7) | collective-permute-done | bytes 442400 | tf_op jit(solution)/shard_map/ppermute | solution.py:185
  34.5 6.2 %collective-permute-done.3 = bf16[528,768]{1,0:T(8,128)(2,1)S(1)} collective-permute-done((bf16[528,768]{1,0:T(8,128)(2,1)S(1)}, bf16[528,768]{1,0:T(8,128)(2,1)S(1)}, u32[]{:S(2)}, u32[]{:S(2)}) %collective-permute-start.3) | collective-permute-done | bytes 811040 | tf_op jit(solution)/shard_map/ppermute | solution.py:180
  49.5 11.1 %collective-permute-done.11 = bf16[384,768]{1,0:T(8,128)(2,1)S(1)} collective-permute-done((bf16[384,768]{1,0:T(8,128)(2,1)S(1)}, bf16[384,768]{1,0:T(8,128)(2,1)S(1)}, u32[]{:S(2)}, u32[]{:S(2)}) %collective-permute-start.11) | collective-permute-done | bytes 589856 | tf_op jit(solution)/shard_map/ppermute | solution.py:180
  66.5 3.1 %collective-permute-start.15 = (bf16[768,768]{1,0:T(8,128)(2,1)S(1)}, bf16[768,768]{1,0:T(8,128)(2,1)S(1)}, u32[]{:S(2)}, u32[]{:S(2)}) collective-permute-start(bf16[768,768]{1,0:T(8,128)(2,1)S(1)} %pad_maximum_fusion.3), channel_id=1, source_target_pairs={{0,1},{1,0},{2,3},{3,2},{4,5},{5,4},{6,7},{7,6},{8,9},{9,8},{10,11... | collective-permute-start | bytes 3538952 | tf_op jit(solution)/shard_map/ppermute | solution.py:172
  70.0 5.3 %collective-permute-done.12 = bf16[384,768]{1,0:T(8,128)(2,1)S(1)} collective-permute-done((bf16[384,768]{1,0:T(8,128)(2,1)S(1)}, bf16[384,768]{1,0:T(8,128)(2,1)S(1)}, u32[]{:S(2)}, u32[]{:S(2)}) %collective-permute-start.12) | collective-permute-done | bytes 589856 | tf_op jit(solution)/shard_map/ppermute | solution.py:176
  75.3 2.9 %collective-permute-done.13 = bf16[432,768]{1,0:T(8,128)(2,1)S(1)} collective-permute-done((bf16[432,768]{1,0:T(8,128)(2,1)S(1)}, bf16[432,768]{1,0:T(8,128)(2,1)S(1)}, u32[]{:S(2)}, u32[]{:S(2)}) %collective-permute-start.13) | collective-permute-done | bytes 663584 | tf_op jit(solution)/shard_map/ppermute | solution.py:164
  81.0 4.0 %collective-permute-start.18 = (bf16[4,384,768]{2,1,0:T(8,128)(2,1)S(1)}, bf16[4,384,768]{2,1,0:T(8,128)(2,1)S(1)}, u32[]{:S(2)}, u32[]{:S(2)}) collective-permute-start(bf16[4,384,768]{2,1,0:T(8,128)(2,1)S(1)} %bitcast_dynamic-update-slice_fusion.2), channel_id=1, source_target_pairs={{0,1},{1,0},{2,3},{3,2},{4,5},{5,4},{6,7},{7,6},{8,9},{9,8},{10,11... | collective-permute-start | bytes 7077896 | tf_op jit(solution)/shard_map/ppermute | solution.py:172
  86.2 3.0 %collective-permute-done.18 = bf16[4,384,768]{2,1,0:T(8,128)(2,1)S(1)} collective-permute-done((bf16[4,384,768]{2,1,0:T(8,128)(2,1)S(1)}, bf16[4,384,768]{2,1,0:T(8,128)(2,1)S(1)}, u32[]{:S(2)}, u32[]{:S(2)}) %collective-permute-start.18) | collective-permute-done | bytes 2359328 | tf_op jit(solution)/shard_map/ppermute | solution.py:172
  110.0 3.3 %fusion = f32[384,768]{1,0:T(8,128)} fusion(bf16[768,1536]{1,0:T(8,128)(2,1)} %bitcast.146, s32[]{:T(128)S(6)} %select_n.371, f32[384,768]{1,0:T(8,128)S(1)} %copy-done.3, bf16[768,1536]{1,0:T(8,128)(2,1)} %copy-done.6, s32[]{:T(128)S(6)} %select_n.383, pred[]{:T(512)S(6)} %eq.36), kind=kOutput, calls=%fused_computation.7 | convolution fusion | flops 454164480 | bytes 4718601 | tf_op jit(solution)/shard_map/dot_general | solution.py:145
  124.9 3.0 %collective-permute-start.33 = (bf16[1152,768]{1,0:T(8,128)(2,1)S(1)}, bf16[1152,768]{1,0:T(8,128)(2,1)S(1)}, u32[]{:S(2)}, u32[]{:S(2)}) collective-permute-start(bf16[1152,768]{1,0:T(8,128)(2,1)S(1)} %constant_dynamic-update-slice_fusion.refs_4_), channel_id=1, source_target_pairs={{0,1},{1,0},{2,3},{3,2},{4,5},{5,4},{6,7},{7,6},{8,9},{9,8},{10,11... | collective-permute-start | bytes 5308424 | tf_op jit(solution)/shard_map/ppermute | solution.py:172
  129.0 10.3 %collective-permute-done.27 = bf16[576,768]{1,0:T(8,128)(2,1)S(1)} collective-permute-done((bf16[576,768]{1,0:T(8,128)(2,1)S(1)}, bf16[576,768]{1,0:T(8,128)(2,1)S(1)}, u32[]{:S(2)}, u32[]{:S(2)}) %collective-permute-start.27) | collective-permute-done | bytes 884768 | tf_op jit(solution)/shard_map/ppermute | solution.py:164
  140.1 2.8 %collective-permute-start.32 = (bf16[208,768]{1,0:T(8,128)(2,1)S(1)}, bf16[208,768]{1,0:T(8,128)(2,1)S(1)}, u32[]{:S(2)}, u32[]{:S(2)}) collective-permute-start(bf16[208,768]{1,0:T(8,128)(2,1)S(1)} %slice.222), channel_id=1, source_target_pairs={{8,16},{9,17},{10,18},{11,19},{12,20},{13,21},{14,22},{15,23},{16,... | collective-permute-start | bytes 958472 | tf_op jit(solution)/shard_map/ppermute | solution.py:180
  143.1 4.1 %collective-permute-start.37 = (bf16[1536,768]{1,0:T(8,128)(2,1)S(1)}, bf16[1536,768]{1,0:T(8,128)(2,1)S(1)}, u32[]{:S(2)}, u32[]{:S(2)}) collective-permute-start(bf16[1536,768]{1,0:T(8,128)(2,1)S(1)} %constant_dynamic-update-slice_fusion.3.refs_6_), channel_id=1, source_target_pairs={{0,1},{1,0},{2,3},{3,2},{4,5},{5,4},{6,7},{7,6},{8,9},{9,8},{10,11... | collective-permute-start | bytes 7077896 | tf_op jit(solution)/shard_map/ppermute | solution.py:172
  150.1 6.2 %collective-permute-start.38 = (bf16[96,768]{1,0:T(8,128)(2,1)S(1)}, bf16[96,768]{1,0:T(8,128)(2,1)S(1)}, u32[]{:S(2)}, u32[]{:S(2)}) collective-permute-start(bf16[96,768]{1,0:T(8,128)(2,1)S(1)} %copy-done.30), channel_id=1, source_target_pairs={{1,4},{3,6},{4,1},{6,3},{9,12},{11,14},{12,9},{14,11},{17,20},{19,... | collective-permute-start | bytes 442376 | tf_op jit(solution)/shard_map/ppermute | solution.py:185
  156.2 12.5 %collective-permute-done.29 = bf16[576,768]{1,0:T(8,128)(2,1)S(1)} collective-permute-done((bf16[576,768]{1,0:T(8,128)(2,1)S(1)}, bf16[576,768]{1,0:T(8,128)(2,1)S(1)}, u32[]{:S(2)}, u32[]{:S(2)}) %collective-permute-start.29) | collective-permute-done | bytes 884768 | tf_op jit(solution)/shard_map/ppermute | solution.py:164
  171.5 3.0 %collective-permute-start.46 = (bf16[1536,768]{1,0:T(8,128)(2,1)S(1)}, bf16[1536,768]{1,0:T(8,128)(2,1)}, u32[]{:S(2)}, u32[]{:S(2)}) collective-permute-start(bf16[1536,768]{1,0:T(8,128)(2,1)S(1)} %pad_maximum_fusion.refs_8_), channel_id=1, source_target_pairs={{0,1},{1,0},{2,3},{3,2},{4,5},{5,4},{6,7},{7,6},{8,9},{9,8},{10,11... | collective-permute-start | bytes 7077896 | tf_op jit(solution)/shard_map/ppermute | solution.py:172
  176.6 4.9 %collective-permute-done.34 = bf16[384,768]{1,0:T(8,128)(2,1)S(1)} collective-permute-done((bf16[384,768]{1,0:T(8,128)(2,1)S(1)}, bf16[384,768]{1,0:T(8,128)(2,1)S(1)}, u32[]{:S(2)}, u32[]{:S(2)}) %collective-permute-start.34) | collective-permute-done | bytes 589856 | tf_op jit(solution)/shard_map/ppermute | solution.py:164
  181.6 4.0 %collective-permute-start.39 = (bf16[832,768]{1,0:T(8,128)(2,1)S(1)}, bf16[832,768]{1,0:T(8,128)(2,1)S(1)}, u32[]{:S(2)}, u32[]{:S(2)}) collective-permute-start(bf16[832,768]{1,0:T(8,128)(2,1)S(1)} %pad_maximum_fusion.2.core_ref), channel_id=1, source_target_pairs={{0,1},{1,0},{2,3},{3,2},{4,5},{5,4},{6,7},{7,6},{8,9},{9,8},{10,11... | collective-permute-start | bytes 3833864 | tf_op jit(solution)/shard_map/ppermute | solution.py:172
  190.6 8.7 %shard_map.126 = (f32[96,768]{1,0:T(8,128)}, f32[8,128]{1,0:T(8,128)}, bf16[96,768]{1,0:T(8,128)(2,1)}, bf16[96,768]{1,0:T(8,128)(2,1)}, bf16[96,768]{1,0:T(8,128)(2,1)}, /*index=5*/bf16[96,768]{1,0:T(8,128)(2,1)}) custom-call(s32[12]{0:T(128)} %stack.63.place_ref, bf16[832,768]{1,0:T(8,128)(2,1)} %copy-done.1, bf16[832,768]{1,0:T(8,128)(2,1)} %copy-done.13, ...), custom_call_target="tpu_custom_call" | custom-call | flops 1472200704 | bytes 7077888 | tf_op jit(solution)/shard_map/pallas_call | solution.py:386
  210.5 4.3 %collective-permute-start.40 = (bf16[96,768]{1,0:T(8,128)(2,1)S(1)}, bf16[96,768]{1,0:T(8,128)(2,1)S(1)}, u32[]{:S(2)}, u32[]{:S(2)}) collective-permute-start(bf16[96,768]{1,0:T(8,128)(2,1)S(1)} %copy-done.34), channel_id=1, source_target_pairs={{0,0},{1,4},{2,2},{3,6},{4,1},{5,5},{6,3},{7,7},{8,8},{9,12},{10,1... | collective-permute-start | bytes 442376 | tf_op jit(solution)/shard_map/ppermute | solution.py:197
  214.8 45.9 %shard_map.127 = (f32[192,768]{1,0:T(8,128)}, f32[192,768]{1,0:T(8,128)}) custom-call(s32[2]{0:T(128)} %pad_add_fusion.place_ref, f32[8,128]{1,0:T(8,128)} %get-tuple-element.124.refs_0_, f32[8,128]{1,0:T(8,128)} %copy-done.36, f32[8,128]{1,0:T(8,128)} %copy-done.37, f32[8,128]{1,0:T(8,128)} %copy-done.38, bf16[1152,768]{1,0:T(8,128)(2,1)} %copy-done.27, ...), custom_call_target="tpu_custom_call" | custom-call | flops 27179089920 | bytes 18874368 | tf_op jit(solution)/shard_map/pallas_call | solution.py:320
  (290 shorter events, 92.9 us)
Async XLA Ops:
  13.0 21.4 %collective-permute-start.5 = (bf16[384,768]{1,0:T(8,128)(2,1)}, bf16[384,768]{1,0:T(8,128)(2,1)S(1)}, u32[]{:S(2)}, u32[]{:S(2)}) collective-permute-start(bf16[384,768]{1,0:T(8,128)(2,1)} %convert_element_type.65), channel_id=1, source_target_pairs={{0,2},{1,3},{2,0},{3,1},{4,6},{5,7},{6,4},{7,5},{8,10},{9,11},{10,... | collective-permute-start | bytes 1769480 | tf_op jit(solution)/shard_map/ppermute | solution.py:168
  14.3 20.2 %collective-permute-start.6 = (bf16[384,768]{1,0:T(8,128)(2,1)}, bf16[384,768]{1,0:T(8,128)(2,1)}, u32[]{:S(2)}, u32[]{:S(2)}) collective-permute-start(bf16[384,768]{1,0:T(8,128)(2,1)} %convert_element_type.65), channel_id=1, source_target_pairs={{0,4},{1,5},{2,6},{3,7},{4,0},{5,1},{6,2},{7,3},{8,12},{9,13},{10,... | collective-permute-start | bytes 1769480 | tf_op jit(solution)/shard_map/ppermute | solution.py:164
  18.4 22.3 %collective-permute-start.3 = (bf16[528,768]{1,0:T(8,128)(2,1)S(1)}, bf16[528,768]{1,0:T(8,128)(2,1)S(1)}, u32[]{:S(2)}, u32[]{:S(2)}) collective-permute-start(bf16[528,768]{1,0:T(8,128)(2,1)S(1)} %get-tuple-element.150), channel_id=1, source_target_pairs={{8,16},{9,17},{10,18},{11,19},{12,20},{13,21},{14,22},{15,23},{16,... | collective-permute-start | bytes 2433032 | tf_op jit(solution)/shard_map/ppermute | solution.py:180
  22.2 19.8 %collective-permute-start.4 = (bf16[528,768]{1,0:T(8,128)(2,1)S(1)}, bf16[528,768]{1,0:T(8,128)(2,1)S(1)}, u32[]{:S(2)}, u32[]{:S(2)}) collective-permute-start(bf16[528,768]{1,0:T(8,128)(2,1)S(1)} %get-tuple-element.149), channel_id=1, source_target_pairs={{0,8},{1,9},{2,10},{3,11},{4,12},{5,13},{6,14},{7,15},{8,0},{9,1},... | collective-permute-start | bytes 2433032 | tf_op jit(solution)/shard_map/ppermute | solution.py:176
  43.0 18.9 %collective-permute-start.10 = (bf16[528,768]{1,0:T(8,128)(2,1)S(1)}, bf16[528,768]{1,0:T(8,128)(2,1)S(1)}, u32[]{:S(2)}, u32[]{:S(2)}) collective-permute-start(bf16[528,768]{1,0:T(8,128)(2,1)S(1)} %collective-permute-done.3), channel_id=1, source_target_pairs={{0,8},{1,9},{2,10},{3,11},{4,12},{5,13},{6,14},{7,15},{8,0},{9,1},... | collective-permute-start | bytes 2433032 | tf_op jit(solution)/shard_map/ppermute | solution.py:176
  43.4 17.3 %collective-permute-start.8 = (bf16[480,768]{1,0:T(8,128)(2,1)S(1)}, bf16[480,768]{1,0:T(8,128)(2,1)S(1)}, u32[]{:S(2)}, u32[]{:S(2)}) collective-permute-start(bf16[480,768]{1,0:T(8,128)(2,1)S(1)} %get-tuple-element.154), channel_id=1, source_target_pairs={{0,4},{1,5},{2,6},{3,7},{4,0},{5,1},{6,2},{7,3},{8,12},{9,13},{10,... | collective-permute-start | bytes 2211848 | tf_op jit(solution)/shard_map/ppermute | solution.py:164
  43.5 17.3 %collective-permute-start.9 = (bf16[480,768]{1,0:T(8,128)(2,1)S(1)}, bf16[480,768]{1,0:T(8,128)(2,1)S(1)}, u32[]{:S(2)}, u32[]{:S(2)}) collective-permute-start(bf16[480,768]{1,0:T(8,128)(2,1)S(1)} %get-tuple-element.153), channel_id=1, source_target_pairs={{0,2},{1,3},{2,0},{3,1},{4,6},{5,7},{6,4},{7,5},{8,10},{9,11},{10,... | collective-permute-start | bytes 2211848 | tf_op jit(solution)/shard_map/ppermute | solution.py:168
  97.0 16.3 %collective-permute-start.21 = (bf16[384,768]{1,0:T(8,128)(2,1)S(1)}, bf16[384,768]{1,0:T(8,128)(2,1)}, u32[]{:S(2)}, u32[]{:S(2)}) collective-permute-start(bf16[384,768]{1,0:T(8,128)(2,1)S(1)} %fusion.2), channel_id=1, source_target_pairs={{0,4},{1,5},{2,6},{3,7},{4,0},{5,1},{6,2},{7,3},{8,12},{9,13},{10,... | collective-permute-start | bytes 1769480 | tf_op jit(solution)/shard_map/ppermute | solution.py:164
  116.0 24.0 %collective-permute-start.25 = (bf16[592,768]{1,0:T(8,128)(2,1)S(1)}, bf16[592,768]{1,0:T(8,128)(2,1)S(1)}, u32[]{:S(2)}, u32[]{:S(2)}) collective-permute-start(bf16[592,768]{1,0:T(8,128)(2,1)S(1)} %get-tuple-element.156), channel_id=1, source_target_pairs={{0,8},{1,9},{2,10},{3,11},{4,12},{5,13},{6,14},{7,15},{8,0},{9,1},... | collective-permute-start | bytes 2727944 | tf_op jit(solution)/shard_map/ppermute | solution.py:176
  116.1 23.9 %collective-permute-start.26 = (bf16[592,768]{1,0:T(8,128)(2,1)S(1)}, bf16[592,768]{1,0:T(8,128)(2,1)S(1)}, u32[]{:S(2)}, u32[]{:S(2)}) collective-permute-start(bf16[592,768]{1,0:T(8,128)(2,1)S(1)} %get-tuple-element.155), channel_id=1, source_target_pairs={{8,16},{9,17},{10,18},{11,19},{12,20},{13,21},{14,22},{15,23},{16,... | collective-permute-start | bytes 2727944 | tf_op jit(solution)/shard_map/ppermute | solution.py:180
  120.6 18.7 %collective-permute-start.27 = (bf16[576,768]{1,0:T(8,128)(2,1)S(1)}, bf16[576,768]{1,0:T(8,128)(2,1)S(1)}, u32[]{:S(2)}, u32[]{:S(2)}) collective-permute-start(bf16[576,768]{1,0:T(8,128)(2,1)S(1)} %get-tuple-element.148), channel_id=1, source_target_pairs={{0,4},{1,5},{2,6},{3,7},{4,0},{5,1},{6,2},{7,3},{8,12},{9,13},{10,... | collective-permute-start | bytes 2654216 | tf_op jit(solution)/shard_map/ppermute | solution.py:164
  121.6 18.3 %collective-permute-start.28 = (bf16[576,768]{1,0:T(8,128)(2,1)S(1)}, bf16[576,768]{1,0:T(8,128)(2,1)S(1)}, u32[]{:S(2)}, u32[]{:S(2)}) collective-permute-start(bf16[576,768]{1,0:T(8,128)(2,1)S(1)} %get-tuple-element.147), channel_id=1, source_target_pairs={{0,2},{1,3},{2,0},{3,1},{4,6},{5,7},{6,4},{7,5},{8,10},{9,11},{10,... | collective-permute-start | bytes 2654216 | tf_op jit(solution)/shard_map/ppermute | solution.py:168
  124.9 25.2 %collective-permute-start.33 = (bf16[1152,768]{1,0:T(8,128)(2,1)S(1)}, bf16[1152,768]{1,0:T(8,128)(2,1)S(1)}, u32[]{:S(2)}, u32[]{:S(2)}) collective-permute-start(bf16[1152,768]{1,0:T(8,128)(2,1)S(1)} %constant_dynamic-update-slice_fusion.refs_4_), channel_id=1, source_target_pairs={{0,1},{1,0},{2,3},{3,2},{4,5},{5,4},{6,7},{7,6},{8,9},{9,8},{10,11... | collective-permute-start | bytes 5308424 | tf_op jit(solution)/shard_map/ppermute | solution.py:172
  140.0 28.8 %collective-permute-start.31 = (bf16[592,768]{1,0:T(8,128)(2,1)S(1)}, bf16[592,768]{1,0:T(8,128)(2,1)S(1)}, u32[]{:S(2)}, u32[]{:S(2)}) collective-permute-start(bf16[592,768]{1,0:T(8,128)(2,1)S(1)} %collective-permute-done.26), channel_id=1, source_target_pairs={{0,8},{1,9},{2,10},{3,11},{4,12},{5,13},{6,14},{7,15},{8,0},{9,1},... | collective-permute-start | bytes 2727944 | tf_op jit(solution)/shard_map/ppermute | solution.py:176
  143.1 38.4 %collective-permute-start.37 = (bf16[1536,768]{1,0:T(8,128)(2,1)S(1)}, bf16[1536,768]{1,0:T(8,128)(2,1)S(1)}, u32[]{:S(2)}, u32[]{:S(2)}) collective-permute-start(bf16[1536,768]{1,0:T(8,128)(2,1)S(1)} %constant_dynamic-update-slice_fusion.3.refs_6_), channel_id=1, source_target_pairs={{0,1},{1,0},{2,3},{3,2},{4,5},{5,4},{6,7},{7,6},{8,9},{9,8},{10,11... | collective-permute-start | bytes 7077896 | tf_op jit(solution)/shard_map/ppermute | solution.py:172
  148.4 20.3 %collective-permute-start.29 = (bf16[576,768]{1,0:T(8,128)(2,1)S(1)}, bf16[576,768]{1,0:T(8,128)(2,1)S(1)}, u32[]{:S(2)}, u32[]{:S(2)}) collective-permute-start(bf16[576,768]{1,0:T(8,128)(2,1)S(1)} %get-tuple-element.146), channel_id=1, source_target_pairs={{0,4},{1,5},{2,6},{3,7},{4,0},{5,1},{6,2},{7,3},{8,12},{9,13},{10,... | collective-permute-start | bytes 2654216 | tf_op jit(solution)/shard_map/ppermute | solution.py:164
  149.2 19.5 %collective-permute-start.30 = (bf16[576,768]{1,0:T(8,128)(2,1)S(1)}, bf16[576,768]{1,0:T(8,128)(2,1)S(1)}, u32[]{:S(2)}, u32[]{:S(2)}) collective-permute-start(bf16[576,768]{1,0:T(8,128)(2,1)S(1)} %get-tuple-element.145), channel_id=1, source_target_pairs={{0,2},{1,3},{2,0},{3,1},{4,6},{5,7},{6,4},{7,5},{8,10},{9,11},{10,... | collective-permute-start | bytes 2654216 | tf_op jit(solution)/shard_map/ppermute | solution.py:168
  150.1 21.5 %collective-permute-start.38 = (bf16[96,768]{1,0:T(8,128)(2,1)S(1)}, bf16[96,768]{1,0:T(8,128)(2,1)S(1)}, u32[]{:S(2)}, u32[]{:S(2)}) collective-permute-start(bf16[96,768]{1,0:T(8,128)(2,1)S(1)} %copy-done.30), channel_id=1, source_target_pairs={{1,4},{3,6},{4,1},{6,3},{9,12},{11,14},{12,9},{14,11},{17,20},{19,... | collective-permute-start | bytes 442376 | tf_op jit(solution)/shard_map/ppermute | solution.py:185
  171.5 28.6 %collective-permute-start.46 = (bf16[1536,768]{1,0:T(8,128)(2,1)S(1)}, bf16[1536,768]{1,0:T(8,128)(2,1)}, u32[]{:S(2)}, u32[]{:S(2)}) collective-permute-start(bf16[1536,768]{1,0:T(8,128)(2,1)S(1)} %pad_maximum_fusion.refs_8_), channel_id=1, source_target_pairs={{0,1},{1,0},{2,3},{3,2},{4,5},{5,4},{6,7},{7,6},{8,9},{9,8},{10,11... | collective-permute-start | bytes 7077896 | tf_op jit(solution)/shard_map/ppermute | solution.py:172
  189.4 25.4 %collective-permute-start.50 = (bf16[1152,768]{1,0:T(8,128)(2,1)S(1)}, bf16[1152,768]{1,0:T(8,128)(2,1)}, u32[]{:S(2)}, u32[]{:S(2)}) collective-permute-start(bf16[1152,768]{1,0:T(8,128)(2,1)S(1)} %pad_maximum_fusion.1.refs_10_), channel_id=1, source_target_pairs={{0,1},{1,0},{2,3},{3,2},{4,5},{5,4},{6,7},{7,6},{8,9},{9,8},{10,11... | collective-permute-start | bytes 5308424 | tf_op jit(solution)/shard_map/ppermute | solution.py:172
  206.9 54.8 %collective-permute-start.43 = (bf16[96,768]{1,0:T(8,128)(2,1)}, bf16[96,768]{1,0:T(8,128)(2,1)S(1)}, u32[]{:S(2)}, u32[]{:S(2)}) collective-permute-start(bf16[96,768]{1,0:T(8,128)(2,1)} %get-tuple-element.112), channel_id=1, source_target_pairs={{0,3},{1,7},{2,1},{3,5},{4,2},{5,6},{6,0},{7,4},{8,11},{9,15},{10,... | collective-permute-start | bytes 442376 | tf_op jit(solution)/shard_map/ppermute | solution.py:197
  208.1 53.6 %collective-permute-start.42 = (bf16[96,768]{1,0:T(8,128)(2,1)}, bf16[96,768]{1,0:T(8,128)(2,1)S(1)}, u32[]{:S(2)}, u32[]{:S(2)}) collective-permute-start(bf16[96,768]{1,0:T(8,128)(2,1)} %get-tuple-element.111), channel_id=1, source_target_pairs={{0,2},{1,6},{2,0},{3,4},{4,3},{5,7},{6,1},{7,5},{8,10},{9,14},{10,... | collective-permute-start | bytes 442376 | tf_op jit(solution)/shard_map/ppermute | solution.py:197
  210.4 51.3 %collective-permute-start.41 = (bf16[96,768]{1,0:T(8,128)(2,1)}, bf16[96,768]{1,0:T(8,128)(2,1)S(1)}, u32[]{:S(2)}, u32[]{:S(2)}) collective-permute-start(bf16[96,768]{1,0:T(8,128)(2,1)} %get-tuple-element.110), channel_id=1, source_target_pairs={{0,1},{1,5},{2,3},{3,7},{4,0},{5,4},{6,2},{7,6},{8,9},{9,13},{10,1... | collective-permute-start | bytes 442376 | tf_op jit(solution)/shard_map/ppermute | solution.py:197
  210.5 51.3 %collective-permute-start.40 = (bf16[96,768]{1,0:T(8,128)(2,1)S(1)}, bf16[96,768]{1,0:T(8,128)(2,1)S(1)}, u32[]{:S(2)}, u32[]{:S(2)}) collective-permute-start(bf16[96,768]{1,0:T(8,128)(2,1)S(1)} %copy-done.34), channel_id=1, source_target_pairs={{0,0},{1,4},{2,2},{3,6},{4,1},{5,5},{6,3},{7,7},{8,8},{9,12},{10,1... | collective-permute-start | bytes 442376 | tf_op jit(solution)/shard_map/ppermute | solution.py:197
  (75 other events, 686.9 us)
